TPU v7x, 32 devices: a whole 2x2x4 slice. The times are simulated.
32 devices in a mesh: dp: 16 (over z, x, core), seq: 2 (over y).
Axes of the slice: x: 2, y: 2, z: 4, core: 2. Of those that a mesh axis runs over, the one named last changes fastest.
Arguments:
- grad_out: bfloat16 [16, 256, 6144], P('dp', 'seq'), may hold values from -6 to 6
- queries: bfloat16 [16, 256, 3072], P('dp', 'seq'), may hold values from -40 to 40
- keys: bfloat16 [16, 256, 3072], P('dp', 'seq'), may hold values from -12 to 12
- values: bfloat16 [16, 256, 3072], P('dp', 'seq'), may hold values from -6 to 6
- out_weight: bfloat16 [6144, 3072], P('dp', 'seq'), may hold values from -0.109375 to 0.109375
Outputs:
- query_grad: bfloat16 [16, 256, 3072], P('dp', 'seq')
- key_grad: bfloat16 [16, 256, 3072], P('dp', 'seq')
- value_grad: bfloat16 [16, 256, 3072], P('dp', 'seq')
- weight_grad: float32 [6144, 3072], P('dp', 'seq')
All inputs are finite; a program needn't handle non-finite values.
Results may differ from a plain program's by a relative error of at most 0.03.
Values may be sent and summed in bfloat16 or wider, within the bound.
No kernel may reach another device: no remote copies, remote signals or barrier semaphores. Data moves between devices by JAX's collectives and lax.ppermute only.
A program may use at most 128 MiB of HBM per device.

v0:
```python
import functools
import math

import jax
import jax.numpy as jnp
from jax import lax
from jax.experimental import pallas as pl
from jax.experimental.pallas import tpu as pltpu
from jax.sharding import PartitionSpec as P

HEAD_DIM = 128


def dot(a, b, contract):
    return lax.dot_general(a, b, (contract, ((), ())), preferred_element_type=jnp.float32)


def attention_kernel(
    heads,
    mine_ref,
    q_own,
    q_far,
    k_own,
    k_far,
    v_own,
    v_far,
    grad_ref,
    dq_own,
    dq_far,
    dk_own,
    dk_far,
    dv_own,
    dv_far,
    att_ref,
):
    inverse_root = 1.0 / math.sqrt(HEAD_DIM)
    tokens = q_own.shape[0]
    for head in range(heads):
        at = slice(head * HEAD_DIM, (head + 1) * HEAD_DIM)
        q = jnp.concatenate([q_own[:, at], q_far[:, at]], axis=0)
        k = jnp.concatenate([k_own[:, at], k_far[:, at]], axis=0)
        v = jnp.concatenate([v_own[:, at], v_far[:, at]], axis=0)
        g = grad_ref[:, at]
        scores = dot(q, k, ((1,), (1,))) * inverse_root
        raised = jnp.exp(scores - jnp.max(scores, axis=-1, keepdims=True))
        probs = raised * (1.0 / jnp.sum(raised, axis=-1, keepdims=True))
        low = probs.astype(jnp.bfloat16)
        att = dot(low, v, ((1,), (0,))).astype(jnp.bfloat16)
        att_ref[:, at] = att
        delta = jnp.sum(
            g.astype(jnp.float32) * att.astype(jnp.float32), axis=-1, keepdims=True
        )
        d_probs = dot(g, v, ((1,), (1,)))
        d_low = (probs * (d_probs - delta)).astype(jnp.bfloat16)
        dq = (dot(d_low, k, ((1,), (0,))) * inverse_root).astype(jnp.bfloat16)
        dk = (dot(d_low, q, ((0,), (0,))) * inverse_root).astype(jnp.bfloat16)
        dv = dot(low, g, ((0,), (0,))).astype(jnp.bfloat16)
        for own, far, value in ((dq_own, dq_far, dq), (dk_own, dk_far, dk), (dv_own, dv_far, dv)):
            own[:, at] = value[:tokens]
            far[:, at] = value[tokens:]


def attention(mine, own, far, grad):
    tokens, width = own[0].shape
    features = far[0].shape[1]
    heads = features // HEAD_DIM
    length = grad.shape[0]
    step = 2 if heads % 2 == 0 and length <= 512 else 1
    grid = heads // step
    block = step * HEAD_DIM
    own_spec = pl.BlockSpec((tokens, block), lambda h, mine: (0, mine[0] * grid + h))
    far_spec = pl.BlockSpec((length - tokens, block), lambda h, mine: (0, h))
    all_spec = pl.BlockSpec((length, block), lambda h, mine: (0, h))
    shape = lambda rows, columns: jax.ShapeDtypeStruct((rows, columns), jnp.bfloat16)
    outs = [shape(tokens, width), shape(length - tokens, features)] * 3 + [shape(length, features)]
    return pl.pallas_call(
        functools.partial(attention_kernel, step),
        grid_spec=pltpu.PrefetchScalarGridSpec(
            num_scalar_prefetch=1,
            grid=(grid,),
            in_specs=[own_spec, far_spec] * 3 + [all_spec],
            out_specs=[own_spec, far_spec] * 3 + [all_spec],
        ),
        out_shape=outs,
        compiler_params=pltpu.CompilerParams(vmem_limit_bytes=48 * 1024 * 1024),
        cost_estimate=pl.CostEstimate(
            flops=12 * heads * length * length * HEAD_DIM,
            bytes_accessed=16 * length * features,
            transcendentals=heads * length * length,
        ),
        name="attention",
    )(mine, own[0], far[0], own[1], far[1], own[2], far[2], grad)


def shards(grad_out, queries, keys, values, out_weight):
    dp = lax.axis_size("dp")
    seq = lax.axis_size("seq")
    mine = lax.axis_index("seq")
    tokens, width = grad_out.shape[1:]
    features = out_weight.shape[1]
    length = tokens * seq
    rows = out_weight.shape[0]
    token_scale = 1.0 / math.sqrt(dp * length)

    def shift(array, by):
        return lax.ppermute(array, "seq", [(i, (i + by) % seq) for i in range(seq)])

    whole_rows = lax.all_gather(out_weight, "dp", axis=0, tiled=True)

    own_grad = grad_out[0]
    own = (queries[0], keys[0], values[0])
    pieces = []
    for by in range(1, seq):
        start = ((mine + by) % seq) * features
        pieces.append(
            shift(
                jnp.stack([lax.dynamic_slice_in_dim(part, start, features, 1) for part in own]), by
            )
        )
    arrived = pieces[0] if seq == 2 else jnp.concatenate(pieces, axis=1)
    far = (arrived[0], arrived[1], arrived[2])
    all_grad = jnp.concatenate([own_grad] + [shift(own_grad, by) for by in range(1, seq)], axis=0)

    by_rows = jnp.transpose(own_grad.reshape(tokens, dp, rows), (1, 0, 2))
    by_rows = lax.all_to_all(by_rows, "dp", split_axis=0, concat_axis=0, tiled=True)
    row_grad = jnp.concatenate([by_rows] + [shift(by_rows, by) for by in range(1, seq)], axis=1)
    row_grad = row_grad.reshape(dp * length, rows)

    d_attn = jnp.dot(all_grad, whole_rows, preferred_element_type=jnp.float32).astype(jnp.bfloat16)
    dq, dq_far, dk, dk_far, dv, dv_far, attended = attention(
        mine.astype(jnp.int32).reshape(1), own, far, d_attn
    )
    every = lax.all_gather(attended, "dp", axis=0, tiled=True)
    weight_grad = dot(row_grad, every, ((0,), (0,))) * token_scale

    leaving = jnp.stack([dq_far, dk_far, dv_far])
    result = [dq, dk, dv]
    for by in range(1, seq):
        back = shift(leaving[:, (by - 1) * tokens : by * tokens], seq - by)
        start = ((mine + by) % seq) * features
        result = [
            lax.dynamic_update_slice_in_dim(whole, back[i], start, 1)
            for i, whole in enumerate(result)
        ]
    return (result[0][None], result[1][None], result[2][None], weight_grad)


def solution(mesh):
    in_specs = (
        P("dp", "seq", None),
        P("dp", "seq", None),
        P("dp", "seq", None),
        P("dp", "seq", None),
        P("dp", "seq"),
    )
    out_specs = (P("dp", "seq", None), P("dp", "seq", None), P("dp", "seq", None), P("dp", "seq"))
    return jax.shard_map(shards, mesh=mesh, in_specs=in_specs, out_specs=out_specs, check_vma=False)
```

profile of v0, /device:TPU:0, one launch (start us, length us, event | category | flops | bytes accessed | tf_op | source)
XLA Modules:
  0.0 285.5 jit_solution(547348605971864530)
XLA Ops:
  7.2 0.0 all-gather.3.cloned.1.call-start
  7.2 0.7 all-gather.3.cloned.1.call-update
  7.9 0.0 all-gather.5.cloned.1.call-start
  8.0 0.0 copy-start.3
  8.0 1.1 constant_dynamic-slice_fusion.2
  9.1 1.2 constant_dynamic-slice_fusion
  10.3 0.1 pad_maximum_fusion.1
  10.4 3.0 %collective-permute-start = (bf16[3,128,1536]{2,1,0:T(8,128)(2,1)S(1)}, bf16[3,128,1536]{2,1,0:T(8,128)(2,1)S(1)}, u32[]{:S(2)}, u32[]{:S(2)}) collective-permute-start(bf16[3,128,1536]{2,1,0:T(8,128)(2,1)S(1)} %pad_maximum_fusion.1), channel_id=1, source_target_pairs={{0,1},{1,0},{2,3},{3,2},{4,5},{5,4},{6,7},{7,6},{8,9},{9,8},{10,11... | collective-permute-start | bytes 3538952 | tf_op jit(solution)/shard_map/ppermute | solution.py:106
  13.5 0.0 copy-done.3
  13.5 0.1 collective-permute-start.1
  13.6 26.7 %collective-permute-done = bf16[3,128,1536]{2,1,0:T(8,128)(2,1)S(1)} collective-permute-done((bf16[3,128,1536]{2,1,0:T(8,128)(2,1)S(1)}, bf16[3,128,1536]{2,1,0:T(8,128)(2,1)S(1)}, u32[]{:S(2)}, u32[]{:S(2)}) %collective-permute-start) | collective-permute-done | bytes 1179680 | tf_op jit(solution)/shard_map/ppermute | solution.py:106
  40.3 0.1 slice_bitcast_fusion
  40.4 0.0 copy-start
  40.4 32.9 %collective-permute-done.1 = bf16[128,6144]{1,0:T(8,128)(2,1)} collective-permute-done((bf16[128,6144]{1,0:T(8,128)(2,1)S(1)}, bf16[128,6144]{1,0:T(8,128)(2,1)}, u32[]{:S(2)}, u32[]{:S(2)}) %collective-permute-start.1) | collective-permute-done | bytes 1572896 | tf_op jit(solution)/shard_map/ppermute | solution.py:106
  73.2 38.0 %all-gather.3.cloned.1.call-done = bf16[6144,1536]{1,0:T(8,128)(2,1)} async-done(((bf16[384,1536]{1,0:T(8,128)(2,1)}), bf16[6144,1536]{1,0:T(8,128)(2,1)}) %all-gather.3.cloned.1.call-update) | async-done | bytes 18874384 | tf_op jit(solution)/shard_map/all_gather | solution.py:108
  111.3 10.6 %fusion.4.grad_ref = bf16[256,1536]{1,0:T(8,128)(2,1)} fusion(bf16[6144,1536]{1,0:T(8,128)(2,1)} %all-gather.3.cloned.1.call-done, bf16[128,6144]{1,0:T(8,128)(2,1)} %collective-permute-done.1, bf16[128,6144]{1,0:T(8,128)(2,1)} %bitcast.32), kind=kOutput, calls=%fused_computation.6 | convolution fusion | flops 4838522880 | bytes 22806528 | tf_op jit(solution)/shard_map/dot_general | solution.py:129
  121.9 0.0 copy-done
  121.9 0.0 copy-start.1
  121.9 1.1 copy-done.1
  123.0 0.0 copy-start.2
  123.0 1.1 copy-done.2
  124.2 12.0 %attention.1 = (bf16[128,3072]{1,0:T(8,128)(2,1)}, bf16[128,1536]{1,0:T(8,128)(2,1)S(1)}, bf16[128,3072]{1,0:T(8,128)(2,1)}, bf16[128,1536]{1,0:T(8,128)(2,1)S(1...) custom-call(s32[1]{0:T(128)} %bitcast.mine_ref, ...), custom_call_target="tpu_custom_call" | custom-call | flops 1207959552 | bytes 6291456 | tf_op jit(solution)/shard_map/attention/pallas_call | solution.py:76
  136.1 0.0 all-gather.5.cloned.1.call-update
  136.2 1.9 copy.9
  138.1 65.8 %all_to_all.5 = bf16[16,128,384]{1,2,0:T(8,128)(2,1)S(1)} all-to-all(bf16[16,128,384]{1,2,0:T(8,128)(2,1)S(1)} %bitcast.30), channel_id=1, replica_groups=mesh['dp'=16,'seq'=2] {'dp'}, dimensions={0} | all-to-all | bytes 3145728 | tf_op jit(solution)/shard_map/all_to_all | solution.py:125
  203.9 1.5 collective-permute-start.3
  205.4 1.1 pad_maximum_fusion.2
  206.5 0.5 collective-permute-start.2
  207.1 34.1 %collective-permute-done.3 = bf16[16,128,384]{1,2,0:T(8,128)(2,1)S(1)} collective-permute-done((bf16[16,128,384]{1,2,0:T(8,128)(2,1)S(1)}, bf16[16,128,384]{1,2,0:T(8,128)(2,1)S(1)}, u32[]{:S(2)}, u32[]{:S(2)}) %collective-permute-start.3) | collective-permute-done | bytes 1572896 | tf_op jit(solution)/shard_map/ppermute | solution.py:106
  241.2 0.4 pad_maximum_fusion
  241.6 2.9 %copy.10 = bf16[16,256,384]{2,1,0:T(8,128)(2,1)} copy(bf16[16,256,384]{1,2,0:T(8,128)(2,1)S(1)} %pad_maximum_fusion) | data formatting | bytes 6291456 | tf_op jit(solution)/shard_map/concatenate | solution.py:126
  244.5 21.9 %collective-permute-done.2 = bf16[3,128,1536]{2,1,0:T(8,128)(2,1)} collective-permute-done((bf16[3,128,1536]{2,1,0:T(8,128)(2,1)}, bf16[3,128,1536]{2,1,0:T(8,128)(2,1)}, u32[]{:S(2)}, u32[]{:S(2)}) %collective-permute-start.2) | collective-permute-done | bytes 1179680 | tf_op jit(solution)/shard_map/ppermute | solution.py:106
  266.4 2.3 slice_dynamic-update-slice_fusion
  268.6 0.0 all-gather.5.cloned.1.call-done
  268.6 10.0 %convolution_multiply_fusion = f32[384,1536]{1,0:T(8,128)} fusion(bf16[4096,384]{1,0:T(8,128)(2,1)} %bitcast.31, bf16[4096,1536]{1,0:T(8,128)(2,1)} %all-gather.5.cloned.1.call-done), kind=kOutput, calls=%fused_computation.5 | convolution fusion | flops 4832428032 | bytes 18087936 | tf_op jit(solution)/shard_map/dot_general | solution.py:15
Async XLA Ops:
  7.2 104.1 %all-gather.3.cloned.1.call-start = ((), (), s32[]{:S(2)}) async-start(), calls=%async_computation.1 | async-start | bytes 20054016 | tf_op jit(solution)/shard_map/all_gather | solution.py:108
  7.9 260.7 %all-gather.5.cloned.1.call-start = ((), (), s32[]{:S(2)}) async-start(), calls=%async_computation.2 | async-start | bytes 13369344 | tf_op jit(solution)/shard_map/all_gather | solution.py:133
  8.0 5.5 %copy-start.3 = (bf16[1,128,6144]{2,1,0:T(8,128)(2,1)S(1)}, bf16[1,128,6144]{2,1,0:T(8,128)(2,1)}, u32[]{:S(2)}) copy-start(bf16[1,128,6144]{2,1,0:T(8,128)(2,1)} %param.5) | copy-start | bytes 4718596
  10.4 29.8 %collective-permute-start = (bf16[3,128,1536]{2,1,0:T(8,128)(2,1)S(1)}, bf16[3,128,1536]{2,1,0:T(8,128)(2,1)S(1)}, u32[]{:S(2)}, u32[]{:S(2)}) collective-permute-start(bf16[3,128,1536]{2,1,0:T(8,128)(2,1)S(1)} %pad_maximum_fusion.1), channel_id=1, source_target_pairs={{0,1},{1,0},{2,3},{3,2},{4,5},{5,4},{6,7},{7,6},{8,9},{9,8},{10,11... | collective-permute-start | bytes 3538952 | tf_op jit(solution)/shard_map/ppermute | solution.py:106
  13.5 59.8 %collective-permute-start.1 = (bf16[128,6144]{1,0:T(8,128)(2,1)S(1)}, bf16[128,6144]{1,0:T(8,128)(2,1)}, u32[]{:S(2)}, u32[]{:S(2)}) collective-permute-start(bf16[128,6144]{1,0:T(8,128)(2,1)S(1)} %bitcast.33), channel_id=1, source_target_pairs={{0,1},{1,0},{2,3},{3,2},{4,5},{5,4},{6,7},{7,6},{8,9},{9,8},{10,11... | collective-permute-start | bytes 4718600 | tf_op jit(solution)/shard_map/ppermute | solution.py:106
  40.4 81.5 %copy-start = (bf16[1,128,3072]{2,1,0:T(8,128)(2,1)S(1)}, bf16[1,128,3072]{2,1,0:T(8,128)(2,1)}, u32[]{:S(2)}) copy-start(bf16[1,128,3072]{2,1,0:T(8,128)(2,1)} %param.6) | copy-start | bytes 2359300
  121.9 1.1 copy-start.1
  123.0 1.1 copy-start.2
  203.9 37.3 %collective-permute-start.3 = (bf16[16,128,384]{1,2,0:T(8,128)(2,1)S(1)}, bf16[16,128,384]{1,2,0:T(8,128)(2,1)S(1)}, u32[]{:S(2)}, u32[]{:S(2)}) collective-permute-start(bf16[16,128,384]{1,2,0:T(8,128)(2,1)S(1)} %all_to_all.5), channel_id=1, source_target_pairs={{0,1},{1,0},{2,3},{3,2},{4,5},{5,4},{6,7},{7,6},{8,9},{9,8},{10,11... | collective-permute-start | bytes 4718600 | tf_op jit(solution)/shard_map/ppermute | solution.py:106
  206.5 59.8 %collective-permute-start.2 = (bf16[3,128,1536]{2,1,0:T(8,128)(2,1)}, bf16[3,128,1536]{2,1,0:T(8,128)(2,1)}, u32[]{:S(2)}, u32[]{:S(2)}) collective-permute-start(bf16[3,128,1536]{2,1,0:T(8,128)(2,1)} %pad_maximum_fusion.2), channel_id=1, source_target_pairs={{0,1},{1,0},{2,3},{3,2},{4,5},{5,4},{6,7},{7,6},{8,9},{9,8},{10,11... | collective-permute-start | bytes 3538952 | tf_op jit(solution)/shard_map/ppermute | solution.py:106
Sparse Core Ops, SparseCore 0:
  9.6 101.6 all-gather.2
  136.3 128.9 all-gather.4
where the time goes:
time: 286 us
  waiting for transfers between devices  154 us (54%)
  blocking collectives  65.8 us (23%)
  matrix products  20.6 us (7%)
  between operations  14.1 us (5%)
  Pallas kernels  12 us (4%)
  local copies, waits for them, and re-layouts  11.7 us (4%)
  starting transfers between devices  5.22 us (2%)
    ppermute x4, waiting for transfers between devices, shift(): return lax.ppermute(array, 'seq', [(i, (i + by) % seq) for i in range(seq)])  116 us
    all_to_all x1, blocking collectives, shards(): lax.all_to_all(by_rows, 'dp', split_axis=0, concat_axis=0, tiled=True)  65.8 us
    all_gather x1, waiting for transfers between devices, shards(): whole_rows = lax.all_gather(out_weight, 'dp', axis=0, tiled=True)  38 us
    pallas_call x1, Pallas kernels, attention(): pl.pallas_call(functools.partial(attention_kernel, step), grid_spec=pltpu...  12 us
    dot_general x1, matrix products, shards(): jnp.dot(all_grad, whole_rows, preferred_element_type=jnp.float32)  10.6 us
    dot_general x1, matrix products, dot(): lax.dot_general(a, b, (contract, ((), ())), preferred_element_type=jnp.fl...  10 us
  transfers between devices with their start and end apart: 6, of which 5 were waited for; matrix products, arithmetic and copies ran while one was open for 4% of the time, Pallas kernels for 0%

commit v1 on v0

v1 whole, which is shorter than its diff:
```python
import functools
import math

import jax
import jax.numpy as jnp
from jax import lax
from jax.experimental import pallas as pl
from jax.experimental.pallas import tpu as pltpu
from jax.sharding import Mesh
from jax.sharding import PartitionSpec as P

HEAD_DIM = 128
INVERSE_ROOT = 1.0 / math.sqrt(HEAD_DIM)
DP = ("zh", "zl", "x", "core")


def dot(a, b, contract):
    return lax.dot_general(a, b, (contract, ((), ())), preferred_element_type=jnp.float32)


def shift(array, axis, by):
    count = lax.axis_size(axis)
    return lax.ppermute(array, axis, [(i, (i + by) % count) for i in range(count)])


def others(axis):
    return range(1, lax.axis_size(axis))


def part_of(array, axis, by, dim):
    count = lax.axis_size(axis)
    size = array.shape[dim] // count
    at = (lax.axis_index(axis) + by) % count
    return lax.dynamic_slice_in_dim(array, at * size, size, dim)


def softmax(q, k):
    scores = dot(q, k, ((1,), (1,))) * INVERSE_ROOT
    raised = jnp.exp(scores - jnp.max(scores, axis=-1, keepdims=True))
    return raised * (1.0 / jnp.sum(raised, axis=-1, keepdims=True))


def both(own, far, at):
    return jnp.concatenate([own[:, at], far[:, at]], axis=0)


def forward_kernel(heads, mine_ref, q_own, k_own, v_own, far, att_ref):
    for head in range(heads):
        at = slice(head * HEAD_DIM, (head + 1) * HEAD_DIM)
        q, k, v = (both(own, far.at[i], at) for i, own in enumerate((q_own, k_own, v_own)))
        low = softmax(q, k).astype(jnp.bfloat16)
        att_ref[:, at] = dot(low, v, ((1,), (0,))).astype(jnp.bfloat16)


def backward_kernel(heads, held, terms, mine_ref, q_own, k_own, v_own, far, *refs):
    grad_refs, refs = refs[:terms], refs[terms + held :]
    dq_own, dk_own, dv_own, leaving = refs
    tokens = q_own.shape[0]
    for head in range(heads):
        at = slice(head * HEAD_DIM, (head + 1) * HEAD_DIM)
        q, k, v = (both(own, far.at[i], at) for i, own in enumerate((q_own, k_own, v_own)))
        total = grad_refs[0][:, at].astype(jnp.float32)
        for ref in grad_refs[1:]:
            total = total + ref[:, at].astype(jnp.float32)
        g = total.astype(jnp.bfloat16)
        probs = softmax(q, k)
        low = probs.astype(jnp.bfloat16)
        att = dot(low, v, ((1,), (0,))).astype(jnp.bfloat16)
        delta = jnp.sum(
            g.astype(jnp.float32) * att.astype(jnp.float32), axis=-1, keepdims=True
        )
        d_probs = dot(g, v, ((1,), (1,)))
        d_low = (probs * (d_probs - delta)).astype(jnp.bfloat16)
        dq = (dot(d_low, k, ((1,), (0,))) * INVERSE_ROOT).astype(jnp.bfloat16)
        dk = (dot(d_low, q, ((0,), (0,))) * INVERSE_ROOT).astype(jnp.bfloat16)
        dv = dot(low, g, ((0,), (0,))).astype(jnp.bfloat16)
        for i, (own, value) in enumerate(((dq_own, dq), (dk_own, dk), (dv_own, dv))):
            own[:, at] = value[:tokens]
            leaving[i, :, at] = value[tokens:]


def heads_a_step(heads, length):
    return 2 if heads % 2 == 0 and length <= 512 else 1


def params():
    return pltpu.CompilerParams(vmem_limit_bytes=48 * 1024 * 1024)


def cost(dots, heads, length, arrays):
    return pl.CostEstimate(
        flops=2 * dots * heads * length * length * HEAD_DIM,
        bytes_accessed=2 * arrays * length * heads * HEAD_DIM,
        transcendentals=heads * length * length,
    )


def forward(mine, own, far):
    tokens = own[0].shape[0]
    _, rest, features = far.shape
    length = tokens + rest
    heads = features // HEAD_DIM
    step = heads_a_step(heads, length)
    grid = heads // step
    block = step * HEAD_DIM
    own_spec = pl.BlockSpec((tokens, block), lambda h, mine: (0, mine[0] * grid + h))
    far_spec = pl.BlockSpec((3, rest, block), lambda h, mine: (0, 0, h))
    return pl.pallas_call(
        functools.partial(forward_kernel, step),
        grid_spec=pltpu.PrefetchScalarGridSpec(
            num_scalar_prefetch=1,
            grid=(grid,),
            in_specs=[own_spec] * 3 + [far_spec],
            out_specs=pl.BlockSpec((length, block), lambda h, mine: (0, h)),
        ),
        out_shape=jax.ShapeDtypeStruct((length, features), jnp.bfloat16),
        compiler_params=params(),
        cost_estimate=cost(2, heads, length, 4),
        name="forward",
    )(mine, *own, far)


def backward(mine, own, far, grads, first_head, heads, held):
    tokens, width = own[0].shape
    _, rest, features = far.shape
    length = tokens + rest
    step = heads_a_step(heads, length)
    grid = heads // step
    block = step * HEAD_DIM
    every = features // block
    start = first_head // step
    own_spec = pl.BlockSpec((tokens, block), lambda h, mine: (0, mine[0] * every + start + h))
    far_spec = pl.BlockSpec((3, rest, block), lambda h, mine: (0, 0, start + h))
    grad_spec = pl.BlockSpec((length, block), lambda h, mine: (0, h))
    any_spec = pl.BlockSpec(memory_space=pl.ANY)
    before = 5 + len(grads)
    return pl.pallas_call(
        functools.partial(backward_kernel, step, len(held), len(grads)),
        grid_spec=pltpu.PrefetchScalarGridSpec(
            num_scalar_prefetch=1,
            grid=(grid,),
            in_specs=[own_spec] * 3
            + [far_spec]
            + [grad_spec] * len(grads)
            + [any_spec] * len(held),
            out_specs=[own_spec] * 3
            + [pl.BlockSpec((3, rest, block), lambda h, mine: (0, 0, h))],
        ),
        out_shape=[jax.ShapeDtypeStruct((tokens, width), jnp.bfloat16)] * 3
        + [jax.ShapeDtypeStruct((3, rest, heads * HEAD_DIM), jnp.bfloat16)],
        input_output_aliases={before + i: i for i in range(len(held))},
        compiler_params=params(),
        cost_estimate=cost(6, heads, length, 9),
        name="backward",
    )(mine, *own, far, *grads, *held)


def summed_rows(grads, attended, first, second):
    tokens, _, _, rows = grads.shape
    inner = lax.axis_size(second)

    def product(by):
        chosen = part_of(grads, first, by, 1).reshape(tokens, inner * rows)
        return dot(chosen, attended, ((0,), (0,)))

    sent = [shift(product(by).astype(jnp.bfloat16), first, by) for by in others(first)]
    total = product(0)
    for term in sent:
        total = total + term.astype(jnp.float32)
    sent = [
        shift(part_of(total, second, by, 0).astype(jnp.bfloat16), second, by)
        for by in others(second)
    ]
    final = part_of(total, second, 0, 0)
    for term in sent:
        final = final + term.astype(jnp.float32)
    return final


def shards(grad_out, queries, keys, values, out_weight):
    seq = lax.axis_size("seq")
    mine = lax.axis_index("seq")
    tokens = grad_out.shape[1]
    rows, features = out_weight.shape
    length = tokens * seq
    heads = features // HEAD_DIM
    clips = math.prod(lax.axis_size(axis) for axis in DP)
    token_scale = 1.0 / math.sqrt(clips * length)
    me = mine.astype(jnp.int32).reshape(1)

    weight = lax.all_gather(out_weight, ("zl", "x", "core"), axis=0, tiled=True)

    own_grad = grad_out[0]
    halves = [part_of(own_grad, "zh", 0, 1)]
    halves += [shift(part_of(own_grad, "zh", by, 1), "zh", by) for by in others("zh")]

    own = (queries[0], keys[0], values[0])
    pieces = [
        shift(jnp.stack([part_of(part, "seq", by, 1) for part in own]), "seq", by)
        for by in others("seq")
    ]
    far = pieces[0] if seq == 2 else jnp.concatenate(pieces, axis=1)

    grads = [
        jnp.concatenate([half] + [shift(half, "seq", by) for by in others("seq")], axis=0)
        for half in halves
    ]

    attended = forward(me, own, far)
    attends = [attended] + [shift(attended, "zh", by) for by in others("zh")]

    groups = 2 if heads % 4 == 0 else 1
    wide = features // groups
    partial = []
    for group in range(groups):
        chosen = weight[:, group * wide : (group + 1) * wide]
        terms = [
            shift(dot(grads[by], chosen, ((1,), (0,))).astype(jnp.bfloat16), "zh", -by)
            for by in others("zh")
        ]
        partial.append([dot(grads[0], chosen, ((1,), (0,)))] + terms)

    every_grad, every_attended = [], []
    cores = lax.axis_size("core")
    stacked = jnp.concatenate(grads, axis=0)
    count = stacked.shape[0]
    stacked = stacked.reshape(count, -1, cores, rows)
    attends = jnp.concatenate(attends, axis=0)
    for by in range(cores):
        chosen = part_of(stacked, "core", by, 2)[:, :, 0]
        every_grad.append(shift(chosen, "core", by) if by else chosen)
        every_attended.append(shift(attends, "core", by) if by else attends)
    every_grad = jnp.concatenate(every_grad, axis=0)
    every_attended = jnp.concatenate(every_attended, axis=0)
    every_grad = every_grad.reshape(
        every_grad.shape[0], lax.axis_size("zl"), lax.axis_size("x"), rows
    )
    middle = features // 2
    left = summed_rows(
        jnp.swapaxes(every_grad, 1, 2), every_attended[:, :middle], "x", "zl"
    )
    right = summed_rows(every_grad, every_attended[:, middle:], "zl", "x")
    weight_grad = jnp.concatenate([left, right], axis=1) * token_scale

    result, arrivals = [], []
    for group in range(groups):
        first = group * wide // HEAD_DIM
        *result, leaving = backward(
            me, own, far, partial[group], first, wide // HEAD_DIM, result
        )
        arrivals.append(
            [
                shift(leaving[:, (by - 1) * tokens : by * tokens], "seq", -by)
                for by in others("seq")
            ]
        )
    for group in range(groups):
        for by, back in zip(others("seq"), arrivals[group]):
            start = ((mine + by) % seq) * features + group * wide
            result = [
                lax.dynamic_update_slice_in_dim(whole, back[i], start, 1)
                for i, whole in enumerate(result)
            ]
    return (result[0][None], result[1][None], result[2][None], weight_grad)


def solution(mesh):
    dp, seq = mesh.devices.shape
    finer = Mesh(mesh.devices.reshape(2, dp // 8, 2, 2, seq), DP + ("seq",))
    tokens = P(DP, "seq", None)
    return jax.shard_map(
        shards,
        mesh=finer,
        in_specs=(tokens, tokens, tokens, tokens, P(DP, "seq")),
        out_specs=(tokens, tokens, tokens, P(DP, "seq")),
        check_vma=False,
    )
```

time: 286 us -> 250 us (0.87)
  blocking collectives: 65.8 us -> 0 us
  waiting for transfers between devices: 154 us -> 114 us
  local copies, waits for them, and re-layouts: 11.7 us -> 38 us
  other arithmetic: 1.72 us -> 19.2 us
  starting transfers between devices: 5.22 us -> 18.6 us
  Pallas kernels: 12 us -> 18.5 us
  matrix products: 20.6 us -> 26.9 us
    all_to_all x1 -> x0, blocking collectives: 65.8 us -> none  [shards(): lax.all_to_all(by_rows, 'dp', split_axis=0, concat_axis=0, tiled=True)]
    all_gather x2 -> x1, waiting for transfers between devices: 38 us -> 0.01 us  [shards(): weight = lax.all_gather(out_weight, ('zl', 'x', 'core'), axis=0, tiled=True)]
    dot_general x1 -> x8, matrix products: 10 us -> 26.9 us  [dot(): lax.dot_general(a, b, (contract, ((), ())), preferred_element_type=jnp.fl...]
    concatenate x1 -> x5, other arithmetic: 0.44 us -> 14.5 us  [the longest x2 7.69 us: shards(): every_grad = jnp.concatenate(every_grad, axis=0)]
    dynamic_slice x2 -> x9, local copies, waits for them, and re-layouts: 2.32 us -> 15.8 us  [part_of(): return lax.dynamic_slice_in_dim(array, at * size, size, dim)]
    ppermute x4 -> x15, starting transfers between devices: 5.14 us -> 18.5 us  [shift(): lax.ppermute(array, axis, [(i, (i + by) % count) for i in range(count)])]
    dot_general x1 -> x0, matrix products: 10.6 us -> none  [shards(): jnp.dot(all_grad, whole_rows, preferred_element_type=jnp.float32)]
    pallas_call x1 -> x3, Pallas kernels: 12 us -> 18.5 us  [the longest x2 11.9 us: backward(): pl.pallas_call(functools.partial(backward_kernel, step, len(held), len(gr...]
  transfers between devices with their start and end apart: 6 -> 16, of which waited for: 5 -> 9; matrix products, arithmetic and copies ran while one was open for 4% -> 32% of each run, Pallas kernels for 0% -> 7%
where the time goes in v1:
time: 250 us
  waiting for transfers between devices  114 us (46%)
  local copies, waits for them, and re-layouts  38 us (15%)
  matrix products  26.9 us (11%)
  other arithmetic  19.2 us (8%)
  starting transfers between devices  18.6 us (7%)
  Pallas kernels  18.5 us (7%)
  between operations  14.2 us (6%)
    ppermute x15, waiting for transfers between devices, shift(): lax.ppermute(array, axis, [(i, (i + by) % count) for i in range(count)])  113 us
    dot_general x8, matrix products, dot(): lax.dot_general(a, b, (contract, ((), ())), preferred_element_type=jnp.fl...  26.9 us
    ppermute x15, starting transfers between devices, shift(): lax.ppermute(array, axis, [(i, (i + by) % count) for i in range(count)])  18.5 us
    dynamic_slice x9, local copies, waits for them, and re-layouts, part_of(): return lax.dynamic_slice_in_dim(array, at * size, size, dim)  15.8 us
    pallas_call x2, Pallas kernels, backward(): pl.pallas_call(functools.partial(backward_kernel, step, len(held), len(gr...  11.9 us
    unnamed x27, local copies, waits for them, and re-layouts  9.36 us
    concatenate x2, other arithmetic, shards(): every_grad = jnp.concatenate(every_grad, axis=0)  7.69 us
    pallas_call x1, Pallas kernels, forward(): pl.pallas_call(functools.partial(forward_kernel, step), grid_spec=pltpu.P...  6.55 us
  transfers between devices with their start and end apart: 16, of which 9 were waited for; matrix products, arithmetic and copies ran while one was open for 32% of the time, Pallas kernels for 7%

profile of v1, /device:TPU:0, one launch (start us, length us, event | category | flops | bytes accessed | tf_op | source)
XLA Modules:
  0.0 249.5 jit_solution(1753561414717918867)
XLA Ops:
  7.2 0.0 all-gather.2.cloned.1.call-start
  7.2 0.7 all-gather.2.cloned.1.call-update
  7.9 2.4 constant_dynamic-slice_fusion.2
  10.3 1.2 copy.21
  11.4 4.0 %collective-permute-start.2 = (bf16[128,3072]{0,1:T(8,128)(2,1)}, bf16[128,3072]{0,1:T(8,128)(2,1)}, u32[]{:S(2)}, u32[]{:S(2)}) collective-permute-start(bf16[128,3072]{0,1:T(8,128)(2,1)} %bitcast.49), channel_id=1, source_target_pairs={{0,16},{16,0},{1,17},{17,1},{2,18},{18,2},{3,19},{19,3},{4,20},{20... | collective-permute-start | bytes 2359304 | tf_op jit(solution)/shard_map/ppermute | solution.py:23
  15.5 0.1 constant_dynamic-slice_fusion.4
  15.6 1.1 pad_maximum_fusion.4
  16.7 1.5 collective-permute-start
  18.3 2.4 copy.33
  20.6 0.4 collective-permute-start.1
  21.1 29.2 %collective-permute-done.2 = bf16[128,3072]{0,1:T(8,128)(2,1)} collective-permute-done((bf16[128,3072]{0,1:T(8,128)(2,1)}, bf16[128,3072]{0,1:T(8,128)(2,1)}, u32[]{:S(2)}, u32[]{:S(2)}) %collective-permute-start.2) | collective-permute-done | bytes 786464 | tf_op jit(solution)/shard_map/ppermute | solution.py:23
  50.2 1.6 collective-permute-start.3
  51.8 6.5 %forward.1 = bf16[256,1536]{1,0:T(8,128)(2,1)} custom-call(s32[1]{0:T(128)} %bitcast.mine_ref, bf16[128,3072]{1,0:T(8,128)(2,1)S(1)} %bitcast.26, bf16[128,3072]{1,0:T(8,128)(2,1)S(1)} %bitcast.29, bf16[128,3072]{1,0:T(8,128)(2,1)S(1)} %bitcast.32, bf16[3,128,1536]{2,1,0:T(8,128)(2,1)S(1)} %collective-permute-done.far), custom_call_target="tpu_custom_call" | custom-call | flops 402653184 | bytes 3145728 | tf_op jit(solution)/shard_map/forward/pallas_call | solution.py:108
  58.4 4.4 %collective-permute-done.1 = bf16[128,3072]{0,1:T(8,128)(2,1)} collective-permute-done((bf16[128,3072]{0,1:T(8,128)(2,1)}, bf16[128,3072]{0,1:T(8,128)(2,1)}, u32[]{:S(2)}, u32[]{:S(2)}) %collective-permute-start.1) | collective-permute-done | bytes 786464 | tf_op jit(solution)/shard_map/ppermute | solution.py:23
  62.8 15.4 %collective-permute-done.3 = bf16[128,3072]{0,1:T(8,128)(2,1)} collective-permute-done((bf16[128,3072]{0,1:T(8,128)(2,1)}, bf16[128,3072]{0,1:T(8,128)(2,1)}, u32[]{:S(2)}, u32[]{:S(2)}) %collective-permute-start.3) | collective-permute-done | bytes 786464 | tf_op jit(solution)/shard_map/ppermute | solution.py:23
  78.2 2.0 pad_maximum_fusion
  80.2 1.9 constant_dynamic-slice_fusion
  82.1 2.6 %copy.23 = bf16[512,4,1,384]{3,0,2,1:T(8,128)(2,1)} copy(bf16[512,4,1,384]{0,3,2,1:T(8,128)(2,1)} %get-tuple-element.36) | data formatting | bytes 3145728 | tf_op jit(solution)/shard_map/dynamic_slice | solution.py:34
  84.7 9.9 %collective-permute-done.9 = bf16[256,1536]{1,0:T(8,128)(2,1)} collective-permute-done((bf16[256,1536]{1,0:T(8,128)(2,1)}, bf16[256,1536]{1,0:T(8,128)(2,1)}, u32[]{:S(2)}, u32[]{:S(2)}) %collective-permute-start.9) | collective-permute-done | bytes 786464 | tf_op jit(solution)/shard_map/ppermute | solution.py:23
  94.6 2.7 %pad_maximum_fusion.3 = bf16[512,1536]{1,0:T(8,128)(2,1)} fusion(bf16[256,1536]{1,0:T(8,128)(2,1)} %collective-permute-done.9, bf16[256,1536]{1,0:T(8,128)(2,1)} %forward.1), kind=kLoop, calls=%fused_computation.26 | loop fusion | flops 3145728 | bytes 3145728 | tf_op jit(solution)/shard_map/concatenate | solution.py:228
  97.2 2.6 %copy.22 = bf16[512,4,1,384]{3,0,1,2:T(8,128)(2,1)} copy(bf16[512,4,1,384]{0,3,2,1:T(8,128)(2,1)} %get-tuple-element.37) | data formatting | bytes 3145728 | tf_op jit(solution)/shard_map/dynamic_slice | solution.py:34
  99.8 3.9 %fusion.11 = (bf16[1024,1,2,384]{3,0,2,1:T(8,128)(2,1)}, bf16[1024,1,2,384]{3,0,2,1:T(8,128)(2,1)}) fusion(s32[]{:T(128)S(6)} %select_n.123, bf16[512,2,2,384]{3,0,2,1:T(8,128)(2,1)} %bitcast.35, bf16[512,2,2,384]{3,0,2,1:T(8,128)(2,1)} %bitcast.15, s32[]{:T(128)S(6)} %select_n.124), kind=kLoop, calls=%fused_computation.24 | loop fusion | flops 6291456 | bytes 6291464 | tf_op jit(solution)/shard_map/concatenate | solution.py:233
  103.7 2.6 %copy.28 = bf16[1024,1,2,384]{0,3,2,1:T(8,128)(2,1)} copy(bf16[1024,1,2,384]{3,0,2,1:T(8,128)(2,1)} %get-tuple-element.35) | data formatting | bytes 3145728 | tf_op jit(solution)/shard_map/dynamic_slice | solution.py:34
  106.3 2.2 pad_maximum_fusion.1
  108.4 0.2 copy-done.6
  108.6 2.5 %convolution_convert_fusion = bf16[768,768]{0,1:T(8,128)(2,1)} fusion(bf16[1024,768]{0,1:T(8,128)(2,1)S(1)} %bitcast.42, bf16[1024,1536]{1,0:T(8,128)(2,1)S(1)} %pad_maximum_fusion.1), kind=kOutput, calls=%fused_computation.27 | convolution fusion | flops 1208549376 | bytes 4325376 | tf_op jit(solution)/shard_map/dot_general | solution.py:18
  111.1 0.4 collective-permute-start.13
  111.5 3.8 %fusion.9 = (bf16[1024,2,1,384]{3,0,2,1:T(8,128)(2,1)}, bf16[1024,2,1,384]{3,0,2,1:T(8,128)(2,1)}) fusion(s32[]{:T(128)S(6)} %select_n.116, bf16[512,2,2,384]{3,0,2,1:T(8,128)(2,1)} %bitcast.36, bf16[512,2,2,384]{3,0,2,1:T(8,128)(2,1)} %bitcast.15, s32[]{:T(128)S(6)} %select_n.118), kind=kLoop, calls=%fused_computation.22 | loop fusion | flops 6291456 | bytes 6291464 | tf_op jit(solution)/shard_map/concatenate | solution.py:233
  115.3 2.6 %copy.25 = bf16[1024,2,1,384]{0,3,1,2:T(8,128)(2,1)} copy(bf16[1024,2,1,384]{3,0,2,1:T(8,128)(2,1)} %get-tuple-element.33) | data formatting | bytes 3145728 | tf_op jit(solution)/shard_map/dynamic-slice.6
  117.9 4.4 %convolution_convert_fusion.1 = bf16[768,768]{0,1:T(8,128)(2,1)} fusion(bf16[1024,768]{0,1:T(8,128)(2,1)} %bitcast.45, bf16[1024,1536]{1,0:T(8,128)(2,1)} %copy-done.5), kind=kOutput, calls=%fused_computation.28 | convolution fusion | flops 1208549376 | bytes 4325376 | tf_op jit(solution)/shard_map/dot_general | solution.py:18
  122.2 1.4 collective-permute-start.11
  123.7 2.1 constant_dynamic-update-slice_fusion.1
  125.8 2.6 %copy.27 = bf16[1024,1,2,384]{0,3,2,1:T(8,128)(2,1)} copy(bf16[1024,1,2,384]{3,0,2,1:T(8,128)(2,1)} %get-tuple-element.34) | data formatting | bytes 3145728 | tf_op jit(solution)/shard_map/dynamic_slice | solution.py:34
  128.3 11.5 %collective-permute-done.13 = bf16[768,768]{0,1:T(8,128)(2,1)} collective-permute-done((bf16[768,768]{0,1:T(8,128)(2,1)}, bf16[768,768]{0,1:T(8,128)(2,1)}, u32[]{:S(2)}, u32[]{:S(2)}) %collective-permute-start.13) | collective-permute-done | bytes 1179680 | tf_op jit(solution)/shard_map/ppermute | solution.py:23
  139.8 3.7 %convert_add_fusion = f32[768,768]{0,1:T(8,128)S(1)} fusion(bf16[768,768]{0,1:T(8,128)(2,1)} %collective-permute-done.13, bf16[1024,768]{0,1:T(8,128)(2,1)} %bitcast.44, bf16[1024,1536]{1,0:T(8,128)(2,1)} %copy-done.5), kind=kOutput, calls=%fused_computation.19 | convolution fusion | flops 1209139200 | bytes 6684672 | tf_op jit(solution)/shard_map/dot_general | solution.py:18
  143.6 1.4 copy-done.9
  145.0 0.9 dynamic-slice_convert_fusion
  145.9 1.6 collective-permute-start.14
  147.5 2.1 constant_dynamic-update-slice_fusion
  149.5 2.6 %copy.24 = bf16[1024,2,1,384]{0,3,1,2:T(8,128)(2,1)} copy(bf16[1024,2,1,384]{3,0,2,1:T(8,128)(2,1)} %get-tuple-element.32) | data formatting | bytes 3145728 | tf_op jit(solution)/shard_map/dynamic-slice.5
  152.1 3.9 %convert_add_fusion.1 = f32[768,768]{0,1:T(8,128)S(1)} fusion(bf16[768,768]{0,1:T(8,128)(2,1)} %collective-permute-done.11, bf16[1024,768]{0,1:T(8,128)(2,1)} %bitcast.43, bf16[1024,1536]{1,0:T(8,128)(2,1)} %copy-done.5), kind=kOutput, calls=%fused_computation.20 | convolution fusion | flops 1209139200 | bytes 6684672 | tf_op jit(solution)/shard_map/dot_general | solution.py:18
  156.1 1.4 copy-done.7
  157.4 0.9 dynamic-slice_convert_fusion.1
  158.3 0.9 collective-permute-start.12
  159.2 4.1 %collective-permute-done.14 = bf16[384,768]{0,1:T(8,128)(2,1)} collective-permute-done((bf16[384,768]{0,1:T(8,128)(2,1)}, bf16[384,768]{0,1:T(8,128)(2,1)}, u32[]{:S(2)}, u32[]{:S(2)}) %collective-permute-start.14) | collective-permute-done | bytes 589856 | tf_op jit(solution)/shard_map/ppermute | solution.py:23
  163.3 2.2 convert_add_fusion.2
  165.5 4.4 %fusion.16 = bf16[256,768]{1,0:T(8,128)(2,1)S(1)} fusion(bf16[256,3072]{0,1:T(8,128)(2,1)} %constant_dynamic-update-slice_fusion, bf16[3072,1536]{1,0:T(8,128)(2,1)} %all-gather.2.cloned.1.call-done), kind=kOutput, calls=%fused_computation.33 | convolution fusion | flops 1208156160 | bytes 6684672 | tf_op jit(solution)/shard_map/dot_general | solution.py:18
  169.9 3.5 %collective-permute-start.4 = (bf16[256,768]{1,0:T(8,128)(2,1)S(1)}, bf16[256,768]{1,0:T(8,128)(2,1)S(1)}, u32[]{:S(2)}, u32[]{:S(2)}) collective-permute-start(bf16[256,768]{1,0:T(8,128)(2,1)S(1)} %fusion.16), channel_id=1, source_target_pairs={{0,16},{16,0},{1,17},{17,1},{2,18},{18,2},{3,19},{19,3},{4,20},{20... | collective-permute-start | bytes 1179656 | tf_op jit(solution)/shard_map/ppermute | solution.py:23
  173.4 2.8 %fusion.19 = bf16[256,768]{1,0:T(8,128)(2,1)S(1)} fusion(bf16[256,3072]{0,1:T(8,128)(2,1)} %constant_dynamic-update-slice_fusion, bf16[3072,1536]{1,0:T(8,128)(2,1)S(1)} %copy-done.11), kind=kOutput, calls=%fused_computation.34 | convolution fusion | flops 1208156160 | bytes 6684672 | tf_op jit(solution)/shard_map/dot_general | solution.py:18
  176.3 1.1 collective-permute-start.5
  177.4 2.6 %fusion.6.refs_0_ = f32[256,768]{1,0:T(8,128)S(1)} fusion(bf16[3072,1536]{1,0:T(8,128)(2,1)S(1)} %copy-done.11, bf16[128,3072]{0,1:T(8,128)(2,1)} %collective-permute-done.1, bf16[128,3072]{0,1:T(8,128)(2,1)S(1)} %bitcast.39), kind=kOutput, calls=%fused_computation.14 | convolution fusion | flops 1211105280 | bytes 7077888 | tf_op jit(solution)/shard_map/dot_general | solution.py:18
  179.9 2.6 %fusion.2.refs_0_ = f32[256,768]{1,0:T(8,128)S(1)} fusion(bf16[3072,1536]{1,0:T(8,128)(2,1)S(1)} %copy-done.11, bf16[128,3072]{0,1:T(8,128)(2,1)} %collective-permute-done.1, bf16[128,3072]{0,1:T(8,128)(2,1)S(1)} %bitcast.40), kind=kOutput, calls=%fused_computation.10 | convolution fusion | flops 1211105280 | bytes 7077888 | tf_op jit(solution)/shard_map/dot_general | solution.py:18
  182.5 24.9 %collective-permute-done.5.refs_1_ = bf16[256,768]{1,0:T(8,128)(2,1)S(1)} collective-permute-done((bf16[256,768]{1,0:T(8,128)(2,1)S(1)}, bf16[256,768]{1,0:T(8,128)(2,1)S(1)}, u32[]{:S(2)}, u32[]{:S(2)}) %collective-permute-start.5) | collective-permute-done | bytes 393248 | tf_op jit(solution)/shard_map/ppermute | solution.py:23
  207.4 5.9 %backward.2 = (bf16[128,3072]{1,0:T(8,128)(2,1)}, bf16[128,3072]{1,0:T(8,128)(2,1)}, bf16[128,3072]{1,0:T(8,128)(2,1)}, bf16[3,128,768]{2,1,0:T(8,128)(2,1)}) custom-call(s32[1]{0:T(128)} %bitcast.mine_ref, bf16[128,3072]{1,0:T(8,128)(2,1)S(1)} %bitcast.27, bf16[128,3072]{1,0:T(8,128)(2,1)S(1)} %bitcast.30, bf16[128,3072]{1,0:T(8,128)(2,1)S(1)} %bitcast.33, ...), custom_call_target="tpu_custom_call" | custom-call | flops 603979776 | bytes 3538944 | tf_op jit(solution)/shard_map/backward/pallas_call | solution.py:137
  213.3 0.6 collective-permute-start.6
  213.9 6.0 %backward.3 = (bf16[128,3072]{1,0:T(8,128)(2,1)}, bf16[128,3072]{1,0:T(8,128)(2,1)}, bf16[128,3072]{1,0:T(8,128)(2,1)}, bf16[3,128,768]{2,1,0:T(8,128)(2,1)}) custom-call(s32[1]{0:T(128)} %bitcast.mine_ref, bf16[128,3072]{1,0:T(8,128)(2,1)S(1)} %bitcast.28, ...), custom_call_target="tpu_custom_call", output_to_operand_aliasing={{0}: (7, {}), {1}: (8, {}), {2}: (9, {})} | custom-call | flops 603979776 | bytes 3538944 | tf_op jit(solution)/shard_map/backward/pallas_call | solution.py:137
  219.9 1.4 collective-permute-start.7
  221.3 1.2 convert_add_fusion.3
  222.5 0.2 maximum_multiply_fusion
  222.7 2.0 copy.30
  224.7 5.2 %collective-permute-done.6 = bf16[3,128,768]{2,1,0:T(8,128)(2,1)} collective-permute-done((bf16[3,128,768]{2,1,0:T(8,128)(2,1)}, bf16[3,128,768]{2,1,0:T(8,128)(2,1)}, u32[]{:S(2)}, u32[]{:S(2)}) %collective-permute-start.6) | collective-permute-done | bytes 589856 | tf_op jit(solution)/shard_map/ppermute | solution.py:23
  229.9 1.9 slice_dynamic-update-slice_fusion.1
  231.8 8.9 %collective-permute-done.7 = bf16[3,128,768]{2,1,0:T(8,128)(2,1)} collective-permute-done((bf16[3,128,768]{2,1,0:T(8,128)(2,1)}, bf16[3,128,768]{2,1,0:T(8,128)(2,1)}, u32[]{:S(2)}, u32[]{:S(2)}) %collective-permute-start.7) | collective-permute-done | bytes 589856 | tf_op jit(solution)/shard_map/ppermute | solution.py:23
  240.7 1.9 slice_dynamic-update-slice_fusion
  (32 shorter events, 0.1 us)
Async XLA Ops:
  7.2 158.3 %all-gather.2.cloned.1.call-start = ((), (), s32[]{:S(2)}) async-start(), calls=%async_computation | async-start | bytes 10616832 | tf_op jit(solution)/shard_map/all_gather | solution.py:191
  10.3 5.2 %copy-start = (bf16[1,128,3072]{2,1,0:T(8,128)(2,1)S(1)}, bf16[1,128,3072]{2,1,0:T(8,128)(2,1)}, u32[]{:S(2)}) copy-start(bf16[1,128,3072]{2,1,0:T(8,128)(2,1)} %param.6) | copy-start | bytes 2359300
  10.3 5.2 %copy-start.1 = (bf16[1,128,3072]{2,1,0:T(8,128)(2,1)S(1)}, bf16[1,128,3072]{2,1,0:T(8,128)(2,1)}, u32[]{:S(2)}) copy-start(bf16[1,128,3072]{2,1,0:T(8,128)(2,1)} %param.7) | copy-start | bytes 2359300
  10.3 5.2 %copy-start.2 = (bf16[1,128,3072]{2,1,0:T(8,128)(2,1)S(1)}, bf16[1,128,3072]{2,1,0:T(8,128)(2,1)}, u32[]{:S(2)}) copy-start(bf16[1,128,3072]{2,1,0:T(8,128)(2,1)} %param.8) | copy-start | bytes 2359300
  11.4 38.8 %collective-permute-start.2 = (bf16[128,3072]{0,1:T(8,128)(2,1)}, bf16[128,3072]{0,1:T(8,128)(2,1)}, u32[]{:S(2)}, u32[]{:S(2)}) collective-permute-start(bf16[128,3072]{0,1:T(8,128)(2,1)} %bitcast.49), channel_id=1, source_target_pairs={{0,16},{16,0},{1,17},{17,1},{2,18},{18,2},{3,19},{19,3},{4,20},{20... | collective-permute-start | bytes 2359304 | tf_op jit(solution)/shard_map/ppermute | solution.py:23
  16.7 35.1 %collective-permute-start = (bf16[3,128,1536]{2,1,0:T(8,128)(2,1)}, bf16[3,128,1536]{2,1,0:T(8,128)(2,1)S(1)}, u32[]{:S(2)}, u32[]{:S(2)}) collective-permute-start(bf16[3,128,1536]{2,1,0:T(8,128)(2,1)} %pad_maximum_fusion.4), channel_id=1, source_target_pairs={{0,1},{1,0},{2,3},{3,2},{4,5},{5,4},{6,7},{7,6},{8,9},{9,8},{10,11... | collective-permute-start | bytes 3538952 | tf_op jit(solution)/shard_map/ppermute | solution.py:23
  20.6 42.2 %collective-permute-start.1 = (bf16[128,3072]{0,1:T(8,128)(2,1)}, bf16[128,3072]{0,1:T(8,128)(2,1)}, u32[]{:S(2)}, u32[]{:S(2)}) collective-permute-start(bf16[128,3072]{0,1:T(8,128)(2,1)} %bitcast.37), channel_id=1, source_target_pairs={{0,1},{1,0},{2,3},{3,2},{4,5},{5,4},{6,7},{7,6},{8,9},{9,8},{10,11... | collective-permute-start | bytes 2359304 | tf_op jit(solution)/shard_map/ppermute | solution.py:23
  50.2 27.9 %collective-permute-start.3 = (bf16[128,3072]{0,1:T(8,128)(2,1)}, bf16[128,3072]{0,1:T(8,128)(2,1)}, u32[]{:S(2)}, u32[]{:S(2)}) collective-permute-start(bf16[128,3072]{0,1:T(8,128)(2,1)} %collective-permute-done.2), channel_id=1, source_target_pairs={{0,1},{1,0},{2,3},{3,2},{4,5},{5,4},{6,7},{7,6},{8,9},{9,8},{10,11... | collective-permute-start | bytes 2359304 | tf_op jit(solution)/shard_map/ppermute | solution.py:23
  58.4 36.2 %collective-permute-start.9 = (bf16[256,1536]{1,0:T(8,128)(2,1)}, bf16[256,1536]{1,0:T(8,128)(2,1)}, u32[]{:S(2)}, u32[]{:S(2)}) collective-permute-start(bf16[256,1536]{1,0:T(8,128)(2,1)} %forward.1), channel_id=1, source_target_pairs={{0,16},{16,0},{1,17},{17,1},{2,18},{18,2},{3,19},{19,3},{4,20},{20... | collective-permute-start | bytes 2359304 | tf_op jit(solution)/shard_map/ppermute | solution.py:23
  84.7 15.1 %collective-permute-start.8 = (bf16[512,4,384]{2,0,1:T(8,128)(2,1)}, bf16[512,4,384]{2,0,1:T(8,128)(2,1)}, u32[]{:S(2)}, u32[]{:S(2)}) collective-permute-start(bf16[512,4,384]{2,0,1:T(8,128)(2,1)} %bitcast.41), channel_id=1, source_target_pairs={{0,2},{2,0},{1,3},{3,1},{4,6},{6,4},{5,7},{7,5},{8,10},{10,8},{9,1... | collective-permute-start | bytes 4718600 | tf_op jit(solution)/shard_map/ppermute | solution.py:23
  97.2 9.0 %collective-permute-start.10 = (bf16[512,1536]{1,0:T(8,128)(2,1)}, bf16[512,1536]{1,0:T(8,128)(2,1)}, u32[]{:S(2)}, u32[]{:S(2)}) collective-permute-start(bf16[512,1536]{1,0:T(8,128)(2,1)} %pad_maximum_fusion.3), channel_id=1, source_target_pairs={{0,2},{2,0},{1,3},{3,1},{4,6},{6,4},{5,7},{7,5},{8,10},{10,8},{9,1... | collective-permute-start | bytes 4718600 | tf_op jit(solution)/shard_map/ppermute | solution.py:23
  106.3 2.4 copy-start.6
  108.4 2.7 %copy-start.5 = (bf16[1024,1536]{1,0:T(8,128)(2,1)}, bf16[1024,1536]{1,0:T(8,128)(2,1)S(1)}, u32[]{:S(2)}) copy-start(bf16[1024,1536]{1,0:T(8,128)(2,1)S(1)} %pad_maximum_fusion.1) | copy-start | bytes 9437188
  111.1 28.7 %collective-permute-start.13 = (bf16[768,768]{0,1:T(8,128)(2,1)}, bf16[768,768]{0,1:T(8,128)(2,1)}, u32[]{:S(2)}, u32[]{:S(2)}) collective-permute-start(bf16[768,768]{0,1:T(8,128)(2,1)} %convolution_convert_fusion), channel_id=1, source_target_pairs={{0,8},{8,0},{1,9},{9,1},{2,10},{10,2},{3,11},{11,3},{4,12},{12,4},... | collective-permute-start | bytes 3538952 | tf_op jit(solution)/shard_map/ppermute | solution.py:23
  122.2 29.9 %collective-permute-start.11 = (bf16[768,768]{0,1:T(8,128)(2,1)}, bf16[768,768]{0,1:T(8,128)(2,1)}, u32[]{:S(2)}, u32[]{:S(2)}) collective-permute-start(bf16[768,768]{0,1:T(8,128)(2,1)} %convolution_convert_fusion.1), channel_id=1, source_target_pairs={{0,4},{4,0},{1,5},{5,1},{2,6},{6,2},{3,7},{7,3},{8,12},{12,8},{9,1... | collective-permute-start | bytes 3538952 | tf_op jit(solution)/shard_map/ppermute | solution.py:23
  143.6 1.4 copy-start.9
  145.9 17.4 %collective-permute-start.14 = (bf16[384,768]{0,1:T(8,128)(2,1)}, bf16[384,768]{0,1:T(8,128)(2,1)}, u32[]{:S(2)}, u32[]{:S(2)}) collective-permute-start(bf16[384,768]{0,1:T(8,128)(2,1)} %dynamic-slice_convert_fusion), channel_id=1, source_target_pairs={{0,4},{4,0},{1,5},{5,1},{2,6},{6,2},{3,7},{7,3},{8,12},{12,8},{9,1... | collective-permute-start | bytes 1769480 | tf_op jit(solution)/shard_map/ppermute | solution.py:23
  152.1 11.2 %copy-start.10 = (f32[768,768]{0,1:T(8,128)S(1)}, f32[768,768]{0,1:T(8,128)}, u32[]{:S(2)}) copy-start(f32[768,768]{0,1:T(8,128)} %copy-done.9) | copy-start | bytes 7077892
  156.0 1.4 copy-start.7
  158.3 63.0 %collective-permute-start.12 = (bf16[384,768]{0,1:T(8,128)(2,1)}, bf16[384,768]{0,1:T(8,128)(2,1)}, u32[]{:S(2)}, u32[]{:S(2)}) collective-permute-start(bf16[384,768]{0,1:T(8,128)(2,1)} %dynamic-slice_convert_fusion.1), channel_id=1, source_target_pairs={{0,8},{8,0},{1,9},{9,1},{2,10},{10,2},{3,11},{11,3},{4,12},{12,4},... | collective-permute-start | bytes 1769480 | tf_op jit(solution)/shard_map/ppermute | solution.py:23
  165.5 7.9 %copy-start.11 = (bf16[3072,1536]{1,0:T(8,128)(2,1)S(1)}, bf16[3072,1536]{1,0:T(8,128)(2,1)}, u32[]{:S(2)}) copy-start(bf16[3072,1536]{1,0:T(8,128)(2,1)} %all-gather.2.cloned.1.call-done) | copy-start | bytes 28311556
  169.9 7.5 %copy-start.4 = (bf16[1,128,3072]{1,2,0:T(8,128)(2,1)S(1)}, bf16[1,128,3072]{1,2,0:T(8,128)(2,1)}, u32[]{:S(2)}) copy-start(bf16[1,128,3072]{1,2,0:T(8,128)(2,1)} %copy.33) | copy-start | bytes 2359300
  169.9 44.0 %collective-permute-start.4 = (bf16[256,768]{1,0:T(8,128)(2,1)S(1)}, bf16[256,768]{1,0:T(8,128)(2,1)S(1)}, u32[]{:S(2)}, u32[]{:S(2)}) collective-permute-start(bf16[256,768]{1,0:T(8,128)(2,1)S(1)} %fusion.16), channel_id=1, source_target_pairs={{0,16},{16,0},{1,17},{17,1},{2,18},{18,2},{3,19},{19,3},{4,20},{20... | collective-permute-start | bytes 1179656 | tf_op jit(solution)/shard_map/ppermute | solution.py:23
  176.3 31.1 %collective-permute-start.5 = (bf16[256,768]{1,0:T(8,128)(2,1)S(1)}, bf16[256,768]{1,0:T(8,128)(2,1)S(1)}, u32[]{:S(2)}, u32[]{:S(2)}) collective-permute-start(bf16[256,768]{1,0:T(8,128)(2,1)S(1)} %fusion.19), channel_id=1, source_target_pairs={{0,16},{16,0},{1,17},{17,1},{2,18},{18,2},{3,19},{19,3},{4,20},{20... | collective-permute-start | bytes 1179656 | tf_op jit(solution)/shard_map/ppermute | solution.py:23
  213.3 16.6 %collective-permute-start.6 = (bf16[3,128,768]{2,1,0:T(8,128)(2,1)}, bf16[3,128,768]{2,1,0:T(8,128)(2,1)}, u32[]{:S(2)}, u32[]{:S(2)}) collective-permute-start(bf16[3,128,768]{2,1,0:T(8,128)(2,1)} %get-tuple-element.16), channel_id=1, source_target_pairs={{0,1},{1,0},{2,3},{3,2},{4,5},{5,4},{6,7},{7,6},{8,9},{9,8},{10,11... | collective-permute-start | bytes 1769480 | tf_op jit(solution)/shard_map/ppermute | solution.py:23
  213.9 7.4 %copy-start.8 = (f32[768,768]{0,1:T(8,128)S(1)}, f32[768,768]{0,1:T(8,128)}, u32[]{:S(2)}) copy-start(f32[768,768]{0,1:T(8,128)} %copy-done.7) | copy-start | bytes 7077892
  219.9 2.6 %copy-start.3 = (f32[384,768]{0,1:T(8,128)S(1)}, f32[384,768]{0,1:T(8,128)}, u32[]{:S(2)}) copy-start(f32[384,768]{0,1:T(8,128)} %convert_add_fusion.2) | copy-start | bytes 3538948
  219.9 20.8 %collective-permute-start.7 = (bf16[3,128,768]{2,1,0:T(8,128)(2,1)}, bf16[3,128,768]{2,1,0:T(8,128)(2,1)}, u32[]{:S(2)}, u32[]{:S(2)}) collective-permute-start(bf16[3,128,768]{2,1,0:T(8,128)(2,1)} %get-tuple-element.17), channel_id=1, source_target_pairs={{0,1},{1,0},{2,3},{3,2},{4,5},{5,4},{6,7},{7,6},{8,9},{9,8},{10,11... | collective-permute-start | bytes 1769480 | tf_op jit(solution)/shard_map/ppermute | solution.py:23
Sparse Core Ops, SparseCore 0:
  9.6 80.8 all-gather.1

commit v2 on v1

--- a/solution.py
+++ b/solution.py
@@ -120,7 +120,7 @@
     )(mine, *own, far)
 
 
-def backward(mine, own, far, grads, first_head, heads, held):
+def backward(mine, own, far, partial, terms, first_head, heads, held):
     tokens, width = own[0].shape
     _, rest, features = far.shape
     length = tokens + rest
@@ -133,15 +133,16 @@
     far_spec = pl.BlockSpec((3, rest, block), lambda h, mine: (0, 0, start + h))
     grad_spec = pl.BlockSpec((length, block), lambda h, mine: (0, h))
     any_spec = pl.BlockSpec(memory_space=pl.ANY)
-    before = 5 + len(grads)
+    before = 6 + len(terms)
     return pl.pallas_call(
-        functools.partial(backward_kernel, step, len(held), len(grads)),
+        functools.partial(backward_kernel, step, len(held), 1 + len(terms)),
         grid_spec=pltpu.PrefetchScalarGridSpec(
             num_scalar_prefetch=1,
             grid=(grid,),
             in_specs=[own_spec] * 3
             + [far_spec]
-            + [grad_spec] * len(grads)
+            + [pl.BlockSpec((length, block), lambda h, mine: (0, start + h))]
+            + [grad_spec] * len(terms)
             + [any_spec] * len(held),
             out_specs=[own_spec] * 3
             + [pl.BlockSpec((3, rest, block), lambda h, mine: (0, 0, h))],
@@ -152,29 +153,141 @@
         compiler_params=params(),
         cost_estimate=cost(6, heads, length, 9),
         name="backward",
-    )(mine, *own, far, *grads, *held)
-
-
-def summed_rows(grads, attended, first, second):
-    tokens, _, _, rows = grads.shape
-    inner = lax.axis_size(second)
-
-    def product(by):
-        chosen = part_of(grads, first, by, 1).reshape(tokens, inner * rows)
-        return dot(chosen, attended, ((0,), (0,)))
-
-    sent = [shift(product(by).astype(jnp.bfloat16), first, by) for by in others(first)]
-    total = product(0)
-    for term in sent:
-        total = total + term.astype(jnp.float32)
-    sent = [
-        shift(part_of(total, second, by, 0).astype(jnp.bfloat16), second, by)
-        for by in others(second)
-    ]
-    final = part_of(total, second, 0, 0)
-    for term in sent:
-        final = final + term.astype(jnp.float32)
-    return final
+    )(mine, *own, far, partial, *terms, *held)
+
+
+def partial_kernel(pieces, at_ref, own_ref, far_ref, *refs):
+    weights, (out_ref, every_row, every_weight) = refs[:pieces], refs[pieces:]
+    tokens = own_ref.shape[0]
+    rows = weights[0].shape[0]
+
+    @pl.when(pl.program_id(0) == 0)
+    def _():
+        every_row[:tokens] = own_ref[...]
+        every_row[tokens:] = far_ref[...]
+
+    for i, weight in enumerate(weights):
+        every_weight[pl.ds(pl.multiple_of(at_ref[i] * rows, rows), rows), :] = weight[...]
+    out_ref[...] = dot(every_row[...], every_weight[...], ((1,), (0,))).astype(out_ref.dtype)
+
+
+def partial_product(at, own, far, weights, start, wide, dtype):
+    tokens, depth = own.shape
+    rest = far.shape[0]
+    rows = weights[0].shape[0]
+    block = 256 if wide % 256 == 0 else 128
+    first = start // block
+    return pl.pallas_call(
+        functools.partial(partial_kernel, len(weights)),
+        grid_spec=pltpu.PrefetchScalarGridSpec(
+            num_scalar_prefetch=1,
+            grid=(wide // block,),
+            in_specs=[
+                pl.BlockSpec((tokens, depth), lambda i, at: (0, 0)),
+                pl.BlockSpec((rest, depth), lambda i, at: (0, 0)),
+            ]
+            + [pl.BlockSpec((rows, block), lambda i, at: (0, first + i))] * len(weights),
+            out_specs=pl.BlockSpec((tokens + rest, block), lambda i, at: (0, i)),
+            scratch_shapes=[
+                pltpu.VMEM((tokens + rest, depth), jnp.bfloat16),
+                pltpu.VMEM((depth, block), jnp.bfloat16),
+            ],
+        ),
+        out_shape=jax.ShapeDtypeStruct((tokens + rest, wide), dtype),
+        compiler_params=params(),
+        cost_estimate=pl.CostEstimate(
+            flops=2 * (tokens + rest) * depth * wide,
+            bytes_accessed=2 * depth * (tokens + rest + wide),
+            transcendentals=0,
+        ),
+        name="partial",
+    )(at, own, far, *weights)
+
+
+def rows_kernel(pieces, at_ref, *refs):
+    inputs, (out_ref, every_grad, every_attended) = refs[: 3 * pieces], refs[3 * pieces :]
+    tokens = inputs[0].shape[0]
+    length = inputs[2].shape[0]
+
+    @pl.when(pl.program_id(0) == 0)
+    def _():
+        for i in range(pieces):
+            every_attended[i * length : (i + 1) * length] = inputs[3 * i + 2][...]
+
+    for i in range(pieces):
+        every_grad[i * length : i * length + tokens] = inputs[3 * i][...]
+        every_grad[i * length + tokens : (i + 1) * length] = inputs[3 * i + 1][...]
+    out_ref[...] = dot(every_grad[...], every_attended[...], ((0,), (0,))).astype(out_ref.dtype)
+
+
+def rows_product(at, pieces, rows, group, groups, dtype):
+    length, features = pieces[0][2].shape
+    wide = features // groups
+    operands, specs = [], []
+    for own, far, attended in pieces:
+        for grad in (own, far):
+            tokens = grad.shape[0]
+            if rows % 128 == 0:
+                operands.append(grad)
+                specs.append(pl.BlockSpec((tokens, rows), lambda i, at: (0, at[i])))
+            else:
+                operands.append(jnp.swapaxes(grad.reshape(tokens, -1, rows), 0, 1))
+                specs.append(pl.BlockSpec((None, tokens, rows), lambda i, at: (at[i], 0, 0)))
+        operands.append(attended)
+        specs.append(pl.BlockSpec((length, wide), lambda i, at: (0, group)))
+    depth = length * len(pieces)
+    count = at.shape[0]
+    return pl.pallas_call(
+        functools.partial(rows_kernel, len(pieces)),
+        grid_spec=pltpu.PrefetchScalarGridSpec(
+            num_scalar_prefetch=1,
+            grid=(count,),
+            in_specs=specs,
+            out_specs=pl.BlockSpec((None, rows, wide), lambda i, at: (i, 0, 0)),
+            scratch_shapes=[
+                pltpu.VMEM((depth, rows), jnp.bfloat16),
+                pltpu.VMEM((depth, wide), jnp.bfloat16),
+            ],
+        ),
+        out_shape=jax.ShapeDtypeStruct((count, rows, wide), dtype),
+        compiler_params=params(),
+        cost_estimate=pl.CostEstimate(
+            flops=2 * depth * count * rows * wide,
+            bytes_accessed=2 * depth * (count * rows + wide),
+            transcendentals=0,
+        ),
+        name="rows",
+    )(at, *operands)
+
+
+def place(axis, by=0):
+    return (lax.axis_index(axis) + by) % lax.axis_size(axis)
+
+
+def block_at(zl, x, core):
+    return ((zl * lax.axis_size("x") + x) * lax.axis_size("core") + core).astype(jnp.int32)
+
+
+def blocks_along(axis, by):
+    if axis == "x":
+        zl = jnp.arange(lax.axis_size("zl"))
+        return block_at(zl, place("x", by), place("core"))
+    return block_at(place("zl", by), jnp.arange(lax.axis_size("x")), place("core"))
+
+
+def gathered_weights(own):
+    found = [((0, 0), own)]
+    found += [((0, by), shift(own, "x", by)) for by in others("x")]
+    for by in others("zl"):
+        far = shift(own, "zl", by)
+        found.append(((by, 0), far))
+        found += [((by, bx), shift(far, "x", bx)) for bx in others("x")]
+    every = [((zl, x, 0), block) for (zl, x), block in found]
+    every += [
+        ((zl, x, by), shift(block, "core", by)) for by in others("core") for (zl, x), block in found
+    ]
+    at = [block_at(place("zl", -zl), place("x", -x), place("core", -c)) for (zl, x, c), _ in every]
+    return jnp.stack(at), [block for _, block in every]
 
 
 def shards(grad_out, queries, keys, values, out_weight):
@@ -188,11 +301,14 @@
     token_scale = 1.0 / math.sqrt(clips * length)
     me = mine.astype(jnp.int32).reshape(1)
 
-    weight = lax.all_gather(out_weight, ("zl", "x", "core"), axis=0, tiled=True)
+    def along_seq(array, dim=0):
+        arrived = [shift(array, "seq", by) for by in others("seq")]
+        return arrived[0] if seq == 2 else jnp.concatenate(arrived, axis=dim)
+
+    at, weights = gathered_weights(out_weight)
 
     own_grad = grad_out[0]
-    halves = [part_of(own_grad, "zh", 0, 1)]
-    halves += [shift(part_of(own_grad, "zh", by, 1), "zh", by) for by in others("zh")]
+    halves = [shift(part_of(own_grad, "zh", by, 1), "zh", by) for by in others("zh")]
 
     own = (queries[0], keys[0], values[0])
     pieces = [
@@ -200,53 +316,64 @@
         for by in others("seq")
     ]
     far = pieces[0] if seq == 2 else jnp.concatenate(pieces, axis=1)
-
-    grads = [
-        jnp.concatenate([half] + [shift(half, "seq", by) for by in others("seq")], axis=0)
-        for half in halves
-    ]
+    halves = [part_of(own_grad, "zh", 0, 1)] + halves
+
+    grads = [(half, along_seq(half)) for half in halves]
 
     attended = forward(me, own, far)
     attends = [attended] + [shift(attended, "zh", by) for by in others("zh")]
 
     groups = 2 if heads % 4 == 0 else 1
     wide = features // groups
-    partial = []
-    for group in range(groups):
-        chosen = weight[:, group * wide : (group + 1) * wide]
-        terms = [
-            shift(dot(grads[by], chosen, ((1,), (0,))).astype(jnp.bfloat16), "zh", -by)
+    sent = [
+        [
+            partial_product(at, *grads[by], weights, group * wide, wide, jnp.bfloat16)
             for by in others("zh")
         ]
-        partial.append([dot(grads[0], chosen, ((1,), (0,)))] + terms)
-
-    every_grad, every_attended = [], []
-    cores = lax.axis_size("core")
-    stacked = jnp.concatenate(grads, axis=0)
-    count = stacked.shape[0]
-    stacked = stacked.reshape(count, -1, cores, rows)
-    attends = jnp.concatenate(attends, axis=0)
-    for by in range(cores):
-        chosen = part_of(stacked, "core", by, 2)[:, :, 0]
-        every_grad.append(shift(chosen, "core", by) if by else chosen)
-        every_attended.append(shift(attends, "core", by) if by else attends)
-    every_grad = jnp.concatenate(every_grad, axis=0)
-    every_attended = jnp.concatenate(every_attended, axis=0)
-    every_grad = every_grad.reshape(
-        every_grad.shape[0], lax.axis_size("zl"), lax.axis_size("x"), rows
-    )
-    middle = features // 2
-    left = summed_rows(
-        jnp.swapaxes(every_grad, 1, 2), every_attended[:, :middle], "x", "zl"
-    )
-    right = summed_rows(every_grad, every_attended[:, middle:], "zl", "x")
-    weight_grad = jnp.concatenate([left, right], axis=1) * token_scale
+        for group in range(groups)
+    ]
+    partial = partial_product(at, *grads[0], weights, 0, features, jnp.float32)
+    terms = [
+        [shift(term, "zh", -by) for by, term in zip(others("zh"), group)] for group in sent
+    ]
+
+    clip_pieces = [(*grad, attend) for grad, attend in zip(grads, attends)]
+    clip_pieces += [
+        tuple(shift(array, "core", by) for array in piece)
+        for by in others("core")
+        for piece in clip_pieces
+    ]
+    clip_pieces, sent = lax.optimization_barrier((clip_pieces, sent))
+    splits = 2 if features % 256 == 0 else 1
+    orders = [("x", "zl"), ("zl", "x")][:splits]
+
+    def product(axis, by, split, dtype):
+        return rows_product(blocks_along(axis, by), clip_pieces, rows, split, splits, dtype)
+
+    first = [
+        [shift(product(axis, by, split, jnp.bfloat16), axis, by) for by in others(axis)]
+        for split, (axis, _) in enumerate(orders)
+    ]
+    kept = [product(axis, 0, split, jnp.float32) for split, (axis, _) in enumerate(orders)]
+    columns = []
+    for (_, axis), arrived, total in zip(orders, first, kept):
+        for term in arrived:
+            total = total + term.astype(jnp.float32)
+        second = [
+            shift(part_of(total, axis, by, 0).astype(jnp.bfloat16), axis, by)
+            for by in others(axis)
+        ]
+        final = part_of(total, axis, 0, 0)
+        for term in second:
+            final = final + term.astype(jnp.float32)
+        columns.append(final[0])
+    weight_grad = jnp.concatenate(columns, axis=1) * token_scale
 
     result, arrivals = [], []
     for group in range(groups):
-        first = group * wide // HEAD_DIM
+        start = group * wide // HEAD_DIM
         *result, leaving = backward(
-            me, own, far, partial[group], first, wide // HEAD_DIM, result
+            me, own, far, partial, terms[group], start, wide // HEAD_DIM, result
         )
         arrivals.append(
             [

time: 250 us -> 222 us (0.89)
  Pallas kernels: 18.5 us -> 57.1 us
  matrix products: 26.9 us -> 0 us
  local copies, waits for them, and re-layouts: 38 us -> 13.4 us
  other arithmetic: 19.2 us -> 5.38 us
  between operations: 14.2 us -> 0.98 us
  starting transfers between devices: 18.6 us -> 27.3 us
  waiting for transfers between devices: 114 us -> 117 us
    pallas_call x2 -> x9, Pallas kernels: 11.9 us -> 50.5 us  [the longest x4 19.9 us: rows_product(): pl.pallas_call(functools.partial(rows_kernel, len(pieces)), grid_spec=plt...]
    dot_general x8 -> x0, matrix products: 26.9 us -> none  [dot(): lax.dot_general(a, b, (contract, ((), ())), preferred_element_type=jnp.fl...]
    concatenate x5 -> x0, other arithmetic: 14.5 us -> none  [the longest x2 7.69 us: shards(): every_grad = jnp.concatenate(every_grad, axis=0)]
    dynamic_slice x9 -> x3, local copies, waits for them, and re-layouts: 15.8 us -> 3.62 us  [part_of(): return lax.dynamic_slice_in_dim(array, at * size, size, dim)]
    ppermute x15 -> x26, starting transfers between devices: 18.5 us -> 27.3 us  [shift(): lax.ppermute(array, axis, [(i, (i + by) % count) for i in range(count)])]
    another operation x2 -> x1, local copies, waits for them, and re-layouts: 5.16 us -> 0.08 us  [gathered_weights(): return (jnp.stack(at), [block for _, block in every])]
    ppermute x15 -> x26, waiting for transfers between devices: 113 us -> 117 us  [shift(): lax.ppermute(array, axis, [(i, (i + by) % count) for i in range(count)])]
    unnamed x27 -> x50, local copies, waits for them, and re-layouts: 9.36 us -> 7.87 us
  transfers between devices with their start and end apart: 16 -> 26, of which waited for: 9 -> 8; matrix products, arithmetic and copies ran while one was open for 32% -> 4% of each run, Pallas kernels for 7% -> 24%
where the time goes in v2:
time: 222 us; the launch traced here: 221 us
  waiting for transfers between devices  117 us (53%)
  Pallas kernels  57.1 us (26%)
  starting transfers between devices  27.3 us (12%)
  local copies, waits for them, and re-layouts  13.4 us (6%)
  other arithmetic  5.38 us (2%)
    ppermute x26, waiting for transfers between devices, shift(): lax.ppermute(array, axis, [(i, (i + by) % count) for i in range(count)])  117 us
    ppermute x26, starting transfers between devices, shift(): lax.ppermute(array, axis, [(i, (i + by) % count) for i in range(count)])  27.3 us
    pallas_call x4, Pallas kernels, rows_product(): pl.pallas_call(functools.partial(rows_kernel, len(pieces)), grid_spec=plt...  19.9 us
    pallas_call x3, Pallas kernels, partial_product(): pl.pallas_call(functools.partial(partial_kernel, len(weights)), grid_spec...  18.9 us
    pallas_call x2, Pallas kernels, backward(): pl.pallas_call(functools.partial(backward_kernel, step, len(held), 1 + le...  11.7 us
    unnamed x50, local copies, waits for them, and re-layouts  7.87 us
    pallas_call x1, Pallas kernels, forward(): pl.pallas_call(functools.partial(forward_kernel, step), grid_spec=pltpu.P...  6.58 us
  transfers between devices with their start and end apart: 26, of which 8 were waited for; matrix products, arithmetic and copies ran while one was open for 4% of the time, Pallas kernels for 24%

profile of v2, /device:TPU:0, one launch (start us, length us, event | category | flops | bytes accessed | tf_op | source)
XLA Modules:
  0.0 220.8 jit_solution(10995819406825997057)
XLA Ops:
  0.6 3.1 %collective-permute-start.3 = (bf16[384,1536]{1,0:T(8,128)(2,1)}, bf16[384,1536]{1,0:T(8,128)(2,1)}, u32[]{:S(2)}, u32[]{:S(2)}) collective-permute-start(bf16[384,1536]{1,0:T(8,128)(2,1)} %refs_0_.5), channel_id=1, source_target_pairs={{0,8},{8,0},{1,9},{9,1},{2,10},{10,2},{3,11},{11,3},{4,12},{12,4},... | collective-permute-start | bytes 3538952 | tf_op jit(solution)/shard_map/ppermute | solution.py:23
  3.7 1.5 collective-permute-start.2
  5.2 2.4 %dynamic-slice_bitcast_fusion = (bf16[128,3072]{1,0:T(8,128)(2,1)}, bf16[128,3072]{1,0:T(8,128)(2,1)S(1)}) fusion(bf16[1,128,6144]{2,1,0:T(8,128)(2,1)} %param.5, s32[]{:T(128)S(6)} %select_n.153, s32[]{:T(128)S(6)} %select_n.151), kind=kLoop, calls=%fused_computation.8 | loop fusion | bytes 3145736 | tf_op jit(solution)/shard_map/dynamic_slice | solution.py:34
  7.6 1.5 collective-permute-start.1
  9.1 2.6 %collective-permute-start.9 = (bf16[128,3072]{1,0:T(8,128)(2,1)}, bf16[128,3072]{1,0:T(8,128)(2,1)S(1)}, u32[]{:S(2)}, u32[]{:S(2)}) collective-permute-start(bf16[128,3072]{1,0:T(8,128)(2,1)} %get-tuple-element.44), channel_id=1, source_target_pairs={{0,16},{16,0},{1,17},{17,1},{2,18},{18,2},{3,19},{19,3},{4,20},{20... | collective-permute-start | bytes 2359304 | tf_op jit(solution)/shard_map/ppermute | solution.py:23
  11.7 1.2 constant_dynamic-slice_fusion
  13.0 0.0 copy-start.11
  13.0 0.1 pad_maximum_fusion
  13.1 0.6 collective-permute-start
  13.7 33.1 %collective-permute-done.3.refs_2_ = bf16[384,1536]{1,0:T(8,128)(2,1)} collective-permute-done((bf16[384,1536]{1,0:T(8,128)(2,1)}, bf16[384,1536]{1,0:T(8,128)(2,1)}, u32[]{:S(2)}, u32[]{:S(2)}) %collective-permute-start.3) | collective-permute-done | bytes 1179680 | tf_op jit(solution)/shard_map/ppermute | solution.py:23
  46.9 1.7 collective-permute-start.4
  48.5 0.5 collective-permute-start.16
  49.0 0.1 collective-permute-start.6
  49.1 2.5 %collective-permute-done.far = bf16[3,128,1536]{2,1,0:T(8,128)(2,1)S(1)} collective-permute-done((bf16[3,128,1536]{2,1,0:T(8,128)(2,1)S(1)}, bf16[3,128,1536]{2,1,0:T(8,128)(2,1)S(1)}, u32[]{:S(2)}, u32[]{:S(2)}) %collective-permute-start) | collective-permute-done | bytes 1179680 | tf_op jit(solution)/shard_map/ppermute | solution.py:23
  51.6 22.7 %collective-permute-done.4.refs_3_ = bf16[384,1536]{1,0:T(8,128)(2,1)S(1)} collective-permute-done((bf16[384,1536]{1,0:T(8,128)(2,1)}, bf16[384,1536]{1,0:T(8,128)(2,1)S(1)}, u32[]{:S(2)}, u32[]{:S(2)}) %collective-permute-start.4) | collective-permute-done | bytes 1179680 | tf_op jit(solution)/shard_map/ppermute | solution.py:23
  74.3 6.6 %forward.1.refs_2_ = bf16[256,1536]{1,0:T(8,128)(2,1)} custom-call(s32[1]{0:T(128)} %bitcast.mine_ref, bf16[128,3072]{1,0:T(8,128)(2,1)S(1)} %bitcast.23, bf16[128,3072]{1,0:T(8,128)(2,1)S(1)} %bitcast.26, bf16[128,3072]{1,0:T(8,128)(2,1)S(1)} %bitcast.29, bf16[3,128,1536]{2,1,0:T(8,128)(2,1)S(1)} %collective-permute-done.far), custom_call_target="tpu_custom_call" | custom-call | flops 402653184 | bytes 3145728 | tf_op jit(solution)/shard_map/forward/pallas_call | solution.py:108
  80.9 0.9 copy-done.1
  81.7 1.4 collective-permute-start.10
  83.1 1.7 collective-permute-start.15
  84.8 16.9 %collective-permute-done.10.far_ref.refs_4_ = bf16[128,3072]{1,0:T(8,128)(2,1)S(1)} collective-permute-done((bf16[128,3072]{1,0:T(8,128)(2,1)S(1)}, bf16[128,3072]{1,0:T(8,128)(2,1)S(1)}, u32[]{:S(2)}, u32[]{:S(2)}) %collective-permute-start.10) | collective-permute-done | bytes 786464 | tf_op jit(solution)/shard_map/ppermute | solution.py:23
  101.7 19.1 %collective-permute-done.15.refs_5_ = bf16[256,1536]{1,0:T(8,128)(2,1)} collective-permute-done((bf16[256,1536]{1,0:T(8,128)(2,1)}, bf16[256,1536]{1,0:T(8,128)(2,1)}, u32[]{:S(2)}, u32[]{:S(2)}) %collective-permute-start.15) | collective-permute-done | bytes 786464 | tf_op jit(solution)/shard_map/ppermute | solution.py:23
  120.8 0.5 collective-permute-start.18
  121.3 0.1 collective-permute-start.20
  121.4 0.4 copy-done.20
  121.9 0.5 copy-done.21
  122.4 1.0 copy-done.22
  123.4 0.4 collective-permute-start.21
  123.8 0.1 stack.42.at_ref
  123.9 1.3 copy-done.6
  125.2 4.9 %partial.4 = bf16[256,768]{1,0:T(8,128)(2,1)S(1)} custom-call(s32[8]{0:T(128)S(1)} %stack.42.at_ref, bf16[128,3072]{1,0:T(8,128)(2,1)S(1)} %collective-permute-done.9.own_ref.refs_3_, bf16[128,3072]{1,0:T(8,128)(2,1)S(1)} %collective-permute-done.10.far_ref.refs_4_, bf16[384,1536]{1,0:T(8,128)(2,1)S(1)} %copy-done.6, ...), custom_call_target="tpu_custom_call" | custom-call | flops 1207959552 | bytes 6291456 | tf_op jit(solution)/shard_map/partial/pallas_call | solution.py:180
  130.1 0.0 copy-start.2
  130.1 4.9 %partial.5 = bf16[256,768]{1,0:T(8,128)(2,1)S(1)} custom-call(s32[8]{0:T(128)S(1)} %stack.42.at_ref, bf16[128,3072]{1,0:T(8,128)(2,1)S(1)} %collective-permute-done.9.own_ref.refs_3_, bf16[128,3072]{1,0:T(8,128)(2,1)S(1)} %collective-permute-done.10.far_ref.refs_4_, bf16[384,1536]{1,0:T(8,128)(2,1)S(1)} %copy-done.6, ...), custom_call_target="tpu_custom_call" | custom-call | flops 1207959552 | bytes 6291456 | tf_op jit(solution)/shard_map/partial/pallas_call | solution.py:180
  135.1 0.0 copy-start.17
  135.1 4.9 %rows.7 = bf16[2,384,768]{2,1,0:T(8,128)(2,1)} custom-call(s32[2]{0:T(128)S(1)} %multiply_add_fusion.at_ref, bf16[128,3072]{1,0:T(8,128)(2,1)S(1)} %get-tuple-element.32.own_ref.refs_0_, bf16[128,3072]{1,0:T(8,128)(2,1)S(1)} %collective-permute-done.1.far_ref.refs_1_, bf16[256,1536]{1,0:T(8,128)(2,1)} %forward.1.refs_2_, ...), custom_call_target="tpu_custom_call" | custom-call | flops 1207959552 | bytes 3145728 | tf_op jit(solution)/shard_map/rows/pallas_call | solution.py:240
  140.1 0.0 copy-start.3
  140.1 1.1 copy-done.3
  141.2 4.9 %rows.5 = bf16[2,384,768]{2,1,0:T(8,128)(2,1)} custom-call(s32[2]{0:T(128)S(1)} %multiply_add_fusion.2.at_ref, bf16[128,3072]{1,0:T(8,128)(2,1)S(1)} %get-tuple-element.32.own_ref.refs_0_, bf16[128,3072]{1,0:T(8,128)(2,1)S(1)} %collective-permute-done.1.far_ref.refs_1_, bf16[256,1536]{1,0:T(8,128)(2,1)} %forward.1.refs_2_, ...), custom_call_target="tpu_custom_call" | custom-call | flops 1207959552 | bytes 3145728 | tf_op jit(solution)/shard_map/rows/pallas_call | solution.py:240
  146.1 1.5 collective-permute-start.22
  147.6 3.1 %collective-permute-start.11 = (bf16[256,768]{1,0:T(8,128)(2,1)S(1)}, bf16[256,768]{1,0:T(8,128)(2,1)S(1)}, u32[]{:S(2)}, u32[]{:S(2)}) collective-permute-start(bf16[256,768]{1,0:T(8,128)(2,1)S(1)} %partial.4), channel_id=1, source_target_pairs={{0,16},{16,0},{1,17},{17,1},{2,18},{18,2},{3,19},{19,3},{4,20},{20... | collective-permute-start | bytes 1179656 | tf_op jit(solution)/shard_map/ppermute | solution.py:23
  150.7 0.1 collective-permute-start.12
  150.8 1.1 copy-done.4
  151.9 5.1 %rows.6 = f32[2,384,768]{2,1,0:T(8,128)} custom-call(s32[2]{0:T(128)S(1)} %multiply_add_fusion.1.at_ref, bf16[128,3072]{1,0:T(8,128)(2,1)S(1)} %get-tuple-element.32.own_ref.refs_0_, bf16[128,3072]{1,0:T(8,128)(2,1)S(1)} %collective-permute-done.1.far_ref.refs_1_, bf16[256,1536]{1,0:T(8,128)(2,1)} %forward.1.refs_2_, ...), custom_call_target="tpu_custom_call" | custom-call | flops 1207959552 | bytes 3145728 | tf_op jit(solution)/shard_map/rows/pallas_call | solution.py:240
  157.0 5.1 %rows.4 = f32[2,384,768]{2,1,0:T(8,128)} custom-call(s32[2]{0:T(128)S(1)} %multiply_add_fusion.3.at_ref, bf16[128,3072]{1,0:T(8,128)(2,1)S(1)} %get-tuple-element.32.own_ref.refs_0_, bf16[128,3072]{1,0:T(8,128)(2,1)S(1)} %collective-permute-done.1.far_ref.refs_1_, bf16[256,1536]{1,0:T(8,128)(2,1)} %forward.1.refs_2_, ...), custom_call_target="tpu_custom_call" | custom-call | flops 1207959552 | bytes 3145728 | tf_op jit(solution)/shard_map/rows/pallas_call | solution.py:240
  162.1 0.0 copy-start.12
  162.1 9.0 %partial.3.refs_0_ = f32[256,1536]{1,0:T(8,128)} custom-call(s32[8]{0:T(128)S(1)} %stack.42.at_ref, bf16[128,3072]{1,0:T(8,128)(2,1)S(1)} %get-tuple-element.32.own_ref.refs_0_, bf16[128,3072]{1,0:T(8,128)(2,1)S(1)} %collective-permute-done.1.far_ref.refs_1_, bf16[384,1536]{1,0:T(8,128)(2,1)S(1)} %copy-done.7, ...), custom_call_target="tpu_custom_call" | custom-call | flops 2415919104 | bytes 11010048 | tf_op jit(solution)/shard_map/partial/pallas_call | solution.py:180
  171.1 11.9 %collective-permute-done.12.refs_1_ = bf16[256,768]{1,0:T(8,128)(2,1)S(1)} collective-permute-done((bf16[256,768]{1,0:T(8,128)(2,1)}, bf16[256,768]{1,0:T(8,128)(2,1)S(1)}, u32[]{:S(2)}, u32[]{:S(2)}) %collective-permute-start.12) | collective-permute-done | bytes 393248 | tf_op jit(solution)/shard_map/ppermute | solution.py:23
  183.1 1.4 copy-done
  184.5 5.8 %backward.2 = (bf16[128,3072]{1,0:T(8,128)(2,1)}, bf16[128,3072]{1,0:T(8,128)(2,1)}, bf16[128,3072]{1,0:T(8,128)(2,1)}, bf16[3,128,768]{2,1,0:T(8,128)(2,1)S(1)}) custom-call(s32[1]{0:T(128)} %bitcast.mine_ref, bf16[128,3072]{1,0:T(8,128)(2,1)S(1)} %bitcast.24, bf16[128,3072]{1,0:T(8,128)(2,1)S(1)} %bitcast.27, bf16[128,3072]{1,0:T(8,128)(2,1)S(1)} %bitcast.30, ...), custom_call_target="tpu_custom_call" | custom-call | flops 603979776 | bytes 3538944 | tf_op jit(solution)/shard_map/backward/pallas_call | solution.py:137
  190.3 0.6 collective-permute-start.13
  190.9 5.9 %backward.3 = (bf16[128,3072]{1,0:T(8,128)(2,1)}, bf16[128,3072]{1,0:T(8,128)(2,1)}, bf16[128,3072]{1,0:T(8,128)(2,1)}, bf16[3,128,768]{2,1,0:T(8,128)(2,1)S(1)}) custom-call(s32[1]{0:T(128)} %bitcast.mine_ref, bf16[128,3072]{1,0:T(8,128)(2,1)S(1)} %bitcast.25, ...), custom_call_target="tpu_custom_call", output_to_operand_aliasing={{0}: (7, {}), {1}: (8, {}), {2}: (9, {})} | custom-call | flops 603979776 | bytes 3538944 | tf_op jit(solution)/shard_map/backward/pallas_call | solution.py:137
  196.8 1.4 collective-permute-start.14
  198.2 1.6 convert_add_fusion
  199.8 0.1 dynamic-slice_convert_fusion
  199.9 1.5 collective-permute-start.25
  201.4 1.6 convert_add_fusion.1
  203.0 0.1 dynamic-slice_convert_fusion.1
  203.1 3.6 %collective-permute-start.23 = (bf16[1,384,768]{2,1,0:T(8,128)(2,1)S(1)}, bf16[1,384,768]{2,1,0:T(8,128)(2,1)S(1)}, u32[]{:S(2)}, u32[]{:S(2)}) collective-permute-start(bf16[1,384,768]{2,1,0:T(8,128)(2,1)S(1)} %dynamic-slice_convert_fusion.1), channel_id=1, source_target_pairs={{0,8},{8,0},{1,9},{9,1},{2,10},{10,2},{3,11},{11,3},{4,12},{12,4},... | collective-permute-start | bytes 1769480 | tf_op jit(solution)/shard_map/ppermute | solution.py:23
  206.7 0.8 slice_dynamic-update-slice_fusion.1
  207.5 10.3 %collective-permute-done.14 = bf16[3,128,768]{2,1,0:T(8,128)(2,1)S(1)} collective-permute-done((bf16[3,128,768]{2,1,0:T(8,128)(2,1)S(1)}, bf16[3,128,768]{2,1,0:T(8,128)(2,1)S(1)}, u32[]{:S(2)}, u32[]{:S(2)}) %collective-permute-start.14) | collective-permute-done | bytes 589856 | tf_op jit(solution)/shard_map/ppermute | solution.py:23
  217.8 0.8 slice_dynamic-update-slice_fusion
  218.6 0.1 add_bitcast_fusion
  218.7 0.2 collective-permute-done.23
  218.9 0.1 add_bitcast_fusion.1
  219.1 1.7 maximum_multiply_fusion
  (66 shorter events, 0.2 us)
Async XLA Ops:
  0.6 46.2 %collective-permute-start.3 = (bf16[384,1536]{1,0:T(8,128)(2,1)}, bf16[384,1536]{1,0:T(8,128)(2,1)}, u32[]{:S(2)}, u32[]{:S(2)}) collective-permute-start(bf16[384,1536]{1,0:T(8,128)(2,1)} %refs_0_.5), channel_id=1, source_target_pairs={{0,8},{8,0},{1,9},{9,1},{2,10},{10,2},{3,11},{11,3},{4,12},{12,4},... | collective-permute-start | bytes 3538952 | tf_op jit(solution)/shard_map/ppermute | solution.py:23
  3.7 45.3 %collective-permute-start.2 = (bf16[384,1536]{1,0:T(8,128)(2,1)}, bf16[384,1536]{1,0:T(8,128)(2,1)}, u32[]{:S(2)}, u32[]{:S(2)}) collective-permute-start(bf16[384,1536]{1,0:T(8,128)(2,1)} %refs_0_.5), channel_id=1, source_target_pairs={{0,4},{4,0},{1,5},{5,1},{2,6},{6,2},{3,7},{7,3},{8,12},{12,8},{9,1... | collective-permute-start | bytes 3538952 | tf_op jit(solution)/shard_map/ppermute | solution.py:23
  7.6 5.4 %copy-start.10 = (bf16[1,128,3072]{2,1,0:T(8,128)(2,1)S(1)}, bf16[1,128,3072]{2,1,0:T(8,128)(2,1)}, u32[]{:S(2)}) copy-start(bf16[1,128,3072]{2,1,0:T(8,128)(2,1)} %param.6) | copy-start | bytes 2359300
  7.6 41.0 %collective-permute-start.1 = (bf16[128,3072]{1,0:T(8,128)(2,1)S(1)}, bf16[128,3072]{1,0:T(8,128)(2,1)S(1)}, u32[]{:S(2)}, u32[]{:S(2)}) collective-permute-start(bf16[128,3072]{1,0:T(8,128)(2,1)S(1)} %get-tuple-element.32.own_ref.refs_0_), channel_id=1, source_target_pairs={{0,1},{1,0},{2,3},{3,2},{4,5},{5,4},{6,7},{7,6},{8,9},{9,8},{10,11... | collective-permute-start | bytes 2359304 | tf_op jit(solution)/shard_map/ppermute | solution.py:23
  9.1 39.4 %collective-permute-start.9 = (bf16[128,3072]{1,0:T(8,128)(2,1)}, bf16[128,3072]{1,0:T(8,128)(2,1)S(1)}, u32[]{:S(2)}, u32[]{:S(2)}) collective-permute-start(bf16[128,3072]{1,0:T(8,128)(2,1)} %get-tuple-element.44), channel_id=1, source_target_pairs={{0,16},{16,0},{1,17},{17,1},{2,18},{18,2},{3,19},{19,3},{4,20},{20... | collective-permute-start | bytes 2359304 | tf_op jit(solution)/shard_map/ppermute | solution.py:23
  11.7 62.6 %copy-start.15 = (bf16[1,128,3072]{2,1,0:T(8,128)(2,1)S(1)}, bf16[1,128,3072]{2,1,0:T(8,128)(2,1)}, u32[]{:S(2)}) copy-start(bf16[1,128,3072]{2,1,0:T(8,128)(2,1)} %param.8) | copy-start | bytes 2359300
  12.9 61.3 %copy-start.13 = (bf16[1,128,3072]{2,1,0:T(8,128)(2,1)S(1)}, bf16[1,128,3072]{2,1,0:T(8,128)(2,1)}, u32[]{:S(2)}) copy-start(bf16[1,128,3072]{2,1,0:T(8,128)(2,1)} %param.7) | copy-start | bytes 2359300
  13.0 35.5 %copy-start.5 = (bf16[384,1536]{1,0:T(8,128)(2,1)S(1)}, bf16[384,1536]{1,0:T(8,128)(2,1)}, u32[]{:S(2)}) copy-start(bf16[384,1536]{1,0:T(8,128)(2,1)} %refs_0_.5) | copy-start | bytes 3538948
  13.0 61.3 %copy-start.11 = (bf16[1,128,3072]{2,1,0:T(8,128)(2,1)S(1)}, bf16[1,128,3072]{2,1,0:T(8,128)(2,1)}, u32[]{:S(2)}) copy-start(bf16[1,128,3072]{2,1,0:T(8,128)(2,1)} %param.6) | copy-start | bytes 2359300
  13.1 38.4 %collective-permute-start = (bf16[3,128,1536]{2,1,0:T(8,128)(2,1)S(1)}, bf16[3,128,1536]{2,1,0:T(8,128)(2,1)S(1)}, u32[]{:S(2)}, u32[]{:S(2)}) collective-permute-start(bf16[3,128,1536]{2,1,0:T(8,128)(2,1)S(1)} %pad_maximum_fusion), channel_id=1, source_target_pairs={{0,1},{1,0},{2,3},{3,2},{4,5},{5,4},{6,7},{7,6},{8,9},{9,8},{10,11... | collective-permute-start | bytes 3538952 | tf_op jit(solution)/shard_map/ppermute | solution.py:23
  46.9 27.4 %collective-permute-start.4 = (bf16[384,1536]{1,0:T(8,128)(2,1)}, bf16[384,1536]{1,0:T(8,128)(2,1)S(1)}, u32[]{:S(2)}, u32[]{:S(2)}) collective-permute-start(bf16[384,1536]{1,0:T(8,128)(2,1)} %collective-permute-done.3.refs_2_), channel_id=1, source_target_pairs={{0,4},{4,0},{1,5},{5,1},{2,6},{6,2},{3,7},{7,3},{8,12},{12,8},{9,1... | collective-permute-start | bytes 3538952 | tf_op jit(solution)/shard_map/ppermute | solution.py:23
  48.5 34.6 %collective-permute-start.5 = (bf16[384,1536]{1,0:T(8,128)(2,1)S(1)}, bf16[384,1536]{1,0:T(8,128)(2,1)S(1)}, u32[]{:S(2)}, u32[]{:S(2)}) collective-permute-start(bf16[384,1536]{1,0:T(8,128)(2,1)S(1)} %copy-done.5), channel_id=1, source_target_pairs={{0,2},{2,0},{1,3},{3,1},{4,6},{6,4},{5,7},{7,5},{8,10},{10,8},{9,1... | collective-permute-start | bytes 3538952 | tf_op jit(solution)/shard_map/ppermute | solution.py:23
  48.5 32.3 %collective-permute-start.16 = (bf16[128,3072]{1,0:T(8,128)(2,1)S(1)}, bf16[128,3072]{1,0:T(8,128)(2,1)S(1)}, u32[]{:S(2)}, u32[]{:S(2)}) collective-permute-start(bf16[128,3072]{1,0:T(8,128)(2,1)S(1)} %get-tuple-element.32.own_ref.refs_0_), channel_id=1, source_target_pairs={{0,2},{2,0},{1,3},{3,1},{4,6},{6,4},{5,7},{7,5},{8,10},{10,8},{9,1... | collective-permute-start | bytes 2359304 | tf_op jit(solution)/shard_map/ppermute | solution.py:23
  49.0 71.8 %collective-permute-start.6 = (bf16[384,1536]{1,0:T(8,128)(2,1)}, bf16[384,1536]{1,0:T(8,128)(2,1)S(1)}, u32[]{:S(2)}, u32[]{:S(2)}) collective-permute-start(bf16[384,1536]{1,0:T(8,128)(2,1)} %collective-permute-done.2.refs_1_), channel_id=1, source_target_pairs={{0,2},{2,0},{1,3},{3,1},{4,6},{6,4},{5,7},{7,5},{8,10},{10,8},{9,1... | collective-permute-start | bytes 3538952 | tf_op jit(solution)/shard_map/ppermute | solution.py:23
  51.6 29.3 %copy-start.8 = (bf16[3,128,1536]{2,1,0:T(8,128)(2,1)}, bf16[3,128,1536]{2,1,0:T(8,128)(2,1)S(1)}, u32[]{:S(2)}) copy-start(bf16[3,128,1536]{2,1,0:T(8,128)(2,1)S(1)} %collective-permute-done.far) | copy-start | bytes 3538948
  51.6 69.8 %collective-permute-start.7 = (bf16[384,1536]{1,0:T(8,128)(2,1)}, bf16[384,1536]{1,0:T(8,128)(2,1)S(1)}, u32[]{:S(2)}, u32[]{:S(2)}) collective-permute-start(bf16[384,1536]{1,0:T(8,128)(2,1)} %collective-permute-done.3.refs_2_), channel_id=1, source_target_pairs={{0,2},{2,0},{1,3},{3,1},{4,6},{6,4},{5,7},{7,5},{8,10},{10,8},{9,1... | collective-permute-start | bytes 3538952 | tf_op jit(solution)/shard_map/ppermute | solution.py:23
  74.2 6.6 %copy-start.18 = (bf16[384,1536]{1,0:T(8,128)(2,1)}, bf16[384,1536]{1,0:T(8,128)(2,1)S(1)}, u32[]{:S(2)}) copy-start(bf16[384,1536]{1,0:T(8,128)(2,1)S(1)} %collective-permute-done.4.refs_3_) | copy-start | bytes 3538948
  74.2 47.2 %collective-permute-start.8 = (bf16[384,1536]{1,0:T(8,128)(2,1)S(1)}, bf16[384,1536]{1,0:T(8,128)(2,1)S(1)}, u32[]{:S(2)}, u32[]{:S(2)}) collective-permute-start(bf16[384,1536]{1,0:T(8,128)(2,1)S(1)} %collective-permute-done.4.refs_3_), channel_id=1, source_target_pairs={{0,2},{2,0},{1,3},{3,1},{4,6},{6,4},{5,7},{7,5},{8,10},{10,8},{9,1... | collective-permute-start | bytes 3538952 | tf_op jit(solution)/shard_map/ppermute | solution.py:23
  80.8 0.9 copy-start.1
  81.7 19.9 %collective-permute-start.10 = (bf16[128,3072]{1,0:T(8,128)(2,1)S(1)}, bf16[128,3072]{1,0:T(8,128)(2,1)S(1)}, u32[]{:S(2)}, u32[]{:S(2)}) collective-permute-start(bf16[128,3072]{1,0:T(8,128)(2,1)S(1)} %collective-permute-done.9.own_ref.refs_3_), channel_id=1, source_target_pairs={{0,1},{1,0},{2,3},{3,2},{4,5},{5,4},{6,7},{7,6},{8,9},{9,8},{10,11... | collective-permute-start | bytes 2359304 | tf_op jit(solution)/shard_map/ppermute | solution.py:23
  83.1 38.3 %copy-start.19 = (bf16[384,1536]{1,0:T(8,128)(2,1)}, bf16[384,1536]{1,0:T(8,128)(2,1)S(1)}, u32[]{:S(2)}) copy-start(bf16[384,1536]{1,0:T(8,128)(2,1)S(1)} %collective-permute-done.5.refs_4_) | copy-start | bytes 3538948
  83.1 37.7 %collective-permute-start.15 = (bf16[256,1536]{1,0:T(8,128)(2,1)}, bf16[256,1536]{1,0:T(8,128)(2,1)}, u32[]{:S(2)}, u32[]{:S(2)}) collective-permute-start(bf16[256,1536]{1,0:T(8,128)(2,1)} %forward.1.refs_2_), channel_id=1, source_target_pairs={{0,16},{16,0},{1,17},{17,1},{2,18},{18,2},{3,19},{19,3},{4,20},{20... | collective-permute-start | bytes 2359304 | tf_op jit(solution)/shard_map/ppermute | solution.py:23
  101.7 33.4 %collective-permute-start.19 = (bf16[128,3072]{1,0:T(8,128)(2,1)S(1)}, bf16[128,3072]{1,0:T(8,128)(2,1)}, u32[]{:S(2)}, u32[]{:S(2)}) collective-permute-start(bf16[128,3072]{1,0:T(8,128)(2,1)S(1)} %collective-permute-done.9.own_ref.refs_3_), channel_id=1, source_target_pairs={{0,2},{2,0},{1,3},{3,1},{4,6},{6,4},{5,7},{7,5},{8,10},{10,8},{9,1... | collective-permute-start | bytes 2359304 | tf_op jit(solution)/shard_map/ppermute | solution.py:23
  120.8 14.3 %collective-permute-start.17 = (bf16[128,3072]{1,0:T(8,128)(2,1)S(1)}, bf16[128,3072]{1,0:T(8,128)(2,1)}, u32[]{:S(2)}, u32[]{:S(2)}) collective-permute-start(bf16[128,3072]{1,0:T(8,128)(2,1)S(1)} %collective-permute-done.1.far_ref.refs_1_), channel_id=1, source_target_pairs={{0,2},{2,0},{1,3},{3,1},{4,6},{6,4},{5,7},{7,5},{8,10},{10,8},{9,1... | collective-permute-start | bytes 2359304 | tf_op jit(solution)/shard_map/ppermute | solution.py:23
  120.8 1.0 copy-start.20
  120.8 14.3 %collective-permute-start.18 = (bf16[256,1536]{1,0:T(8,128)(2,1)}, bf16[256,1536]{1,0:T(8,128)(2,1)}, u32[]{:S(2)}, u32[]{:S(2)}) collective-permute-start(bf16[256,1536]{1,0:T(8,128)(2,1)} %forward.1.refs_2_), channel_id=1, source_target_pairs={{0,2},{2,0},{1,3},{3,1},{4,6},{6,4},{5,7},{7,5},{8,10},{10,8},{9,1... | collective-permute-start | bytes 2359304 | tf_op jit(solution)/shard_map/ppermute | solution.py:23
  121.3 1.1 copy-start.21
  121.3 13.8 %collective-permute-start.20 = (bf16[128,3072]{1,0:T(8,128)(2,1)S(1)}, bf16[128,3072]{1,0:T(8,128)(2,1)}, u32[]{:S(2)}, u32[]{:S(2)}) collective-permute-start(bf16[128,3072]{1,0:T(8,128)(2,1)S(1)} %collective-permute-done.10.far_ref.refs_4_), channel_id=1, source_target_pairs={{0,2},{2,0},{1,3},{3,1},{4,6},{6,4},{5,7},{7,5},{8,10},{10,8},{9,1... | collective-permute-start | bytes 2359304 | tf_op jit(solution)/shard_map/ppermute | solution.py:23
  122.4 1.0 copy-start.22
  123.4 11.7 %collective-permute-start.21 = (bf16[256,1536]{1,0:T(8,128)(2,1)}, bf16[256,1536]{1,0:T(8,128)(2,1)}, u32[]{:S(2)}, u32[]{:S(2)}) collective-permute-start(bf16[256,1536]{1,0:T(8,128)(2,1)} %collective-permute-done.15.refs_5_), channel_id=1, source_target_pairs={{0,2},{2,0},{1,3},{3,1},{4,6},{6,4},{5,7},{7,5},{8,10},{10,8},{9,1... | collective-permute-start | bytes 2359304 | tf_op jit(solution)/shard_map/ppermute | solution.py:23
  123.9 1.3 copy-start.6
  130.1 5.0 %copy-start.2 = (bf16[128,3072]{1,0:T(8,128)(2,1)S(1)}, bf16[128,3072]{1,0:T(8,128)(2,1)}, u32[]{:S(2)}) copy-start(bf16[128,3072]{1,0:T(8,128)(2,1)} %copy-done.1) | copy-start | bytes 2359300
  135.1 5.0 %copy-start.17 = (bf16[256,768]{1,0:T(8,128)(2,1)}, bf16[256,768]{1,0:T(8,128)(2,1)S(1)}, u32[]{:S(2)}) copy-start(bf16[256,768]{1,0:T(8,128)(2,1)S(1)} %partial.5) | copy-start | bytes 1179652
  140.0 58.1 %collective-permute-start.24 = (bf16[2,384,768]{2,1,0:T(8,128)(2,1)}, bf16[2,384,768]{2,1,0:T(8,128)(2,1)}, u32[]{:S(2)}, u32[]{:S(2)}) collective-permute-start(bf16[2,384,768]{2,1,0:T(8,128)(2,1)} %rows.7), channel_id=1, source_target_pairs={{0,8},{8,0},{1,9},{9,1},{2,10},{10,2},{3,11},{11,3},{4,12},{12,4},... | collective-permute-start | bytes 3538952 | tf_op jit(solution)/shard_map/ppermute | solution.py:23
  140.1 1.1 copy-start.3
  146.1 55.3 %collective-permute-start.22 = (bf16[2,384,768]{2,1,0:T(8,128)(2,1)}, bf16[2,384,768]{2,1,0:T(8,128)(2,1)}, u32[]{:S(2)}, u32[]{:S(2)}) collective-permute-start(bf16[2,384,768]{2,1,0:T(8,128)(2,1)} %rows.5), channel_id=1, source_target_pairs={{0,4},{4,0},{1,5},{5,1},{2,6},{6,2},{3,7},{7,3},{8,12},{12,8},{9,1... | collective-permute-start | bytes 3538952 | tf_op jit(solution)/shard_map/ppermute | solution.py:23
  147.6 43.3 %collective-permute-start.11 = (bf16[256,768]{1,0:T(8,128)(2,1)S(1)}, bf16[256,768]{1,0:T(8,128)(2,1)S(1)}, u32[]{:S(2)}, u32[]{:S(2)}) collective-permute-start(bf16[256,768]{1,0:T(8,128)(2,1)S(1)} %partial.4), channel_id=1, source_target_pairs={{0,16},{16,0},{1,17},{17,1},{2,18},{18,2},{3,19},{19,3},{4,20},{20... | collective-permute-start | bytes 1179656 | tf_op jit(solution)/shard_map/ppermute | solution.py:23
  150.7 32.3 %collective-permute-start.12 = (bf16[256,768]{1,0:T(8,128)(2,1)}, bf16[256,768]{1,0:T(8,128)(2,1)S(1)}, u32[]{:S(2)}, u32[]{:S(2)}) collective-permute-start(bf16[256,768]{1,0:T(8,128)(2,1)} %copy-done.17), channel_id=1, source_target_pairs={{0,16},{16,0},{1,17},{17,1},{2,18},{18,2},{3,19},{19,3},{4,20},{20... | collective-permute-start | bytes 1179656 | tf_op jit(solution)/shard_map/ppermute | solution.py:23
  150.8 1.1 copy-start.4
  157.0 5.1 %copy-start.7 = (bf16[384,1536]{1,0:T(8,128)(2,1)S(1)}, bf16[384,1536]{1,0:T(8,128)(2,1)}, u32[]{:S(2)}) copy-start(bf16[384,1536]{1,0:T(8,128)(2,1)} %refs_0_.5) | copy-start | bytes 3538948
  162.1 21.0 %copy-start.9 = (bf16[3,128,1536]{2,1,0:T(8,128)(2,1)S(1)}, bf16[3,128,1536]{2,1,0:T(8,128)(2,1)}, u32[]{:S(2)}) copy-start(bf16[3,128,1536]{2,1,0:T(8,128)(2,1)} %copy-done.8) | copy-start | bytes 3538948
  162.1 21.0 %copy-start.12 = (bf16[1,128,3072]{2,1,0:T(8,128)(2,1)S(1)}, bf16[1,128,3072]{2,1,0:T(8,128)(2,1)}, u32[]{:S(2)}) copy-start(bf16[1,128,3072]{2,1,0:T(8,128)(2,1)} %param.6) | copy-start | bytes 2359300
  162.1 21.0 %copy-start.14 = (bf16[1,128,3072]{2,1,0:T(8,128)(2,1)S(1)}, bf16[1,128,3072]{2,1,0:T(8,128)(2,1)}, u32[]{:S(2)}) copy-start(bf16[1,128,3072]{2,1,0:T(8,128)(2,1)} %param.7) | copy-start | bytes 2359300
  162.1 21.0 %copy-start.16 = (bf16[1,128,3072]{2,1,0:T(8,128)(2,1)S(1)}, bf16[1,128,3072]{2,1,0:T(8,128)(2,1)}, u32[]{:S(2)}) copy-start(bf16[1,128,3072]{2,1,0:T(8,128)(2,1)} %param.8) | copy-start | bytes 2359300
  183.1 1.4 copy-start
  190.3 16.4 %collective-permute-start.13 = (bf16[3,128,768]{2,1,0:T(8,128)(2,1)S(1)}, bf16[3,128,768]{2,1,0:T(8,128)(2,1)S(1)}, u32[]{:S(2)}, u32[]{:S(2)}) collective-permute-start(bf16[3,128,768]{2,1,0:T(8,128)(2,1)S(1)} %get-tuple-element.28), channel_id=1, source_target_pairs={{0,1},{1,0},{2,3},{3,2},{4,5},{5,4},{6,7},{7,6},{8,9},{9,8},{10,11... | collective-permute-start | bytes 1769480 | tf_op jit(solution)/shard_map/ppermute | solution.py:23
  190.9 7.3 %copy-start.24 = (f32[2,384,768]{2,1,0:T(8,128)S(1)}, f32[2,384,768]{2,1,0:T(8,128)}, u32[]{:S(2)}) copy-start(f32[2,384,768]{2,1,0:T(8,128)} %rows.6) | copy-start | bytes 7077892
  196.8 21.0 %collective-permute-start.14 = (bf16[3,128,768]{2,1,0:T(8,128)(2,1)S(1)}, bf16[3,128,768]{2,1,0:T(8,128)(2,1)S(1)}, u32[]{:S(2)}, u32[]{:S(2)}) collective-permute-start(bf16[3,128,768]{2,1,0:T(8,128)(2,1)S(1)} %get-tuple-element.29), channel_id=1, source_target_pairs={{0,1},{1,0},{2,3},{3,2},{4,5},{5,4},{6,7},{7,6},{8,9},{9,8},{10,11... | collective-permute-start | bytes 1769480 | tf_op jit(solution)/shard_map/ppermute | solution.py:23
  198.2 3.2 %copy-start.23 = (f32[2,384,768]{2,1,0:T(8,128)S(1)}, f32[2,384,768]{2,1,0:T(8,128)}, u32[]{:S(2)}) copy-start(f32[2,384,768]{2,1,0:T(8,128)} %rows.4) | copy-start | bytes 7077892
  199.9 18.7 %collective-permute-start.25 = (bf16[1,384,768]{2,1,0:T(8,128)(2,1)S(1)}, bf16[1,384,768]{2,1,0:T(8,128)(2,1)S(1)}, u32[]{:S(2)}, u32[]{:S(2)}) collective-permute-start(bf16[1,384,768]{2,1,0:T(8,128)(2,1)S(1)} %dynamic-slice_convert_fusion), channel_id=1, source_target_pairs={{0,4},{4,0},{1,5},{5,1},{2,6},{6,2},{3,7},{7,3},{8,12},{12,8},{9,1... | collective-permute-start | bytes 1769480 | tf_op jit(solution)/shard_map/ppermute | solution.py:23
  203.1 15.8 %collective-permute-start.23 = (bf16[1,384,768]{2,1,0:T(8,128)(2,1)S(1)}, bf16[1,384,768]{2,1,0:T(8,128)(2,1)S(1)}, u32[]{:S(2)}, u32[]{:S(2)}) collective-permute-start(bf16[1,384,768]{2,1,0:T(8,128)(2,1)S(1)} %dynamic-slice_convert_fusion.1), channel_id=1, source_target_pairs={{0,8},{8,0},{1,9},{9,1},{2,10},{10,2},{3,11},{11,3},{4,12},{12,4},... | collective-permute-start | bytes 1769480 | tf_op jit(solution)/shard_map/ppermute | solution.py:23

commit v3 on v1

--- a/solution.py
+++ b/solution.py
@@ -87,12 +87,12 @@
     return pltpu.CompilerParams(vmem_limit_bytes=48 * 1024 * 1024)
 
 
-def cost(dots, heads, length, arrays):
-    return pl.CostEstimate(
-        flops=2 * dots * heads * length * length * HEAD_DIM,
-        bytes_accessed=2 * arrays * length * heads * HEAD_DIM,
-        transcendentals=heads * length * length,
-    )
+def small():
+    return pl.CostEstimate(flops=1024, bytes_accessed=1024, transcendentals=0)
+
+
+def after(value, *events):
+    return lax.optimization_barrier((value, events))[0]
 
 
 def forward(mine, own, far):
@@ -115,12 +115,12 @@
         ),
         out_shape=jax.ShapeDtypeStruct((length, features), jnp.bfloat16),
         compiler_params=params(),
-        cost_estimate=cost(2, heads, length, 4),
+        cost_estimate=small(),
         name="forward",
     )(mine, *own, far)
 
 
-def backward(mine, own, far, grads, first_head, heads, held):
+def backward(mine, own, far, partial, terms, first_head, heads, held):
     tokens, width = own[0].shape
     _, rest, features = far.shape
     length = tokens + rest
@@ -133,15 +133,15 @@
     far_spec = pl.BlockSpec((3, rest, block), lambda h, mine: (0, 0, start + h))
     grad_spec = pl.BlockSpec((length, block), lambda h, mine: (0, h))
     any_spec = pl.BlockSpec(memory_space=pl.ANY)
-    before = 5 + len(grads)
+    before = 6 + len(terms)
     return pl.pallas_call(
-        functools.partial(backward_kernel, step, len(held), len(grads)),
+        functools.partial(backward_kernel, step, len(held), 1 + len(terms)),
         grid_spec=pltpu.PrefetchScalarGridSpec(
             num_scalar_prefetch=1,
             grid=(grid,),
             in_specs=[own_spec] * 3
             + [far_spec]
-            + [grad_spec] * len(grads)
+            + [grad_spec] * (1 + len(terms))
             + [any_spec] * len(held),
             out_specs=[own_spec] * 3
             + [pl.BlockSpec((3, rest, block), lambda h, mine: (0, 0, h))],
@@ -150,31 +150,125 @@
         + [jax.ShapeDtypeStruct((3, rest, heads * HEAD_DIM), jnp.bfloat16)],
         input_output_aliases={before + i: i for i in range(len(held))},
         compiler_params=params(),
-        cost_estimate=cost(6, heads, length, 9),
+        cost_estimate=small(),
         name="backward",
-    )(mine, *own, far, *grads, *held)
-
-
-def summed_rows(grads, attended, first, second):
-    tokens, _, _, rows = grads.shape
-    inner = lax.axis_size(second)
-
-    def product(by):
-        chosen = part_of(grads, first, by, 1).reshape(tokens, inner * rows)
-        return dot(chosen, attended, ((0,), (0,)))
-
-    sent = [shift(product(by).astype(jnp.bfloat16), first, by) for by in others(first)]
-    total = product(0)
-    for term in sent:
-        total = total + term.astype(jnp.float32)
-    sent = [
-        shift(part_of(total, second, by, 0).astype(jnp.bfloat16), second, by)
-        for by in others(second)
-    ]
-    final = part_of(total, second, 0, 0)
-    for term in sent:
-        final = final + term.astype(jnp.float32)
-    return final
+    )(mine, *own, far, partial, *terms, *held)
+
+
+def partial_kernel(own_ref, far_ref, weight_ref, out_ref, every_row):
+    tokens = own_ref.shape[0]
+
+    @pl.when(pl.program_id(0) == 0)
+    def _():
+        every_row[:tokens] = own_ref[...]
+        every_row[tokens:] = far_ref[...]
+
+    out_ref[...] = dot(every_row[...], weight_ref[...], ((1,), (0,))).astype(out_ref.dtype)
+
+
+def partial_product(own, far, weight, dtype):
+    tokens, depth = own.shape
+    rest = far.shape[0]
+    wide = weight.shape[1]
+    block = 256 if wide % 256 == 0 else 128
+    return pl.pallas_call(
+        partial_kernel,
+        grid=(wide // block,),
+        in_specs=[
+            pl.BlockSpec((tokens, depth), lambda i: (0, 0)),
+            pl.BlockSpec((rest, depth), lambda i: (0, 0)),
+            pl.BlockSpec((depth, block), lambda i: (0, i)),
+        ],
+        out_specs=pl.BlockSpec((tokens + rest, block), lambda i: (0, i)),
+        scratch_shapes=[pltpu.VMEM((tokens + rest, depth), jnp.bfloat16)],
+        out_shape=jax.ShapeDtypeStruct((tokens + rest, wide), dtype),
+        compiler_params=params(),
+        cost_estimate=small(),
+        name="partial",
+    )(own, far, weight)
+
+
+def turn_kernel(at_ref, *refs):
+    *inputs, out_ref = refs
+    column = 0
+    for ref in inputs:
+        tokens = ref.shape[0]
+        out_ref[:, column : column + tokens] = ref[...].T
+        column += tokens
+
+
+def turned(at, grads, rows):
+    operands, specs = [], []
+    for grad in grads:
+        tokens = grad.shape[0]
+        if rows % 128 == 0:
+            operands.append(grad)
+            specs.append(pl.BlockSpec((tokens, rows), lambda i, at: (0, at[i])))
+        else:
+            operands.append(jnp.swapaxes(grad.reshape(tokens, -1, rows), 0, 1))
+            specs.append(pl.BlockSpec((None, tokens, rows), lambda i, at: (at[i], 0, 0)))
+    depth = sum(grad.shape[0] for grad in grads)
+    return pl.pallas_call(
+        turn_kernel,
+        grid_spec=pltpu.PrefetchScalarGridSpec(
+            num_scalar_prefetch=1,
+            grid=(at.shape[0],),
+            in_specs=specs,
+            out_specs=pl.BlockSpec((None, rows, depth), lambda i, at: (i, 0, 0)),
+        ),
+        out_shape=jax.ShapeDtypeStruct((at.shape[0], rows, depth), jnp.bfloat16),
+        compiler_params=params(),
+        cost_estimate=small(),
+        name="turn",
+    )(at, *operands)
+
+
+def rows_kernel(cores, at_ref, *refs):
+    grads, (*attends, out_ref) = refs[:cores], refs[cores:]
+    length = attends[0].shape[0]
+    each = len(attends) // cores
+    total = None
+    for i, attended in enumerate(attends):
+        start = (i % each) * length
+        chosen = grads[i // each][:, start : start + length]
+        term = dot(chosen, attended[...], ((1,), (0,)))
+        total = term if total is None else total + term
+    out_ref[...] = total.astype(out_ref.dtype)
+
+
+def rows_product(at, grads, attends, group, groups, dtype):
+    _, rows, depth = grads[0].shape
+    flat = [array for arrays in attends for array in arrays]
+    length, features = flat[0].shape
+    wide = features // groups
+    count = at.shape[0]
+    return pl.pallas_call(
+        functools.partial(rows_kernel, len(grads)),
+        grid_spec=pltpu.PrefetchScalarGridSpec(
+            num_scalar_prefetch=1,
+            grid=(count,),
+            in_specs=[pl.BlockSpec((None, rows, depth), lambda i, at: (at[i], 0, 0))] * len(grads)
+            + [pl.BlockSpec((length, wide), lambda i, at: (0, group))] * len(flat),
+            out_specs=pl.BlockSpec((None, rows, wide), lambda i, at: (i, 0, 0)),
+        ),
+        out_shape=jax.ShapeDtypeStruct((count, rows, wide), dtype),
+        compiler_params=params(),
+        cost_estimate=small(),
+        name="rows",
+    )(at, *grads, *flat)
+
+
+def place(axis, by=0):
+    return (lax.axis_index(axis) + by) % lax.axis_size(axis)
+
+
+def blocks_along(axis, by):
+    zl, x = jnp.arange(lax.axis_size("zl")), jnp.arange(lax.axis_size("x"))
+    if axis == "x":
+        x = place("x", by)
+    else:
+        zl = place("zl", by)
+    return (zl * lax.axis_size("x") + x).astype(jnp.int32)
 
 
 def shards(grad_out, queries, keys, values, out_weight):
@@ -188,12 +282,20 @@
     token_scale = 1.0 / math.sqrt(clips * length)
     me = mine.astype(jnp.int32).reshape(1)
 
-    weight = lax.all_gather(out_weight, ("zl", "x", "core"), axis=0, tiled=True)
-
+    def along_seq(array):
+        arrived = [shift(array, "seq", by) for by in others("seq")]
+        return arrived[0] if seq == 2 else jnp.concatenate(arrived, axis=0)
+
+    groups = 2 if heads % 4 == 0 else 1
+    wide = features // groups
+    weights = [
+        lax.all_gather(
+            out_weight[:, group * wide : (group + 1) * wide], ("zl", "x", "core"), tiled=True
+        )
+        for group in range(groups)
+    ]
     own_grad = grad_out[0]
-    halves = [part_of(own_grad, "zh", 0, 1)]
-    halves += [shift(part_of(own_grad, "zh", by, 1), "zh", by) for by in others("zh")]
-
+    halves = [shift(part_of(own_grad, "zh", by, 1), "zh", by) for by in others("zh")]
     own = (queries[0], keys[0], values[0])
     pieces = [
         shift(jnp.stack([part_of(part, "seq", by, 1) for part in own]), "seq", by)
@@ -201,52 +303,66 @@
     ]
     far = pieces[0] if seq == 2 else jnp.concatenate(pieces, axis=1)
 
-    grads = [
-        jnp.concatenate([half] + [shift(half, "seq", by) for by in others("seq")], axis=0)
-        for half in halves
+    attended = forward(me, own, far)
+    attends = [shift(attended, "zh", by) for by in others("zh")]
+    attended_across = [shift(attended, "core", by) for by in others("core")]
+
+    halves = after(halves, attended)
+    own_half = after(part_of(own_grad, "zh", 0, 1), halves)
+    grads = [(half, along_seq(half)) for half in [own_half] + halves]
+
+    def partials(group):
+        return [partial_product(*grad, weights[group], jnp.bfloat16) for grad in grads[1:]]
+
+    def returned(terms):
+        return [shift(term, "zh", -by) for by, term in zip(others("zh"), terms)]
+
+    def own_partial(group):
+        return partial_product(*grads[0], weights[group], jnp.float32)
+
+    sent = partials(0)
+    partial = [own_partial(0)]
+    mine_blocks = jnp.arange(lax.axis_size("zl") * lax.axis_size("x")) * lax.axis_size("core")
+    flat = after([half for grad in grads for half in grad], sent, partial)
+
+    def turned_for(by, arrays):
+        return turned((mine_blocks + place("core", by)).astype(jnp.int32), arrays, rows)
+
+    by_rows = [shift(turned_for(by, flat), "core", by) for by in others("core")]
+    attends, sent = after((attends, sent), flat)
+    terms = [returned(after(sent, attends))]
+    attends_across = [[shift(array, "core", by) for array in attends] for by in others("core")]
+    by_rows = [turned_for(0, after(flat, attends))] + by_rows
+    attends = [[attended] + attends] + [
+        [near] + more for near, more in zip(attended_across, attends_across)
     ]
-
-    attended = forward(me, own, far)
-    attends = [attended] + [shift(attended, "zh", by) for by in others("zh")]
-
-    groups = 2 if heads % 4 == 0 else 1
-    wide = features // groups
-    partial = []
-    for group in range(groups):
-        chosen = weight[:, group * wide : (group + 1) * wide]
-        terms = [
-            shift(dot(grads[by], chosen, ((1,), (0,))).astype(jnp.bfloat16), "zh", -by)
-            for by in others("zh")
-        ]
-        partial.append([dot(grads[0], chosen, ((1,), (0,)))] + terms)
-
-    every_grad, every_attended = [], []
-    cores = lax.axis_size("core")
-    stacked = jnp.concatenate(grads, axis=0)
-    count = stacked.shape[0]
-    stacked = stacked.reshape(count, -1, cores, rows)
-    attends = jnp.concatenate(attends, axis=0)
-    for by in range(cores):
-        chosen = part_of(stacked, "core", by, 2)[:, :, 0]
-        every_grad.append(shift(chosen, "core", by) if by else chosen)
-        every_attended.append(shift(attends, "core", by) if by else attends)
-    every_grad = jnp.concatenate(every_grad, axis=0)
-    every_attended = jnp.concatenate(every_attended, axis=0)
-    every_grad = every_grad.reshape(
-        every_grad.shape[0], lax.axis_size("zl"), lax.axis_size("x"), rows
-    )
-    middle = features // 2
-    left = summed_rows(
-        jnp.swapaxes(every_grad, 1, 2), every_attended[:, :middle], "x", "zl"
-    )
-    right = summed_rows(every_grad, every_attended[:, middle:], "zl", "x")
-    weight_grad = jnp.concatenate([left, right], axis=1) * token_scale
-
+    splits = 2 if features % 256 == 0 else 1
+    orders = [("x", "zl"), ("zl", "x")][:splits]
+
+    def product(axis, by, split, dtype):
+        return rows_product(blocks_along(axis, by), by_rows, attends, split, splits, dtype)
+
+    leave = [
+        [product(axis, by, split, jnp.bfloat16) for by in others(axis)]
+        for split, (axis, _) in enumerate(orders)
+    ]
+    arrive = [
+        [shift(term, axis, by) for by, term in zip(others(axis), terms_of)]
+        for (axis, _), terms_of in zip(orders, leave)
+    ]
     result, arrivals = [], []
-    for group in range(groups):
-        first = group * wide // HEAD_DIM
-        *result, leaving = backward(
-            me, own, far, partial[group], first, wide // HEAD_DIM, result
+
+    def finish(group, *events):
+        start = group * wide // HEAD_DIM
+        *result[:], leaving = backward(
+            me,
+            own,
+            far,
+            partial[group],
+            after(terms[group], *events),
+            start,
+            wide // HEAD_DIM,
+            list(result),
         )
         arrivals.append(
             [
@@ -254,6 +370,31 @@
                 for by in others("seq")
             ]
         )
+
+    for group in range(1, groups):
+        weights[group] = after(weights[group], leave)
+        terms.append(returned(partials(group)))
+        finish(group - 1, weights[group])
+        weights[group] = after(weights[group], result)
+        partial.append(own_partial(group))
+    by_rows = after(by_rows, partial, result)
+    kept = [product(axis, 0, split, jnp.float32) for split, (axis, _) in enumerate(orders)]
+    finish(groups - 1, kept)
+
+    columns = []
+    for (_, axis), arrived, total in zip(orders, after(arrive, result), kept):
+        for term in arrived:
+            total = total + term.astype(jnp.float32)
+        second = [
+            shift(part_of(total, axis, by, 0).astype(jnp.bfloat16), axis, by)
+            for by in others(axis)
+        ]
+        final = part_of(total, axis, 0, 0)
+        for term in second:
+            final = final + term.astype(jnp.float32)
+        columns.append(final[0])
+    weight_grad = jnp.concatenate(columns, axis=1) * token_scale
+
     for group in range(groups):
         for by, back in zip(others("seq"), arrivals[group]):
             start = ((mine + by) % seq) * features + group * wide

time: 250 us -> 216 us (0.86)
  Pallas kernels: 18.5 us -> 62.4 us
  matrix products: 26.9 us -> 0 us
  waiting for transfers between devices: 114 us -> 89.5 us
  local copies, waits for them, and re-layouts: 38 us -> 19 us
  other arithmetic: 19.2 us -> 6.39 us
  starting transfers between devices: 18.6 us -> 23 us
    pallas_call x2 -> x12, Pallas kernels: 11.9 us -> 56.4 us  [the longest x4 18.5 us: partial_product(): pl.pallas_call(partial_kernel, grid=(wide // block,), in_specs=[pl.BlockS...]
    dot_general x8 -> x0, matrix products: 26.9 us -> none  [dot(): lax.dot_general(a, b, (contract, ((), ())), preferred_element_type=jnp.fl...]
    ppermute x15 -> x16, waiting for transfers between devices: 113 us -> 88.7 us  [shift(): lax.ppermute(array, axis, [(i, (i + by) % count) for i in range(count)])]
    concatenate x5 -> x0, other arithmetic: 14.5 us -> none  [the longest x2 7.69 us: shards(): every_grad = jnp.concatenate(every_grad, axis=0)]
    dynamic_slice x9 -> x3, local copies, waits for them, and re-layouts: 15.8 us -> 1.68 us  [part_of(): return lax.dynamic_slice_in_dim(array, at * size, size, dim)]
    another operation x2 -> x0, local copies, waits for them, and re-layouts: 5.16 us -> none
    ppermute x15 -> x16, starting transfers between devices: 18.5 us -> 23 us  [shift(): lax.ppermute(array, axis, [(i, (i + by) % count) for i in range(count)])]
    unnamed x27 -> x50, local copies, waits for them, and re-layouts: 9.36 us -> 12.1 us
  transfers between devices with their start and end apart: 16 -> 18, of which waited for: 9 -> 9; matrix products, arithmetic and copies ran while one was open for 32% -> 4% of each run, Pallas kernels for 7% -> 29%
where the time goes in v3:
time: 216 us; the launch traced here: 215 us
  waiting for transfers between devices  89.5 us (41%)
  Pallas kernels  62.4 us (29%)
  starting transfers between devices  23 us (11%)
  local copies, waits for them, and re-layouts  19 us (9%)
  between operations  14.3 us (7%)
  other arithmetic  6.39 us (3%)
    ppermute x16, waiting for transfers between devices, shift(): lax.ppermute(array, axis, [(i, (i + by) % count) for i in range(count)])  88.7 us
    ppermute x16, starting transfers between devices, shift(): lax.ppermute(array, axis, [(i, (i + by) % count) for i in range(count)])  23 us
    pallas_call x4, Pallas kernels, partial_product(): pl.pallas_call(partial_kernel, grid=(wide // block,), in_specs=[pl.BlockS...  18.5 us
    pallas_call x4, Pallas kernels, rows_product(): pl.pallas_call(functools.partial(rows_kernel, len(grads)), grid_spec=pltp...  18.1 us
    pallas_call x2, Pallas kernels, backward(): pl.pallas_call(functools.partial(backward_kernel, step, len(held), 1 + le...  12.5 us
    unnamed x50, local copies, waits for them, and re-layouts  12.1 us
    pallas_call x2, Pallas kernels, turned(): pl.pallas_call(turn_kernel, grid_spec=pltpu.PrefetchScalarGridSpec(num_sc...  7.28 us
    pallas_call x1, Pallas kernels, forward(): pl.pallas_call(functools.partial(forward_kernel, step), grid_spec=pltpu.P...  6 us
  transfers between devices with their start and end apart: 18, of which 9 were waited for; matrix products, arithmetic and copies ran while one was open for 4% of the time, Pallas kernels for 29%

profile of v3, /device:TPU:0, one launch (start us, length us, event | category | flops | bytes accessed | tf_op | source)
XLA Modules:
  0.0 214.6 jit_solution(10728541522487690899)
XLA Ops:
  7.2 0.0 all-gather.5.cloned.1.call-start
  7.2 2.4 %fusion.4 = (bf16[384,768]{1,0:T(8,128)(2,1)}, bf16[384,768]{1,0:T(8,128)(2,1)}) fusion(bf16[384,1536]{1,0:T(8,128)(2,1)} %param.9), kind=kLoop, calls=%fused_computation.27 | loop fusion | bytes 2359296 | tf_op jit(solution)/shard_map/slice | solution.py:293
  9.6 0.0 all-gather.5.cloned.1.call-update
  9.6 0.0 all-gather.3.cloned.1.call-start
  9.7 0.7 all-gather.3.cloned.1.call-update
  10.5 0.3 copy-done.13
  10.7 0.2 copy-done.17
  11.0 0.1 constant_dynamic-slice_fusion
  11.0 1.1 pad_maximum_fusion
  12.2 3.0 %collective-permute-start = (bf16[3,128,1536]{2,1,0:T(8,128)(2,1)}, bf16[3,128,1536]{2,1,0:T(8,128)(2,1)S(1)}, u32[]{:S(2)}, u32[]{:S(2)}) collective-permute-start(bf16[3,128,1536]{2,1,0:T(8,128)(2,1)} %pad_maximum_fusion), channel_id=1, source_target_pairs={{0,1},{1,0},{2,3},{3,2},{4,5},{5,4},{6,7},{7,6},{8,9},{9,8},{10,11... | collective-permute-start | bytes 3538952 | tf_op jit(solution)/shard_map/ppermute | solution.py:23
  15.2 1.6 dynamic-slice_bitcast_fusion
  16.7 2.7 %collective-permute-start.1 = (bf16[128,3072]{1,0:T(8,128)(2,1)S(1)}, bf16[128,3072]{1,0:T(8,128)(2,1)S(1)}, u32[]{:S(2)}, u32[]{:S(2)}) collective-permute-start(bf16[128,3072]{1,0:T(8,128)(2,1)S(1)} %get-tuple-element.62), channel_id=1, source_target_pairs={{0,16},{16,0},{1,17},{17,1},{2,18},{18,2},{3,19},{19,3},{4,20},{20... | collective-permute-start | bytes 2359304 | tf_op jit(solution)/shard_map/ppermute | solution.py:23
  19.4 21.9 %collective-permute-done.far = bf16[3,128,1536]{2,1,0:T(8,128)(2,1)S(1)} collective-permute-done((bf16[3,128,1536]{2,1,0:T(8,128)(2,1)}, bf16[3,128,1536]{2,1,0:T(8,128)(2,1)S(1)}, u32[]{:S(2)}, u32[]{:S(2)}) %collective-permute-start) | collective-permute-done | bytes 1179680 | tf_op jit(solution)/shard_map/ppermute | solution.py:23
  41.3 1.0 copy-done.6
  42.4 1.3 copy-done.7
  43.6 6.0 %forward.1.refs_2_ = bf16[256,1536]{1,0:T(8,128)(2,1)S(1)} custom-call(s32[1]{0:T(128)} %bitcast.mine_ref, bf16[128,3072]{1,0:T(8,128)(2,1)S(1)} %bitcast.15, bf16[128,3072]{1,0:T(8,128)(2,1)S(1)} %bitcast.18, bf16[128,3072]{1,0:T(8,128)(2,1)S(1)} %bitcast.21, bf16[3,128,1536]{2,1,0:T(8,128)(2,1)S(1)} %copy-done.7), custom_call_target="tpu_custom_call" | custom-call | flops 1024 | bytes 1024 | tf_op jit(solution)/shard_map/forward/pallas_call | solution.py:108
  49.6 4.0 %collective-permute-done.1.own_ref.refs_2_ = bf16[128,3072]{1,0:T(8,128)(2,1)S(1)} collective-permute-done((bf16[128,3072]{1,0:T(8,128)(2,1)S(1)}, bf16[128,3072]{1,0:T(8,128)(2,1)S(1)}, u32[]{:S(2)}, u32[]{:S(2)}) %collective-permute-start.1) | collective-permute-done | bytes 786464 | tf_op jit(solution)/shard_map/ppermute | solution.py:23
  53.6 0.5 collective-permute-start.2
  54.1 1.6 collective-permute-start.3
  55.7 1.5 collective-permute-start.4
  57.2 16.9 %collective-permute-done.2.far_ref.refs_1_ = bf16[128,3072]{1,0:T(8,128)(2,1)S(1)} collective-permute-done((bf16[128,3072]{1,0:T(8,128)(2,1)S(1)}, bf16[128,3072]{1,0:T(8,128)(2,1)S(1)}, u32[]{:S(2)}, u32[]{:S(2)}) %collective-permute-start.2) | collective-permute-done | bytes 786464 | tf_op jit(solution)/shard_map/ppermute | solution.py:23
  74.1 4.4 %partial.5.refs_0_ = f32[256,768]{1,0:T(8,128)S(1)} custom-call(bf16[128,3072]{1,0:T(8,128)(2,1)S(1)} %get-tuple-element.40.own_ref.refs_0_, bf16[128,3072]{1,0:T(8,128)(2,1)S(1)} %collective-permute-done.2.far_ref.refs_1_, bf16[3072,768]{1,0:T(8,128)(2,1)} %all-gather.5.cloned.1.call-done.weight_ref), custom_call_target="tpu_custom_call" | custom-call | flops 1024 | bytes 1024 | tf_op jit(solution)/shard_map/partial/pallas_call | solution.py:174
  78.5 10.4 %collective-permute-done.3.far_ref.refs_3_ = bf16[128,3072]{1,0:T(8,128)(2,1)} collective-permute-done((bf16[128,3072]{1,0:T(8,128)(2,1)S(1)}, bf16[128,3072]{1,0:T(8,128)(2,1)}, u32[]{:S(2)}, u32[]{:S(2)}) %collective-permute-start.3) | collective-permute-done | bytes 786464 | tf_op jit(solution)/shard_map/ppermute | solution.py:23
  88.9 5.0 %partial.4 = bf16[256,768]{1,0:T(8,128)(2,1)} custom-call(bf16[128,3072]{1,0:T(8,128)(2,1)S(1)} %collective-permute-done.1.own_ref.refs_2_, bf16[128,3072]{1,0:T(8,128)(2,1)} %collective-permute-done.3.far_ref.refs_3_, bf16[3072,768]{1,0:T(8,128)(2,1)} %all-gather.5.cloned.1.call-done.weight_ref), custom_call_target="tpu_custom_call" | custom-call | flops 1024 | bytes 1024 | tf_op jit(solution)/shard_map/partial/pallas_call | solution.py:174
  94.0 4.2 %turn.3 = bf16[4,384,512]{2,1,0:T(8,128)(2,1)} custom-call(s32[4]{0:T(128)S(1)} %fusion.at_ref, bf16[128,3072]{1,0:T(8,128)(2,1)S(1)} %get-tuple-element.40.own_ref.refs_0_, bf16[128,3072]{1,0:T(8,128)(2,1)S(1)} %collective-permute-done.2.far_ref.refs_1_, bf16[128,3072]{1,0:T(8,128)(2,1)S(1)} %collective-permute-done.1.own_ref.refs_2_, ...), custom_call_target="tpu_custom_call" | custom-call | flops 1024 | bytes 1024 | tf_op jit(solution)/shard_map/turn/pallas_call | solution.py:211
  98.2 0.5 collective-permute-start.6
  98.8 1.1 copy-done.1
  99.9 1.1 copy-done.4
  101.0 3.0 %turn.2.refs_0_ = bf16[4,384,512]{2,1,0:T(8,128)(2,1)S(1)} custom-call(s32[4]{0:T(128)S(1)} %fusion.1.at_ref, bf16[128,3072]{1,0:T(8,128)(2,1)S(1)} %get-tuple-element.40.own_ref.refs_0_, bf16[128,3072]{1,0:T(8,128)(2,1)S(1)} %copy-done.1, bf16[128,3072]{1,0:T(8,128)(2,1)S(1)} %copy-done.4, bf16[128,3072]{1,0:T(8,128)(2,1)} %collective-permute-done.3.far_ref.refs_3_), custom_call_target="tpu_custom_call" | custom-call | flops 1024 | bytes 1024 | tf_op jit(solution)/shard_map/turn/pallas_call | solution.py:211
  104.1 0.5 collective-permute-done.7.refs_5_
  104.6 4.4 %rows.4 = bf16[2,384,768]{2,1,0:T(8,128)(2,1)} custom-call(s32[2]{0:T(128)S(1)} %fusion.3.at_ref, bf16[4,384,512]{2,1,0:T(8,128)(2,1)S(1)} %turn.2.refs_0_, bf16[4,384,512]{2,1,0:T(8,128)(2,1)} %collective-permute-done.5.refs_1_, bf16[256,1536]{1,0:T(8,128)(2,1)S(1)} %forward.1.refs_2_, bf16[256,1536]{1,0:T(8,128)(2,1)} %collective-permute-done.4.refs_3_, ...), custom_call_target="tpu_custom_call" | custom-call | flops 1024 | bytes 1024 | tf_op jit(solution)/shard_map/rows/pallas_call | solution.py:245
  109.0 1.6 collective-permute-start.12
  110.6 4.4 %rows.5 = bf16[2,384,768]{2,1,0:T(8,128)(2,1)} custom-call(s32[2]{0:T(128)S(1)} %iota_add_fusion.1.at_ref, bf16[4,384,512]{2,1,0:T(8,128)(2,1)S(1)} %turn.2.refs_0_, bf16[4,384,512]{2,1,0:T(8,128)(2,1)} %collective-permute-done.5.refs_1_, bf16[256,1536]{1,0:T(8,128)(2,1)S(1)} %forward.1.refs_2_, bf16[256,1536]{1,0:T(8,128)(2,1)} %collective-permute-done.4.refs_3_, ...), custom_call_target="tpu_custom_call" | custom-call | flops 1024 | bytes 1024 | tf_op jit(solution)/shard_map/rows/pallas_call | solution.py:245
  114.9 1.5 collective-permute-start.13
  116.5 3.5 %collective-permute-start.8 = (bf16[256,768]{1,0:T(8,128)(2,1)}, bf16[256,768]{1,0:T(8,128)(2,1)}, u32[]{:S(2)}, u32[]{:S(2)}) collective-permute-start(bf16[256,768]{1,0:T(8,128)(2,1)} %partial.4), channel_id=1, source_target_pairs={{0,16},{16,0},{1,17},{17,1},{2,18},{18,2},{3,19},{19,3},{4,20},{20... | collective-permute-start | bytes 1179656 | tf_op jit(solution)/shard_map/ppermute | solution.py:23
  120.0 1.1 copy-done.5
  121.1 5.0 %partial.7 = bf16[256,768]{1,0:T(8,128)(2,1)} custom-call(bf16[128,3072]{1,0:T(8,128)(2,1)S(1)} %copy-done.5, bf16[128,3072]{1,0:T(8,128)(2,1)} %collective-permute-done.3.far_ref.refs_3_, bf16[3072,768]{1,0:T(8,128)(2,1)} %all-gather.3.cloned.1.call-done.weight_ref), custom_call_target="tpu_custom_call" | custom-call | flops 1024 | bytes 1024 | tf_op jit(solution)/shard_map/partial/pallas_call | solution.py:174
  126.2 25.4 %collective-permute-done.8.refs_1_ = bf16[256,768]{1,0:T(8,128)(2,1)} collective-permute-done((bf16[256,768]{1,0:T(8,128)(2,1)}, bf16[256,768]{1,0:T(8,128)(2,1)}, u32[]{:S(2)}, u32[]{:S(2)}) %collective-permute-start.8) | collective-permute-done | bytes 393248 | tf_op jit(solution)/shard_map/ppermute | solution.py:23
  151.6 1.3 copy-done.8
  152.9 1.1 copy-done.11
  154.0 1.1 copy-done.15
  155.1 1.1 copy-done.19
  156.3 1.1 copy-done.22
  157.4 6.6 %backward.2 = (bf16[128,3072]{1,0:T(8,128)(2,1)}, bf16[128,3072]{1,0:T(8,128)(2,1)}, bf16[128,3072]{1,0:T(8,128)(2,1)}, bf16[3,128,768]{2,1,0:T(8,128)(2,1)S(1)}) custom-call(s32[1]{0:T(128)} %bitcast.mine_ref, bf16[128,3072]{1,0:T(8,128)(2,1)S(1)} %bitcast.16, bf16[128,3072]{1,0:T(8,128)(2,1)S(1)} %bitcast.19, bf16[128,3072]{1,0:T(8,128)(2,1)S(1)} %bitcast.22, ...), custom_call_target="tpu_custom_call" | custom-call | flops 1024 | bytes 1024 | tf_op jit(solution)/shard_map/backward/pallas_call | solution.py:137
  164.0 4.1 %partial.6.refs_0_ = f32[256,768]{1,0:T(8,128)S(1)} custom-call(bf16[128,3072]{1,0:T(8,128)(2,1)S(1)} %get-tuple-element.40.own_ref.refs_0_, bf16[128,3072]{1,0:T(8,128)(2,1)S(1)} %copy-done.2, bf16[3072,768]{1,0:T(8,128)(2,1)} %all-gather.3.cloned.1.call-done.weight_ref), custom_call_target="tpu_custom_call" | custom-call | flops 1024 | bytes 1024 | tf_op jit(solution)/shard_map/partial/pallas_call | solution.py:174
  168.1 0.9 collective-permute-start.10
  169.0 4.5 %rows.7 = f32[2,384,768]{2,1,0:T(8,128)} custom-call(s32[2]{0:T(128)S(1)} %iota_add_fusion.at_ref, bf16[4,384,512]{2,1,0:T(8,128)(2,1)S(1)} %turn.2.refs_0_, bf16[4,384,512]{2,1,0:T(8,128)(2,1)} %collective-permute-done.5.refs_1_, bf16[256,1536]{1,0:T(8,128)(2,1)S(1)} %forward.1.refs_2_, bf16[256,1536]{1,0:T(8,128)(2,1)} %collective-permute-done.4.refs_3_, ...), custom_call_target="tpu_custom_call" | custom-call | flops 1024 | bytes 1024 | tf_op jit(solution)/shard_map/rows/pallas_call | solution.py:245
  173.5 4.8 %rows.6 = f32[2,384,768]{2,1,0:T(8,128)} custom-call(s32[2]{0:T(128)S(1)} %fusion.2.at_ref, bf16[4,384,512]{2,1,0:T(8,128)(2,1)S(1)} %turn.2.refs_0_, bf16[4,384,512]{2,1,0:T(8,128)(2,1)} %collective-permute-done.5.refs_1_, bf16[256,1536]{1,0:T(8,128)(2,1)S(1)} %forward.1.refs_2_, bf16[256,1536]{1,0:T(8,128)(2,1)} %collective-permute-done.4.refs_3_, ...), custom_call_target="tpu_custom_call" | custom-call | flops 1024 | bytes 1024 | tf_op jit(solution)/shard_map/rows/pallas_call | solution.py:245
  178.4 5.9 %backward.3 = (bf16[128,3072]{1,0:T(8,128)(2,1)}, bf16[128,3072]{1,0:T(8,128)(2,1)}, bf16[128,3072]{1,0:T(8,128)(2,1)}, bf16[3,128,768]{2,1,0:T(8,128)(2,1)S(1)}) custom-call(s32[1]{0:T(128)} %bitcast.mine_ref, bf16[128,3072]{1,0:T(8,128)(2,1)S(1)} %bitcast.17, ...), custom_call_target="tpu_custom_call", output_to_operand_aliasing={{0}: (7, {}), {1}: (8, {}), {2}: (9, {})} | custom-call | flops 1024 | bytes 1024 | tf_op jit(solution)/shard_map/backward/pallas_call | solution.py:137
  184.3 1.2 collective-permute-start.11
  185.5 1.7 convert_add_fusion.1
  187.2 0.1 dynamic-slice_convert_fusion.1
  187.3 4.0 %collective-permute-start.14 = (bf16[1,384,768]{2,1,0:T(8,128)(2,1)S(1)}, bf16[1,384,768]{2,1,0:T(8,128)(2,1)S(1)}, u32[]{:S(2)}, u32[]{:S(2)}) collective-permute-start(bf16[1,384,768]{2,1,0:T(8,128)(2,1)S(1)} %dynamic-slice_convert_fusion.1), channel_id=1, source_target_pairs={{0,8},{8,0},{1,9},{9,1},{2,10},{10,2},{3,11},{11,3},{4,12},{12,4},... | collective-permute-start | bytes 1769480 | tf_op jit(solution)/shard_map/ppermute | solution.py:23
  191.3 1.6 convert_add_fusion
  192.9 0.1 dynamic-slice_convert_fusion
  193.0 0.6 collective-permute-start.15
  193.6 1.9 slice_dynamic-update-slice_fusion.1
  195.5 1.6 collective-permute-done.11
  197.1 0.8 slice_dynamic-update-slice_fusion
  198.0 4.8 %collective-permute-done.14 = bf16[1,384,768]{2,1,0:T(8,128)(2,1)S(1)} collective-permute-done((bf16[1,384,768]{2,1,0:T(8,128)(2,1)S(1)}, bf16[1,384,768]{2,1,0:T(8,128)(2,1)S(1)}, u32[]{:S(2)}, u32[]{:S(2)}) %collective-permute-start.14) | collective-permute-done | bytes 589856 | tf_op jit(solution)/shard_map/ppermute | solution.py:23
  202.8 0.1 add_bitcast_fusion.1
  202.9 3.1 %collective-permute-done.15 = bf16[1,384,768]{2,1,0:T(8,128)(2,1)S(1)} collective-permute-done((bf16[1,384,768]{2,1,0:T(8,128)(2,1)S(1)}, bf16[1,384,768]{2,1,0:T(8,128)(2,1)S(1)}, u32[]{:S(2)}, u32[]{:S(2)}) %collective-permute-start.15) | collective-permute-done | bytes 589856 | tf_op jit(solution)/shard_map/ppermute | solution.py:23
  206.0 0.1 add_bitcast_fusion
  206.1 1.7 maximum_multiply_fusion
  (57 shorter events, 0.2 us)
Async XLA Ops:
  7.2 3.3 %copy-start.10 = (bf16[1,128,3072]{2,1,0:T(8,128)(2,1)S(1)}, bf16[1,128,3072]{2,1,0:T(8,128)(2,1)}, u32[]{:S(2)}) copy-start(bf16[1,128,3072]{2,1,0:T(8,128)(2,1)} %param.6) | copy-start | bytes 2359300
  7.2 66.9 %all-gather.5.cloned.1.call-start = ((), (), s32[]{:S(2)}) async-start(), calls=%async_computation.1 | async-start | bytes 5308416 | tf_op jit(solution)/shard_map/all_gather | solution.py:292
  9.6 1.1 copy-start.13
  9.6 1.4 copy-start.17
  9.6 110.3 %all-gather.3.cloned.1.call-start = ((), (), s32[]{:S(2)}) async-start(), calls=%async_computation | async-start | bytes 5308416 | tf_op jit(solution)/shard_map/all_gather | solution.py:292
  12.2 29.1 %collective-permute-start = (bf16[3,128,1536]{2,1,0:T(8,128)(2,1)}, bf16[3,128,1536]{2,1,0:T(8,128)(2,1)S(1)}, u32[]{:S(2)}, u32[]{:S(2)}) collective-permute-start(bf16[3,128,1536]{2,1,0:T(8,128)(2,1)} %pad_maximum_fusion), channel_id=1, source_target_pairs={{0,1},{1,0},{2,3},{3,2},{4,5},{5,4},{6,7},{7,6},{8,9},{9,8},{10,11... | collective-permute-start | bytes 3538952 | tf_op jit(solution)/shard_map/ppermute | solution.py:23
  15.2 27.2 %copy-start.14 = (bf16[1,128,3072]{2,1,0:T(8,128)(2,1)S(1)}, bf16[1,128,3072]{2,1,0:T(8,128)(2,1)}, u32[]{:S(2)}) copy-start(bf16[1,128,3072]{2,1,0:T(8,128)(2,1)} %param.7) | copy-start | bytes 2359300
  15.2 27.2 %copy-start.18 = (bf16[1,128,3072]{2,1,0:T(8,128)(2,1)S(1)}, bf16[1,128,3072]{2,1,0:T(8,128)(2,1)}, u32[]{:S(2)}) copy-start(bf16[1,128,3072]{2,1,0:T(8,128)(2,1)} %param.8) | copy-start | bytes 2359300
  16.7 36.9 %collective-permute-start.1 = (bf16[128,3072]{1,0:T(8,128)(2,1)S(1)}, bf16[128,3072]{1,0:T(8,128)(2,1)S(1)}, u32[]{:S(2)}, u32[]{:S(2)}) collective-permute-start(bf16[128,3072]{1,0:T(8,128)(2,1)S(1)} %get-tuple-element.62), channel_id=1, source_target_pairs={{0,16},{16,0},{1,17},{17,1},{2,18},{18,2},{3,19},{19,3},{4,20},{20... | collective-permute-start | bytes 2359304 | tf_op jit(solution)/shard_map/ppermute | solution.py:23
  41.3 1.0 copy-start.6
  42.4 1.3 copy-start.7
  53.6 40.3 %copy-start.3 = (bf16[128,3072]{1,0:T(8,128)(2,1)}, bf16[128,3072]{1,0:T(8,128)(2,1)S(1)}, u32[]{:S(2)}) copy-start(bf16[128,3072]{1,0:T(8,128)(2,1)S(1)} %collective-permute-done.1.own_ref.refs_2_) | copy-start | bytes 2359300
  53.6 20.5 %collective-permute-start.2 = (bf16[128,3072]{1,0:T(8,128)(2,1)S(1)}, bf16[128,3072]{1,0:T(8,128)(2,1)S(1)}, u32[]{:S(2)}, u32[]{:S(2)}) collective-permute-start(bf16[128,3072]{1,0:T(8,128)(2,1)S(1)} %get-tuple-element.40.own_ref.refs_0_), channel_id=1, source_target_pairs={{0,1},{1,0},{2,3},{3,2},{4,5},{5,4},{6,7},{7,6},{8,9},{9,8},{10,11... | collective-permute-start | bytes 2359304 | tf_op jit(solution)/shard_map/ppermute | solution.py:23
  54.1 34.8 %collective-permute-start.3 = (bf16[128,3072]{1,0:T(8,128)(2,1)S(1)}, bf16[128,3072]{1,0:T(8,128)(2,1)}, u32[]{:S(2)}, u32[]{:S(2)}) collective-permute-start(bf16[128,3072]{1,0:T(8,128)(2,1)S(1)} %collective-permute-done.1.own_ref.refs_2_), channel_id=1, source_target_pairs={{0,1},{1,0},{2,3},{3,2},{4,5},{5,4},{6,7},{7,6},{8,9},{9,8},{10,11... | collective-permute-start | bytes 2359304 | tf_op jit(solution)/shard_map/ppermute | solution.py:23
  55.7 43.1 %collective-permute-start.4 = (bf16[256,1536]{1,0:T(8,128)(2,1)S(1)}, bf16[256,1536]{1,0:T(8,128)(2,1)}, u32[]{:S(2)}, u32[]{:S(2)}) collective-permute-start(bf16[256,1536]{1,0:T(8,128)(2,1)S(1)} %forward.1.refs_2_), channel_id=1, source_target_pairs={{0,16},{16,0},{1,17},{17,1},{2,18},{18,2},{3,19},{19,3},{4,20},{20... | collective-permute-start | bytes 2359304 | tf_op jit(solution)/shard_map/ppermute | solution.py:23
  74.1 19.8 %copy-start = (bf16[128,3072]{1,0:T(8,128)(2,1)}, bf16[128,3072]{1,0:T(8,128)(2,1)S(1)}, u32[]{:S(2)}) copy-start(bf16[128,3072]{1,0:T(8,128)(2,1)S(1)} %collective-permute-done.2.far_ref.refs_1_) | copy-start | bytes 2359300
  78.5 15.4 %copy-start.21 = (f32[256,768]{1,0:T(8,128)}, f32[256,768]{1,0:T(8,128)S(1)}, u32[]{:S(2)}) copy-start(f32[256,768]{1,0:T(8,128)S(1)} %partial.5.refs_0_) | copy-start | bytes 2359300
  98.2 6.4 %collective-permute-start.5 = (bf16[4,384,512]{2,1,0:T(8,128)(2,1)}, bf16[4,384,512]{2,1,0:T(8,128)(2,1)}, u32[]{:S(2)}, u32[]{:S(2)}) collective-permute-start(bf16[4,384,512]{2,1,0:T(8,128)(2,1)} %turn.3), channel_id=1, source_target_pairs={{0,2},{2,0},{1,3},{3,1},{4,6},{6,4},{5,7},{7,5},{8,10},{10,8},{9,1... | collective-permute-start | bytes 4718600 | tf_op jit(solution)/shard_map/ppermute | solution.py:23
  98.2 5.9 %collective-permute-start.6 = (bf16[256,1536]{1,0:T(8,128)(2,1)S(1)}, bf16[256,1536]{1,0:T(8,128)(2,1)}, u32[]{:S(2)}, u32[]{:S(2)}) collective-permute-start(bf16[256,1536]{1,0:T(8,128)(2,1)S(1)} %forward.1.refs_2_), channel_id=1, source_target_pairs={{0,2},{2,0},{1,3},{3,1},{4,6},{6,4},{5,7},{7,5},{8,10},{10,8},{9,1... | collective-permute-start | bytes 2359304 | tf_op jit(solution)/shard_map/ppermute | solution.py:23
  98.7 5.9 %collective-permute-start.7 = (bf16[256,1536]{1,0:T(8,128)(2,1)}, bf16[256,1536]{1,0:T(8,128)(2,1)}, u32[]{:S(2)}, u32[]{:S(2)}) collective-permute-start(bf16[256,1536]{1,0:T(8,128)(2,1)} %collective-permute-done.4.refs_3_), channel_id=1, source_target_pairs={{0,2},{2,0},{1,3},{3,1},{4,6},{6,4},{5,7},{7,5},{8,10},{10,8},{9,1... | collective-permute-start | bytes 2359304 | tf_op jit(solution)/shard_map/ppermute | solution.py:23
  98.8 1.1 copy-start.1
  99.9 1.1 copy-start.4
  109.0 76.5 %collective-permute-start.12 = (bf16[2,384,768]{2,1,0:T(8,128)(2,1)}, bf16[2,384,768]{2,1,0:T(8,128)(2,1)}, u32[]{:S(2)}, u32[]{:S(2)}) collective-permute-start(bf16[2,384,768]{2,1,0:T(8,128)(2,1)} %rows.4), channel_id=1, source_target_pairs={{0,4},{4,0},{1,5},{5,1},{2,6},{6,2},{3,7},{7,3},{8,12},{12,8},{9,1... | collective-permute-start | bytes 3538952 | tf_op jit(solution)/shard_map/ppermute | solution.py:23
  114.9 70.6 %collective-permute-start.13 = (bf16[2,384,768]{2,1,0:T(8,128)(2,1)}, bf16[2,384,768]{2,1,0:T(8,128)(2,1)}, u32[]{:S(2)}, u32[]{:S(2)}) collective-permute-start(bf16[2,384,768]{2,1,0:T(8,128)(2,1)} %rows.5), channel_id=1, source_target_pairs={{0,8},{8,0},{1,9},{9,1},{2,10},{10,2},{3,11},{11,3},{4,12},{12,4},... | collective-permute-start | bytes 3538952 | tf_op jit(solution)/shard_map/ppermute | solution.py:23
  116.5 35.1 %collective-permute-start.8 = (bf16[256,768]{1,0:T(8,128)(2,1)}, bf16[256,768]{1,0:T(8,128)(2,1)}, u32[]{:S(2)}, u32[]{:S(2)}) collective-permute-start(bf16[256,768]{1,0:T(8,128)(2,1)} %partial.4), channel_id=1, source_target_pairs={{0,16},{16,0},{1,17},{17,1},{2,18},{18,2},{3,19},{19,3},{4,20},{20... | collective-permute-start | bytes 1179656 | tf_op jit(solution)/shard_map/ppermute | solution.py:23
  120.0 1.1 copy-start.5
  126.1 52.3 %collective-permute-start.9 = (bf16[256,768]{1,0:T(8,128)(2,1)}, bf16[256,768]{1,0:T(8,128)(2,1)S(1)}, u32[]{:S(2)}, u32[]{:S(2)}) collective-permute-start(bf16[256,768]{1,0:T(8,128)(2,1)} %partial.7), channel_id=1, source_target_pairs={{0,16},{16,0},{1,17},{17,1},{2,18},{18,2},{3,19},{19,3},{4,20},{20... | collective-permute-start | bytes 1179656 | tf_op jit(solution)/shard_map/ppermute | solution.py:23
  126.1 37.8 %copy-start.2 = (bf16[128,3072]{1,0:T(8,128)(2,1)S(1)}, bf16[128,3072]{1,0:T(8,128)(2,1)}, u32[]{:S(2)}) copy-start(bf16[128,3072]{1,0:T(8,128)(2,1)} %copy-done) | copy-start | bytes 2359300
  151.6 1.3 copy-start.8
  152.9 1.1 copy-start.11
  154.0 1.1 copy-start.15
  155.1 1.1 copy-start.19
  156.3 1.1 copy-start.22
  168.1 25.5 %collective-permute-start.10 = (bf16[3,128,768]{2,1,0:T(8,128)(2,1)S(1)}, bf16[3,128,768]{2,1,0:T(8,128)(2,1)}, u32[]{:S(2)}, u32[]{:S(2)}) collective-permute-start(bf16[3,128,768]{2,1,0:T(8,128)(2,1)S(1)} %get-tuple-element.56), channel_id=1, source_target_pairs={{0,1},{1,0},{2,3},{3,2},{4,5},{5,4},{6,7},{7,6},{8,9},{9,8},{10,11... | collective-permute-start | bytes 1769480 | tf_op jit(solution)/shard_map/ppermute | solution.py:23
  173.5 4.9 %copy-start.9 = (bf16[3,128,1536]{2,1,0:T(8,128)(2,1)S(1)}, bf16[3,128,1536]{2,1,0:T(8,128)(2,1)}, u32[]{:S(2)}) copy-start(bf16[3,128,1536]{2,1,0:T(8,128)(2,1)} %copy-done.6) | copy-start | bytes 3538948
  173.5 4.9 %copy-start.12 = (bf16[1,128,3072]{2,1,0:T(8,128)(2,1)S(1)}, bf16[1,128,3072]{2,1,0:T(8,128)(2,1)}, u32[]{:S(2)}) copy-start(bf16[1,128,3072]{2,1,0:T(8,128)(2,1)} %param.6) | copy-start | bytes 2359300
  173.5 4.9 %copy-start.16 = (bf16[1,128,3072]{2,1,0:T(8,128)(2,1)S(1)}, bf16[1,128,3072]{2,1,0:T(8,128)(2,1)}, u32[]{:S(2)}) copy-start(bf16[1,128,3072]{2,1,0:T(8,128)(2,1)} %param.7) | copy-start | bytes 2359300
  173.5 4.9 %copy-start.20 = (bf16[1,128,3072]{2,1,0:T(8,128)(2,1)S(1)}, bf16[1,128,3072]{2,1,0:T(8,128)(2,1)}, u32[]{:S(2)}) copy-start(bf16[1,128,3072]{2,1,0:T(8,128)(2,1)} %param.8) | copy-start | bytes 2359300
  178.4 7.1 %copy-start.24 = (f32[2,384,768]{2,1,0:T(8,128)S(1)}, f32[2,384,768]{2,1,0:T(8,128)}, u32[]{:S(2)}) copy-start(f32[2,384,768]{2,1,0:T(8,128)} %rows.6) | copy-start | bytes 7077892
  184.3 12.8 %collective-permute-start.11 = (bf16[3,128,768]{2,1,0:T(8,128)(2,1)S(1)}, bf16[3,128,768]{2,1,0:T(8,128)(2,1)S(1)}, u32[]{:S(2)}, u32[]{:S(2)}) collective-permute-start(bf16[3,128,768]{2,1,0:T(8,128)(2,1)S(1)} %get-tuple-element.57), channel_id=1, source_target_pairs={{0,1},{1,0},{2,3},{3,2},{4,5},{5,4},{6,7},{7,6},{8,9},{9,8},{10,11... | collective-permute-start | bytes 1769480 | tf_op jit(solution)/shard_map/ppermute | solution.py:23
  185.5 5.8 %copy-start.23 = (f32[2,384,768]{2,1,0:T(8,128)S(1)}, f32[2,384,768]{2,1,0:T(8,128)}, u32[]{:S(2)}) copy-start(f32[2,384,768]{2,1,0:T(8,128)} %rows.7) | copy-start | bytes 7077892
  187.3 15.4 %collective-permute-start.14 = (bf16[1,384,768]{2,1,0:T(8,128)(2,1)S(1)}, bf16[1,384,768]{2,1,0:T(8,128)(2,1)S(1)}, u32[]{:S(2)}, u32[]{:S(2)}) collective-permute-start(bf16[1,384,768]{2,1,0:T(8,128)(2,1)S(1)} %dynamic-slice_convert_fusion.1), channel_id=1, source_target_pairs={{0,8},{8,0},{1,9},{9,1},{2,10},{10,2},{3,11},{11,3},{4,12},{12,4},... | collective-permute-start | bytes 1769480 | tf_op jit(solution)/shard_map/ppermute | solution.py:23
  193.0 13.0 %collective-permute-start.15 = (bf16[1,384,768]{2,1,0:T(8,128)(2,1)S(1)}, bf16[1,384,768]{2,1,0:T(8,128)(2,1)S(1)}, u32[]{:S(2)}, u32[]{:S(2)}) collective-permute-start(bf16[1,384,768]{2,1,0:T(8,128)(2,1)S(1)} %dynamic-slice_convert_fusion), channel_id=1, source_target_pairs={{0,4},{4,0},{1,5},{5,1},{2,6},{6,2},{3,7},{7,3},{8,12},{12,8},{9,1... | collective-permute-start | bytes 1769480 | tf_op jit(solution)/shard_map/ppermute | solution.py:23
Sparse Core Ops, SparseCore 0:
  10.2 51.5 all-gather.4
  64.0 45.0 all-gather.2

commit v4 on v3

--- a/solution.py
+++ b/solution.py
@@ -84,7 +84,7 @@
 
 
 def params():
-    return pltpu.CompilerParams(vmem_limit_bytes=48 * 1024 * 1024)
+    return pltpu.CompilerParams(vmem_limit_bytes=56 * 1024 * 1024)
 
 
 def small():
@@ -93,6 +93,10 @@
 
 def after(value, *events):
     return lax.optimization_barrier((value, events))[0]
+
+
+def within(start, end):
+    return lambda step, *_: (0, jnp.clip(step - start, 0, end - start - 1))
 
 
 def forward(mine, own, far):
@@ -155,51 +159,82 @@
     )(mine, *own, far, partial, *terms, *held)
 
 
-def partial_kernel(own_ref, far_ref, weight_ref, out_ref, every_row):
-    tokens = own_ref.shape[0]
-
-    @pl.when(pl.program_id(0) == 0)
+def partial_kernel(clips, bounds, at_ref, *refs):
+    owns, fars, refs = refs[:clips], refs[clips : 2 * clips], refs[2 * clips :]
+    groups = len(bounds)
+    *weights, every_row, every_weight = refs
+    weights, outs = weights[: -clips * groups], weights[-clips * groups :]
+    tokens = owns[0].shape[0]
+    length = tokens + fars[0].shape[0]
+    rows = weights[0].shape[0]
+    step = pl.program_id(0)
+
+    @pl.when(step == 0)
     def _():
-        every_row[:tokens] = own_ref[...]
-        every_row[tokens:] = far_ref[...]
-
-    out_ref[...] = dot(every_row[...], weight_ref[...], ((1,), (0,))).astype(out_ref.dtype)
-
-
-def partial_product(own, far, weight, dtype):
-    tokens, depth = own.shape
-    rest = far.shape[0]
-    wide = weight.shape[1]
+        for i, (own, far) in enumerate(zip(owns, fars)):
+            every_row[i * length : i * length + tokens] = own[...]
+            every_row[i * length + tokens : (i + 1) * length] = far[...]
+
+    for i, weight in enumerate(weights):
+        every_weight[pl.ds(pl.multiple_of(at_ref[i] * rows, rows), rows), :] = weight[...]
+    product = dot(every_row[...], every_weight[...], ((1,), (0,)))
+    for i in range(clips):
+        for (start, end), out_ref in zip(bounds, outs[i * groups : (i + 1) * groups]):
+
+            @pl.when((step >= start) & (step < end))
+            def _():
+                out_ref[...] = product[i * length : (i + 1) * length].astype(out_ref.dtype)
+
+
+def partial_products(at, owns, fars, weights, groups, dtype):
+    tokens, depth = owns[0].shape
+    clips, rest = len(owns), fars[0].shape[0]
+    length = tokens + rest
+    rows, features = weights[0].shape
+    wide = features // groups
     block = 256 if wide % 256 == 0 else 128
-    return pl.pallas_call(
-        partial_kernel,
-        grid=(wide // block,),
-        in_specs=[
-            pl.BlockSpec((tokens, depth), lambda i: (0, 0)),
-            pl.BlockSpec((rest, depth), lambda i: (0, 0)),
-            pl.BlockSpec((depth, block), lambda i: (0, i)),
+    steps = wide // block
+    bounds = [(group * steps, (group + 1) * steps) for group in range(groups)]
+    once = pl.Buffered(1)
+    found = pl.pallas_call(
+        functools.partial(partial_kernel, clips, bounds),
+        grid_spec=pltpu.PrefetchScalarGridSpec(
+            num_scalar_prefetch=1,
+            grid=(groups * steps,),
+            in_specs=[
+                pl.BlockSpec(array.shape, lambda i, at: (0, 0), pipeline_mode=once)
+                for array in [*owns, *fars]
+            ]
+            + [pl.BlockSpec((rows, block), lambda i, at: (0, i))] * len(weights),
+            out_specs=[pl.BlockSpec((length, block), within(*bound)) for bound in bounds] * clips,
+            scratch_shapes=[
+                pltpu.VMEM((clips * length, depth), jnp.bfloat16),
+                pltpu.VMEM((depth, block), jnp.bfloat16),
+            ],
+        ),
+        out_shape=[
+            jax.ShapeDtypeStruct((length, wide), dtype) for _ in range(clips * groups)
         ],
-        out_specs=pl.BlockSpec((tokens + rest, block), lambda i: (0, i)),
-        scratch_shapes=[pltpu.VMEM((tokens + rest, depth), jnp.bfloat16)],
-        out_shape=jax.ShapeDtypeStruct((tokens + rest, wide), dtype),
         compiler_params=params(),
         cost_estimate=small(),
         name="partial",
-    )(own, far, weight)
-
-
-def turn_kernel(at_ref, *refs):
-    *inputs, out_ref = refs
-    column = 0
-    for ref in inputs:
-        tokens = ref.shape[0]
-        out_ref[:, column : column + tokens] = ref[...].T
-        column += tokens
-
-
-def turned(at, grads, rows):
+    )(at, *owns, *fars, *weights)
+    return [found[i * groups : (i + 1) * groups] for i in range(clips)]
+
+
+def turn_kernel(clips, at_ref, *refs):
+    out_ref = refs[-1]
+    start = 0
+    for i in range(clips):
+        for ref in (refs[i], refs[clips + i]):
+            tokens = ref.shape[0]
+            out_ref[:, start : start + tokens] = ref[...].T
+            start += tokens
+
+
+def turned(at, owns, fars, rows):
     operands, specs = [], []
-    for grad in grads:
+    for grad in [*owns, *fars]:
         tokens = grad.shape[0]
         if rows % 128 == 0:
             operands.append(grad)
@@ -207,9 +242,9 @@
         else:
             operands.append(jnp.swapaxes(grad.reshape(tokens, -1, rows), 0, 1))
             specs.append(pl.BlockSpec((None, tokens, rows), lambda i, at: (at[i], 0, 0)))
-    depth = sum(grad.shape[0] for grad in grads)
+    depth = sum(grad.shape[0] for grad in [*owns, *fars])
     return pl.pallas_call(
-        turn_kernel,
+        functools.partial(turn_kernel, len(owns)),
         grid_spec=pltpu.PrefetchScalarGridSpec(
             num_scalar_prefetch=1,
             grid=(at.shape[0],),
@@ -224,23 +259,19 @@
 
 
 def rows_kernel(cores, at_ref, *refs):
-    grads, (*attends, out_ref) = refs[:cores], refs[cores:]
-    length = attends[0].shape[0]
-    each = len(attends) // cores
+    grads, attends, out_ref = refs[:cores], refs[cores : 2 * cores], refs[-1]
     total = None
-    for i, attended in enumerate(attends):
-        start = (i % each) * length
-        chosen = grads[i // each][:, start : start + length]
-        term = dot(chosen, attended[...], ((1,), (0,)))
+    for grad, attended in zip(grads, attends):
+        clips, length, wide = attended.shape
+        term = dot(grad[...], attended[...].reshape(clips * length, wide), ((1,), (0,)))
         total = term if total is None else total + term
     out_ref[...] = total.astype(out_ref.dtype)
 
 
-def rows_product(at, grads, attends, group, groups, dtype):
+def rows_product(at, grads, attends, start, wide, dtype):
     _, rows, depth = grads[0].shape
-    flat = [array for arrays in attends for array in arrays]
-    length, features = flat[0].shape
-    wide = features // groups
+    clips, length, _ = attends[0].shape
+    column = start // wide
     count = at.shape[0]
     return pl.pallas_call(
         functools.partial(rows_kernel, len(grads)),
@@ -248,18 +279,30 @@
             num_scalar_prefetch=1,
             grid=(count,),
             in_specs=[pl.BlockSpec((None, rows, depth), lambda i, at: (at[i], 0, 0))] * len(grads)
-            + [pl.BlockSpec((length, wide), lambda i, at: (0, group))] * len(flat),
+            + [pl.BlockSpec((clips, length, wide), lambda i, at: (0, 0, column))] * len(attends),
             out_specs=pl.BlockSpec((None, rows, wide), lambda i, at: (i, 0, 0)),
         ),
         out_shape=jax.ShapeDtypeStruct((count, rows, wide), dtype),
         compiler_params=params(),
         cost_estimate=small(),
         name="rows",
-    )(at, *grads, *flat)
+    )(at, *grads, *attends)
 
 
 def place(axis, by=0):
     return (lax.axis_index(axis) + by) % lax.axis_size(axis)
+
+
+def block_at(zl, x, core):
+    return ((zl * lax.axis_size("x") + x) * lax.axis_size("core") + core).astype(jnp.int32)
+
+
+def shift_both(array, zl, x):
+    zls, xs = lax.axis_size("zl"), lax.axis_size("x")
+    pairs = [
+        (i * xs + j, ((i + zl) % zls) * xs + (j + x) % xs) for i in range(zls) for j in range(xs)
+    ]
+    return lax.ppermute(array, ("zl", "x"), pairs)
 
 
 def blocks_along(axis, by):
@@ -282,65 +325,74 @@
     token_scale = 1.0 / math.sqrt(clips * length)
     me = mine.astype(jnp.int32).reshape(1)
 
-    def along_seq(array):
-        arrived = [shift(array, "seq", by) for by in others("seq")]
-        return arrived[0] if seq == 2 else jnp.concatenate(arrived, axis=0)
+    def across(array):
+        return [shift(array, "core", by) for by in others("core")]
 
     groups = 2 if heads % 4 == 0 else 1
     wide = features // groups
-    weights = [
-        lax.all_gather(
-            out_weight[:, group * wide : (group + 1) * wide], ("zl", "x", "core"), tiled=True
-        )
-        for group in range(groups)
-    ]
-    own_grad = grad_out[0]
-    halves = [shift(part_of(own_grad, "zh", by, 1), "zh", by) for by in others("zh")]
+    unit = heads_a_step(heads, length)
+    larger = (2 * heads // 3) // unit * unit
+    widths = [count * HEAD_DIM for count in (larger, heads - larger) if count]
+    orders = [("x", "zl"), ("zl", "x")][: len(widths)]
+
     own = (queries[0], keys[0], values[0])
     pieces = [
         shift(jnp.stack([part_of(part, "seq", by, 1) for part in own]), "seq", by)
         for by in others("seq")
     ]
     far = pieces[0] if seq == 2 else jnp.concatenate(pieces, axis=1)
-
-    attended = forward(me, own, far)
+    own_grad = grad_out[0]
+    halves = [shift(part_of(own_grad, "zh", by, 1), "zh", by) for by in others("zh")]
+    near_x = [shift(out_weight, "x", by) for by in others("x")]
+    near_zl = [shift(out_weight, "zl", by) for by in others("zl")]
+    own_across = across(out_weight)
+
+    attended = forward(me, own, after(far, own_across))
+
+    def along_seq(array):
+        arrived = [shift(array, "seq", by) for by in others("seq")]
+        return arrived[0] if seq == 2 else jnp.concatenate(arrived, axis=0)
+
+    halves = after(halves, attended)
     attends = [shift(attended, "zh", by) for by in others("zh")]
-    attended_across = [shift(attended, "core", by) for by in others("core")]
-
-    halves = after(halves, attended)
-    own_half = after(part_of(own_grad, "zh", 0, 1), halves)
-    grads = [(half, along_seq(half)) for half in [own_half] + halves]
-
-    def partials(group):
-        return [partial_product(*grad, weights[group], jnp.bfloat16) for grad in grads[1:]]
-
-    def returned(terms):
-        return [shift(term, "zh", -by) for by, term in zip(others("zh"), terms)]
-
-    def own_partial(group):
-        return partial_product(*grads[0], weights[group], jnp.float32)
-
-    sent = partials(0)
-    partial = [own_partial(0)]
-    mine_blocks = jnp.arange(lax.axis_size("zl") * lax.axis_size("x")) * lax.axis_size("core")
-    flat = after([half for grad in grads for half in grad], sent, partial)
-
-    def turned_for(by, arrays):
-        return turned((mine_blocks + place("core", by)).astype(jnp.int32), arrays, rows)
-
-    by_rows = [shift(turned_for(by, flat), "core", by) for by in others("core")]
-    attends, sent = after((attends, sent), flat)
-    terms = [returned(after(sent, attends))]
-    attends_across = [[shift(array, "core", by) for array in attends] for by in others("core")]
-    by_rows = [turned_for(0, after(flat, attends))] + by_rows
-    attends = [[attended] + attends] + [
-        [near] + more for near, more in zip(attended_across, attends_across)
-    ]
-    splits = 2 if features % 256 == 0 else 1
-    orders = [("x", "zl"), ("zl", "x")][:splits]
+    owns = [after(part_of(own_grad, "zh", 0, 1), halves)] + halves
+    fars = [along_seq(half) for half in owns]
+    near_zl = after(near_zl, halves)
+    places = [(zl, x) for zl in others("zl") for x in others("x")]
+    diagonal = [shift(block, "x", by) for block in near_zl for by in others("x")]
+
+    near_x, near_zl, diagonal, attends, owns, fars = lax.optimization_barrier(
+        (near_x, near_zl, diagonal, attends, owns, fars)
+    )
+    x_across = [across(block) for block in near_x]
+    zl_across = [across(block) for block in near_zl]
+    diagonal_across = [across(block) for block in diagonal]
+    pair = jnp.stack([attended] + attends)
+    attends = [pair] + across(pair)
+
+    weights = [((0, 0), out_weight, own_across)]
+    weights += [((0, by), *both_of) for by, *both_of in zip(others("x"), near_x, x_across)]
+    weights += [((by, 0), *both_of) for by, *both_of in zip(others("zl"), near_zl, zl_across)]
+    weights += zip(places, diagonal, diagonal_across)
+    at, blocks = [], []
+    for (zl, x), block, from_cores in weights:
+        for core, array in enumerate([block] + from_cores):
+            at.append(block_at(place("zl", -zl), place("x", -x), place("core", -core)))
+            blocks.append(array)
+
+    turns = jnp.arange(lax.axis_size("zl") * lax.axis_size("x")) * lax.axis_size("core")
+
+    def turned_for(by):
+        return turned((turns + place("core", by)).astype(jnp.int32), owns, fars, rows)
+
+    others_rows = [turned_for(by) for by in others("core")]
+    by_rows = [turned_for(0)] + [
+        shift(array, "core", by) for by, array in zip(others("core"), others_rows)
+    ]
 
     def product(axis, by, split, dtype):
-        return rows_product(blocks_along(axis, by), by_rows, attends, split, splits, dtype)
+        start = sum(widths[:split])
+        return rows_product(blocks_along(axis, by), by_rows, attends, start, widths[split], dtype)
 
     leave = [
         [product(axis, by, split, jnp.bfloat16) for by in others(axis)]
@@ -350,19 +402,24 @@
         [shift(term, axis, by) for by, term in zip(others(axis), terms_of)]
         for (axis, _), terms_of in zip(orders, leave)
     ]
+    owns, fars = after((owns, fars), leave)
+    sent = partial_products(jnp.stack(at), owns[1:], fars[1:], blocks, groups, jnp.bfloat16)
+    terms = [
+        [shift(clip[group], "zh", -by) for by, clip in zip(others("zh"), sent)]
+        for group in range(groups)
+    ]
+    owns, fars = after((owns, fars), sent)
+    (partial,) = partial_products(
+        jnp.stack(at), owns[:1], fars[:1], blocks, groups, jnp.float32
+    )
+    by_rows = after(by_rows, partial)
+    kept = [product(axis, 0, split, jnp.float32) for split, (axis, _) in enumerate(orders)]
+
     result, arrivals = [], []
-
-    def finish(group, *events):
+    for group in range(groups):
         start = group * wide // HEAD_DIM
-        *result[:], leaving = backward(
-            me,
-            own,
-            far,
-            partial[group],
-            after(terms[group], *events),
-            start,
-            wide // HEAD_DIM,
-            list(result),
+        *result, leaving = backward(
+            me, own, far, partial[group], after(terms[group], kept), start, wide // HEAD_DIM, result
         )
         arrivals.append(
             [
@@ -370,16 +427,6 @@
                 for by in others("seq")
             ]
         )
-
-    for group in range(1, groups):
-        weights[group] = after(weights[group], leave)
-        terms.append(returned(partials(group)))
-        finish(group - 1, weights[group])
-        weights[group] = after(weights[group], result)
-        partial.append(own_partial(group))
-    by_rows = after(by_rows, partial, result)
-    kept = [product(axis, 0, split, jnp.float32) for split, (axis, _) in enumerate(orders)]
-    finish(groups - 1, kept)
 
     columns = []
     for (_, axis), arrived, total in zip(orders, after(arrive, result), kept):

time: 216 us -> 198 us (0.917)
  between operations: 14.3 us -> 0.84 us
  waiting for transfers between devices: 89.5 us -> 81.6 us
  local copies, waits for them, and re-layouts: 19 us -> 11.4 us
  Pallas kernels: 62.4 us -> 69.6 us
  other arithmetic: 6.39 us -> 8.6 us
    ppermute x16 -> x22, waiting for transfers between devices: 88.7 us -> 81.6 us  [shift(): lax.ppermute(array, axis, [(i, (i + by) % count) for i in range(count)])]
    unnamed x50 -> x24, local copies, waits for them, and re-layouts: 12.1 us -> 5.28 us
    pallas_call x6 -> x4, Pallas kernels: 25.8 us -> 28.8 us  [the longest x2 19.6 us: partial_products(): pl.pallas_call(functools.partial(partial_kernel, clips, bounds), grid_spe...]
    add x2, other arithmetic: 3.31 us -> 0.84 us  [shards(): total = total + term.astype(jnp.float32)]
    slice x1 -> x0, local copies, waits for them, and re-layouts: 2.39 us -> none  [shards(): out_weight[:, group * wide:(group + 1) * wide]]
    add x4, other arithmetic: 0.02 us -> 2.24 us  [blocks_along(): return (zl * lax.axis_size('x') + x).astype(jnp.int32)]
    ppermute x16 -> x22, starting transfers between devices: 23 us -> 24.7 us  [shift(): lax.ppermute(array, axis, [(i, (i + by) % count) for i in range(count)])]
  transfers between devices with their start and end apart: 18 -> 22, of which waited for: 9 -> 8; matrix products, arithmetic and copies ran while one was open for 4% -> 5% of each run, Pallas kernels for 29% -> 33%
where the time goes in v4:
time: 198 us; the launch traced here: 197 us
  waiting for transfers between devices  81.6 us (41%)
  Pallas kernels  69.6 us (35%)
  starting transfers between devices  24.7 us (12%)
  local copies, waits for them, and re-layouts  11.4 us (6%)
  other arithmetic  8.6 us (4%)
    ppermute x22, waiting for transfers between devices, shift(): lax.ppermute(array, axis, [(i, (i + by) % count) for i in range(count)])  81.6 us
    ppermute x22, starting transfers between devices, shift(): lax.ppermute(array, axis, [(i, (i + by) % count) for i in range(count)])  24.7 us
    pallas_call x2, Pallas kernels, partial_products(): pl.pallas_call(functools.partial(partial_kernel, clips, bounds), grid_spe...  19.6 us
    pallas_call x4, Pallas kernels, rows_product(): pl.pallas_call(functools.partial(rows_kernel, len(grads)), grid_spec=pltp...  19.3 us
    pallas_call x2, Pallas kernels, backward(): pl.pallas_call(functools.partial(backward_kernel, step, len(held), 1 + le...  13.9 us
    pallas_call x2, Pallas kernels, turned(): pl.pallas_call(functools.partial(turn_kernel, len(owns)), grid_spec=pltpu...  9.22 us
    pallas_call x1, Pallas kernels, forward(): pl.pallas_call(functools.partial(forward_kernel, step), grid_spec=pltpu.P...  7.58 us
    unnamed x24, local copies, waits for them, and re-layouts  5.28 us
  transfers between devices with their start and end apart: 22, of which 8 were waited for; matrix products, arithmetic and copies ran while one was open for 5% of the time, Pallas kernels for 33%

profile of v4, /device:TPU:0, one launch (start us, length us, event | category | flops | bytes accessed | tf_op | source)
XLA Modules:
  0.0 196.7 jit_solution(11835446935229791046)
XLA Ops:
  0.6 1.0 constant_dynamic-slice_fusion.2
  1.7 1.2 constant_dynamic-slice_fusion
  2.9 1.1 pad_maximum_fusion.1
  4.0 3.0 %collective-permute-start = (bf16[3,128,1536]{2,1,0:T(8,128)(2,1)}, bf16[3,128,1536]{2,1,0:T(8,128)(2,1)S(1)}, u32[]{:S(2)}, u32[]{:S(2)}) collective-permute-start(bf16[3,128,1536]{2,1,0:T(8,128)(2,1)} %pad_maximum_fusion.1), channel_id=1, source_target_pairs={{0,1},{1,0},{2,3},{3,2},{4,5},{5,4},{6,7},{7,6},{8,9},{9,8},{10,11... | collective-permute-start | bytes 3538952 | tf_op jit(solution)/shard_map/ppermute | solution.py:23
  7.0 1.6 collective-permute-start.2
  8.5 1.5 dynamic-slice_bitcast_fusion
  10.0 2.7 %collective-permute-start.3 = (bf16[128,3072]{1,0:T(8,128)(2,1)S(1)}, bf16[128,3072]{1,0:T(8,128)(2,1)S(1)}, u32[]{:S(2)}, u32[]{:S(2)}) collective-permute-start(bf16[128,3072]{1,0:T(8,128)(2,1)S(1)} %get-tuple-element.77), channel_id=1, source_target_pairs={{0,16},{16,0},{1,17},{17,1},{2,18},{18,2},{3,19},{19,3},{4,20},{20... | collective-permute-start | bytes 2359304 | tf_op jit(solution)/shard_map/ppermute | solution.py:23
  12.7 1.5 collective-permute-start.1
  14.2 19.0 %collective-permute-done.far = bf16[3,128,1536]{2,1,0:T(8,128)(2,1)S(1)} collective-permute-done((bf16[3,128,1536]{2,1,0:T(8,128)(2,1)}, bf16[3,128,1536]{2,1,0:T(8,128)(2,1)S(1)}, u32[]{:S(2)}, u32[]{:S(2)}) %collective-permute-start) | collective-permute-done | bytes 1179680 | tf_op jit(solution)/shard_map/ppermute | solution.py:23
  33.1 1.0 copy-done.4
  34.2 7.6 %forward.1 = bf16[256,1536]{1,0:T(8,128)(2,1)} custom-call(s32[1]{0:T(128)} %bitcast.mine_ref, bf16[128,3072]{1,0:T(8,128)(2,1)} %bitcast.25, bf16[128,3072]{1,0:T(8,128)(2,1)} %bitcast.28, bf16[128,3072]{1,0:T(8,128)(2,1)} %bitcast.31, bf16[3,128,1536]{2,1,0:T(8,128)(2,1)} %copy-done.4), custom_call_target="tpu_custom_call" | custom-call | flops 1024 | bytes 1024 | tf_op jit(solution)/shard_map/forward/pallas_call | solution.py:112
  41.8 9.7 %collective-permute-done.3.refs_1_.refs_0_ = bf16[128,3072]{1,0:T(8,128)(2,1)S(1)} collective-permute-done((bf16[128,3072]{1,0:T(8,128)(2,1)S(1)}, bf16[128,3072]{1,0:T(8,128)(2,1)S(1)}, u32[]{:S(2)}, u32[]{:S(2)}) %collective-permute-start.3) | collective-permute-done | bytes 786464 | tf_op jit(solution)/shard_map/ppermute | solution.py:23
  51.5 1.0 collective-permute-done.2.refs_6_
  52.5 1.5 collective-permute-start.5
  54.0 2.4 %collective-permute-start.6 = (bf16[256,1536]{1,0:T(8,128)(2,1)}, bf16[256,1536]{1,0:T(8,128)(2,1)}, u32[]{:S(2)}, u32[]{:S(2)}) collective-permute-start(bf16[256,1536]{1,0:T(8,128)(2,1)} %forward.1), channel_id=1, source_target_pairs={{0,16},{16,0},{1,17},{17,1},{2,18},{18,2},{3,19},{19,3},{4,20},{20... | collective-permute-start | bytes 2359304 | tf_op jit(solution)/shard_map/ppermute | solution.py:23
  56.4 0.5 collective-permute-start.7
  56.9 1.5 collective-permute-start.8
  58.4 0.6 fusion.at_ref
  59.0 32.0 %collective-permute-done.6 = bf16[256,1536]{1,0:T(8,128)(2,1)} collective-permute-done((bf16[256,1536]{1,0:T(8,128)(2,1)}, bf16[256,1536]{1,0:T(8,128)(2,1)}, u32[]{:S(2)}, u32[]{:S(2)}) %collective-permute-start.6) | collective-permute-done | bytes 786464 | tf_op jit(solution)/shard_map/ppermute | solution.py:23
  91.0 0.9 collective-permute-done.8.refs_3_.refs_1_
  91.9 0.9 copy-done.7
  92.7 4.6 %turn.3 = bf16[4,384,512]{2,1,0:T(8,128)(2,1)} custom-call(s32[4]{0:T(128)} %fusion.at_ref, bf16[128,3072]{1,0:T(8,128)(2,1)} %copy-done.3, bf16[128,3072]{1,0:T(8,128)(2,1)} %copy-done.6, bf16[128,3072]{1,0:T(8,128)(2,1)} %copy-done.5, bf16[128,3072]{1,0:T(8,128)(2,1)} %copy-done.7), custom_call_target="tpu_custom_call" | custom-call | flops 1024 | bytes 1024 | tf_op jit(solution)/shard_map/turn/pallas_call | solution.py:246
  97.4 1.3 pad_maximum_fusion.refs_2_
  98.7 0.6 collective-permute-start.10
  99.2 0.6 fusion.1.at_ref
  99.8 0.1 collective-permute-start.11
  99.9 0.4 collective-permute-start.12
  100.3 0.1 collective-permute-start.13
  100.5 0.6 fusion.3.at_ref
  101.0 4.6 %turn.2.refs_0_ = bf16[4,384,512]{2,1,0:T(8,128)(2,1)} custom-call(s32[4]{0:T(128)} %fusion.1.at_ref, bf16[128,3072]{1,0:T(8,128)(2,1)} %copy-done.3, bf16[128,3072]{1,0:T(8,128)(2,1)} %copy-done.6, bf16[128,3072]{1,0:T(8,128)(2,1)} %copy-done.5, bf16[128,3072]{1,0:T(8,128)(2,1)} %copy-done.7), custom_call_target="tpu_custom_call" | custom-call | flops 1024 | bytes 1024 | tf_op jit(solution)/shard_map/turn/pallas_call | solution.py:246
  105.7 1.2 copy-done.1
  106.9 5.4 %rows.4 = bf16[2,384,1024]{2,1,0:T(8,128)(2,1)} custom-call(s32[2]{0:T(128)} %fusion.3.at_ref, bf16[4,384,512]{2,1,0:T(8,128)(2,1)} %turn.2.refs_0_, bf16[4,384,512]{2,1,0:T(8,128)(2,1)} %copy-done.1, bf16[2,256,1536]{2,1,0:T(8,128)(2,1)} %copy-done, bf16[2,256,1536]{2,1,0:T(8,128)(2,1)} %collective-permute-done.10.refs_3_), custom_call_target="tpu_custom_call" | custom-call | flops 1024 | bytes 1024 | tf_op jit(solution)/shard_map/rows/pallas_call | solution.py:276
  112.2 0.5 collective-permute-start.18
  112.8 0.6 iota_add_fusion.1.at_ref
  113.3 4.1 %rows.5 = bf16[2,384,512]{2,1,0:T(8,128)(2,1)} custom-call(s32[2]{0:T(128)} %iota_add_fusion.1.at_ref, bf16[4,384,512]{2,1,0:T(8,128)(2,1)} %turn.2.refs_0_, bf16[4,384,512]{2,1,0:T(8,128)(2,1)} %copy-done.1, bf16[2,256,1536]{2,1,0:T(8,128)(2,1)} %copy-done, bf16[2,256,1536]{2,1,0:T(8,128)(2,1)} %collective-permute-done.10.refs_3_), custom_call_target="tpu_custom_call" | custom-call | flops 1024 | bytes 1024 | tf_op jit(solution)/shard_map/rows/pallas_call | solution.py:276
  117.4 1.8 collective-permute-start.19
  119.2 0.6 stack.60.at_ref
  119.8 9.7 %partial.2 = (bf16[256,768]{1,0:T(8,128)(2,1)}, bf16[256,768]{1,0:T(8,128)(2,1)}) custom-call(s32[8]{0:T(128)} %stack.60.at_ref, bf16[128,3072]{1,0:T(8,128)(2,1)} %copy-done.6, bf16[128,3072]{1,0:T(8,128)(2,1)} %copy-done.7, bf16[384,1536]{1,0:T(8,128)(2,1)} %refs_2_.3, bf16[384,1536]{1,0:T(8,128)(2,1)} %collective-permute-done.4.refs_3_, ...), custom_call_target="tpu_custom_call" | custom-call | flops 1024 | bytes 1024 | tf_op jit(solution)/shard_map/partial/pallas_call | solution.py:199
  129.5 1.5 collective-permute-start.15
  131.0 1.5 collective-permute-start.14
  132.5 0.6 fusion.2.at_ref
  133.1 0.5 iota_add_fusion.at_ref
  133.6 9.9 %partial.3 = (f32[256,768]{1,0:T(8,128)}, f32[256,768]{1,0:T(8,128)}) custom-call(s32[8]{0:T(128)} %stack.60.at_ref, bf16[128,3072]{1,0:T(8,128)(2,1)} %copy-done.3, bf16[128,3072]{1,0:T(8,128)(2,1)} %copy-done.5, bf16[384,1536]{1,0:T(8,128)(2,1)} %refs_2_.3, bf16[384,1536]{1,0:T(8,128)(2,1)} %collective-permute-done.4.refs_3_, ...), custom_call_target="tpu_custom_call" | custom-call | flops 1024 | bytes 1024 | tf_op jit(solution)/shard_map/partial/pallas_call | solution.py:199
  143.5 5.6 %rows.6 = f32[2,384,1024]{2,1,0:T(8,128)} custom-call(s32[2]{0:T(128)} %fusion.2.at_ref, bf16[4,384,512]{2,1,0:T(8,128)(2,1)} %turn.2.refs_0_, bf16[4,384,512]{2,1,0:T(8,128)(2,1)} %copy-done.1, bf16[2,256,1536]{2,1,0:T(8,128)(2,1)} %copy-done, bf16[2,256,1536]{2,1,0:T(8,128)(2,1)} %collective-permute-done.10.refs_3_), custom_call_target="tpu_custom_call" | custom-call | flops 1024 | bytes 1024 | tf_op jit(solution)/shard_map/rows/pallas_call | solution.py:276
  149.1 4.3 %rows.7 = f32[2,384,512]{2,1,0:T(8,128)} custom-call(s32[2]{0:T(128)} %iota_add_fusion.at_ref, bf16[4,384,512]{2,1,0:T(8,128)(2,1)} %turn.2.refs_0_, bf16[4,384,512]{2,1,0:T(8,128)(2,1)} %copy-done.1, bf16[2,256,1536]{2,1,0:T(8,128)(2,1)} %copy-done, bf16[2,256,1536]{2,1,0:T(8,128)(2,1)} %collective-permute-done.10.refs_3_), custom_call_target="tpu_custom_call" | custom-call | flops 1024 | bytes 1024 | tf_op jit(solution)/shard_map/rows/pallas_call | solution.py:276
  153.4 6.1 %collective-permute-done.15.refs_1_ = bf16[256,768]{1,0:T(8,128)(2,1)S(1)} collective-permute-done((bf16[256,768]{1,0:T(8,128)(2,1)}, bf16[256,768]{1,0:T(8,128)(2,1)S(1)}, u32[]{:S(2)}, u32[]{:S(2)}) %collective-permute-start.15) | collective-permute-done | bytes 393248 | tf_op jit(solution)/shard_map/ppermute | solution.py:23
  159.6 0.8 copy-done.11
  160.3 6.8 %backward.2 = (bf16[128,3072]{1,0:T(8,128)(2,1)}, bf16[128,3072]{1,0:T(8,128)(2,1)}, bf16[128,3072]{1,0:T(8,128)(2,1)}, bf16[3,128,768]{2,1,0:T(8,128)(2,1)}) custom-call(s32[1]{0:T(128)} %bitcast.mine_ref, bf16[128,3072]{1,0:T(8,128)(2,1)} %bitcast.26, bf16[128,3072]{1,0:T(8,128)(2,1)} %bitcast.29, bf16[128,3072]{1,0:T(8,128)(2,1)} %bitcast.32, ...), custom_call_target="tpu_custom_call" | custom-call | flops 1024 | bytes 1024 | tf_op jit(solution)/shard_map/backward/pallas_call | solution.py:141
  167.2 0.6 collective-permute-start.16
  167.8 0.2 copy-done.10
  167.9 7.0 %backward.3 = (bf16[128,3072]{1,0:T(8,128)(2,1)}, bf16[128,3072]{1,0:T(8,128)(2,1)}, bf16[128,3072]{1,0:T(8,128)(2,1)}, bf16[3,128,768]{2,1,0:T(8,128)(2,1)}) custom-call(s32[1]{0:T(128)} %bitcast.mine_ref, bf16[128,3072]{1,0:T(8,128)(2,1)} %bitcast.27, bf16[128,3072]{1,0:T(8,128)(2,1)} %bitcast.30, ...), custom_call_target="tpu_custom_call", output_to_operand_aliasing={{0}: (7, {}), {1}: (8, {}), {2}: (9, {})} | custom-call | flops 1024 | bytes 1024 | tf_op jit(solution)/shard_map/backward/pallas_call | solution.py:141
  175.0 1.4 collective-permute-start.17
  176.3 0.5 convert_add_fusion
  176.9 0.1 dynamic-slice_convert_fusion
  177.1 1.2 copy-done.8
  178.3 0.3 convert_add_fusion.1
  178.7 1.6 collective-permute-start.21
  180.2 3.5 %collective-permute-done.16 = bf16[3,128,768]{2,1,0:T(8,128)(2,1)S(1)} collective-permute-done((bf16[3,128,768]{2,1,0:T(8,128)(2,1)}, bf16[3,128,768]{2,1,0:T(8,128)(2,1)S(1)}, u32[]{:S(2)}, u32[]{:S(2)}) %collective-permute-start.16) | collective-permute-done | bytes 589856 | tf_op jit(solution)/shard_map/ppermute | solution.py:23
  183.7 0.8 slice_dynamic-update-slice_fusion.1
  184.6 9.3 %collective-permute-done.17 = bf16[3,128,768]{2,1,0:T(8,128)(2,1)S(1)} collective-permute-done((bf16[3,128,768]{2,1,0:T(8,128)(2,1)}, bf16[3,128,768]{2,1,0:T(8,128)(2,1)S(1)}, u32[]{:S(2)}, u32[]{:S(2)}) %collective-permute-start.17) | collective-permute-done | bytes 589856 | tf_op jit(solution)/shard_map/ppermute | solution.py:23
  193.9 0.8 slice_dynamic-update-slice_fusion
  194.7 0.1 add_bitcast_fusion.1
  194.8 0.3 add_bitcast_fusion
  195.1 1.6 maximum_multiply_fusion
  (36 shorter events, 0.2 us)
Async XLA Ops:
  4.0 29.1 %collective-permute-start = (bf16[3,128,1536]{2,1,0:T(8,128)(2,1)}, bf16[3,128,1536]{2,1,0:T(8,128)(2,1)S(1)}, u32[]{:S(2)}, u32[]{:S(2)}) collective-permute-start(bf16[3,128,1536]{2,1,0:T(8,128)(2,1)} %pad_maximum_fusion.1), channel_id=1, source_target_pairs={{0,1},{1,0},{2,3},{3,2},{4,5},{5,4},{6,7},{7,6},{8,9},{9,8},{10,11... | collective-permute-start | bytes 3538952 | tf_op jit(solution)/shard_map/ppermute | solution.py:23
  7.0 26.2 %collective-permute-start.4 = (bf16[384,1536]{1,0:T(8,128)(2,1)}, bf16[384,1536]{1,0:T(8,128)(2,1)}, u32[]{:S(2)}, u32[]{:S(2)}) collective-permute-start(bf16[384,1536]{1,0:T(8,128)(2,1)} %refs_2_.3), channel_id=1, source_target_pairs={{0,2},{2,0},{1,3},{3,1},{4,6},{6,4},{5,7},{7,5},{8,10},{10,8},{9,1... | collective-permute-start | bytes 3538952 | tf_op jit(solution)/shard_map/ppermute | solution.py:23
  7.0 45.5 %collective-permute-start.2 = (bf16[384,1536]{1,0:T(8,128)(2,1)}, bf16[384,1536]{1,0:T(8,128)(2,1)}, u32[]{:S(2)}, u32[]{:S(2)}) collective-permute-start(bf16[384,1536]{1,0:T(8,128)(2,1)} %refs_2_.3), channel_id=1, source_target_pairs={{0,8},{8,0},{1,9},{9,1},{2,10},{10,2},{3,11},{11,3},{4,12},{12,4},... | collective-permute-start | bytes 3538952 | tf_op jit(solution)/shard_map/ppermute | solution.py:23
  10.0 46.4 %copy-start.3 = (bf16[128,3072]{1,0:T(8,128)(2,1)}, bf16[128,3072]{1,0:T(8,128)(2,1)S(1)}, u32[]{:S(2)}) copy-start(bf16[128,3072]{1,0:T(8,128)(2,1)S(1)} %get-tuple-element.58.refs_0_) | copy-start | bytes 2359300
  10.0 41.5 %collective-permute-start.3 = (bf16[128,3072]{1,0:T(8,128)(2,1)S(1)}, bf16[128,3072]{1,0:T(8,128)(2,1)S(1)}, u32[]{:S(2)}, u32[]{:S(2)}) collective-permute-start(bf16[128,3072]{1,0:T(8,128)(2,1)S(1)} %get-tuple-element.77), channel_id=1, source_target_pairs={{0,16},{16,0},{1,17},{17,1},{2,18},{18,2},{3,19},{19,3},{4,20},{20... | collective-permute-start | bytes 2359304 | tf_op jit(solution)/shard_map/ppermute | solution.py:23
  12.7 46.3 %collective-permute-start.1 = (bf16[384,1536]{1,0:T(8,128)(2,1)}, bf16[384,1536]{1,0:T(8,128)(2,1)}, u32[]{:S(2)}, u32[]{:S(2)}) collective-permute-start(bf16[384,1536]{1,0:T(8,128)(2,1)} %refs_2_.3), channel_id=1, source_target_pairs={{0,4},{4,0},{1,5},{5,1},{2,6},{6,2},{3,7},{7,3},{8,12},{12,8},{9,1... | collective-permute-start | bytes 3538952 | tf_op jit(solution)/shard_map/ppermute | solution.py:23
  33.1 1.0 copy-start.4
  51.5 40.4 %copy-start.6 = (bf16[128,3072]{1,0:T(8,128)(2,1)}, bf16[128,3072]{1,0:T(8,128)(2,1)S(1)}, u32[]{:S(2)}) copy-start(bf16[128,3072]{1,0:T(8,128)(2,1)S(1)} %collective-permute-done.3.refs_1_.refs_0_) | copy-start | bytes 2359300
  52.5 39.3 %collective-permute-start.5 = (bf16[384,1536]{1,0:T(8,128)(2,1)}, bf16[384,1536]{1,0:T(8,128)(2,1)}, u32[]{:S(2)}, u32[]{:S(2)}) collective-permute-start(bf16[384,1536]{1,0:T(8,128)(2,1)} %collective-permute-done.2.refs_6_), channel_id=1, source_target_pairs={{0,4},{4,0},{1,5},{5,1},{2,6},{6,2},{3,7},{7,3},{8,12},{12,8},{9,1... | collective-permute-start | bytes 3538952 | tf_op jit(solution)/shard_map/ppermute | solution.py:23
  54.0 37.0 %collective-permute-start.6 = (bf16[256,1536]{1,0:T(8,128)(2,1)}, bf16[256,1536]{1,0:T(8,128)(2,1)}, u32[]{:S(2)}, u32[]{:S(2)}) collective-permute-start(bf16[256,1536]{1,0:T(8,128)(2,1)} %forward.1), channel_id=1, source_target_pairs={{0,16},{16,0},{1,17},{17,1},{2,18},{18,2},{3,19},{19,3},{4,20},{20... | collective-permute-start | bytes 2359304 | tf_op jit(solution)/shard_map/ppermute | solution.py:23
  56.4 34.6 %collective-permute-start.7 = (bf16[128,3072]{1,0:T(8,128)(2,1)S(1)}, bf16[128,3072]{1,0:T(8,128)(2,1)S(1)}, u32[]{:S(2)}, u32[]{:S(2)}) collective-permute-start(bf16[128,3072]{1,0:T(8,128)(2,1)S(1)} %get-tuple-element.58.refs_0_), channel_id=1, source_target_pairs={{0,1},{1,0},{2,3},{3,2},{4,5},{5,4},{6,7},{7,6},{8,9},{9,8},{10,11... | collective-permute-start | bytes 2359304 | tf_op jit(solution)/shard_map/ppermute | solution.py:23
  56.9 35.0 %collective-permute-start.8 = (bf16[128,3072]{1,0:T(8,128)(2,1)S(1)}, bf16[128,3072]{1,0:T(8,128)(2,1)S(1)}, u32[]{:S(2)}, u32[]{:S(2)}) collective-permute-start(bf16[128,3072]{1,0:T(8,128)(2,1)S(1)} %collective-permute-done.3.refs_1_.refs_0_), channel_id=1, source_target_pairs={{0,1},{1,0},{2,3},{3,2},{4,5},{5,4},{6,7},{7,6},{8,9},{9,8},{10,11... | collective-permute-start | bytes 2359304 | tf_op jit(solution)/shard_map/ppermute | solution.py:23
  59.0 38.4 %copy-start.9 = (bf16[256,1536]{1,0:T(8,128)(2,1)S(1)}, bf16[256,1536]{1,0:T(8,128)(2,1)}, u32[]{:S(2)}) copy-start(bf16[256,1536]{1,0:T(8,128)(2,1)} %forward.1) | copy-start | bytes 2359300
  91.0 0.9 copy-start.5
  91.9 0.9 copy-start.7
  97.4 8.3 %collective-permute-start.9 = (bf16[4,384,512]{2,1,0:T(8,128)(2,1)}, bf16[4,384,512]{2,1,0:T(8,128)(2,1)S(1)}, u32[]{:S(2)}, u32[]{:S(2)}) collective-permute-start(bf16[4,384,512]{2,1,0:T(8,128)(2,1)} %turn.3), channel_id=1, source_target_pairs={{0,2},{2,0},{1,3},{3,1},{4,6},{6,4},{5,7},{7,5},{8,10},{10,8},{9,1... | collective-permute-start | bytes 4718600 | tf_op jit(solution)/shard_map/ppermute | solution.py:23
  98.7 7.0 %copy-start = (bf16[2,256,1536]{2,1,0:T(8,128)(2,1)}, bf16[2,256,1536]{2,1,0:T(8,128)(2,1)S(1)}, u32[]{:S(2)}) copy-start(bf16[2,256,1536]{2,1,0:T(8,128)(2,1)S(1)} %pad_maximum_fusion.refs_2_) | copy-start | bytes 4718596
  98.7 7.0 %collective-permute-start.10 = (bf16[2,256,1536]{2,1,0:T(8,128)(2,1)S(1)}, bf16[2,256,1536]{2,1,0:T(8,128)(2,1)}, u32[]{:S(2)}, u32[]{:S(2)}) collective-permute-start(bf16[2,256,1536]{2,1,0:T(8,128)(2,1)S(1)} %pad_maximum_fusion.refs_2_), channel_id=1, source_target_pairs={{0,2},{2,0},{1,3},{3,1},{4,6},{6,4},{5,7},{7,5},{8,10},{10,8},{9,1... | collective-permute-start | bytes 4718600 | tf_op jit(solution)/shard_map/ppermute | solution.py:23
  99.8 20.0 %collective-permute-start.11 = (bf16[384,1536]{1,0:T(8,128)(2,1)}, bf16[384,1536]{1,0:T(8,128)(2,1)}, u32[]{:S(2)}, u32[]{:S(2)}) collective-permute-start(bf16[384,1536]{1,0:T(8,128)(2,1)} %collective-permute-done.1.refs_4_), channel_id=1, source_target_pairs={{0,2},{2,0},{1,3},{3,1},{4,6},{6,4},{5,7},{7,5},{8,10},{10,8},{9,1... | collective-permute-start | bytes 3538952 | tf_op jit(solution)/shard_map/ppermute | solution.py:23
  99.9 19.9 %collective-permute-start.12 = (bf16[384,1536]{1,0:T(8,128)(2,1)}, bf16[384,1536]{1,0:T(8,128)(2,1)}, u32[]{:S(2)}, u32[]{:S(2)}) collective-permute-start(bf16[384,1536]{1,0:T(8,128)(2,1)} %collective-permute-done.2.refs_6_), channel_id=1, source_target_pairs={{0,2},{2,0},{1,3},{3,1},{4,6},{6,4},{5,7},{7,5},{8,10},{10,8},{9,1... | collective-permute-start | bytes 3538952 | tf_op jit(solution)/shard_map/ppermute | solution.py:23
  100.3 19.5 %collective-permute-start.13 = (bf16[384,1536]{1,0:T(8,128)(2,1)}, bf16[384,1536]{1,0:T(8,128)(2,1)}, u32[]{:S(2)}, u32[]{:S(2)}) collective-permute-start(bf16[384,1536]{1,0:T(8,128)(2,1)} %collective-permute-done.5.refs_8_), channel_id=1, source_target_pairs={{0,2},{2,0},{1,3},{3,1},{4,6},{6,4},{5,7},{7,5},{8,10},{10,8},{9,1... | collective-permute-start | bytes 3538952 | tf_op jit(solution)/shard_map/ppermute | solution.py:23
  105.6 1.2 copy-start.1
  112.2 64.1 %collective-permute-start.18 = (bf16[2,384,1024]{2,1,0:T(8,128)(2,1)}, bf16[2,384,1024]{2,1,0:T(8,128)(2,1)S(1)}, u32[]{:S(2)}, u32[]{:S(2)}) collective-permute-start(bf16[2,384,1024]{2,1,0:T(8,128)(2,1)} %rows.4), channel_id=1, source_target_pairs={{0,4},{4,0},{1,5},{5,1},{2,6},{6,2},{3,7},{7,3},{8,12},{12,8},{9,1... | collective-permute-start | bytes 4718600 | tf_op jit(solution)/shard_map/ppermute | solution.py:23
  117.4 58.9 %collective-permute-start.19 = (bf16[2,384,512]{2,1,0:T(8,128)(2,1)}, bf16[2,384,512]{2,1,0:T(8,128)(2,1)S(1)}, u32[]{:S(2)}, u32[]{:S(2)}) collective-permute-start(bf16[2,384,512]{2,1,0:T(8,128)(2,1)} %rows.5), channel_id=1, source_target_pairs={{0,8},{8,0},{1,9},{9,1},{2,10},{10,2},{3,11},{11,3},{4,12},{12,4},... | collective-permute-start | bytes 2359304 | tf_op jit(solution)/shard_map/ppermute | solution.py:23
  129.5 30.0 %collective-permute-start.15 = (bf16[256,768]{1,0:T(8,128)(2,1)}, bf16[256,768]{1,0:T(8,128)(2,1)S(1)}, u32[]{:S(2)}, u32[]{:S(2)}) collective-permute-start(bf16[256,768]{1,0:T(8,128)(2,1)} %get-tuple-element.56), channel_id=1, source_target_pairs={{0,16},{16,0},{1,17},{17,1},{2,18},{18,2},{3,19},{19,3},{4,20},{20... | collective-permute-start | bytes 1179656 | tf_op jit(solution)/shard_map/ppermute | solution.py:23
  131.0 36.2 %collective-permute-start.14 = (bf16[256,768]{1,0:T(8,128)(2,1)}, bf16[256,768]{1,0:T(8,128)(2,1)S(1)}, u32[]{:S(2)}, u32[]{:S(2)}) collective-permute-start(bf16[256,768]{1,0:T(8,128)(2,1)} %get-tuple-element.57), channel_id=1, source_target_pairs={{0,16},{16,0},{1,17},{17,1},{2,18},{18,2},{3,19},{19,3},{4,20},{20... | collective-permute-start | bytes 1179656 | tf_op jit(solution)/shard_map/ppermute | solution.py:23
  159.6 0.8 copy-start.11
  167.2 0.8 copy-start.10
  167.2 16.5 %collective-permute-start.16 = (bf16[3,128,768]{2,1,0:T(8,128)(2,1)}, bf16[3,128,768]{2,1,0:T(8,128)(2,1)S(1)}, u32[]{:S(2)}, u32[]{:S(2)}) collective-permute-start(bf16[3,128,768]{2,1,0:T(8,128)(2,1)} %get-tuple-element.70), channel_id=1, source_target_pairs={{0,1},{1,0},{2,3},{3,2},{4,5},{5,4},{6,7},{7,6},{8,9},{9,8},{10,11... | collective-permute-start | bytes 1769480 | tf_op jit(solution)/shard_map/ppermute | solution.py:23
  167.9 8.4 %copy-start.2 = (f32[2,384,1024]{2,1,0:T(8,128)S(1)}, f32[2,384,1024]{2,1,0:T(8,128)}, u32[]{:S(2)}) copy-start(f32[2,384,1024]{2,1,0:T(8,128)} %rows.6) | copy-start | bytes 9437188
  175.0 18.9 %collective-permute-start.17 = (bf16[3,128,768]{2,1,0:T(8,128)(2,1)}, bf16[3,128,768]{2,1,0:T(8,128)(2,1)S(1)}, u32[]{:S(2)}, u32[]{:S(2)}) collective-permute-start(bf16[3,128,768]{2,1,0:T(8,128)(2,1)} %get-tuple-element.71), channel_id=1, source_target_pairs={{0,1},{1,0},{2,3},{3,2},{4,5},{5,4},{6,7},{7,6},{8,9},{9,8},{10,11... | collective-permute-start | bytes 1769480 | tf_op jit(solution)/shard_map/ppermute | solution.py:23
  176.9 1.4 copy-start.8
  177.0 17.8 %collective-permute-start.20 = (bf16[1,384,1024]{2,1,0:T(8,128)(2,1)S(1)}, bf16[1,384,1024]{2,1,0:T(8,128)(2,1)S(1)}, u32[]{:S(2)}, u32[]{:S(2)}) collective-permute-start(bf16[1,384,1024]{2,1,0:T(8,128)(2,1)S(1)} %dynamic-slice_convert_fusion), channel_id=1, source_target_pairs={{0,8},{8,0},{1,9},{9,1},{2,10},{10,2},{3,11},{11,3},{4,12},{12,4},... | collective-permute-start | bytes 2359304 | tf_op jit(solution)/shard_map/ppermute | solution.py:23
  178.7 16.1 %collective-permute-start.21 = (bf16[1,384,512]{2,1,0:T(8,128)(2,1)S(1)}, bf16[1,384,512]{2,1,0:T(8,128)(2,1)S(1)}, u32[]{:S(2)}, u32[]{:S(2)}) collective-permute-start(bf16[1,384,512]{2,1,0:T(8,128)(2,1)S(1)} %dynamic-slice_convert_fusion.1), channel_id=1, source_target_pairs={{0,4},{4,0},{1,5},{5,1},{2,6},{6,2},{3,7},{7,3},{8,12},{12,8},{9,1... | collective-permute-start | bytes 1179656 | tf_op jit(solution)/shard_map/ppermute | solution.py:23

commit v5 on v0

v5 whole, which is shorter than its diff:
```python
import functools
import math

import jax
import jax.numpy as jnp
from jax import lax
from jax.experimental import pallas as pl
from jax.experimental.pallas import tpu as pltpu
from jax.sharding import Mesh
from jax.sharding import PartitionSpec as P

HEAD_DIM = 128
INVERSE_ROOT = 1.0 / math.sqrt(HEAD_DIM)
DP = ("zh", "zl", "x", "core")


def dot(a, b, contract):
    return lax.dot_general(a, b, (contract, ((), ())), preferred_element_type=jnp.float32)


def shift(array, axis, by):
    count = lax.axis_size(axis)
    return lax.ppermute(array, axis, [(i, (i + by) % count) for i in range(count)])


def others(axis):
    return range(1, lax.axis_size(axis))


def part_of(array, axis, by, dim):
    count = lax.axis_size(axis)
    size = array.shape[dim] // count
    at = (lax.axis_index(axis) + by) % count
    return lax.dynamic_slice_in_dim(array, at * size, size, dim)


def softmax(q, k):
    scores = dot(q, k, ((1,), (1,))) * INVERSE_ROOT
    raised = jnp.exp(scores - jnp.max(scores, axis=-1, keepdims=True))
    return raised * (1.0 / jnp.sum(raised, axis=-1, keepdims=True))


def all_tokens(own, far, at):
    return (jnp.concatenate([own[i, :, at], far[i, :, at]], axis=0) for i in range(3))


def forward_kernel(own, far, att_ref):
    for start in range(0, att_ref.shape[1], HEAD_DIM):
        at = slice(start, start + HEAD_DIM)
        q, k, v = all_tokens(own, far, at)
        low = softmax(q, k).astype(jnp.bfloat16)
        att_ref[:, at] = dot(low, v, ((1,), (0,))).astype(jnp.bfloat16)


def backward_kernel(first, own, far, *refs):
    *grad_refs, staying, leaving = refs
    tokens = own.shape[1]
    for start in range(0, staying.shape[2], HEAD_DIM):
        at = slice(start, start + HEAD_DIM)
        q, k, v = all_tokens(own, far, slice(first + start, first + start + HEAD_DIM))
        total = grad_refs[0][:, at].astype(jnp.float32)
        for ref in grad_refs[1:]:
            total = total + ref[:, at].astype(jnp.float32)
        g = total.astype(jnp.bfloat16)
        probs = softmax(q, k)
        low = probs.astype(jnp.bfloat16)
        att = dot(low, v, ((1,), (0,))).astype(jnp.bfloat16)
        delta = jnp.sum(
            g.astype(jnp.float32) * att.astype(jnp.float32), axis=-1, keepdims=True
        )
        d_probs = dot(g, v, ((1,), (1,)))
        d_low = (probs * (d_probs - delta)).astype(jnp.bfloat16)
        dq = (dot(d_low, k, ((1,), (0,))) * INVERSE_ROOT).astype(jnp.bfloat16)
        dk = (dot(d_low, q, ((0,), (0,))) * INVERSE_ROOT).astype(jnp.bfloat16)
        dv = dot(low, g, ((0,), (0,))).astype(jnp.bfloat16)
        for i, value in enumerate((dq, dk, dv)):
            staying[i, :, at] = value[:tokens]
            leaving[i, :, at] = value[tokens:]


def params(length):
    mebibytes = 32 if length <= 512 else 48
    return pltpu.CompilerParams(vmem_limit_bytes=mebibytes * 1024 * 1024)


def small():
    return pl.CostEstimate(flops=1024, bytes_accessed=1024, transcendentals=0)


def after(value, *events):
    return lax.optimization_barrier((value, events))[0]


def within(start, end):
    return lambda step, *_: (0, jnp.clip(step - start, 0, end - start - 1))


def whole_call(kernel, length, out_shape, operands, name, scalars=None, scratch_shapes=()):
    whole = pl.BlockSpec(memory_space=pltpu.VMEM)
    in_specs = [whole] * len(operands)
    if scalars is not None:
        operands = [scalars, *operands]
        in_specs = [pl.BlockSpec(memory_space=pltpu.SMEM)] + in_specs
    return pl.pallas_call(
        kernel,
        in_specs=in_specs,
        out_specs=jax.tree.map(lambda _: whole, out_shape),
        out_shape=out_shape,
        scratch_shapes=scratch_shapes,
        compiler_params=params(length),
        cost_estimate=small(),
        name=name,
    )(*operands)


def forward(own, far):
    _, tokens, features = own.shape
    length = tokens + far.shape[1]
    shape = jax.ShapeDtypeStruct((length, features), jnp.bfloat16)
    return whole_call(forward_kernel, length, shape, [own, far], "forward")


def backward(own, far, partial, terms, first):
    tokens, rest = own.shape[1], far.shape[1]
    wide = partial.shape[1]
    return whole_call(
        functools.partial(backward_kernel, first),
        tokens + rest,
        [jax.ShapeDtypeStruct((3, count, wide), jnp.bfloat16) for count in (tokens, rest)],
        [own, far, partial, *terms],
        "backward",
    )


def partial_kernel(pieces, at_ref, own, far, *refs):
    weights, outs, every = refs[:pieces], refs[pieces:-1], refs[-1]
    tokens = own.shape[0]
    rows = weights[0].shape[0]
    wide = outs[0].shape[1]
    block = 256 if wide % 256 == 0 else 128
    for i in range(pieces):
        columns = slice(i * rows, (i + 1) * rows)
        every[i, :tokens] = own[:, columns]
        every[i, tokens:] = far[:, columns]
    for group, out_ref in enumerate(outs):
        for start in range(0, wide, block):
            columns = slice(group * wide + start, group * wide + start + block)
            total = None
            for i, weight in enumerate(weights):
                term = dot(every[at_ref[i]], weight[:, columns], ((1,), (0,)))
                total = term if total is None else total + term
            out_ref[:, start : start + block] = total.astype(out_ref.dtype)


def partial_product(at, own, far, weights, groups, dtype):
    length = own.shape[0] + far.shape[0]
    rows, features = weights[0].shape
    return whole_call(
        functools.partial(partial_kernel, len(weights)),
        length,
        [jax.ShapeDtypeStruct((length, features // groups), dtype)] * groups,
        [own, far, *weights],
        "partial",
        at,
        [pltpu.VMEM((len(weights), length, rows), jnp.bfloat16)],
    )


def turn_kernel(clips, core_ref, *refs):
    grads, outs = refs[: 2 * clips], refs[2 * clips :]
    cores = len(outs)
    blocks, rows, _ = outs[0].shape
    for core in range(cores):

        @pl.when(core_ref[0] == core)
        def _():
            for by, out_ref in enumerate(outs):
                for i in range(blocks):
                    at = (i * cores + (core + by) % cores) * rows
                    start = 0
                    for grad in grads:
                        tokens = grad.shape[0]
                        out_ref[i, :, start : start + tokens] = grad[:, at : at + rows].T
                        start += tokens


def turned(core, owns, fars, rows, cores):
    grads = [grad for pair in zip(owns, fars) for grad in pair]
    depth = sum(grad.shape[0] for grad in grads)
    blocks = owns[0].shape[1] // (rows * cores)
    return whole_call(
        functools.partial(turn_kernel, len(owns)),
        depth,
        [jax.ShapeDtypeStruct((blocks, rows, depth), jnp.bfloat16)] * cores,
        grads,
        "turn",
        core,
    )


def rows_kernel(jobs, cores, at_ref, *refs):
    grads, attends, outs = refs[:cores], refs[cores : 2 * cores], refs[2 * cores :]
    clips, length, _ = attends[0].shape
    first = 0
    for (count, start, wide), out_ref in zip(jobs, outs):
        block = 256 if wide % 256 == 0 else 128
        for i in range(count):
            at = at_ref[first + i]
            for column in range(0, wide, block):
                columns = slice(start + column, start + column + block)
                total = None
                for grad, attended in zip(grads, attends):
                    chosen = attended[:, :, columns].reshape(clips * length, block)
                    term = dot(grad[at], chosen, ((1,), (0,)))
                    total = term if total is None else total + term
                out_ref[i, :, column : column + block] = total.astype(out_ref.dtype)
        first += count


def rows_products(jobs, grads, attends, dtype):
    rows = grads[0].shape[1]
    sizes = [(at.shape[0], start, wide) for at, start, wide in jobs]
    return whole_call(
        functools.partial(rows_kernel, sizes, len(grads)),
        grads[0].shape[2],
        [jax.ShapeDtypeStruct((count, rows, wide), dtype) for count, _, wide in sizes],
        [*grads, *attends],
        "rows",
        jnp.concatenate([at for at, _, _ in jobs]),
    )


def place(axis, by=0):
    return (lax.axis_index(axis) + by) % lax.axis_size(axis)


def block_at(zl, x, core):
    return ((zl * lax.axis_size("x") + x) * lax.axis_size("core") + core).astype(jnp.int32)


def shift_both(array, zl, x):
    zls, xs = lax.axis_size("zl"), lax.axis_size("x")
    pairs = [
        (i * xs + j, ((i + zl) % zls) * xs + (j + x) % xs) for i in range(zls) for j in range(xs)
    ]
    return lax.ppermute(array, ("zl", "x"), pairs)


def blocks_along(axis, by):
    zl, x = jnp.arange(lax.axis_size("zl")), jnp.arange(lax.axis_size("x"))
    if axis == "x":
        x = place("x", by)
    else:
        zl = place("zl", by)
    return (zl * lax.axis_size("x") + x).astype(jnp.int32)


def shards(grad_out, queries, keys, values, out_weight):
    seq = lax.axis_size("seq")
    mine = lax.axis_index("seq")
    tokens = grad_out.shape[1]
    rows, features = out_weight.shape
    length = tokens * seq
    heads = features // HEAD_DIM
    clips = math.prod(lax.axis_size(axis) for axis in DP)
    token_scale = 1.0 / math.sqrt(clips * length)

    def across(array):
        return [shift(array, "core", by) for by in others("core")]

    groups = 2 if heads % 4 == 0 else 1
    wide = features // groups
    larger = 2 * heads // 3
    widths = [count * HEAD_DIM for count in (larger, heads - larger) if count]
    orders = [("x", "zl"), ("zl", "x")][: len(widths)]

    def heads_of(by):
        return jnp.stack([part_of(part[0], "seq", by, 1) for part in (queries, keys, values)])

    pieces = [shift(heads_of(by), "seq", by) for by in others("seq")]
    far = pieces[0] if seq == 2 else jnp.concatenate(pieces, axis=1)
    own_grad = grad_out[0]
    halves = [shift(part_of(own_grad, "zh", by, 1), "zh", by) for by in others("zh")]
    near_x = [shift(out_weight, "x", by) for by in others("x")]
    near_zl = [shift(out_weight, "zl", by) for by in others("zl")]
    own_across = across(out_weight)

    own = heads_of(0)
    attended = forward(own, after(far, own_across))

    def along_seq(array):
        arrived = [shift(array, "seq", by) for by in others("seq")]
        return arrived[0] if seq == 2 else jnp.concatenate(arrived, axis=0)

    halves = after(halves, attended)
    attends = [shift(attended, "zh", by) for by in others("zh")]
    owns = [after(part_of(own_grad, "zh", 0, 1), halves)] + halves
    fars = [along_seq(half) for half in owns]
    near_zl = after(near_zl, halves)
    places = [(zl, x) for zl in others("zl") for x in others("x")]
    diagonal = [shift(block, "x", by) for block in near_zl for by in others("x")]

    near_x, near_zl, diagonal, attends, owns, fars = lax.optimization_barrier(
        (near_x, near_zl, diagonal, attends, owns, fars)
    )
    x_across = [across(block) for block in near_x]
    zl_across = [across(block) for block in near_zl]
    diagonal_across = [across(block) for block in diagonal]
    pair = jnp.stack([attended] + attends)
    attends = [pair] + across(pair)

    weights = [((0, 0), out_weight, own_across)]
    weights += [((0, by), *both_of) for by, *both_of in zip(others("x"), near_x, x_across)]
    weights += [((by, 0), *both_of) for by, *both_of in zip(others("zl"), near_zl, zl_across)]
    weights += zip(places, diagonal, diagonal_across)
    at, blocks = [], []
    for (zl, x), block, from_cores in weights:
        for core, array in enumerate([block] + from_cores):
            at.append(block_at(place("zl", -zl), place("x", -x), place("core", -core)))
            blocks.append(array)

    cores = lax.axis_size("core")
    core = place("core").astype(jnp.int32).reshape(1)
    by_rows = list(turned(core, owns, fars, rows, cores))
    by_rows = by_rows[:1] + [
        shift(array, "core", by) for by, array in zip(others("core"), by_rows[1:])
    ]

    starts = [sum(widths[:split]) for split in range(len(widths))]
    jobs = [
        (blocks_along(axis, by), start, size)
        for (axis, _), start, size in zip(orders, starts, widths)
        for by in others(axis)
    ]
    leave = rows_products(jobs, by_rows, attends, jnp.bfloat16)
    rest = iter(leave)
    arrive = [[shift(next(rest), axis, by) for by in others(axis)] for axis, _ in orders]

    owns, fars = after((owns, fars), leave)
    at = jnp.stack(at)
    sent = [
        partial_product(at, own_part, far_part, blocks, groups, jnp.bfloat16)
        for own_part, far_part in zip(owns[1:], fars[1:])
    ]
    terms = [
        [shift(clip[group], "zh", -by) for by, clip in zip(others("zh"), sent)]
        for group in range(groups)
    ]
    owns, fars = after((owns, fars), sent)
    partial = partial_product(at, owns[0], fars[0], blocks, groups, jnp.float32)
    jobs = [
        (blocks_along(axis, 0), start, size)
        for (axis, _), start, size in zip(orders, starts, widths)
    ]
    kept = rows_products(jobs, after(by_rows, partial), attends, jnp.float32)

    stays, arrivals = [], []
    for group in range(groups):
        start = group * wide
        staying, leaving = backward(own, far, partial[group], after(terms[group], kept), start)
        stays.append((mine * features + start, staying))
        for by in others("seq"):
            sent = leaving[:, (by - 1) * tokens : by * tokens]
            column = ((mine + by) % seq) * features + start
            arrivals.append((column, shift(sent, "seq", -by)))

    columns = []
    for (_, axis), arrived, total in zip(orders, after(arrive, [array for _, array in stays]), kept):
        for term in arrived:
            total = total + term.astype(jnp.float32)
        second = [
            shift(part_of(total, axis, by, 0).astype(jnp.bfloat16), axis, by)
            for by in others(axis)
        ]
        final = part_of(total, axis, 0, 0)
        for term in second:
            final = final + term.astype(jnp.float32)
        columns.append(final[0])
    weight_grad = jnp.concatenate(columns, axis=1) * token_scale

    result = jnp.zeros((3, tokens, queries.shape[2]), jnp.bfloat16)
    result = [result[0], result[1], result[2]]
    for column, arrays in stays + arrivals:
        result = [
            lax.dynamic_update_slice_in_dim(whole, array, column, 1)
            for whole, array in zip(result, arrays)
        ]
    return (result[0][None], result[1][None], result[2][None], weight_grad)


def solution(mesh):
    dp, seq = mesh.devices.shape
    finer = Mesh(mesh.devices.reshape(2, dp // 8, 2, 2, seq), DP + ("seq",))
    tokens = P(DP, "seq", None)
    return jax.shard_map(
        shards,
        mesh=finer,
        in_specs=(tokens, tokens, tokens, tokens, P(DP, "seq")),
        out_specs=(tokens, tokens, tokens, P(DP, "seq")),
        check_vma=False,
    )
```

time: 286 us -> 189 us (0.66)
  blocking collectives: 65.8 us -> 0 us
  waiting for transfers between devices: 154 us -> 101 us
  Pallas kernels: 12 us -> 42.3 us
  matrix products: 20.6 us -> 0 us
  starting transfers between devices: 5.22 us -> 24 us
  between operations: 14.1 us -> 1.01 us
  other arithmetic: 1.72 us -> 7.25 us
    all_to_all x1 -> x0, blocking collectives: 65.8 us -> none  [shards(): lax.all_to_all(by_rows, 'dp', split_axis=0, concat_axis=0, tiled=True)]
    all_gather x2 -> x0, waiting for transfers between devices: 38 us -> none  [the longest x1 38 us: shards(): whole_rows = lax.all_gather(out_weight, 'dp', axis=0, tiled=True)]
    pallas_call x1 -> x8, Pallas kernels: 12 us -> 42.3 us  [whole_call(): pl.pallas_call(kernel, in_specs=in_specs, out_specs=jax.tree.map(lambda _...]
    dot_general x2 -> x0, matrix products: 20.6 us -> none  [the longest x1 10.6 us: shards(): jnp.dot(all_grad, whole_rows, preferred_element_type=jnp.float32)]
    ppermute x4 -> x22, starting transfers between devices: 5.14 us -> 24 us  [shift(): lax.ppermute(array, axis, [(i, (i + by) % count) for i in range(count)])]
    ppermute x4 -> x22, waiting for transfers between devices: 116 us -> 101 us  [shift(): lax.ppermute(array, axis, [(i, (i + by) % count) for i in range(count)])]
    unnamed x9 -> x38, local copies, waits for them, and re-layouts: 4.19 us -> 7.89 us
    concatenate x1 -> x0, local copies, waits for them, and re-layouts: 2.87 us -> none  [shards(): jnp.concatenate([by_rows] + [shift(by_rows, by) for by in range(1, seq)],...]
  transfers between devices with their start and end apart: 6 -> 22, of which waited for: 5 -> 12; matrix products, arithmetic and copies ran while one was open for 4% -> 3% of each run, Pallas kernels for 0% -> 22%
where the time goes in v5:
time: 189 us; the launch traced here: 188 us
  waiting for transfers between devices  101 us (53%)
  Pallas kernels  42.3 us (22%)
  starting transfers between devices  24 us (13%)
  local copies, waits for them, and re-layouts  12.4 us (7%)
  other arithmetic  7.25 us (4%)
    ppermute x22, waiting for transfers between devices, shift(): lax.ppermute(array, axis, [(i, (i + by) % count) for i in range(count)])  101 us
    pallas_call x8, Pallas kernels, whole_call(): pl.pallas_call(kernel, in_specs=in_specs, out_specs=jax.tree.map(lambda _...  42.3 us
    ppermute x22, starting transfers between devices, shift(): lax.ppermute(array, axis, [(i, (i + by) % count) for i in range(count)])  24 us
    unnamed x38, local copies, waits for them, and re-layouts  7.89 us
    dynamic_slice x3, local copies, waits for them, and re-layouts, part_of(): return lax.dynamic_slice_in_dim(array, at * size, size, dim)  3.8 us
  transfers between devices with their start and end apart: 22, of which 12 were waited for; matrix products, arithmetic and copies ran while one was open for 3% of the time, Pallas kernels for 22%

profile of v5, /device:TPU:0, one launch (start us, length us, event | category | flops | bytes accessed | tf_op | source)
XLA Modules:
  0.0 188.1 jit_solution(16045537920647266956)
XLA Ops:
  0.7 1.3 constant_dynamic-slice_fusion.2
  2.0 0.2 copy-done.17
  2.2 1.0 constant_dynamic-slice_fusion
  3.2 1.1 pad_maximum_fusion.2
  4.4 3.0 %collective-permute-start = (bf16[3,128,1536]{2,1,0:T(8,128)(2,1)}, bf16[3,128,1536]{2,1,0:T(8,128)(2,1)S(1)}, u32[]{:S(2)}, u32[]{:S(2)}) collective-permute-start(bf16[3,128,1536]{2,1,0:T(8,128)(2,1)} %pad_maximum_fusion.2), channel_id=1, source_target_pairs={{0,1},{1,0},{2,3},{3,2},{4,5},{5,4},{6,7},{7,6},{8,9},{9,8},{10,11... | collective-permute-start | bytes 3538952 | tf_op jit(solution)/shard_map/ppermute | solution.py:23
  7.3 1.6 collective-permute-start.2
  8.9 1.5 dynamic-slice_bitcast_fusion
  10.5 2.7 %collective-permute-start.3 = (bf16[128,3072]{1,0:T(8,128)(2,1)S(1)}, bf16[128,3072]{1,0:T(8,128)(2,1)}, u32[]{:S(2)}, u32[]{:S(2)}) collective-permute-start(bf16[128,3072]{1,0:T(8,128)(2,1)S(1)} %get-tuple-element.81), channel_id=1, source_target_pairs={{0,16},{16,0},{1,17},{17,1},{2,18},{18,2},{3,19},{19,3},{4,20},{20... | collective-permute-start | bytes 2359304 | tf_op jit(solution)/shard_map/ppermute | solution.py:23
  13.1 1.5 collective-permute-start.1
  14.6 0.1 pad_maximum_fusion.1.own
  14.7 18.8 %collective-permute-done.far = bf16[3,128,1536]{2,1,0:T(8,128)(2,1)S(1)} collective-permute-done((bf16[3,128,1536]{2,1,0:T(8,128)(2,1)}, bf16[3,128,1536]{2,1,0:T(8,128)(2,1)S(1)}, u32[]{:S(2)}, u32[]{:S(2)}) %collective-permute-start) | collective-permute-done | bytes 1179680 | tf_op jit(solution)/shard_map/ppermute | solution.py:23
  33.5 2.9 %forward.1 = bf16[256,1536]{1,0:T(8,128)(2,1)} custom-call(bf16[3,128,1536]{2,1,0:T(8,128)(2,1)S(1)} %pad_maximum_fusion.1.own, bf16[3,128,1536]{2,1,0:T(8,128)(2,1)S(1)} %collective-permute-done.far), custom_call_target="tpu_custom_call" | custom-call | flops 1024 | bytes 1024 | tf_op jit(solution)/shard_map/forward/pallas_call | solution.py:104
  36.4 15.4 %collective-permute-done.3.refs_2_.own = bf16[128,3072]{1,0:T(8,128)(2,1)} collective-permute-done((bf16[128,3072]{1,0:T(8,128)(2,1)S(1)}, bf16[128,3072]{1,0:T(8,128)(2,1)}, u32[]{:S(2)}, u32[]{:S(2)}) %collective-permute-start.3) | collective-permute-done | bytes 786464 | tf_op jit(solution)/shard_map/ppermute | solution.py:23
  51.9 1.0 collective-permute-done.2.refs_4_
  52.9 1.5 collective-permute-start.5
  54.4 0.5 collective-permute-start.7
  54.9 1.5 collective-permute-start.8
  56.4 2.5 %collective-permute-start.6 = (bf16[256,1536]{1,0:T(8,128)(2,1)}, bf16[256,1536]{1,0:T(8,128)(2,1)}, u32[]{:S(2)}, u32[]{:S(2)}) collective-permute-start(bf16[256,1536]{1,0:T(8,128)(2,1)} %forward.1), channel_id=1, source_target_pairs={{0,16},{16,0},{1,17},{17,1},{2,18},{18,2},{3,19},{19,3},{4,20},{20... | collective-permute-start | bytes 2359304 | tf_op jit(solution)/shard_map/ppermute | solution.py:23
  58.9 16.0 %collective-permute-done.7.refs_1_.far = bf16[128,3072]{1,0:T(8,128)(2,1)S(1)} collective-permute-done((bf16[128,3072]{1,0:T(8,128)(2,1)S(1)}, bf16[128,3072]{1,0:T(8,128)(2,1)S(1)}, u32[]{:S(2)}, u32[]{:S(2)}) %collective-permute-start.7) | collective-permute-done | bytes 786464 | tf_op jit(solution)/shard_map/ppermute | solution.py:23
  74.9 0.9 copy-done.5
  75.7 14.4 %collective-permute-done.8.refs_3_.far = bf16[128,3072]{1,0:T(8,128)(2,1)S(1)} collective-permute-done((bf16[128,3072]{1,0:T(8,128)(2,1)}, bf16[128,3072]{1,0:T(8,128)(2,1)S(1)}, u32[]{:S(2)}, u32[]{:S(2)}) %collective-permute-start.8) | collective-permute-done | bytes 786464 | tf_op jit(solution)/shard_map/ppermute | solution.py:23
  90.1 0.9 copy-done.8
  91.0 1.8 collective-permute-done.6
  92.8 1.6 pad_maximum_fusion.refs_2_
  94.4 0.1 collective-permute-start.10
  94.5 0.1 copy-done.9
  94.6 3.3 %turn.1 = (bf16[4,384,512]{2,1,0:T(8,128)(2,1)S(1)}, bf16[4,384,512]{2,1,0:T(8,128)(2,1)}) custom-call(s32[1]{0:T(128)} %bitcast.10.core_ref, bf16[128,3072]{1,0:T(8,128)(2,1)S(1)} %get-tuple-element.64.refs_0_.own, bf16[128,3072]{1,0:T(8,128)(2,1)S(1)} %copy-done.6, bf16[128,3072]{1,0:T(8,128)(2,1)} %collective-permute-done.3.refs_2_.own, ...), custom_call_target="tpu_custom_call" | custom-call | flops 1024 | bytes 1024 | tf_op jit(solution)/shard_map/turn/pallas_call | solution.py:104
  98.0 1.2 copy-done.2
  99.1 0.4 collective-permute-start.9
  99.5 0.1 collective-permute-start.11
  99.6 0.4 collective-permute-start.12
  100.0 0.1 collective-permute-start.13
  100.2 0.1 pad_add_fusion.at_ref
  100.2 2.6 %collective-permute-done.9.refs_1_ = bf16[4,384,512]{2,1,0:T(8,128)(2,1)} collective-permute-done((bf16[4,384,512]{2,1,0:T(8,128)(2,1)}, bf16[4,384,512]{2,1,0:T(8,128)(2,1)}, u32[]{:S(2)}, u32[]{:S(2)}) %collective-permute-start.9) | collective-permute-done | bytes 1572896 | tf_op jit(solution)/shard_map/ppermute | solution.py:23
  102.9 1.4 copy-done.3
  104.3 4.8 %rows.2 = (bf16[2,384,1024]{2,1,0:T(8,128)(2,1)}, bf16[2,384,512]{2,1,0:T(8,128)(2,1)S(1)}) custom-call(s32[4]{0:T(128)S(1)} %pad_add_fusion.at_ref, bf16[4,384,512]{2,1,0:T(8,128)(2,1)S(1)} %copy-done.3, bf16[4,384,512]{2,1,0:T(8,128)(2,1)} %collective-permute-done.9.refs_1_, bf16[2,256,1536]{2,1,0:T(8,128)(2,1)S(1)} %pad_maximum_fusion.refs_2_, ...), custom_call_target="tpu_custom_call" | custom-call | flops 1024 | bytes 1024 | tf_op jit(solution)/shard_map/rows/pallas_call | solution.py:104
  109.1 0.9 copy-done.11
  110.0 0.5 collective-permute-start.18
  110.6 0.1 stack.58.at_ref
  110.7 1.1 copy-done.10
  111.8 8.2 %partial.2 = (bf16[256,768]{1,0:T(8,128)(2,1)}, bf16[256,768]{1,0:T(8,128)(2,1)}) custom-call(s32[8]{0:T(128)S(1)} %stack.58.at_ref, bf16[128,3072]{1,0:T(8,128)(2,1)} %collective-permute-done.3.refs_2_.own, bf16[128,3072]{1,0:T(8,128)(2,1)S(1)} %copy-done.10, bf16[384,1536]{1,0:T(8,128)(2,1)} %refs_0_.3, bf16[384,1536]{1,0:T(8,128)(2,1)} %collective-permute-done.4.refs_1_, ...), custom_call_target="tpu_custom_call" | custom-call | flops 1024 | bytes 1024 | tf_op jit(solution)/shard_map/partial/pallas_call | solution.py:104
  120.0 0.7 collective-permute-start.14
  120.7 2.2 %collective-permute-start.15 = (bf16[256,768]{1,0:T(8,128)(2,1)}, bf16[256,768]{1,0:T(8,128)(2,1)}, u32[]{:S(2)}, u32[]{:S(2)}) collective-permute-start(bf16[256,768]{1,0:T(8,128)(2,1)} %get-tuple-element.63), channel_id=1, source_target_pairs={{0,16},{16,0},{1,17},{17,1},{2,18},{18,2},{3,19},{19,3},{4,20},{20... | collective-permute-start | bytes 1179656 | tf_op jit(solution)/shard_map/ppermute | solution.py:23
  123.0 0.1 pad_add_fusion.1.at_ref
  123.0 1.1 collective-permute-start.19
  124.1 1.1 copy-done.7
  125.2 7.3 %partial.3 = (f32[256,768]{1,0:T(8,128)S(1)}, f32[256,768]{1,0:T(8,128)S(1)}) custom-call(s32[8]{0:T(128)S(1)} %stack.58.at_ref, bf16[128,3072]{1,0:T(8,128)(2,1)S(1)} %get-tuple-element.64.refs_0_.own, bf16[128,3072]{1,0:T(8,128)(2,1)S(1)} %copy-done.7, bf16[384,1536]{1,0:T(8,128)(2,1)} %refs_0_.3, bf16[384,1536]{1,0:T(8,128)(2,1)} %collective-permute-done.4.refs_1_, ...), custom_call_target="tpu_custom_call" | custom-call | flops 1024 | bytes 1024 | tf_op jit(solution)/shard_map/partial/pallas_call | solution.py:104
  132.5 4.6 %rows.3 = (f32[2,384,1024]{2,1,0:T(8,128)S(1)}, f32[2,384,512]{2,1,0:T(8,128)S(1)}) custom-call(s32[4]{0:T(128)S(1)} %pad_add_fusion.1.at_ref, bf16[4,384,512]{2,1,0:T(8,128)(2,1)S(1)} %copy-done.4, bf16[4,384,512]{2,1,0:T(8,128)(2,1)} %collective-permute-done.9.refs_1_, bf16[2,256,1536]{2,1,0:T(8,128)(2,1)S(1)} %pad_maximum_fusion.refs_2_, ...), custom_call_target="tpu_custom_call" | custom-call | flops 1024 | bytes 1024 | tf_op jit(solution)/shard_map/rows/pallas_call | solution.py:104
  137.1 13.0 %collective-permute-done.14.refs_1_ = bf16[256,768]{1,0:T(8,128)(2,1)} collective-permute-done((bf16[256,768]{1,0:T(8,128)(2,1)}, bf16[256,768]{1,0:T(8,128)(2,1)}, u32[]{:S(2)}, u32[]{:S(2)}) %collective-permute-start.14) | collective-permute-done | bytes 393248 | tf_op jit(solution)/shard_map/ppermute | solution.py:23
  150.1 5.5 %backward.2 = (bf16[3,128,768]{2,1,0:T(8,128)(2,1)S(1)}, bf16[3,128,768]{2,1,0:T(8,128)(2,1)S(1)}) custom-call(bf16[3,128,1536]{2,1,0:T(8,128)(2,1)S(1)} %pad_maximum_fusion.1.own, bf16[3,128,1536]{2,1,0:T(8,128)(2,1)S(1)} %copy-done.1, f32[256,768]{1,0:T(8,128)S(1)} %get-tuple-element.66.refs_0_, bf16[256,768]{1,0:T(8,128)(2,1)} %collective-permute-done.14.refs_1_), custom_call_target="tpu_custom_call" | custom-call | flops 1024 | bytes 1024 | tf_op jit(solution)/shard_map/backward/pallas_call | solution.py:104
  155.6 2.1 %collective-permute-done.15.refs_1_ = bf16[256,768]{1,0:T(8,128)(2,1)} collective-permute-done((bf16[256,768]{1,0:T(8,128)(2,1)}, bf16[256,768]{1,0:T(8,128)(2,1)}, u32[]{:S(2)}, u32[]{:S(2)}) %collective-permute-start.15) | collective-permute-done | bytes 393248 | tf_op jit(solution)/shard_map/ppermute | solution.py:23
  157.7 0.5 collective-permute-start.16
  158.3 5.7 %backward.3 = (bf16[3,128,768]{2,1,0:T(8,128)(2,1)S(1)}, bf16[3,128,768]{2,1,0:T(8,128)(2,1)S(1)}) custom-call(bf16[3,128,1536]{2,1,0:T(8,128)(2,1)S(1)} %pad_maximum_fusion.1.own, bf16[3,128,1536]{2,1,0:T(8,128)(2,1)S(1)} %copy-done.1, f32[256,768]{1,0:T(8,128)S(1)} %get-tuple-element.67.refs_0_, bf16[256,768]{1,0:T(8,128)(2,1)} %collective-permute-done.15.refs_1_), custom_call_target="tpu_custom_call" | custom-call | flops 1024 | bytes 1024 | tf_op jit(solution)/shard_map/backward/pallas_call | solution.py:104
  164.0 1.6 collective-permute-start.17
  165.9 1.9 %convert_add_fusion = f32[2,384,1024]{2,1,0:T(8,128)S(1)} fusion(f32[2,384,1024]{2,1,0:T(8,128)S(1)} %get-tuple-element.70, bf16[2,384,1024]{2,1,0:T(8,128)(2,1)} %collective-permute-done.18), kind=kLoop, calls=%fused_computation | loop fusion | flops 1572864 | bytes 7864320 | tf_op jit(solution)/shard_map/add | solution.py:370
  167.9 0.1 dynamic-slice_convert_fusion
  168.1 0.3 convert_add_fusion.1
  168.4 1.6 collective-permute-start.21
  170.0 4.0 %collective-permute-done.16 = bf16[3,128,768]{2,1,0:T(8,128)(2,1)S(1)} collective-permute-done((bf16[3,128,768]{2,1,0:T(8,128)(2,1)S(1)}, bf16[3,128,768]{2,1,0:T(8,128)(2,1)S(1)}, u32[]{:S(2)}, u32[]{:S(2)}) %collective-permute-start.16) | collective-permute-done | bytes 589856 | tf_op jit(solution)/shard_map/ppermute | solution.py:23
  174.1 10.8 %collective-permute-done.17 = bf16[3,128,768]{2,1,0:T(8,128)(2,1)S(1)} collective-permute-done((bf16[3,128,768]{2,1,0:T(8,128)(2,1)S(1)}, bf16[3,128,768]{2,1,0:T(8,128)(2,1)S(1)}, u32[]{:S(2)}, u32[]{:S(2)}) %collective-permute-start.17) | collective-permute-done | bytes 589856 | tf_op jit(solution)/shard_map/ppermute | solution.py:23
  184.9 0.1 add_bitcast_fusion.1
  185.1 1.1 collective-permute-done.20
  186.2 0.3 add_bitcast_fusion
  186.5 1.6 maximum_multiply_fusion
  (53 shorter events, 0.7 us)
Async XLA Ops:
  0.6 1.4 copy-start.18
  0.6 1.6 copy-start.17
  4.4 29.1 %collective-permute-start = (bf16[3,128,1536]{2,1,0:T(8,128)(2,1)}, bf16[3,128,1536]{2,1,0:T(8,128)(2,1)S(1)}, u32[]{:S(2)}, u32[]{:S(2)}) collective-permute-start(bf16[3,128,1536]{2,1,0:T(8,128)(2,1)} %pad_maximum_fusion.2), channel_id=1, source_target_pairs={{0,1},{1,0},{2,3},{3,2},{4,5},{5,4},{6,7},{7,6},{8,9},{9,8},{10,11... | collective-permute-start | bytes 3538952 | tf_op jit(solution)/shard_map/ppermute | solution.py:23
  7.3 26.2 %collective-permute-start.4 = (bf16[384,1536]{1,0:T(8,128)(2,1)}, bf16[384,1536]{1,0:T(8,128)(2,1)}, u32[]{:S(2)}, u32[]{:S(2)}) collective-permute-start(bf16[384,1536]{1,0:T(8,128)(2,1)} %refs_0_.3), channel_id=1, source_target_pairs={{0,2},{2,0},{1,3},{3,1},{4,6},{6,4},{5,7},{7,5},{8,10},{10,8},{9,1... | collective-permute-start | bytes 3538952 | tf_op jit(solution)/shard_map/ppermute | solution.py:23
  7.3 45.5 %collective-permute-start.2 = (bf16[384,1536]{1,0:T(8,128)(2,1)}, bf16[384,1536]{1,0:T(8,128)(2,1)}, u32[]{:S(2)}, u32[]{:S(2)}) collective-permute-start(bf16[384,1536]{1,0:T(8,128)(2,1)} %refs_0_.3), channel_id=1, source_target_pairs={{0,8},{8,0},{1,9},{9,1},{2,10},{10,2},{3,11},{11,3},{4,12},{12,4},... | collective-permute-start | bytes 3538952 | tf_op jit(solution)/shard_map/ppermute | solution.py:23
  8.9 5.7 %copy-start.12 = (bf16[1,128,1536]{2,1,0:T(8,128)(2,1)S(1)}, bf16[1,128,1536]{2,1,0:T(8,128)(2,1)}, u32[]{:S(2)}) copy-start(bf16[1,128,1536]{2,1,0:T(8,128)(2,1)} %get-tuple-element.87) | copy-start | bytes 1179652
  8.9 5.7 %copy-start.13 = (bf16[1,128,1536]{2,1,0:T(8,128)(2,1)S(1)}, bf16[1,128,1536]{2,1,0:T(8,128)(2,1)}, u32[]{:S(2)}) copy-start(bf16[1,128,1536]{2,1,0:T(8,128)(2,1)} %get-tuple-element.97) | copy-start | bytes 1179652
  10.5 41.4 %collective-permute-start.3 = (bf16[128,3072]{1,0:T(8,128)(2,1)S(1)}, bf16[128,3072]{1,0:T(8,128)(2,1)}, u32[]{:S(2)}, u32[]{:S(2)}) collective-permute-start(bf16[128,3072]{1,0:T(8,128)(2,1)S(1)} %get-tuple-element.81), channel_id=1, source_target_pairs={{0,16},{16,0},{1,17},{17,1},{2,18},{18,2},{3,19},{19,3},{4,20},{20... | collective-permute-start | bytes 2359304 | tf_op jit(solution)/shard_map/ppermute | solution.py:23
  13.1 45.8 %collective-permute-start.1 = (bf16[384,1536]{1,0:T(8,128)(2,1)}, bf16[384,1536]{1,0:T(8,128)(2,1)}, u32[]{:S(2)}, u32[]{:S(2)}) collective-permute-start(bf16[384,1536]{1,0:T(8,128)(2,1)} %refs_0_.3), channel_id=1, source_target_pairs={{0,4},{4,0},{1,5},{5,1},{2,6},{6,2},{3,7},{7,3},{8,12},{12,8},{9,1... | collective-permute-start | bytes 3538952 | tf_op jit(solution)/shard_map/ppermute | solution.py:23
  33.5 2.9 %copy-start = (bf16[3,128,1536]{2,1,0:T(8,128)(2,1)}, bf16[3,128,1536]{2,1,0:T(8,128)(2,1)S(1)}, u32[]{:S(2)}) copy-start(bf16[3,128,1536]{2,1,0:T(8,128)(2,1)S(1)} %collective-permute-done.far) | copy-start | bytes 3538948
  52.9 39.9 %collective-permute-start.5 = (bf16[384,1536]{1,0:T(8,128)(2,1)}, bf16[384,1536]{1,0:T(8,128)(2,1)}, u32[]{:S(2)}, u32[]{:S(2)}) collective-permute-start(bf16[384,1536]{1,0:T(8,128)(2,1)} %collective-permute-done.2.refs_4_), channel_id=1, source_target_pairs={{0,4},{4,0},{1,5},{5,1},{2,6},{6,2},{3,7},{7,3},{8,12},{12,8},{9,1... | collective-permute-start | bytes 3538952 | tf_op jit(solution)/shard_map/ppermute | solution.py:23
  54.4 20.5 %collective-permute-start.7 = (bf16[128,3072]{1,0:T(8,128)(2,1)S(1)}, bf16[128,3072]{1,0:T(8,128)(2,1)S(1)}, u32[]{:S(2)}, u32[]{:S(2)}) collective-permute-start(bf16[128,3072]{1,0:T(8,128)(2,1)S(1)} %get-tuple-element.64.refs_0_.own), channel_id=1, source_target_pairs={{0,1},{1,0},{2,3},{3,2},{4,5},{5,4},{6,7},{7,6},{8,9},{9,8},{10,11... | collective-permute-start | bytes 2359304 | tf_op jit(solution)/shard_map/ppermute | solution.py:23
  54.9 35.2 %collective-permute-start.8 = (bf16[128,3072]{1,0:T(8,128)(2,1)}, bf16[128,3072]{1,0:T(8,128)(2,1)S(1)}, u32[]{:S(2)}, u32[]{:S(2)}) collective-permute-start(bf16[128,3072]{1,0:T(8,128)(2,1)} %collective-permute-done.3.refs_2_.own), channel_id=1, source_target_pairs={{0,1},{1,0},{2,3},{3,2},{4,5},{5,4},{6,7},{7,6},{8,9},{9,8},{10,11... | collective-permute-start | bytes 2359304 | tf_op jit(solution)/shard_map/ppermute | solution.py:23
  56.4 36.4 %collective-permute-start.6 = (bf16[256,1536]{1,0:T(8,128)(2,1)}, bf16[256,1536]{1,0:T(8,128)(2,1)}, u32[]{:S(2)}, u32[]{:S(2)}) collective-permute-start(bf16[256,1536]{1,0:T(8,128)(2,1)} %forward.1), channel_id=1, source_target_pairs={{0,16},{16,0},{1,17},{17,1},{2,18},{18,2},{3,19},{19,3},{4,20},{20... | collective-permute-start | bytes 2359304 | tf_op jit(solution)/shard_map/ppermute | solution.py:23
  74.9 0.9 copy-start.5
  90.1 0.9 copy-start.8
  92.8 1.7 copy-start.6
  92.8 1.8 copy-start.9
  94.4 5.8 %collective-permute-start.10 = (bf16[2,256,1536]{2,1,0:T(8,128)(2,1)S(1)}, bf16[2,256,1536]{2,1,0:T(8,128)(2,1)}, u32[]{:S(2)}, u32[]{:S(2)}) collective-permute-start(bf16[2,256,1536]{2,1,0:T(8,128)(2,1)S(1)} %pad_maximum_fusion.refs_2_), channel_id=1, source_target_pairs={{0,2},{2,0},{1,3},{3,1},{4,6},{6,4},{5,7},{7,5},{8,10},{10,8},{9,1... | collective-permute-start | bytes 4718600 | tf_op jit(solution)/shard_map/ppermute | solution.py:23
  98.0 1.2 copy-start.2
  99.1 3.8 %collective-permute-start.9 = (bf16[4,384,512]{2,1,0:T(8,128)(2,1)}, bf16[4,384,512]{2,1,0:T(8,128)(2,1)}, u32[]{:S(2)}, u32[]{:S(2)}) collective-permute-start(bf16[4,384,512]{2,1,0:T(8,128)(2,1)} %get-tuple-element.51), channel_id=1, source_target_pairs={{0,2},{2,0},{1,3},{3,1},{4,6},{6,4},{5,7},{7,5},{8,10},{10,8},{9,1... | collective-permute-start | bytes 4718600 | tf_op jit(solution)/shard_map/ppermute | solution.py:23
  99.5 11.1 %collective-permute-start.11 = (bf16[384,1536]{1,0:T(8,128)(2,1)}, bf16[384,1536]{1,0:T(8,128)(2,1)}, u32[]{:S(2)}, u32[]{:S(2)}) collective-permute-start(bf16[384,1536]{1,0:T(8,128)(2,1)} %collective-permute-done.1.refs_2_), channel_id=1, source_target_pairs={{0,2},{2,0},{1,3},{3,1},{4,6},{6,4},{5,7},{7,5},{8,10},{10,8},{9,1... | collective-permute-start | bytes 3538952 | tf_op jit(solution)/shard_map/ppermute | solution.py:23
  99.6 11.0 %collective-permute-start.12 = (bf16[384,1536]{1,0:T(8,128)(2,1)}, bf16[384,1536]{1,0:T(8,128)(2,1)}, u32[]{:S(2)}, u32[]{:S(2)}) collective-permute-start(bf16[384,1536]{1,0:T(8,128)(2,1)} %collective-permute-done.2.refs_4_), channel_id=1, source_target_pairs={{0,2},{2,0},{1,3},{3,1},{4,6},{6,4},{5,7},{7,5},{8,10},{10,8},{9,1... | collective-permute-start | bytes 3538952 | tf_op jit(solution)/shard_map/ppermute | solution.py:23
  100.0 10.6 %collective-permute-start.13 = (bf16[384,1536]{1,0:T(8,128)(2,1)}, bf16[384,1536]{1,0:T(8,128)(2,1)}, u32[]{:S(2)}, u32[]{:S(2)}) collective-permute-start(bf16[384,1536]{1,0:T(8,128)(2,1)} %collective-permute-done.5.refs_6_), channel_id=1, source_target_pairs={{0,2},{2,0},{1,3},{3,1},{4,6},{6,4},{5,7},{7,5},{8,10},{10,8},{9,1... | collective-permute-start | bytes 3538952 | tf_op jit(solution)/shard_map/ppermute | solution.py:23
  102.9 1.4 copy-start.3
  109.1 0.9 copy-start.11
  110.0 55.9 %collective-permute-start.18 = (bf16[2,384,1024]{2,1,0:T(8,128)(2,1)}, bf16[2,384,1024]{2,1,0:T(8,128)(2,1)}, u32[]{:S(2)}, u32[]{:S(2)}) collective-permute-start(bf16[2,384,1024]{2,1,0:T(8,128)(2,1)} %get-tuple-element.53), channel_id=1, source_target_pairs={{0,4},{4,0},{1,5},{5,1},{2,6},{6,2},{3,7},{7,3},{8,12},{12,8},{9,1... | collective-permute-start | bytes 4718600 | tf_op jit(solution)/shard_map/ppermute | solution.py:23
  110.7 1.1 copy-start.10
  120.0 30.1 %collective-permute-start.14 = (bf16[256,768]{1,0:T(8,128)(2,1)}, bf16[256,768]{1,0:T(8,128)(2,1)}, u32[]{:S(2)}, u32[]{:S(2)}) collective-permute-start(bf16[256,768]{1,0:T(8,128)(2,1)} %get-tuple-element.62), channel_id=1, source_target_pairs={{0,16},{16,0},{1,17},{17,1},{2,18},{18,2},{3,19},{19,3},{4,20},{20... | collective-permute-start | bytes 1179656 | tf_op jit(solution)/shard_map/ppermute | solution.py:23
  120.7 37.0 %collective-permute-start.15 = (bf16[256,768]{1,0:T(8,128)(2,1)}, bf16[256,768]{1,0:T(8,128)(2,1)}, u32[]{:S(2)}, u32[]{:S(2)}) collective-permute-start(bf16[256,768]{1,0:T(8,128)(2,1)} %get-tuple-element.63), channel_id=1, source_target_pairs={{0,16},{16,0},{1,17},{17,1},{2,18},{18,2},{3,19},{19,3},{4,20},{20... | collective-permute-start | bytes 1179656 | tf_op jit(solution)/shard_map/ppermute | solution.py:23
  123.0 9.5 %copy-start.4 = (bf16[4,384,512]{2,1,0:T(8,128)(2,1)S(1)}, bf16[4,384,512]{2,1,0:T(8,128)(2,1)}, u32[]{:S(2)}) copy-start(bf16[4,384,512]{2,1,0:T(8,128)(2,1)} %copy-done.2) | copy-start | bytes 4718596
  123.0 42.9 %collective-permute-start.19 = (bf16[2,384,512]{2,1,0:T(8,128)(2,1)}, bf16[2,384,512]{2,1,0:T(8,128)(2,1)S(1)}, u32[]{:S(2)}, u32[]{:S(2)}) collective-permute-start(bf16[2,384,512]{2,1,0:T(8,128)(2,1)} %copy-done.11), channel_id=1, source_target_pairs={{0,8},{8,0},{1,9},{9,1},{2,10},{10,2},{3,11},{11,3},{4,12},{12,4},... | collective-permute-start | bytes 2359304 | tf_op jit(solution)/shard_map/ppermute | solution.py:23
  124.1 1.1 copy-start.7
  132.5 17.6 %copy-start.1 = (bf16[3,128,1536]{2,1,0:T(8,128)(2,1)S(1)}, bf16[3,128,1536]{2,1,0:T(8,128)(2,1)}, u32[]{:S(2)}) copy-start(bf16[3,128,1536]{2,1,0:T(8,128)(2,1)} %copy-done) | copy-start | bytes 3538948
  157.7 16.3 %collective-permute-start.16 = (bf16[3,128,768]{2,1,0:T(8,128)(2,1)S(1)}, bf16[3,128,768]{2,1,0:T(8,128)(2,1)S(1)}, u32[]{:S(2)}, u32[]{:S(2)}) collective-permute-start(bf16[3,128,768]{2,1,0:T(8,128)(2,1)S(1)} %get-tuple-element.76), channel_id=1, source_target_pairs={{0,1},{1,0},{2,3},{3,2},{4,5},{5,4},{6,7},{7,6},{8,9},{9,8},{10,11... | collective-permute-start | bytes 1769480 | tf_op jit(solution)/shard_map/ppermute | solution.py:23
  164.0 20.9 %collective-permute-start.17 = (bf16[3,128,768]{2,1,0:T(8,128)(2,1)S(1)}, bf16[3,128,768]{2,1,0:T(8,128)(2,1)S(1)}, u32[]{:S(2)}, u32[]{:S(2)}) collective-permute-start(bf16[3,128,768]{2,1,0:T(8,128)(2,1)S(1)} %get-tuple-element.77), channel_id=1, source_target_pairs={{0,1},{1,0},{2,3},{3,2},{4,5},{5,4},{6,7},{7,6},{8,9},{9,8},{10,11... | collective-permute-start | bytes 1769480 | tf_op jit(solution)/shard_map/ppermute | solution.py:23
  168.0 18.2 %collective-permute-start.20 = (bf16[1,384,1024]{2,1,0:T(8,128)(2,1)S(1)}, bf16[1,384,1024]{2,1,0:T(8,128)(2,1)S(1)}, u32[]{:S(2)}, u32[]{:S(2)}) collective-permute-start(bf16[1,384,1024]{2,1,0:T(8,128)(2,1)S(1)} %dynamic-slice_convert_fusion), channel_id=1, source_target_pairs={{0,8},{8,0},{1,9},{9,1},{2,10},{10,2},{3,11},{11,3},{4,12},{12,4},... | collective-permute-start | bytes 2359304 | tf_op jit(solution)/shard_map/ppermute | solution.py:23
  168.4 16.5 %collective-permute-start.21 = (bf16[1,384,512]{2,1,0:T(8,128)(2,1)S(1)}, bf16[1,384,512]{2,1,0:T(8,128)(2,1)S(1)}, u32[]{:S(2)}, u32[]{:S(2)}) collective-permute-start(bf16[1,384,512]{2,1,0:T(8,128)(2,1)S(1)} %dynamic-slice_convert_fusion.1), channel_id=1, source_target_pairs={{0,4},{4,0},{1,5},{5,1},{2,6},{6,2},{3,7},{7,3},{8,12},{12,8},{9,1... | collective-permute-start | bytes 1179656 | tf_op jit(solution)/shard_map/ppermute | solution.py:23
  184.9 1.6 copy-start.14
  184.9 1.6 copy-start.15
  184.9 1.6 copy-start.16

commit v6 on v5

--- a/solution.py
+++ b/solution.py
@@ -145,11 +145,10 @@
     for group, out_ref in enumerate(outs):
         for start in range(0, wide, block):
             columns = slice(group * wide + start, group * wide + start + block)
-            total = None
-            for i, weight in enumerate(weights):
-                term = dot(every[at_ref[i]], weight[:, columns], ((1,), (0,)))
-                total = term if total is None else total + term
-            out_ref[:, start : start + block] = total.astype(out_ref.dtype)
+            grads = jnp.concatenate([every[at_ref[i]] for i in range(pieces)], axis=1)
+            chosen = jnp.concatenate([weight[:, columns] for weight in weights], axis=0)
+            product = dot(grads, chosen, ((1,), (0,)))
+            out_ref[:, start : start + block] = product.astype(out_ref.dtype)
 
 
 def partial_product(at, own, far, weights, groups, dtype):
@@ -208,12 +207,15 @@
             at = at_ref[first + i]
             for column in range(0, wide, block):
                 columns = slice(start + column, start + column + block)
-                total = None
-                for grad, attended in zip(grads, attends):
-                    chosen = attended[:, :, columns].reshape(clips * length, block)
-                    term = dot(grad[at], chosen, ((1,), (0,)))
-                    total = term if total is None else total + term
-                out_ref[i, :, column : column + block] = total.astype(out_ref.dtype)
+                chosen = [
+                    attended[:, :, columns].reshape(clips * length, block) for attended in attends
+                ]
+                product = dot(
+                    jnp.concatenate([grad[at] for grad in grads], axis=1),
+                    jnp.concatenate(chosen, axis=0),
+                    ((1,), (0,)),
+                )
+                out_ref[i, :, column : column + block] = product.astype(out_ref.dtype)
         first += count
 
 
@@ -294,19 +296,23 @@
 
     halves = after(halves, attended)
     attends = [shift(attended, "zh", by) for by in others("zh")]
-    owns = [after(part_of(own_grad, "zh", 0, 1), halves)] + halves
+    owns = [part_of(own_grad, "zh", 0, 1)] + halves
     fars = [along_seq(half) for half in owns]
-    near_zl = after(near_zl, halves)
     places = [(zl, x) for zl in others("zl") for x in others("x")]
-    diagonal = [shift(block, "x", by) for block in near_zl for by in others("x")]
-
-    near_x, near_zl, diagonal, attends, owns, fars = lax.optimization_barrier(
-        (near_x, near_zl, diagonal, attends, owns, fars)
-    )
+    upper = rows // 2
+    first = [[shift(block[:upper], "zl", by) for by in others("zl")] for block in near_x]
+    last = [shift(block[upper:], "x", by) for block in near_zl for by in others("x")]
+    diagonal = [(first[x - 1][zl - 1], low) for (zl, x), low in zip(places, last)]
+
+    attends, fars[0] = lax.optimization_barrier((attends, fars[0]))
+    pair = jnp.stack([attended] + attends)
+    near_x, near_zl, diagonal, owns, fars, pair = lax.optimization_barrier(
+        (near_x, near_zl, diagonal, owns, fars, pair)
+    )
+    diagonal = [jnp.concatenate(halves_of, axis=0) for halves_of in diagonal]
     x_across = [across(block) for block in near_x]
     zl_across = [across(block) for block in near_zl]
     diagonal_across = [across(block) for block in diagonal]
-    pair = jnp.stack([attended] + attends)
     attends = [pair] + across(pair)
 
     weights = [((0, 0), out_weight, own_across)]
@@ -326,6 +332,18 @@
         shift(array, "core", by) for by, array in zip(others("core"), by_rows[1:])
     ]
 
+    at = jnp.stack(at)
+    sent = [
+        partial_product(at, own_part, far_part, blocks, groups, jnp.bfloat16)
+        for own_part, far_part in zip(owns[1:], fars[1:])
+    ]
+    def returned(group, *events):
+        parts = after([clip[group] for clip in sent], *events)
+        return [shift(part, "zh", -by) for by, part in zip(others("zh"), parts)]
+
+    terms = [returned(0)]
+
+    by_rows[1:] = after(by_rows[1:], sent)
     starts = [sum(widths[:split]) for split in range(len(widths))]
     jobs = [
         (blocks_along(axis, by), start, size)
@@ -335,24 +353,15 @@
     leave = rows_products(jobs, by_rows, attends, jnp.bfloat16)
     rest = iter(leave)
     arrive = [[shift(next(rest), axis, by) for by in others(axis)] for axis, _ in orders]
-
     owns, fars = after((owns, fars), leave)
-    at = jnp.stack(at)
-    sent = [
-        partial_product(at, own_part, far_part, blocks, groups, jnp.bfloat16)
-        for own_part, far_part in zip(owns[1:], fars[1:])
-    ]
-    terms = [
-        [shift(clip[group], "zh", -by) for by, clip in zip(others("zh"), sent)]
-        for group in range(groups)
-    ]
-    owns, fars = after((owns, fars), sent)
     partial = partial_product(at, owns[0], fars[0], blocks, groups, jnp.float32)
     jobs = [
         (blocks_along(axis, 0), start, size)
         for (axis, _), start, size in zip(orders, starts, widths)
     ]
     kept = rows_products(jobs, after(by_rows, partial), attends, jnp.float32)
+    for group in range(1, groups):
+        terms.append(returned(group, terms[group - 1], kept))
 
     stays, arrivals = [], []
     for group in range(groups):

time: 189 us -> 189 us (level)
  local copies, waits for them, and re-layouts: 12.4 us -> 14.6 us
  Pallas kernels: 42.3 us -> 40.4 us
    slice x0 -> x2, local copies, waits for them, and re-layouts: none -> 3.83 us  [the longest x1 1.92 us: shards(): block[:upper]]
    unnamed x38 -> x31, local copies, waits for them, and re-layouts: 7.89 us -> 4.33 us
    concatenate x0 -> x1, local copies, waits for them, and re-layouts: none -> 1.94 us  [shards(): diagonal = [jnp.concatenate(halves_of, axis=0) for halves_of in diagonal]]
    pallas_call x8, Pallas kernels: 42.3 us -> 40.4 us  [whole_call(): pl.pallas_call(kernel, in_specs=in_specs, out_specs=jax.tree.map(lambda _...]
    ppermute x22 -> x23, waiting for transfers between devices: 101 us -> 101 us  [shift(): lax.ppermute(array, axis, [(i, (i + by) % count) for i in range(count)])]
    ppermute x22 -> x23, starting transfers between devices: 24 us -> 24 us  [shift(): lax.ppermute(array, axis, [(i, (i + by) % count) for i in range(count)])]
  transfers between devices with their start and end apart: 22 -> 23, of which waited for: 12 -> 10; matrix products, arithmetic and copies ran while one was open for 3% -> 7% of each run, Pallas kernels for 22% -> 17%
where the time goes in v6:
time: 189 us
  waiting for transfers between devices  101 us (53%)
  Pallas kernels  40.4 us (21%)
  starting transfers between devices  24 us (13%)
  local copies, waits for them, and re-layouts  14.6 us (8%)
  other arithmetic  7.05 us (4%)
    ppermute x23, waiting for transfers between devices, shift(): lax.ppermute(array, axis, [(i, (i + by) % count) for i in range(count)])  101 us
    pallas_call x8, Pallas kernels, whole_call(): pl.pallas_call(kernel, in_specs=in_specs, out_specs=jax.tree.map(lambda _...  40.4 us
    ppermute x23, starting transfers between devices, shift(): lax.ppermute(array, axis, [(i, (i + by) % count) for i in range(count)])  24 us
    unnamed x31, local copies, waits for them, and re-layouts  4.33 us
    dynamic_slice x3, local copies, waits for them, and re-layouts, part_of(): return lax.dynamic_slice_in_dim(array, at * size, size, dim)  3.8 us
  transfers between devices with their start and end apart: 23, of which 10 were waited for; matrix products, arithmetic and copies ran while one was open for 7% of the time, Pallas kernels for 17%

profile of v6, /device:TPU:0, one launch (start us, length us, event | category | flops | bytes accessed | tf_op | source)
XLA Modules:
  0.0 188.5 jit_solution(10651228357186659180)
XLA Ops:
  0.7 1.3 constant_dynamic-slice_fusion.2
  2.0 0.0 copy-done.14
  2.0 0.2 copy-done.13
  2.2 1.0 constant_dynamic-slice_fusion
  3.2 1.1 pad_maximum_fusion.2
  4.4 3.0 %collective-permute-start = (bf16[3,128,1536]{2,1,0:T(8,128)(2,1)}, bf16[3,128,1536]{2,1,0:T(8,128)(2,1)S(1)}, u32[]{:S(2)}, u32[]{:S(2)}) collective-permute-start(bf16[3,128,1536]{2,1,0:T(8,128)(2,1)} %pad_maximum_fusion.2), channel_id=1, source_target_pairs={{0,1},{1,0},{2,3},{3,2},{4,5},{5,4},{6,7},{7,6},{8,9},{9,8},{10,11... | collective-permute-start | bytes 3538952 | tf_op jit(solution)/shard_map/ppermute | solution.py:23
  7.3 1.5 collective-permute-start.1
  8.8 1.6 collective-permute-start.2
  10.4 1.5 dynamic-slice_bitcast_fusion
  12.0 2.7 %collective-permute-start.5 = (bf16[128,3072]{1,0:T(8,128)(2,1)S(1)}, bf16[128,3072]{1,0:T(8,128)(2,1)}, u32[]{:S(2)}, u32[]{:S(2)}) collective-permute-start(bf16[128,3072]{1,0:T(8,128)(2,1)S(1)} %get-tuple-element.78), channel_id=1, source_target_pairs={{0,16},{16,0},{1,17},{17,1},{2,18},{18,2},{3,19},{19,3},{4,20},{20... | collective-permute-start | bytes 2359304 | tf_op jit(solution)/shard_map/ppermute | solution.py:23
  14.6 0.1 pad_maximum_fusion.1.own
  14.7 18.8 %collective-permute-done.far = bf16[3,128,1536]{2,1,0:T(8,128)(2,1)S(1)} collective-permute-done((bf16[3,128,1536]{2,1,0:T(8,128)(2,1)}, bf16[3,128,1536]{2,1,0:T(8,128)(2,1)S(1)}, u32[]{:S(2)}, u32[]{:S(2)}) %collective-permute-start) | collective-permute-done | bytes 1179680 | tf_op jit(solution)/shard_map/ppermute | solution.py:23
  33.5 1.7 collective-permute-start.8
  35.3 2.9 %forward.1 = bf16[256,1536]{1,0:T(8,128)(2,1)} custom-call(bf16[3,128,1536]{2,1,0:T(8,128)(2,1)S(1)} %pad_maximum_fusion.1.own, bf16[3,128,1536]{2,1,0:T(8,128)(2,1)S(1)} %collective-permute-done.far), custom_call_target="tpu_custom_call" | custom-call | flops 1024 | bytes 1024 | tf_op jit(solution)/shard_map/forward/pallas_call | solution.py:104
  38.2 2.6 %collective-permute-start.7 = (bf16[256,1536]{1,0:T(8,128)(2,1)}, bf16[256,1536]{1,0:T(8,128)(2,1)}, u32[]{:S(2)}, u32[]{:S(2)}) collective-permute-start(bf16[256,1536]{1,0:T(8,128)(2,1)} %forward.1), channel_id=1, source_target_pairs={{0,16},{16,0},{1,17},{17,1},{2,18},{18,2},{3,19},{19,3},{4,20},{20... | collective-permute-start | bytes 2359304 | tf_op jit(solution)/shard_map/ppermute | solution.py:23
  40.8 13.0 %collective-permute-done.5.refs_2_.own = bf16[128,3072]{1,0:T(8,128)(2,1)} collective-permute-done((bf16[128,3072]{1,0:T(8,128)(2,1)S(1)}, bf16[128,3072]{1,0:T(8,128)(2,1)}, u32[]{:S(2)}, u32[]{:S(2)}) %collective-permute-start.5) | collective-permute-done | bytes 786464 | tf_op jit(solution)/shard_map/ppermute | solution.py:23
  53.8 0.5 collective-permute-start.9
  54.3 1.9 %slice.8 = bf16[192,1536]{1,0:T(8,128)(2,1)} slice(bf16[384,1536]{1,0:T(8,128)(2,1)} %collective-permute-done.1.refs_2_), slice={[0:192], [0:1536]} | slice | bytes 1179648 | tf_op jit(solution)/shard_map/slice | solution.py:303
  56.3 3.7 %collective-permute-start.3 = (bf16[192,1536]{1,0:T(8,128)(2,1)}, bf16[192,1536]{1,0:T(8,128)(2,1)}, u32[]{:S(2)}, u32[]{:S(2)}) collective-permute-start(bf16[192,1536]{1,0:T(8,128)(2,1)} %slice.8), channel_id=1, source_target_pairs={{0,8},{8,0},{1,9},{9,1},{2,10},{10,2},{3,11},{11,3},{4,12},{12,4},... | collective-permute-start | bytes 1769480 | tf_op jit(solution)/shard_map/ppermute | solution.py:23
  59.9 1.9 %slice.9 = bf16[192,1536]{1,0:T(8,128)(2,1)} slice(bf16[384,1536]{1,0:T(8,128)(2,1)} %collective-permute-done.2.refs_4_), slice={[192:384], [0:1536]} | slice | bytes 1179648 | tf_op jit(solution)/shard_map/slice | solution.py:304
  61.8 0.5 collective-permute-start.4
  62.4 27.5 %collective-permute-done.7 = bf16[256,1536]{1,0:T(8,128)(2,1)} collective-permute-done((bf16[256,1536]{1,0:T(8,128)(2,1)}, bf16[256,1536]{1,0:T(8,128)(2,1)}, u32[]{:S(2)}, u32[]{:S(2)}) %collective-permute-start.7) | collective-permute-done | bytes 786464 | tf_op jit(solution)/shard_map/ppermute | solution.py:23
  89.8 1.5 pad_maximum_fusion.refs_2_
  91.4 3.8 %turn.1 = (bf16[4,384,512]{2,1,0:T(8,128)(2,1)S(1)}, bf16[4,384,512]{2,1,0:T(8,128)(2,1)}) custom-call(s32[1]{0:T(128)} %bitcast.12.core_ref, bf16[128,3072]{1,0:T(8,128)(2,1)S(1)} %get-tuple-element.61.refs_0_.own, bf16[128,3072]{1,0:T(8,128)(2,1)} %collective-permute-done.8.refs_1_.far, bf16[128,3072]{1,0:T(8,128)(2,1)} %collective-permute-done.5.refs_2_.own, ...), custom_call_target="tpu_custom_call" | custom-call | flops 1024 | bytes 1024 | tf_op jit(solution)/shard_map/turn/pallas_call | solution.py:104
  95.2 1.2 copy-done.2
  96.4 0.5 collective-permute-start.14
  96.9 1.9 %constant_dynamic-update-slice_fusion.1 = bf16[384,1536]{1,0:T(8,128)(2,1)} fusion(bf16[192,1536]{1,0:T(8,128)(2,1)} %collective-permute-done.3), kind=kLoop, calls=%fused_computation.25 | loop fusion | bytes 1179648
  98.8 1.9 %constant_dynamic-update-slice_fusion.refs_6_ = bf16[384,1536]{1,0:T(8,128)(2,1)} fusion(bf16[384,1536]{1,0:T(8,128)(2,1)} %constant_dynamic-update-slice_fusion.1, bf16[192,1536]{1,0:T(8,128)(2,1)} %collective-permute-done.4), kind=kLoop, calls=%fused_computation.24 | loop fusion | bytes 1179648 | tf_op jit(solution)/shard_map/concatenate | solution.py:312
  100.8 0.5 collective-permute-start.11
  101.3 0.1 stack.58.at_ref
  101.4 0.1 pad_add_fusion
  101.5 2.6 %collective-permute-done.13.refs_7_ = bf16[384,1536]{1,0:T(8,128)(2,1)} collective-permute-done((bf16[384,1536]{1,0:T(8,128)(2,1)}, bf16[384,1536]{1,0:T(8,128)(2,1)}, u32[]{:S(2)}, u32[]{:S(2)}) %collective-permute-start.13) | collective-permute-done | bytes 1179680 | tf_op jit(solution)/shard_map/ppermute | solution.py:23
  104.0 1.7 collective-permute-done.11.refs_3_
  105.7 1.7 collective-permute-done.12.refs_5_
  107.4 6.9 %partial.2 = (bf16[256,768]{1,0:T(8,128)(2,1)}, bf16[256,768]{1,0:T(8,128)(2,1)S(1)}) custom-call(s32[8]{0:T(128)S(1)} %stack.58.at_ref, bf16[128,3072]{1,0:T(8,128)(2,1)} %collective-permute-done.5.refs_2_.own, bf16[128,3072]{1,0:T(8,128)(2,1)} %collective-permute-done.9.refs_3_.far, bf16[384,1536]{1,0:T(8,128)(2,1)} %refs_0_.3, ...), custom_call_target="tpu_custom_call" | custom-call | flops 1024 | bytes 1024 | tf_op jit(solution)/shard_map/partial/pallas_call | solution.py:104
  114.4 5.4 %rows.2 = (bf16[2,384,1024]{2,1,0:T(8,128)(2,1)}, bf16[2,384,512]{2,1,0:T(8,128)(2,1)S(1)}) custom-call(s32[4]{0:T(128)S(1)} %get-tuple-element.95.at_ref, bf16[4,384,512]{2,1,0:T(8,128)(2,1)S(1)} %copy-done.3, bf16[4,384,512]{2,1,0:T(8,128)(2,1)} %collective-permute-done.10.refs_1_, bf16[2,256,1536]{2,1,0:T(8,128)(2,1)S(1)} %pad_maximum_fusion.refs_2_, ...), custom_call_target="tpu_custom_call" | custom-call | flops 1024 | bytes 1024 | tf_op jit(solution)/shard_map/rows/pallas_call | solution.py:104
  119.7 0.9 copy-done.5
  120.6 0.5 collective-permute-start.19
  121.1 1.9 %collective-permute-start.20 = (bf16[2,384,512]{2,1,0:T(8,128)(2,1)}, bf16[2,384,512]{2,1,0:T(8,128)(2,1)S(1)}, u32[]{:S(2)}, u32[]{:S(2)}) collective-permute-start(bf16[2,384,512]{2,1,0:T(8,128)(2,1)} %copy-done.5), channel_id=1, source_target_pairs={{0,8},{8,0},{1,9},{9,1},{2,10},{10,2},{3,11},{11,3},{4,12},{12,4},... | collective-permute-start | bytes 2359304 | tf_op jit(solution)/shard_map/ppermute | solution.py:23
  123.0 6.7 %partial.3 = (f32[256,768]{1,0:T(8,128)S(1)}, f32[256,768]{1,0:T(8,128)S(1)}) custom-call(s32[8]{0:T(128)S(1)} %stack.58.at_ref, bf16[128,3072]{1,0:T(8,128)(2,1)S(1)} %get-tuple-element.61.refs_0_.own, bf16[128,3072]{1,0:T(8,128)(2,1)} %collective-permute-done.8.refs_1_.far, bf16[384,1536]{1,0:T(8,128)(2,1)} %refs_0_.3, ...), custom_call_target="tpu_custom_call" | custom-call | flops 1024 | bytes 1024 | tf_op jit(solution)/shard_map/partial/pallas_call | solution.py:104
  129.7 4.6 %rows.3 = (f32[2,384,1024]{2,1,0:T(8,128)S(1)}, f32[2,384,512]{2,1,0:T(8,128)S(1)}) custom-call(s32[4]{0:T(128)S(1)} %get-tuple-element.96.at_ref, bf16[4,384,512]{2,1,0:T(8,128)(2,1)S(1)} %copy-done.4, bf16[4,384,512]{2,1,0:T(8,128)(2,1)} %collective-permute-done.10.refs_1_, bf16[2,256,1536]{2,1,0:T(8,128)(2,1)S(1)} %pad_maximum_fusion.refs_2_, ...), custom_call_target="tpu_custom_call" | custom-call | flops 1024 | bytes 1024 | tf_op jit(solution)/shard_map/rows/pallas_call | solution.py:104
  134.3 6.1 %collective-permute-done.15.refs_1_ = bf16[256,768]{1,0:T(8,128)(2,1)} collective-permute-done((bf16[256,768]{1,0:T(8,128)(2,1)}, bf16[256,768]{1,0:T(8,128)(2,1)}, u32[]{:S(2)}, u32[]{:S(2)}) %collective-permute-start.15) | collective-permute-done | bytes 393248 | tf_op jit(solution)/shard_map/ppermute | solution.py:23
  140.5 5.5 %backward.2 = (bf16[3,128,768]{2,1,0:T(8,128)(2,1)S(1)}, bf16[3,128,768]{2,1,0:T(8,128)(2,1)S(1)}) custom-call(bf16[3,128,1536]{2,1,0:T(8,128)(2,1)S(1)} %pad_maximum_fusion.1.own, bf16[3,128,1536]{2,1,0:T(8,128)(2,1)S(1)} %copy-done.1, f32[256,768]{1,0:T(8,128)S(1)} %get-tuple-element.63.refs_0_, bf16[256,768]{1,0:T(8,128)(2,1)} %collective-permute-done.15.refs_1_), custom_call_target="tpu_custom_call" | custom-call | flops 1024 | bytes 1024 | tf_op jit(solution)/shard_map/backward/pallas_call | solution.py:104
  145.9 0.6 collective-permute-start.17
  146.6 0.1 broadcast_in_dim.2.clone.2
  146.7 0.1 broadcast_in_dim.2.clone.1
  146.8 0.1 broadcast_in_dim.2.clone
  146.9 13.9 %collective-permute-done.16.refs_1_ = bf16[256,768]{1,0:T(8,128)(2,1)S(1)} collective-permute-done((bf16[256,768]{1,0:T(8,128)(2,1)S(1)}, bf16[256,768]{1,0:T(8,128)(2,1)S(1)}, u32[]{:S(2)}, u32[]{:S(2)}) %collective-permute-start.16) | collective-permute-done | bytes 393248 | tf_op jit(solution)/shard_map/ppermute | solution.py:23
  160.8 4.7 %backward.3 = (bf16[3,128,768]{2,1,0:T(8,128)(2,1)S(1)}, bf16[3,128,768]{2,1,0:T(8,128)(2,1)S(1)}) custom-call(bf16[3,128,1536]{2,1,0:T(8,128)(2,1)S(1)} %pad_maximum_fusion.1.own, bf16[3,128,1536]{2,1,0:T(8,128)(2,1)S(1)} %copy-done.1, f32[256,768]{1,0:T(8,128)S(1)} %get-tuple-element.64.refs_0_, bf16[256,768]{1,0:T(8,128)(2,1)S(1)} %collective-permute-done.16.refs_1_), custom_call_target="tpu_custom_call" | custom-call | flops 1024 | bytes 1024 | tf_op jit(solution)/shard_map/backward/pallas_call | solution.py:104
  165.5 0.6 collective-permute-start.18
  166.1 0.1 slice_dynamic-update-slice_fusion.6
  166.2 1.9 %convert_add_fusion = f32[2,384,1024]{2,1,0:T(8,128)S(1)} fusion(f32[2,384,1024]{2,1,0:T(8,128)S(1)} %get-tuple-element.67, bf16[2,384,1024]{2,1,0:T(8,128)(2,1)} %collective-permute-done.19), kind=kLoop, calls=%fused_computation | loop fusion | flops 1572864 | bytes 7864320 | tf_op jit(solution)/shard_map/add | solution.py:379
  168.1 0.1 dynamic-slice_convert_fusion
  168.3 0.1 collective-permute-start.21
  168.3 0.3 convert_add_fusion.1
  168.6 0.1 dynamic-slice_convert_fusion.1
  168.7 1.5 collective-permute-start.22
  170.2 0.1 slice_dynamic-update-slice_fusion.1
  170.3 9.6 %collective-permute-done.18 = bf16[3,128,768]{2,1,0:T(8,128)(2,1)S(1)} collective-permute-done((bf16[3,128,768]{2,1,0:T(8,128)(2,1)S(1)}, bf16[3,128,768]{2,1,0:T(8,128)(2,1)S(1)}, u32[]{:S(2)}, u32[]{:S(2)}) %collective-permute-start.18) | collective-permute-done | bytes 589856 | tf_op jit(solution)/shard_map/ppermute | solution.py:23
  179.9 0.1 slice_dynamic-update-slice_fusion
  180.0 0.1 add_bitcast_fusion.1
  180.2 6.5 %collective-permute-done.21 = bf16[1,384,1024]{2,1,0:T(8,128)(2,1)S(1)} collective-permute-done((bf16[1,384,1024]{2,1,0:T(8,128)(2,1)S(1)}, bf16[1,384,1024]{2,1,0:T(8,128)(2,1)S(1)}, u32[]{:S(2)}, u32[]{:S(2)}) %collective-permute-start.21) | collective-permute-done | bytes 786464 | tf_op jit(solution)/shard_map/ppermute | solution.py:23
  186.6 0.3 add_bitcast_fusion
  186.9 1.6 maximum_multiply_fusion
  (52 shorter events, 0.2 us)
Async XLA Ops:
  0.6 1.4 copy-start.14
  0.6 1.6 copy-start.13
  4.4 29.1 %collective-permute-start = (bf16[3,128,1536]{2,1,0:T(8,128)(2,1)}, bf16[3,128,1536]{2,1,0:T(8,128)(2,1)S(1)}, u32[]{:S(2)}, u32[]{:S(2)}) collective-permute-start(bf16[3,128,1536]{2,1,0:T(8,128)(2,1)} %pad_maximum_fusion.2), channel_id=1, source_target_pairs={{0,1},{1,0},{2,3},{3,2},{4,5},{5,4},{6,7},{7,6},{8,9},{9,8},{10,11... | collective-permute-start | bytes 3538952 | tf_op jit(solution)/shard_map/ppermute | solution.py:23
  7.3 27.9 %collective-permute-start.6 = (bf16[384,1536]{1,0:T(8,128)(2,1)}, bf16[384,1536]{1,0:T(8,128)(2,1)}, u32[]{:S(2)}, u32[]{:S(2)}) collective-permute-start(bf16[384,1536]{1,0:T(8,128)(2,1)} %refs_0_.3), channel_id=1, source_target_pairs={{0,2},{2,0},{1,3},{3,1},{4,6},{6,4},{5,7},{7,5},{8,10},{10,8},{9,1... | collective-permute-start | bytes 3538952 | tf_op jit(solution)/shard_map/ppermute | solution.py:23
  7.3 47.0 %collective-permute-start.1 = (bf16[384,1536]{1,0:T(8,128)(2,1)}, bf16[384,1536]{1,0:T(8,128)(2,1)}, u32[]{:S(2)}, u32[]{:S(2)}) collective-permute-start(bf16[384,1536]{1,0:T(8,128)(2,1)} %refs_0_.3), channel_id=1, source_target_pairs={{0,4},{4,0},{1,5},{5,1},{2,6},{6,2},{3,7},{7,3},{8,12},{12,8},{9,1... | collective-permute-start | bytes 3538952 | tf_op jit(solution)/shard_map/ppermute | solution.py:23
  8.8 51.1 %collective-permute-start.2 = (bf16[384,1536]{1,0:T(8,128)(2,1)}, bf16[384,1536]{1,0:T(8,128)(2,1)}, u32[]{:S(2)}, u32[]{:S(2)}) collective-permute-start(bf16[384,1536]{1,0:T(8,128)(2,1)} %refs_0_.3), channel_id=1, source_target_pairs={{0,8},{8,0},{1,9},{9,1},{2,10},{10,2},{3,11},{11,3},{4,12},{12,4},... | collective-permute-start | bytes 3538952 | tf_op jit(solution)/shard_map/ppermute | solution.py:23
  10.4 4.2 %copy-start.8 = (bf16[1,128,1536]{2,1,0:T(8,128)(2,1)S(1)}, bf16[1,128,1536]{2,1,0:T(8,128)(2,1)}, u32[]{:S(2)}) copy-start(bf16[1,128,1536]{2,1,0:T(8,128)(2,1)} %get-tuple-element.85) | copy-start | bytes 1179652
  10.4 4.2 %copy-start.9 = (bf16[1,128,1536]{2,1,0:T(8,128)(2,1)S(1)}, bf16[1,128,1536]{2,1,0:T(8,128)(2,1)}, u32[]{:S(2)}) copy-start(bf16[1,128,1536]{2,1,0:T(8,128)(2,1)} %get-tuple-element.97) | copy-start | bytes 1179652
  12.0 41.9 %collective-permute-start.5 = (bf16[128,3072]{1,0:T(8,128)(2,1)S(1)}, bf16[128,3072]{1,0:T(8,128)(2,1)}, u32[]{:S(2)}, u32[]{:S(2)}) collective-permute-start(bf16[128,3072]{1,0:T(8,128)(2,1)S(1)} %get-tuple-element.78), channel_id=1, source_target_pairs={{0,16},{16,0},{1,17},{17,1},{2,18},{18,2},{3,19},{19,3},{4,20},{20... | collective-permute-start | bytes 2359304 | tf_op jit(solution)/shard_map/ppermute | solution.py:23
  33.5 4.7 %copy-start = (bf16[3,128,1536]{2,1,0:T(8,128)(2,1)}, bf16[3,128,1536]{2,1,0:T(8,128)(2,1)S(1)}, u32[]{:S(2)}) copy-start(bf16[3,128,1536]{2,1,0:T(8,128)(2,1)S(1)} %collective-permute-done.far) | copy-start | bytes 3538948
  33.5 28.9 %collective-permute-start.8 = (bf16[128,3072]{1,0:T(8,128)(2,1)S(1)}, bf16[128,3072]{1,0:T(8,128)(2,1)}, u32[]{:S(2)}, u32[]{:S(2)}) collective-permute-start(bf16[128,3072]{1,0:T(8,128)(2,1)S(1)} %get-tuple-element.61.refs_0_.own), channel_id=1, source_target_pairs={{0,1},{1,0},{2,3},{3,2},{4,5},{5,4},{6,7},{7,6},{8,9},{9,8},{10,11... | collective-permute-start | bytes 2359304 | tf_op jit(solution)/shard_map/ppermute | solution.py:23
  38.2 51.6 %collective-permute-start.7 = (bf16[256,1536]{1,0:T(8,128)(2,1)}, bf16[256,1536]{1,0:T(8,128)(2,1)}, u32[]{:S(2)}, u32[]{:S(2)}) collective-permute-start(bf16[256,1536]{1,0:T(8,128)(2,1)} %forward.1), channel_id=1, source_target_pairs={{0,16},{16,0},{1,17},{17,1},{2,18},{18,2},{3,19},{19,3},{4,20},{20... | collective-permute-start | bytes 2359304 | tf_op jit(solution)/shard_map/ppermute | solution.py:23
  53.8 37.5 %collective-permute-start.9 = (bf16[128,3072]{1,0:T(8,128)(2,1)}, bf16[128,3072]{1,0:T(8,128)(2,1)}, u32[]{:S(2)}, u32[]{:S(2)}) collective-permute-start(bf16[128,3072]{1,0:T(8,128)(2,1)} %collective-permute-done.5.refs_2_.own), channel_id=1, source_target_pairs={{0,1},{1,0},{2,3},{3,2},{4,5},{5,4},{6,7},{7,6},{8,9},{9,8},{10,11... | collective-permute-start | bytes 2359304 | tf_op jit(solution)/shard_map/ppermute | solution.py:23
  56.3 35.1 %collective-permute-start.3 = (bf16[192,1536]{1,0:T(8,128)(2,1)}, bf16[192,1536]{1,0:T(8,128)(2,1)}, u32[]{:S(2)}, u32[]{:S(2)}) collective-permute-start(bf16[192,1536]{1,0:T(8,128)(2,1)} %slice.8), channel_id=1, source_target_pairs={{0,8},{8,0},{1,9},{9,1},{2,10},{10,2},{3,11},{11,3},{4,12},{12,4},... | collective-permute-start | bytes 1769480 | tf_op jit(solution)/shard_map/ppermute | solution.py:23
  61.8 29.5 %collective-permute-start.4 = (bf16[192,1536]{1,0:T(8,128)(2,1)}, bf16[192,1536]{1,0:T(8,128)(2,1)}, u32[]{:S(2)}, u32[]{:S(2)}) collective-permute-start(bf16[192,1536]{1,0:T(8,128)(2,1)} %slice.9), channel_id=1, source_target_pairs={{0,4},{4,0},{1,5},{5,1},{2,6},{6,2},{3,7},{7,3},{8,12},{12,8},{9,1... | collective-permute-start | bytes 1769480 | tf_op jit(solution)/shard_map/ppermute | solution.py:23
  95.2 1.2 copy-start.2
  96.4 18.0 %collective-permute-start.10 = (bf16[4,384,512]{2,1,0:T(8,128)(2,1)}, bf16[4,384,512]{2,1,0:T(8,128)(2,1)}, u32[]{:S(2)}, u32[]{:S(2)}) collective-permute-start(bf16[4,384,512]{2,1,0:T(8,128)(2,1)} %get-tuple-element.50), channel_id=1, source_target_pairs={{0,2},{2,0},{1,3},{3,1},{4,6},{6,4},{5,7},{7,5},{8,10},{10,8},{9,1... | collective-permute-start | bytes 4718600 | tf_op jit(solution)/shard_map/ppermute | solution.py:23
  96.4 18.0 %collective-permute-start.14 = (bf16[2,256,1536]{2,1,0:T(8,128)(2,1)S(1)}, bf16[2,256,1536]{2,1,0:T(8,128)(2,1)}, u32[]{:S(2)}, u32[]{:S(2)}) collective-permute-start(bf16[2,256,1536]{2,1,0:T(8,128)(2,1)S(1)} %pad_maximum_fusion.refs_2_), channel_id=1, source_target_pairs={{0,2},{2,0},{1,3},{3,1},{4,6},{6,4},{5,7},{7,5},{8,10},{10,8},{9,1... | collective-permute-start | bytes 4718600 | tf_op jit(solution)/shard_map/ppermute | solution.py:23
  100.8 3.3 %collective-permute-start.13 = (bf16[384,1536]{1,0:T(8,128)(2,1)}, bf16[384,1536]{1,0:T(8,128)(2,1)}, u32[]{:S(2)}, u32[]{:S(2)}) collective-permute-start(bf16[384,1536]{1,0:T(8,128)(2,1)} %constant_dynamic-update-slice_fusion.refs_6_), channel_id=1, source_target_pairs={{0,2},{2,0},{1,3},{3,1},{4,6},{6,4},{5,7},{7,5},{8,10},{10,8},{9,1... | collective-permute-start | bytes 3538952 | tf_op jit(solution)/shard_map/ppermute | solution.py:23
  100.8 5.0 %collective-permute-start.11 = (bf16[384,1536]{1,0:T(8,128)(2,1)}, bf16[384,1536]{1,0:T(8,128)(2,1)}, u32[]{:S(2)}, u32[]{:S(2)}) collective-permute-start(bf16[384,1536]{1,0:T(8,128)(2,1)} %collective-permute-done.1.refs_2_), channel_id=1, source_target_pairs={{0,2},{2,0},{1,3},{3,1},{4,6},{6,4},{5,7},{7,5},{8,10},{10,8},{9,1... | collective-permute-start | bytes 3538952 | tf_op jit(solution)/shard_map/ppermute | solution.py:23
  101.3 6.2 %collective-permute-start.12 = (bf16[384,1536]{1,0:T(8,128)(2,1)}, bf16[384,1536]{1,0:T(8,128)(2,1)}, u32[]{:S(2)}, u32[]{:S(2)}) collective-permute-start(bf16[384,1536]{1,0:T(8,128)(2,1)} %collective-permute-done.2.refs_4_), channel_id=1, source_target_pairs={{0,2},{2,0},{1,3},{3,1},{4,6},{6,4},{5,7},{7,5},{8,10},{10,8},{9,1... | collective-permute-start | bytes 3538952 | tf_op jit(solution)/shard_map/ppermute | solution.py:23
  101.5 12.9 %copy-start.3 = (bf16[4,384,512]{2,1,0:T(8,128)(2,1)S(1)}, bf16[4,384,512]{2,1,0:T(8,128)(2,1)}, u32[]{:S(2)}) copy-start(bf16[4,384,512]{2,1,0:T(8,128)(2,1)} %copy-done.2) | copy-start | bytes 4718596
  114.3 5.4 %copy-start.6 = (bf16[256,768]{1,0:T(8,128)(2,1)}, bf16[256,768]{1,0:T(8,128)(2,1)S(1)}, u32[]{:S(2)}) copy-start(bf16[256,768]{1,0:T(8,128)(2,1)S(1)} %get-tuple-element.71) | copy-start | bytes 1179652
  119.7 0.9 copy-start.5
  120.6 45.6 %collective-permute-start.19 = (bf16[2,384,1024]{2,1,0:T(8,128)(2,1)}, bf16[2,384,1024]{2,1,0:T(8,128)(2,1)}, u32[]{:S(2)}, u32[]{:S(2)}) collective-permute-start(bf16[2,384,1024]{2,1,0:T(8,128)(2,1)} %get-tuple-element.59), channel_id=1, source_target_pairs={{0,4},{4,0},{1,5},{5,1},{2,6},{6,2},{3,7},{7,3},{8,12},{12,8},{9,1... | collective-permute-start | bytes 4718600 | tf_op jit(solution)/shard_map/ppermute | solution.py:23
  121.1 19.3 %collective-permute-start.15 = (bf16[256,768]{1,0:T(8,128)(2,1)}, bf16[256,768]{1,0:T(8,128)(2,1)}, u32[]{:S(2)}, u32[]{:S(2)}) collective-permute-start(bf16[256,768]{1,0:T(8,128)(2,1)} %get-tuple-element.55), channel_id=1, source_target_pairs={{0,16},{16,0},{1,17},{17,1},{2,18},{18,2},{3,19},{19,3},{4,20},{20... | collective-permute-start | bytes 1179656 | tf_op jit(solution)/shard_map/ppermute | solution.py:23
  121.1 8.6 %copy-start.4 = (bf16[4,384,512]{2,1,0:T(8,128)(2,1)S(1)}, bf16[4,384,512]{2,1,0:T(8,128)(2,1)}, u32[]{:S(2)}) copy-start(bf16[4,384,512]{2,1,0:T(8,128)(2,1)} %copy-done.2) | copy-start | bytes 4718596
  121.1 45.0 %collective-permute-start.20 = (bf16[2,384,512]{2,1,0:T(8,128)(2,1)}, bf16[2,384,512]{2,1,0:T(8,128)(2,1)S(1)}, u32[]{:S(2)}, u32[]{:S(2)}) collective-permute-start(bf16[2,384,512]{2,1,0:T(8,128)(2,1)} %copy-done.5), channel_id=1, source_target_pairs={{0,8},{8,0},{1,9},{9,1},{2,10},{10,2},{3,11},{11,3},{4,12},{12,4},... | collective-permute-start | bytes 2359304 | tf_op jit(solution)/shard_map/ppermute | solution.py:23
  129.7 10.7 %copy-start.7 = (bf16[256,768]{1,0:T(8,128)(2,1)S(1)}, bf16[256,768]{1,0:T(8,128)(2,1)}, u32[]{:S(2)}) copy-start(bf16[256,768]{1,0:T(8,128)(2,1)} %copy-done.6) | copy-start | bytes 1179652
  129.7 10.7 %copy-start.1 = (bf16[3,128,1536]{2,1,0:T(8,128)(2,1)S(1)}, bf16[3,128,1536]{2,1,0:T(8,128)(2,1)}, u32[]{:S(2)}) copy-start(bf16[3,128,1536]{2,1,0:T(8,128)(2,1)} %copy-done) | copy-start | bytes 3538948
  140.5 20.3 %collective-permute-start.16 = (bf16[256,768]{1,0:T(8,128)(2,1)S(1)}, bf16[256,768]{1,0:T(8,128)(2,1)S(1)}, u32[]{:S(2)}, u32[]{:S(2)}) collective-permute-start(bf16[256,768]{1,0:T(8,128)(2,1)S(1)} %copy-done.7), channel_id=1, source_target_pairs={{0,16},{16,0},{1,17},{17,1},{2,18},{18,2},{3,19},{19,3},{4,20},{20... | collective-permute-start | bytes 1179656 | tf_op jit(solution)/shard_map/ppermute | solution.py:23
  145.9 24.3 %collective-permute-start.17 = (bf16[3,128,768]{2,1,0:T(8,128)(2,1)S(1)}, bf16[3,128,768]{2,1,0:T(8,128)(2,1)S(1)}, u32[]{:S(2)}, u32[]{:S(2)}) collective-permute-start(bf16[3,128,768]{2,1,0:T(8,128)(2,1)S(1)} %get-tuple-element.74), channel_id=1, source_target_pairs={{0,1},{1,0},{2,3},{3,2},{4,5},{5,4},{6,7},{7,6},{8,9},{9,8},{10,11... | collective-permute-start | bytes 1769480 | tf_op jit(solution)/shard_map/ppermute | solution.py:23
  165.5 14.4 %collective-permute-start.18 = (bf16[3,128,768]{2,1,0:T(8,128)(2,1)S(1)}, bf16[3,128,768]{2,1,0:T(8,128)(2,1)S(1)}, u32[]{:S(2)}, u32[]{:S(2)}) collective-permute-start(bf16[3,128,768]{2,1,0:T(8,128)(2,1)S(1)} %get-tuple-element.75), channel_id=1, source_target_pairs={{0,1},{1,0},{2,3},{3,2},{4,5},{5,4},{6,7},{7,6},{8,9},{9,8},{10,11... | collective-permute-start | bytes 1769480 | tf_op jit(solution)/shard_map/ppermute | solution.py:23
  168.3 18.4 %collective-permute-start.21 = (bf16[1,384,1024]{2,1,0:T(8,128)(2,1)S(1)}, bf16[1,384,1024]{2,1,0:T(8,128)(2,1)S(1)}, u32[]{:S(2)}, u32[]{:S(2)}) collective-permute-start(bf16[1,384,1024]{2,1,0:T(8,128)(2,1)S(1)} %dynamic-slice_convert_fusion), channel_id=1, source_target_pairs={{0,8},{8,0},{1,9},{9,1},{2,10},{10,2},{3,11},{11,3},{4,12},{12,4},... | collective-permute-start | bytes 2359304 | tf_op jit(solution)/shard_map/ppermute | solution.py:23
  168.7 11.4 %collective-permute-start.22 = (bf16[1,384,512]{2,1,0:T(8,128)(2,1)S(1)}, bf16[1,384,512]{2,1,0:T(8,128)(2,1)S(1)}, u32[]{:S(2)}, u32[]{:S(2)}) collective-permute-start(bf16[1,384,512]{2,1,0:T(8,128)(2,1)S(1)} %dynamic-slice_convert_fusion.1), channel_id=1, source_target_pairs={{0,4},{4,0},{1,5},{5,1},{2,6},{6,2},{3,7},{7,3},{8,12},{12,8},{9,1... | collective-permute-start | bytes 1179656 | tf_op jit(solution)/shard_map/ppermute | solution.py:23
  180.0 6.9 %copy-start.10 = (bf16[1,128,3072]{2,1,0:T(8,128)(2,1)}, bf16[1,128,3072]{2,1,0:T(8,128)(2,1)S(1)}, u32[]{:S(2)}) copy-start(bf16[1,128,3072]{2,1,0:T(8,128)(2,1)S(1)} %get-tuple-element.86) | copy-start | bytes 2359300
  180.0 6.9 %copy-start.11 = (bf16[1,128,3072]{2,1,0:T(8,128)(2,1)}, bf16[1,128,3072]{2,1,0:T(8,128)(2,1)S(1)}, u32[]{:S(2)}) copy-start(bf16[1,128,3072]{2,1,0:T(8,128)(2,1)S(1)} %get-tuple-element.88) | copy-start | bytes 2359300
  180.0 6.9 %copy-start.12 = (bf16[1,128,3072]{2,1,0:T(8,128)(2,1)}, bf16[1,128,3072]{2,1,0:T(8,128)(2,1)S(1)}, u32[]{:S(2)}) copy-start(bf16[1,128,3072]{2,1,0:T(8,128)(2,1)S(1)} %get-tuple-element.87) | copy-start | bytes 2359300

commit v7 on v6

--- a/solution.py
+++ b/solution.py
@@ -41,10 +41,12 @@
 
 
 def all_tokens(own, far, at):
-    return (jnp.concatenate([own[i, :, at], far[i, :, at]], axis=0) for i in range(3))
-
-
-def forward_kernel(own, far, att_ref):
+    fars = (far[0][0, :, at], far[0][1, :, at], far[1][0, :, at])
+    return (jnp.concatenate([own[i, :, at], arrived], axis=0) for i, arrived in enumerate(fars))
+
+
+def forward_kernel(own, far_both, far_values, att_ref):
+    far = (far_both, far_values)
     for start in range(0, att_ref.shape[1], HEAD_DIM):
         at = slice(start, start + HEAD_DIM)
         q, k, v = all_tokens(own, far, at)
@@ -52,7 +54,8 @@
         att_ref[:, at] = dot(low, v, ((1,), (0,))).astype(jnp.bfloat16)
 
 
-def backward_kernel(first, own, far, *refs):
+def backward_kernel(first, own, far_both, far_values, *refs):
+    far = (far_both, far_values)
     *grad_refs, staying, leaving = refs
     tokens = own.shape[1]
     for start in range(0, staying.shape[2], HEAD_DIM):
@@ -115,53 +118,60 @@
 
 def forward(own, far):
     _, tokens, features = own.shape
-    length = tokens + far.shape[1]
+    length = tokens + far[0].shape[1]
     shape = jax.ShapeDtypeStruct((length, features), jnp.bfloat16)
-    return whole_call(forward_kernel, length, shape, [own, far], "forward")
+    return whole_call(forward_kernel, length, shape, [own, *far], "forward")
 
 
 def backward(own, far, partial, terms, first):
-    tokens, rest = own.shape[1], far.shape[1]
+    tokens, rest = own.shape[1], far[0].shape[1]
     wide = partial.shape[1]
     return whole_call(
         functools.partial(backward_kernel, first),
         tokens + rest,
         [jax.ShapeDtypeStruct((3, count, wide), jnp.bfloat16) for count in (tokens, rest)],
-        [own, far, partial, *terms],
+        [own, *far, partial, *terms],
         "backward",
     )
 
 
-def partial_kernel(pieces, at_ref, own, far, *refs):
-    weights, outs, every = refs[:pieces], refs[pieces:-1], refs[-1]
+def partial_kernel(count, which, at_ref, own, far, *refs):
+    arrays, outs, every = refs[:count], refs[count:-1], refs[-1]
     tokens = own.shape[0]
-    rows = weights[0].shape[0]
+    rows = every.shape[2]
     wide = outs[0].shape[1]
     block = 256 if wide % 256 == 0 else 128
-    for i in range(pieces):
+    for i in range(len(which)):
         columns = slice(i * rows, (i + 1) * rows)
         every[i, :tokens] = own[:, columns]
         every[i, tokens:] = far[:, columns]
     for group, out_ref in enumerate(outs):
         for start in range(0, wide, block):
             columns = slice(group * wide + start, group * wide + start + block)
-            grads = jnp.concatenate([every[at_ref[i]] for i in range(pieces)], axis=1)
-            chosen = jnp.concatenate([weight[:, columns] for weight in weights], axis=0)
+            grads = jnp.concatenate([every[at_ref[i]] for i in range(len(which))], axis=1)
+            chosen = jnp.concatenate([arrays[j][i, :, columns] for j, i in which], axis=0)
             product = dot(grads, chosen, ((1,), (0,)))
             out_ref[:, start : start + block] = product.astype(out_ref.dtype)
 
 
 def partial_product(at, own, far, weights, groups, dtype):
     length = own.shape[0] + far.shape[0]
-    rows, features = weights[0].shape
+    arrays = []
+    for array, _ in weights:
+        if all(array is not other for other in arrays):
+            arrays.append(array)
+    which = [
+        (next(j for j, other in enumerate(arrays) if other is array), i) for array, i in weights
+    ]
+    rows, features = weights[0][0].shape[1:]
     return whole_call(
-        functools.partial(partial_kernel, len(weights)),
+        functools.partial(partial_kernel, len(arrays), which),
         length,
         [jax.ShapeDtypeStruct((length, features // groups), dtype)] * groups,
-        [own, far, *weights],
+        [own, far, *arrays],
         "partial",
         at,
-        [pltpu.VMEM((len(weights), length, rows), jnp.bfloat16)],
+        [pltpu.VMEM((len(which), length, rows), jnp.bfloat16)],
     )
 
 
@@ -276,19 +286,21 @@
     widths = [count * HEAD_DIM for count in (larger, heads - larger) if count]
     orders = [("x", "zl"), ("zl", "x")][: len(widths)]
 
-    def heads_of(by):
-        return jnp.stack([part_of(part[0], "seq", by, 1) for part in (queries, keys, values)])
-
-    pieces = [shift(heads_of(by), "seq", by) for by in others("seq")]
-    far = pieces[0] if seq == 2 else jnp.concatenate(pieces, axis=1)
+    def heads_of(by, *arrays):
+        return jnp.stack([part_of(part[0], "seq", by, 1) for part in arrays])
+
+    def far_heads(*arrays):
+        pieces = [shift(heads_of(by, *arrays), "seq", by) for by in others("seq")]
+        return pieces[0] if seq == 2 else jnp.concatenate(pieces, axis=1)
+
+    far = [far_heads(queries, keys), far_heads(values)]
     own_grad = grad_out[0]
     halves = [shift(part_of(own_grad, "zh", by, 1), "zh", by) for by in others("zh")]
     near_x = [shift(out_weight, "x", by) for by in others("x")]
     near_zl = [shift(out_weight, "zl", by) for by in others("zl")]
-    own_across = across(out_weight)
-
-    own = heads_of(0)
-    attended = forward(own, after(far, own_across))
+
+    own = heads_of(0, queries, keys, values)
+    attended = forward(own, far)
 
     def along_seq(array):
         arrived = [shift(array, "seq", by) for by in others("seq")]
@@ -298,39 +310,41 @@
     attends = [shift(attended, "zh", by) for by in others("zh")]
     owns = [part_of(own_grad, "zh", 0, 1)] + halves
     fars = [along_seq(half) for half in owns]
+
     places = [(zl, x) for zl in others("zl") for x in others("x")]
     upper = rows // 2
     first = [[shift(block[:upper], "zl", by) for by in others("zl")] for block in near_x]
     last = [shift(block[upper:], "x", by) for block in near_zl for by in others("x")]
-    diagonal = [(first[x - 1][zl - 1], low) for (zl, x), low in zip(places, last)]
-
-    attends, fars[0] = lax.optimization_barrier((attends, fars[0]))
-    pair = jnp.stack([attended] + attends)
-    near_x, near_zl, diagonal, owns, fars, pair = lax.optimization_barrier(
-        (near_x, near_zl, diagonal, owns, fars, pair)
-    )
-    diagonal = [jnp.concatenate(halves_of, axis=0) for halves_of in diagonal]
-    x_across = [across(block) for block in near_x]
-    zl_across = [across(block) for block in near_zl]
-    diagonal_across = [across(block) for block in diagonal]
-    attends = [pair] + across(pair)
-
-    weights = [((0, 0), out_weight, own_across)]
-    weights += [((0, by), *both_of) for by, *both_of in zip(others("x"), near_x, x_across)]
-    weights += [((by, 0), *both_of) for by, *both_of in zip(others("zl"), near_zl, zl_across)]
-    weights += zip(places, diagonal, diagonal_across)
-    at, blocks = [], []
-    for (zl, x), block, from_cores in weights:
-        for core, array in enumerate([block] + from_cores):
-            at.append(block_at(place("zl", -zl), place("x", -x), place("core", -core)))
-            blocks.append(array)
-
+    near = jnp.stack(near_x + near_zl)
+    near_across = across(near)
+    whole_weight = out_weight[None]
     cores = lax.axis_size("core")
     core = place("core").astype(jnp.int32).reshape(1)
-    by_rows = list(turned(core, owns, fars, rows, cores))
+    by_rows = by_rows_here = list(turned(core, owns, fars, rows, cores))
     by_rows = by_rows[:1] + [
         shift(array, "core", by) for by, array in zip(others("core"), by_rows[1:])
     ]
+
+    pair = jnp.stack(after([attended] + attends, by_rows_here))
+    attends = [pair] + across(pair)
+    first, last = after((first, last), pair)
+    diagonal = jnp.stack(
+        [
+            jnp.concatenate([first[x - 1][zl - 1], low], axis=0)
+            for (zl, x), low in zip(places, last)
+        ]
+    )
+    own_across, diagonal_across = across(whole_weight), across(diagonal)
+
+    near_places = [(0, by) for by in others("x")] + [(by, 0) for by in others("zl")]
+    weights = [((0, 0), [whole_weight] + own_across, 0)]
+    weights += [(where, [near] + near_across, i) for i, where in enumerate(near_places)]
+    weights += [(where, [diagonal] + diagonal_across, i) for i, where in enumerate(places)]
+    at, blocks = [], []
+    for (zl, x), arrays, i in weights:
+        for core, array in enumerate(arrays):
+            at.append(block_at(place("zl", -zl), place("x", -x), place("core", -core)))
+            blocks.append((array, i))
 
     at = jnp.stack(at)
     sent = [
@@ -343,7 +357,6 @@
 
     terms = [returned(0)]
 
-    by_rows[1:] = after(by_rows[1:], sent)
     starts = [sum(widths[:split]) for split in range(len(widths))]
     jobs = [
         (blocks_along(axis, by), start, size)

time: 189 us -> 177 us (0.937)
  waiting for transfers between devices: 101 us -> 90.5 us
  local copies, waits for them, and re-layouts: 14.6 us -> 9.4 us
  other arithmetic: 7.05 us -> 11.1 us
    ppermute x23, waiting for transfers between devices: 101 us -> 90.5 us  [shift(): lax.ppermute(array, axis, [(i, (i + by) % count) for i in range(count)])]
    another operation x3 -> x5, other arithmetic: 2.79 us -> 6.75 us  [the longest x1 2.66 us: shards(): pair = jnp.stack(after([attended] + attends, by_rows_here))]
    concatenate x1 -> x0, local copies, waits for them, and re-layouts: 1.94 us -> none  [shards(): diagonal = [jnp.concatenate(halves_of, axis=0) for halves_of in diagonal]]
    unnamed x31 -> x34, local copies, waits for them, and re-layouts: 4.33 us -> 3.1 us
  transfers between devices with their start and end apart: 23 -> 23, of which waited for: 10 -> 10; matrix products, arithmetic and copies ran while one was open for 7% -> 9% of each run, Pallas kernels for 17% -> 23%
where the time goes in v7:
time: 177 us
  waiting for transfers between devices  90.5 us (51%)
  Pallas kernels  40.7 us (23%)
  starting transfers between devices  23.9 us (14%)
  other arithmetic  11.1 us (6%)
  local copies, waits for them, and re-layouts  9.4 us (5%)
    ppermute x23, waiting for transfers between devices, shift(): lax.ppermute(array, axis, [(i, (i + by) % count) for i in range(count)])  90.5 us
    pallas_call x8, Pallas kernels, whole_call(): pl.pallas_call(kernel, in_specs=in_specs, out_specs=jax.tree.map(lambda _...  40.7 us
    ppermute x23, starting transfers between devices, shift(): lax.ppermute(array, axis, [(i, (i + by) % count) for i in range(count)])  23.9 us
  transfers between devices with their start and end apart: 23, of which 10 were waited for; matrix products, arithmetic and copies ran while one was open for 9% of the time, Pallas kernels for 23%

profile of v7, /device:TPU:0, one launch (start us, length us, event | category | flops | bytes accessed | tf_op | source)
XLA Modules:
  0.0 176.6 jit_solution(15909461297141823774)
XLA Ops:
  0.6 3.1 %collective-permute-start.10 = (bf16[384,1536]{1,0:T(8,128)(2,1)}, bf16[384,1536]{1,0:T(8,128)(2,1)}, u32[]{:S(2)}, u32[]{:S(2)}) collective-permute-start(bf16[384,1536]{1,0:T(8,128)(2,1)} %param.9), channel_id=1, source_target_pairs={{0,8},{8,0},{1,9},{9,1},{2,10},{10,2},{3,11},{11,3},{4,12},{12,4},... | collective-permute-start | bytes 3538952 | tf_op jit(solution)/shard_map/ppermute | solution.py:23
  3.7 1.5 collective-permute-start.9
  5.2 2.3 %constant_dynamic-slice_fusion.1 = (bf16[1,128,1536]{2,1,0:T(8,128)(2,1)S(1)}, bf16[1,128,1536]{2,1,0:T(8,128)(2,1)}, bf16[1,128,1536]{2,1,0:T(8,128)(2,1)}, bf16[1,128,1536]{2,1,0:T(8,128)(2,1)S(1)}) fusion(bf16[1,128,3072]{2,1,0:T(8,128)(2,1)} %param.7, s32[]{:T(128)S(6)} %select_n.162, s32[]{:T(128)S(6)} %select_n.160, bf16[1,128,3072]{2,1,0:T(8,128)(2,1)} %param.6), kind=kLoop, calls=%fused_computation.27 | loop fusion | bytes 3145736 | tf_op jit(solution)/shard_map/dynamic_slice | solution.py:34
  7.5 0.9 pad_maximum_fusion.3
  8.5 1.5 collective-permute-start
  10.0 1.0 dynamic-slice_bitcast_fusion
  11.0 2.6 %collective-permute-start.2 = (bf16[128,3072]{1,0:T(8,128)(2,1)S(1)}, bf16[128,3072]{1,0:T(8,128)(2,1)}, u32[]{:S(2)}, u32[]{:S(2)}) collective-permute-start(bf16[128,3072]{1,0:T(8,128)(2,1)S(1)} %get-tuple-element.60), channel_id=1, source_target_pairs={{0,16},{16,0},{1,17},{17,1},{2,18},{18,2},{3,19},{19,3},{4,20},{20... | collective-permute-start | bytes 2359304 | tf_op jit(solution)/shard_map/ppermute | solution.py:23
  13.7 0.8 collective-permute-start.1
  14.5 0.1 pad_maximum_fusion.2.own
  14.6 21.2 %collective-permute-done.1.far_values = bf16[1,128,1536]{2,1,0:T(8,128)(2,1)S(1)} collective-permute-done((bf16[1,128,1536]{2,1,0:T(8,128)(2,1)S(1)}, bf16[1,128,1536]{2,1,0:T(8,128)(2,1)S(1)}, u32[]{:S(2)}, u32[]{:S(2)}) %collective-permute-start.1) | collective-permute-done | bytes 393248 | tf_op jit(solution)/shard_map/ppermute | solution.py:23
  35.9 1.5 collective-permute-start.3
  37.4 2.9 %forward.1 = bf16[256,1536]{1,0:T(8,128)(2,1)} custom-call(bf16[3,128,1536]{2,1,0:T(8,128)(2,1)S(1)} %pad_maximum_fusion.2.own, bf16[2,128,1536]{2,1,0:T(8,128)(2,1)S(1)} %collective-permute-done.far_both, bf16[1,128,1536]{2,1,0:T(8,128)(2,1)S(1)} %collective-permute-done.1.far_values), custom_call_target="tpu_custom_call" | custom-call | flops 1024 | bytes 1024 | tf_op jit(solution)/shard_map/forward/pallas_call | solution.py:107
  40.3 5.7 %collective-permute-done.2.refs_2_.own = bf16[128,3072]{1,0:T(8,128)(2,1)} collective-permute-done((bf16[128,3072]{1,0:T(8,128)(2,1)S(1)}, bf16[128,3072]{1,0:T(8,128)(2,1)}, u32[]{:S(2)}, u32[]{:S(2)}) %collective-permute-start.2) | collective-permute-done | bytes 786464 | tf_op jit(solution)/shard_map/ppermute | solution.py:23
  46.0 1.5 collective-permute-start.4
  47.5 3.5 %collective-permute-start.6 = (bf16[256,1536]{1,0:T(8,128)(2,1)}, bf16[256,1536]{1,0:T(8,128)(2,1)}, u32[]{:S(2)}, u32[]{:S(2)}) collective-permute-start(bf16[256,1536]{1,0:T(8,128)(2,1)} %forward.1), channel_id=1, source_target_pairs={{0,16},{16,0},{1,17},{17,1},{2,18},{18,2},{3,19},{19,3},{4,20},{20... | collective-permute-start | bytes 2359304 | tf_op jit(solution)/shard_map/ppermute | solution.py:23
  51.0 1.8 %pad_maximum_fusion.refs_2_ = bf16[2,384,1536]{2,1,0:T(8,128)(2,1)S(1)} fusion(bf16[1,384,1536]{2,1,0:T(8,128)(2,1)} %bitcast.15, bf16[1,384,1536]{2,1,0:T(8,128)(2,1)} %bitcast.14), kind=kLoop, calls=%fused_computation.1 | loop fusion | flops 1179648 | bytes 4718592 | tf_op jit(solution)/shard_map/stack | solution.py:318
  52.9 0.1 collective-permute-start.11
  53.0 1.1 slice.8
  54.1 0.2 collective-permute-start.12
  54.3 1.1 slice.9
  55.4 1.3 collective-permute-done.3.refs_1_.far
  56.6 0.5 collective-permute-start.13
  57.2 13.7 %collective-permute-done.4.refs_3_.far = bf16[128,3072]{1,0:T(8,128)(2,1)} collective-permute-done((bf16[128,3072]{1,0:T(8,128)(2,1)}, bf16[128,3072]{1,0:T(8,128)(2,1)}, u32[]{:S(2)}, u32[]{:S(2)}) %collective-permute-start.4) | collective-permute-done | bytes 786464 | tf_op jit(solution)/shard_map/ppermute | solution.py:23
  70.9 4.0 %turn.1 = (bf16[4,384,512]{2,1,0:T(8,128)(2,1)S(1)}, bf16[4,384,512]{2,1,0:T(8,128)(2,1)}) custom-call(s32[1]{0:T(128)} %bitcast.10.core_ref, bf16[128,3072]{1,0:T(8,128)(2,1)} %get-tuple-element.39.refs_0_.own, bf16[128,3072]{1,0:T(8,128)(2,1)} %collective-permute-done.3.refs_1_.far, bf16[128,3072]{1,0:T(8,128)(2,1)} %collective-permute-done.2.refs_2_.own, ...), custom_call_target="tpu_custom_call" | custom-call | flops 1024 | bytes 1024 | tf_op jit(solution)/shard_map/turn/pallas_call | solution.py:107
  75.0 9.6 %collective-permute-done.6 = bf16[256,1536]{1,0:T(8,128)(2,1)} collective-permute-done((bf16[256,1536]{1,0:T(8,128)(2,1)}, bf16[256,1536]{1,0:T(8,128)(2,1)}, u32[]{:S(2)}, u32[]{:S(2)}) %collective-permute-start.6) | collective-permute-done | bytes 786464 | tf_op jit(solution)/shard_map/ppermute | solution.py:23
  84.6 2.7 %pad_maximum_fusion.1.refs_2_ = bf16[2,256,1536]{2,1,0:T(8,128)(2,1)} fusion(bf16[1,256,1536]{2,1,0:T(8,128)(2,1)} %bitcast.12, bf16[1,256,1536]{2,1,0:T(8,128)(2,1)} %bitcast.11), kind=kLoop, calls=%fused_computation.3 | loop fusion | flops 786432 | bytes 3145728 | tf_op jit(solution)/shard_map/stack | solution.py:328
  87.2 0.5 collective-permute-start.8
  87.8 1.2 maximum_bitcast_fusion.refs_4_
  88.9 0.1 collective-permute-start.14
  89.0 0.1 pad_add_fusion.at_ref
  89.1 1.9 %collective-permute-done.7.refs_3_ = bf16[2,256,1536]{2,1,0:T(8,128)(2,1)} collective-permute-done((bf16[2,256,1536]{2,1,0:T(8,128)(2,1)}, bf16[2,256,1536]{2,1,0:T(8,128)(2,1)}, u32[]{:S(2)}, u32[]{:S(2)}) %collective-permute-start.7) | collective-permute-done | bytes 1572896 | tf_op jit(solution)/shard_map/ppermute | solution.py:23
  91.0 1.4 copy-done.3
  92.4 5.7 %rows.2 = (bf16[2,384,1024]{2,1,0:T(8,128)(2,1)}, bf16[2,384,512]{2,1,0:T(8,128)(2,1)S(1)}) custom-call(s32[4]{0:T(128)S(1)} %pad_add_fusion.at_ref, bf16[4,384,512]{2,1,0:T(8,128)(2,1)S(1)} %copy-done.3, bf16[4,384,512]{2,1,0:T(8,128)(2,1)} %collective-permute-done.5.refs_1_, bf16[2,256,1536]{2,1,0:T(8,128)(2,1)} %pad_maximum_fusion.1.refs_2_, ...), custom_call_target="tpu_custom_call" | custom-call | flops 1024 | bytes 1024 | tf_op jit(solution)/shard_map/rows/pallas_call | solution.py:107
  98.1 0.9 copy-done.7
  99.0 1.5 collective-permute-start.19
  100.5 0.1 stack.70.at_ref
  100.6 6.6 %partial.3 = (bf16[256,768]{1,0:T(8,128)(2,1)}, bf16[256,768]{1,0:T(8,128)(2,1)S(1)}) custom-call(s32[8]{0:T(128)S(1)} %stack.70.at_ref, bf16[128,3072]{1,0:T(8,128)(2,1)} %collective-permute-done.2.refs_2_.own, bf16[128,3072]{1,0:T(8,128)(2,1)} %collective-permute-done.4.refs_3_.far, bf16[1,384,1536]{2,1,0:T(8,128)(2,1)} %bitcast.13.refs_0_, ...), custom_call_target="tpu_custom_call" | custom-call | flops 1024 | bytes 1024 | tf_op jit(solution)/shard_map/partial/pallas_call | solution.py:107
  107.2 0.8 copy-done.8
  108.0 0.1 pad_add_fusion.1.at_ref
  108.1 3.1 %collective-permute-start.20 = (bf16[2,384,512]{2,1,0:T(8,128)(2,1)}, bf16[2,384,512]{2,1,0:T(8,128)(2,1)S(1)}, u32[]{:S(2)}, u32[]{:S(2)}) collective-permute-start(bf16[2,384,512]{2,1,0:T(8,128)(2,1)} %copy-done.7), channel_id=1, source_target_pairs={{0,8},{8,0},{1,9},{9,1},{2,10},{10,2},{3,11},{11,3},{4,12},{12,4},... | collective-permute-start | bytes 2359304 | tf_op jit(solution)/shard_map/ppermute | solution.py:23
  111.2 6.2 %partial.2 = (f32[256,768]{1,0:T(8,128)S(1)}, f32[256,768]{1,0:T(8,128)S(1)}) custom-call(s32[8]{0:T(128)S(1)} %stack.70.at_ref, bf16[128,3072]{1,0:T(8,128)(2,1)} %get-tuple-element.39.refs_0_.own, bf16[128,3072]{1,0:T(8,128)(2,1)} %collective-permute-done.3.refs_1_.far, bf16[1,384,1536]{2,1,0:T(8,128)(2,1)} %bitcast.13.refs_0_, ...), custom_call_target="tpu_custom_call" | custom-call | flops 1024 | bytes 1024 | tf_op jit(solution)/shard_map/partial/pallas_call | solution.py:107
  117.5 5.1 %rows.3 = (f32[2,384,1024]{2,1,0:T(8,128)S(1)}, f32[2,384,512]{2,1,0:T(8,128)S(1)}) custom-call(s32[4]{0:T(128)S(1)} %pad_add_fusion.1.at_ref, bf16[4,384,512]{2,1,0:T(8,128)(2,1)S(1)} %copy-done.4, bf16[4,384,512]{2,1,0:T(8,128)(2,1)} %collective-permute-done.5.refs_1_, bf16[2,256,1536]{2,1,0:T(8,128)(2,1)} %pad_maximum_fusion.1.refs_2_, ...), custom_call_target="tpu_custom_call" | custom-call | flops 1024 | bytes 1024 | tf_op jit(solution)/shard_map/rows/pallas_call | solution.py:107
  122.5 6.0 %collective-permute-done.15.refs_1_ = bf16[256,768]{1,0:T(8,128)(2,1)} collective-permute-done((bf16[256,768]{1,0:T(8,128)(2,1)}, bf16[256,768]{1,0:T(8,128)(2,1)}, u32[]{:S(2)}, u32[]{:S(2)}) %collective-permute-start.15) | collective-permute-done | bytes 393248 | tf_op jit(solution)/shard_map/ppermute | solution.py:23
  128.5 5.5 %backward.2 = (bf16[3,128,768]{2,1,0:T(8,128)(2,1)S(1)}, bf16[3,128,768]{2,1,0:T(8,128)(2,1)S(1)}) custom-call(bf16[3,128,1536]{2,1,0:T(8,128)(2,1)S(1)} %pad_maximum_fusion.2.own, bf16[2,128,1536]{2,1,0:T(8,128)(2,1)S(1)} %copy-done.1, bf16[1,128,1536]{2,1,0:T(8,128)(2,1)S(1)} %copy-done.6, f32[256,768]{1,0:T(8,128)S(1)} %get-tuple-element.43.refs_0_, ...), custom_call_target="tpu_custom_call" | custom-call | flops 1024 | bytes 1024 | tf_op jit(solution)/shard_map/backward/pallas_call | solution.py:107
  134.0 0.6 collective-permute-start.17
  134.6 0.1 broadcast_in_dim.8.clone
  134.7 0.1 broadcast_in_dim.8.clone.1
  134.8 0.1 broadcast_in_dim.8.clone.2
  134.9 14.0 %collective-permute-done.16.refs_1_ = bf16[256,768]{1,0:T(8,128)(2,1)S(1)} collective-permute-done((bf16[256,768]{1,0:T(8,128)(2,1)S(1)}, bf16[256,768]{1,0:T(8,128)(2,1)S(1)}, u32[]{:S(2)}, u32[]{:S(2)}) %collective-permute-start.16) | collective-permute-done | bytes 393248 | tf_op jit(solution)/shard_map/ppermute | solution.py:23
  148.9 4.7 %backward.3 = (bf16[3,128,768]{2,1,0:T(8,128)(2,1)S(1)}, bf16[3,128,768]{2,1,0:T(8,128)(2,1)S(1)}) custom-call(bf16[3,128,1536]{2,1,0:T(8,128)(2,1)S(1)} %pad_maximum_fusion.2.own, bf16[2,128,1536]{2,1,0:T(8,128)(2,1)S(1)} %copy-done.1, bf16[1,128,1536]{2,1,0:T(8,128)(2,1)S(1)} %copy-done.6, f32[256,768]{1,0:T(8,128)S(1)} %get-tuple-element.45.refs_0_, ...), custom_call_target="tpu_custom_call" | custom-call | flops 1024 | bytes 1024 | tf_op jit(solution)/shard_map/backward/pallas_call | solution.py:107
  153.6 0.6 collective-permute-start.18
  154.1 0.1 slice_dynamic-update-slice_fusion.6
  154.2 1.9 %convert_add_fusion = f32[2,384,1024]{2,1,0:T(8,128)S(1)} fusion(f32[2,384,1024]{2,1,0:T(8,128)S(1)} %get-tuple-element.48, bf16[2,384,1024]{2,1,0:T(8,128)(2,1)} %collective-permute-done.19), kind=kLoop, calls=%fused_computation | loop fusion | flops 1572864 | bytes 7864320 | tf_op jit(solution)/shard_map/add | solution.py:392
  156.2 0.1 dynamic-slice_convert_fusion
  156.3 0.1 collective-permute-start.21
  156.4 0.3 convert_add_fusion.1
  156.7 0.6 collective-permute-start.22
  157.3 0.1 slice_dynamic-update-slice_fusion.1
  157.4 10.6 %collective-permute-done.18 = bf16[3,128,768]{2,1,0:T(8,128)(2,1)S(1)} collective-permute-done((bf16[3,128,768]{2,1,0:T(8,128)(2,1)S(1)}, bf16[3,128,768]{2,1,0:T(8,128)(2,1)S(1)}, u32[]{:S(2)}, u32[]{:S(2)}) %collective-permute-start.18) | collective-permute-done | bytes 589856 | tf_op jit(solution)/shard_map/ppermute | solution.py:23
  168.0 0.1 slice_dynamic-update-slice_fusion
  168.1 0.1 add_bitcast_fusion.1
  168.3 6.4 %collective-permute-done.21 = bf16[1,384,1024]{2,1,0:T(8,128)(2,1)S(1)} collective-permute-done((bf16[1,384,1024]{2,1,0:T(8,128)(2,1)S(1)}, bf16[1,384,1024]{2,1,0:T(8,128)(2,1)S(1)}, u32[]{:S(2)}, u32[]{:S(2)}) %collective-permute-start.21) | collective-permute-done | bytes 786464 | tf_op jit(solution)/shard_map/ppermute | solution.py:23
  174.7 0.3 add_bitcast_fusion
  175.0 1.6 maximum_multiply_fusion
  (55 shorter events, 0.3 us)
Async XLA Ops:
  0.6 50.4 %collective-permute-start.10 = (bf16[384,1536]{1,0:T(8,128)(2,1)}, bf16[384,1536]{1,0:T(8,128)(2,1)}, u32[]{:S(2)}, u32[]{:S(2)}) collective-permute-start(bf16[384,1536]{1,0:T(8,128)(2,1)} %param.9), channel_id=1, source_target_pairs={{0,8},{8,0},{1,9},{9,1},{2,10},{10,2},{3,11},{11,3},{4,12},{12,4},... | collective-permute-start | bytes 3538952 | tf_op jit(solution)/shard_map/ppermute | solution.py:23
  3.7 47.3 %collective-permute-start.9 = (bf16[384,1536]{1,0:T(8,128)(2,1)}, bf16[384,1536]{1,0:T(8,128)(2,1)}, u32[]{:S(2)}, u32[]{:S(2)}) collective-permute-start(bf16[384,1536]{1,0:T(8,128)(2,1)} %param.9), channel_id=1, source_target_pairs={{0,4},{4,0},{1,5},{5,1},{2,6},{6,2},{3,7},{7,3},{8,12},{12,8},{9,1... | collective-permute-start | bytes 3538952 | tf_op jit(solution)/shard_map/ppermute | solution.py:23
  7.5 2.5 %copy-start.10 = (bf16[1,128,6144]{2,1,0:T(8,128)(2,1)S(1)}, bf16[1,128,6144]{2,1,0:T(8,128)(2,1)}, u32[]{:S(2)}) copy-start(bf16[1,128,6144]{2,1,0:T(8,128)(2,1)} %param.5) | copy-start | bytes 4718596
  8.5 28.9 %collective-permute-start = (bf16[2,128,1536]{2,1,0:T(8,128)(2,1)}, bf16[2,128,1536]{2,1,0:T(8,128)(2,1)S(1)}, u32[]{:S(2)}, u32[]{:S(2)}) collective-permute-start(bf16[2,128,1536]{2,1,0:T(8,128)(2,1)} %pad_maximum_fusion.3), channel_id=1, source_target_pairs={{0,1},{1,0},{2,3},{3,2},{4,5},{5,4},{6,7},{7,6},{8,9},{9,8},{10,11... | collective-permute-start | bytes 2359304 | tf_op jit(solution)/shard_map/ppermute | solution.py:23
  10.0 3.6 %copy-start.16 = (bf16[1,128,3072]{2,1,0:T(8,128)(2,1)S(1)}, bf16[1,128,3072]{2,1,0:T(8,128)(2,1)}, u32[]{:S(2)}) copy-start(bf16[1,128,3072]{2,1,0:T(8,128)(2,1)} %param.8) | copy-start | bytes 2359300
  11.0 3.5 %copy-start.11 = (bf16[1,128,1536]{2,1,0:T(8,128)(2,1)S(1)}, bf16[1,128,1536]{2,1,0:T(8,128)(2,1)}, u32[]{:S(2)}) copy-start(bf16[1,128,1536]{2,1,0:T(8,128)(2,1)} %get-tuple-element.67) | copy-start | bytes 1179652
  11.0 3.5 %copy-start.12 = (bf16[1,128,1536]{2,1,0:T(8,128)(2,1)S(1)}, bf16[1,128,1536]{2,1,0:T(8,128)(2,1)}, u32[]{:S(2)}) copy-start(bf16[1,128,1536]{2,1,0:T(8,128)(2,1)} %get-tuple-element.77) | copy-start | bytes 1179652
  11.0 35.0 %collective-permute-start.2 = (bf16[128,3072]{1,0:T(8,128)(2,1)S(1)}, bf16[128,3072]{1,0:T(8,128)(2,1)}, u32[]{:S(2)}, u32[]{:S(2)}) collective-permute-start(bf16[128,3072]{1,0:T(8,128)(2,1)S(1)} %get-tuple-element.60), channel_id=1, source_target_pairs={{0,16},{16,0},{1,17},{17,1},{2,18},{18,2},{3,19},{19,3},{4,20},{20... | collective-permute-start | bytes 2359304 | tf_op jit(solution)/shard_map/ppermute | solution.py:23
  13.7 22.2 %collective-permute-start.1 = (bf16[1,128,1536]{2,1,0:T(8,128)(2,1)S(1)}, bf16[1,128,1536]{2,1,0:T(8,128)(2,1)S(1)}, u32[]{:S(2)}, u32[]{:S(2)}) collective-permute-start(bf16[1,128,1536]{2,1,0:T(8,128)(2,1)S(1)} %get-tuple-element.62), channel_id=1, source_target_pairs={{0,1},{1,0},{2,3},{3,2},{4,5},{5,4},{6,7},{7,6},{8,9},{9,8},{10,11... | collective-permute-start | bytes 1179656 | tf_op jit(solution)/shard_map/ppermute | solution.py:23
  35.8 4.5 %copy-start.5 = (bf16[1,128,1536]{2,1,0:T(8,128)(2,1)}, bf16[1,128,1536]{2,1,0:T(8,128)(2,1)S(1)}, u32[]{:S(2)}) copy-start(bf16[1,128,1536]{2,1,0:T(8,128)(2,1)S(1)} %collective-permute-done.1.far_values) | copy-start | bytes 1179652
  35.9 20.8 %collective-permute-start.3 = (bf16[128,3072]{1,0:T(8,128)(2,1)}, bf16[128,3072]{1,0:T(8,128)(2,1)}, u32[]{:S(2)}, u32[]{:S(2)}) collective-permute-start(bf16[128,3072]{1,0:T(8,128)(2,1)} %get-tuple-element.39.refs_0_.own), channel_id=1, source_target_pairs={{0,1},{1,0},{2,3},{3,2},{4,5},{5,4},{6,7},{7,6},{8,9},{9,8},{10,11... | collective-permute-start | bytes 2359304 | tf_op jit(solution)/shard_map/ppermute | solution.py:23
  37.4 13.7 %copy-start = (bf16[2,128,1536]{2,1,0:T(8,128)(2,1)}, bf16[2,128,1536]{2,1,0:T(8,128)(2,1)S(1)}, u32[]{:S(2)}) copy-start(bf16[2,128,1536]{2,1,0:T(8,128)(2,1)S(1)} %collective-permute-done.far_both) | copy-start | bytes 2359300
  46.0 24.9 %collective-permute-start.4 = (bf16[128,3072]{1,0:T(8,128)(2,1)}, bf16[128,3072]{1,0:T(8,128)(2,1)}, u32[]{:S(2)}, u32[]{:S(2)}) collective-permute-start(bf16[128,3072]{1,0:T(8,128)(2,1)} %collective-permute-done.2.refs_2_.own), channel_id=1, source_target_pairs={{0,1},{1,0},{2,3},{3,2},{4,5},{5,4},{6,7},{7,6},{8,9},{9,8},{10,11... | collective-permute-start | bytes 2359304 | tf_op jit(solution)/shard_map/ppermute | solution.py:23
  47.5 37.0 %collective-permute-start.6 = (bf16[256,1536]{1,0:T(8,128)(2,1)}, bf16[256,1536]{1,0:T(8,128)(2,1)}, u32[]{:S(2)}, u32[]{:S(2)}) collective-permute-start(bf16[256,1536]{1,0:T(8,128)(2,1)} %forward.1), channel_id=1, source_target_pairs={{0,16},{16,0},{1,17},{17,1},{2,18},{18,2},{3,19},{19,3},{4,20},{20... | collective-permute-start | bytes 2359304 | tf_op jit(solution)/shard_map/ppermute | solution.py:23
  52.9 47.7 %collective-permute-start.11 = (bf16[2,384,1536]{2,1,0:T(8,128)(2,1)S(1)}, bf16[2,384,1536]{2,1,0:T(8,128)(2,1)}, u32[]{:S(2)}, u32[]{:S(2)}) collective-permute-start(bf16[2,384,1536]{2,1,0:T(8,128)(2,1)S(1)} %pad_maximum_fusion.refs_2_), channel_id=1, source_target_pairs={{0,2},{2,0},{1,3},{3,1},{4,6},{6,4},{5,7},{7,5},{8,10},{10,8},{9,1... | collective-permute-start | bytes 7077896 | tf_op jit(solution)/shard_map/ppermute | solution.py:23
  54.1 33.2 %collective-permute-start.12 = (bf16[192,1536]{1,0:T(8,128)(2,1)S(1)}, bf16[192,1536]{1,0:T(8,128)(2,1)S(1)}, u32[]{:S(2)}, u32[]{:S(2)}) collective-permute-start(bf16[192,1536]{1,0:T(8,128)(2,1)S(1)} %slice.8), channel_id=1, source_target_pairs={{0,8},{8,0},{1,9},{9,1},{2,10},{10,2},{3,11},{11,3},{4,12},{12,4},... | collective-permute-start | bytes 1769480 | tf_op jit(solution)/shard_map/ppermute | solution.py:23
  56.6 31.1 %collective-permute-start.13 = (bf16[192,1536]{1,0:T(8,128)(2,1)S(1)}, bf16[192,1536]{1,0:T(8,128)(2,1)S(1)}, u32[]{:S(2)}, u32[]{:S(2)}) collective-permute-start(bf16[192,1536]{1,0:T(8,128)(2,1)S(1)} %slice.9), channel_id=1, source_target_pairs={{0,4},{4,0},{1,5},{5,1},{2,6},{6,2},{3,7},{7,3},{8,12},{12,8},{9,1... | collective-permute-start | bytes 1769480 | tf_op jit(solution)/shard_map/ppermute | solution.py:23
  75.0 12.3 %copy-start.2 = (bf16[4,384,512]{2,1,0:T(8,128)(2,1)}, bf16[4,384,512]{2,1,0:T(8,128)(2,1)S(1)}, u32[]{:S(2)}) copy-start(bf16[4,384,512]{2,1,0:T(8,128)(2,1)S(1)} %get-tuple-element.46.refs_0_) | copy-start | bytes 4718596
  75.0 14.1 %collective-permute-start.5 = (bf16[4,384,512]{2,1,0:T(8,128)(2,1)}, bf16[4,384,512]{2,1,0:T(8,128)(2,1)}, u32[]{:S(2)}, u32[]{:S(2)}) collective-permute-start(bf16[4,384,512]{2,1,0:T(8,128)(2,1)} %get-tuple-element.34), channel_id=1, source_target_pairs={{0,2},{2,0},{1,3},{3,1},{4,6},{6,4},{5,7},{7,5},{8,10},{10,8},{9,1... | collective-permute-start | bytes 4718600 | tf_op jit(solution)/shard_map/ppermute | solution.py:23
  87.2 3.8 %collective-permute-start.7 = (bf16[2,256,1536]{2,1,0:T(8,128)(2,1)}, bf16[2,256,1536]{2,1,0:T(8,128)(2,1)}, u32[]{:S(2)}, u32[]{:S(2)}) collective-permute-start(bf16[2,256,1536]{2,1,0:T(8,128)(2,1)} %pad_maximum_fusion.1.refs_2_), channel_id=1, source_target_pairs={{0,2},{2,0},{1,3},{3,1},{4,6},{6,4},{5,7},{7,5},{8,10},{10,8},{9,1... | collective-permute-start | bytes 4718600 | tf_op jit(solution)/shard_map/ppermute | solution.py:23
  87.2 13.3 %collective-permute-start.8 = (bf16[1,384,1536]{2,1,0:T(8,128)(2,1)}, bf16[1,384,1536]{2,1,0:T(8,128)(2,1)}, u32[]{:S(2)}, u32[]{:S(2)}) collective-permute-start(bf16[1,384,1536]{2,1,0:T(8,128)(2,1)} %bitcast.13.refs_0_), channel_id=1, source_target_pairs={{0,2},{2,0},{1,3},{3,1},{4,6},{6,4},{5,7},{7,5},{8,10},{10,8},{9,1... | collective-permute-start | bytes 3538952 | tf_op jit(solution)/shard_map/ppermute | solution.py:23
  88.9 11.7 %collective-permute-start.14 = (bf16[1,384,1536]{2,1,0:T(8,128)(2,1)}, bf16[1,384,1536]{2,1,0:T(8,128)(2,1)}, u32[]{:S(2)}, u32[]{:S(2)}) collective-permute-start(bf16[1,384,1536]{2,1,0:T(8,128)(2,1)} %maximum_bitcast_fusion.refs_4_), channel_id=1, source_target_pairs={{0,2},{2,0},{1,3},{3,1},{4,6},{6,4},{5,7},{7,5},{8,10},{10,8},{9,1... | collective-permute-start | bytes 3538952 | tf_op jit(solution)/shard_map/ppermute | solution.py:23
  91.0 1.4 copy-start.3
  98.1 0.9 copy-start.7
  99.0 55.2 %collective-permute-start.19 = (bf16[2,384,1024]{2,1,0:T(8,128)(2,1)}, bf16[2,384,1024]{2,1,0:T(8,128)(2,1)}, u32[]{:S(2)}, u32[]{:S(2)}) collective-permute-start(bf16[2,384,1024]{2,1,0:T(8,128)(2,1)} %get-tuple-element.37), channel_id=1, source_target_pairs={{0,4},{4,0},{1,5},{5,1},{2,6},{6,2},{3,7},{7,3},{8,12},{12,8},{9,1... | collective-permute-start | bytes 4718600 | tf_op jit(solution)/shard_map/ppermute | solution.py:23
  107.2 0.8 copy-start.8
  108.0 20.6 %collective-permute-start.15 = (bf16[256,768]{1,0:T(8,128)(2,1)}, bf16[256,768]{1,0:T(8,128)(2,1)}, u32[]{:S(2)}, u32[]{:S(2)}) collective-permute-start(bf16[256,768]{1,0:T(8,128)(2,1)} %get-tuple-element.44), channel_id=1, source_target_pairs={{0,16},{16,0},{1,17},{17,1},{2,18},{18,2},{3,19},{19,3},{4,20},{20... | collective-permute-start | bytes 1179656 | tf_op jit(solution)/shard_map/ppermute | solution.py:23
  108.1 9.4 %copy-start.4 = (bf16[4,384,512]{2,1,0:T(8,128)(2,1)S(1)}, bf16[4,384,512]{2,1,0:T(8,128)(2,1)}, u32[]{:S(2)}) copy-start(bf16[4,384,512]{2,1,0:T(8,128)(2,1)} %copy-done.2) | copy-start | bytes 4718596
  108.1 46.2 %collective-permute-start.20 = (bf16[2,384,512]{2,1,0:T(8,128)(2,1)}, bf16[2,384,512]{2,1,0:T(8,128)(2,1)S(1)}, u32[]{:S(2)}, u32[]{:S(2)}) collective-permute-start(bf16[2,384,512]{2,1,0:T(8,128)(2,1)} %copy-done.7), channel_id=1, source_target_pairs={{0,8},{8,0},{1,9},{9,1},{2,10},{10,2},{3,11},{11,3},{4,12},{12,4},... | collective-permute-start | bytes 2359304 | tf_op jit(solution)/shard_map/ppermute | solution.py:23
  117.4 11.1 %copy-start.9 = (bf16[256,768]{1,0:T(8,128)(2,1)S(1)}, bf16[256,768]{1,0:T(8,128)(2,1)}, u32[]{:S(2)}) copy-start(bf16[256,768]{1,0:T(8,128)(2,1)} %copy-done.8) | copy-start | bytes 1179652
  117.4 11.1 %copy-start.1 = (bf16[2,128,1536]{2,1,0:T(8,128)(2,1)S(1)}, bf16[2,128,1536]{2,1,0:T(8,128)(2,1)}, u32[]{:S(2)}) copy-start(bf16[2,128,1536]{2,1,0:T(8,128)(2,1)} %copy-done) | copy-start | bytes 2359300
  117.4 11.1 %copy-start.6 = (bf16[1,128,1536]{2,1,0:T(8,128)(2,1)S(1)}, bf16[1,128,1536]{2,1,0:T(8,128)(2,1)}, u32[]{:S(2)}) copy-start(bf16[1,128,1536]{2,1,0:T(8,128)(2,1)} %copy-done.5) | copy-start | bytes 1179652
  128.5 20.3 %collective-permute-start.16 = (bf16[256,768]{1,0:T(8,128)(2,1)S(1)}, bf16[256,768]{1,0:T(8,128)(2,1)S(1)}, u32[]{:S(2)}, u32[]{:S(2)}) collective-permute-start(bf16[256,768]{1,0:T(8,128)(2,1)S(1)} %copy-done.9), channel_id=1, source_target_pairs={{0,16},{16,0},{1,17},{17,1},{2,18},{18,2},{3,19},{19,3},{4,20},{20... | collective-permute-start | bytes 1179656 | tf_op jit(solution)/shard_map/ppermute | solution.py:23
  134.0 23.3 %collective-permute-start.17 = (bf16[3,128,768]{2,1,0:T(8,128)(2,1)S(1)}, bf16[3,128,768]{2,1,0:T(8,128)(2,1)S(1)}, u32[]{:S(2)}, u32[]{:S(2)}) collective-permute-start(bf16[3,128,768]{2,1,0:T(8,128)(2,1)S(1)} %get-tuple-element.56), channel_id=1, source_target_pairs={{0,1},{1,0},{2,3},{3,2},{4,5},{5,4},{6,7},{7,6},{8,9},{9,8},{10,11... | collective-permute-start | bytes 1769480 | tf_op jit(solution)/shard_map/ppermute | solution.py:23
  153.6 14.4 %collective-permute-start.18 = (bf16[3,128,768]{2,1,0:T(8,128)(2,1)S(1)}, bf16[3,128,768]{2,1,0:T(8,128)(2,1)S(1)}, u32[]{:S(2)}, u32[]{:S(2)}) collective-permute-start(bf16[3,128,768]{2,1,0:T(8,128)(2,1)S(1)} %get-tuple-element.57), channel_id=1, source_target_pairs={{0,1},{1,0},{2,3},{3,2},{4,5},{5,4},{6,7},{7,6},{8,9},{9,8},{10,11... | collective-permute-start | bytes 1769480 | tf_op jit(solution)/shard_map/ppermute | solution.py:23
  156.3 18.4 %collective-permute-start.21 = (bf16[1,384,1024]{2,1,0:T(8,128)(2,1)S(1)}, bf16[1,384,1024]{2,1,0:T(8,128)(2,1)S(1)}, u32[]{:S(2)}, u32[]{:S(2)}) collective-permute-start(bf16[1,384,1024]{2,1,0:T(8,128)(2,1)S(1)} %dynamic-slice_convert_fusion), channel_id=1, source_target_pairs={{0,8},{8,0},{1,9},{9,1},{2,10},{10,2},{3,11},{11,3},{4,12},{12,4},... | collective-permute-start | bytes 2359304 | tf_op jit(solution)/shard_map/ppermute | solution.py:23
  156.7 11.4 %collective-permute-start.22 = (bf16[1,384,512]{2,1,0:T(8,128)(2,1)S(1)}, bf16[1,384,512]{2,1,0:T(8,128)(2,1)S(1)}, u32[]{:S(2)}, u32[]{:S(2)}) collective-permute-start(bf16[1,384,512]{2,1,0:T(8,128)(2,1)S(1)} %dynamic-slice_convert_fusion.1), channel_id=1, source_target_pairs={{0,4},{4,0},{1,5},{5,1},{2,6},{6,2},{3,7},{7,3},{8,12},{12,8},{9,1... | collective-permute-start | bytes 1179656 | tf_op jit(solution)/shard_map/ppermute | solution.py:23
  168.1 6.9 %copy-start.13 = (bf16[1,128,3072]{2,1,0:T(8,128)(2,1)}, bf16[1,128,3072]{2,1,0:T(8,128)(2,1)S(1)}, u32[]{:S(2)}) copy-start(bf16[1,128,3072]{2,1,0:T(8,128)(2,1)S(1)} %get-tuple-element.70) | copy-start | bytes 2359300
  168.1 6.9 %copy-start.14 = (bf16[1,128,3072]{2,1,0:T(8,128)(2,1)}, bf16[1,128,3072]{2,1,0:T(8,128)(2,1)S(1)}, u32[]{:S(2)}) copy-start(bf16[1,128,3072]{2,1,0:T(8,128)(2,1)S(1)} %get-tuple-element.68) | copy-start | bytes 2359300
  168.1 6.9 %copy-start.15 = (bf16[1,128,3072]{2,1,0:T(8,128)(2,1)}, bf16[1,128,3072]{2,1,0:T(8,128)(2,1)S(1)}, u32[]{:S(2)}) copy-start(bf16[1,128,3072]{2,1,0:T(8,128)(2,1)S(1)} %get-tuple-element.69) | copy-start | bytes 2359300

commit v8 on v7

--- a/solution.py
+++ b/solution.py
@@ -377,6 +377,7 @@
         terms.append(returned(group, terms[group - 1], kept))
 
     stays, arrivals = [], []
+    second = []
     for group in range(groups):
         start = group * wide
         staying, leaving = backward(own, far, partial[group], after(terms[group], kept), start)
@@ -385,18 +386,20 @@
             sent = leaving[:, (by - 1) * tokens : by * tokens]
             column = ((mine + by) % seq) * features + start
             arrivals.append((column, shift(sent, "seq", -by)))
+        if group == 0:
+            for (_, axis), arrived, total in zip(orders, after(arrive, staying), kept):
+                for term in arrived:
+                    total = total + term.astype(jnp.float32)
+                passed = [part_of(total, axis, by, 0).astype(jnp.bfloat16) for by in others(axis)]
+                final = part_of(total, axis, 0, 0)
+                second.append((final, passed))
+            if groups > 1:
+                terms[1] = after(terms[1], [passed for _, passed in second])
 
     columns = []
-    for (_, axis), arrived, total in zip(orders, after(arrive, [array for _, array in stays]), kept):
-        for term in arrived:
-            total = total + term.astype(jnp.float32)
-        second = [
-            shift(part_of(total, axis, by, 0).astype(jnp.bfloat16), axis, by)
-            for by in others(axis)
-        ]
-        final = part_of(total, axis, 0, 0)
-        for term in second:
-            final = final + term.astype(jnp.float32)
+    for (_, axis), (final, passed) in zip(orders, second):
+        for by, term in zip(others(axis), passed):
+            final = final + shift(term, axis, by).astype(jnp.float32)
         columns.append(final[0])
     weight_grad = jnp.concatenate(columns, axis=1) * token_scale
 

time: 177 us -> 185 us (1.045)
  waiting for transfers between devices: 90.5 us -> 99.3 us
    ppermute x23, waiting for transfers between devices: 90.5 us -> 99.3 us  [shift(): lax.ppermute(array, axis, [(i, (i + by) % count) for i in range(count)])]
    unnamed x34 -> x42, local copies, waits for them, and re-layouts: 3.1 us -> 5.27 us
  transfers between devices with their start and end apart: 23 -> 23, of which waited for: 10 -> 11; matrix products, arithmetic and copies ran while one was open for 9% -> 5% of each run, Pallas kernels for 23% -> 22%
where the time goes in v8:
time: 185 us; the launch traced here: 184 us
  waiting for transfers between devices  99.3 us (54%)
  Pallas kernels  40.6 us (22%)
  starting transfers between devices  23.9 us (13%)
  other arithmetic  10.2 us (6%)
  local copies, waits for them, and re-layouts  9.42 us (5%)
    ppermute x23, waiting for transfers between devices, shift(): lax.ppermute(array, axis, [(i, (i + by) % count) for i in range(count)])  99.3 us
    pallas_call x8, Pallas kernels, whole_call(): pl.pallas_call(kernel, in_specs=in_specs, out_specs=jax.tree.map(lambda _...  40.6 us
    ppermute x23, starting transfers between devices, shift(): lax.ppermute(array, axis, [(i, (i + by) % count) for i in range(count)])  23.9 us
    unnamed x42, local copies, waits for them, and re-layouts  5.27 us
  transfers between devices with their start and end apart: 23, of which 11 were waited for; matrix products, arithmetic and copies ran while one was open for 5% of the time, Pallas kernels for 22%

profile of v8, /device:TPU:0, one launch (start us, length us, event | category | flops | bytes accessed | tf_op | source)
XLA Modules:
  0.0 184.4 jit_solution(9386415112000145448)
XLA Ops:
  0.7 2.3 %constant_dynamic-slice_fusion.1 = (bf16[1,128,1536]{2,1,0:T(8,128)(2,1)S(1)}, bf16[1,128,1536]{2,1,0:T(8,128)(2,1)}, bf16[1,128,1536]{2,1,0:T(8,128)(2,1)}, bf16[1,128,1536]{2,1,0:T(8,128)(2,1)S(1)}) fusion(bf16[1,128,3072]{2,1,0:T(8,128)(2,1)} %param.7, s32[]{:T(128)S(6)} %select_n.162, s32[]{:T(128)S(6)} %select_n.160, bf16[1,128,3072]{2,1,0:T(8,128)(2,1)} %param.6), kind=kLoop, calls=%fused_computation.27 | loop fusion | bytes 3145736 | tf_op jit(solution)/shard_map/dynamic_slice | solution.py:34
  3.0 0.9 pad_maximum_fusion.3
  3.9 3.0 %collective-permute-start = (bf16[2,128,1536]{2,1,0:T(8,128)(2,1)}, bf16[2,128,1536]{2,1,0:T(8,128)(2,1)S(1)}, u32[]{:S(2)}, u32[]{:S(2)}) collective-permute-start(bf16[2,128,1536]{2,1,0:T(8,128)(2,1)} %pad_maximum_fusion.3), channel_id=1, source_target_pairs={{0,1},{1,0},{2,3},{3,2},{4,5},{5,4},{6,7},{7,6},{8,9},{9,8},{10,11... | collective-permute-start | bytes 2359304 | tf_op jit(solution)/shard_map/ppermute | solution.py:23
  6.9 1.0 dynamic-slice_bitcast_fusion
  7.9 2.6 %collective-permute-start.2 = (bf16[128,3072]{1,0:T(8,128)(2,1)S(1)}, bf16[128,3072]{1,0:T(8,128)(2,1)}, u32[]{:S(2)}, u32[]{:S(2)}) collective-permute-start(bf16[128,3072]{1,0:T(8,128)(2,1)S(1)} %get-tuple-element.62), channel_id=1, source_target_pairs={{0,16},{16,0},{1,17},{17,1},{2,18},{18,2},{3,19},{19,3},{4,20},{20... | collective-permute-start | bytes 2359304 | tf_op jit(solution)/shard_map/ppermute | solution.py:23
  10.5 1.6 collective-permute-start.10
  12.1 1.5 collective-permute-start.9
  13.6 0.8 collective-permute-start.1
  14.4 0.1 pad_maximum_fusion.2.own
  14.6 18.5 %collective-permute-done.1.far_values = bf16[1,128,1536]{2,1,0:T(8,128)(2,1)S(1)} collective-permute-done((bf16[1,128,1536]{2,1,0:T(8,128)(2,1)S(1)}, bf16[1,128,1536]{2,1,0:T(8,128)(2,1)S(1)}, u32[]{:S(2)}, u32[]{:S(2)}) %collective-permute-start.1) | collective-permute-done | bytes 393248 | tf_op jit(solution)/shard_map/ppermute | solution.py:23
  33.1 1.7 collective-permute-start.3
  34.8 2.9 %forward.1 = bf16[256,1536]{1,0:T(8,128)(2,1)} custom-call(bf16[3,128,1536]{2,1,0:T(8,128)(2,1)S(1)} %pad_maximum_fusion.2.own, bf16[2,128,1536]{2,1,0:T(8,128)(2,1)S(1)} %collective-permute-done.far_both, bf16[1,128,1536]{2,1,0:T(8,128)(2,1)S(1)} %collective-permute-done.1.far_values), custom_call_target="tpu_custom_call" | custom-call | flops 1024 | bytes 1024 | tf_op jit(solution)/shard_map/forward/pallas_call | solution.py:107
  37.8 7.1 %collective-permute-done.2.refs_2_.own = bf16[128,3072]{1,0:T(8,128)(2,1)} collective-permute-done((bf16[128,3072]{1,0:T(8,128)(2,1)S(1)}, bf16[128,3072]{1,0:T(8,128)(2,1)}, u32[]{:S(2)}, u32[]{:S(2)}) %collective-permute-start.2) | collective-permute-done | bytes 786464 | tf_op jit(solution)/shard_map/ppermute | solution.py:23
  44.9 1.0 collective-permute-start.4
  45.9 13.7 %collective-permute-done.10 = bf16[384,1536]{1,0:T(8,128)(2,1)S(1)} collective-permute-done((bf16[384,1536]{1,0:T(8,128)(2,1)}, bf16[384,1536]{1,0:T(8,128)(2,1)S(1)}, u32[]{:S(2)}, u32[]{:S(2)}) %collective-permute-start.10) | collective-permute-done | bytes 1179680 | tf_op jit(solution)/shard_map/ppermute | solution.py:23
  59.6 0.2 pad_maximum_fusion.refs_2_
  59.8 0.8 copy-done.10
  60.6 0.4 copy-done.12
  61.0 8.1 %collective-permute-done.4.refs_3_.far = bf16[128,3072]{1,0:T(8,128)(2,1)} collective-permute-done((bf16[128,3072]{1,0:T(8,128)(2,1)}, bf16[128,3072]{1,0:T(8,128)(2,1)}, u32[]{:S(2)}, u32[]{:S(2)}) %collective-permute-start.4) | collective-permute-done | bytes 786464 | tf_op jit(solution)/shard_map/ppermute | solution.py:23
  69.1 4.0 %turn.1 = (bf16[4,384,512]{2,1,0:T(8,128)(2,1)S(1)}, bf16[4,384,512]{2,1,0:T(8,128)(2,1)}) custom-call(s32[1]{0:T(128)} %bitcast.10.core_ref, bf16[128,3072]{1,0:T(8,128)(2,1)} %get-tuple-element.40.refs_0_.own, bf16[128,3072]{1,0:T(8,128)(2,1)} %collective-permute-done.3.refs_1_.far, bf16[128,3072]{1,0:T(8,128)(2,1)} %collective-permute-done.2.refs_2_.own, ...), custom_call_target="tpu_custom_call" | custom-call | flops 1024 | bytes 1024 | tf_op jit(solution)/shard_map/turn/pallas_call | solution.py:107
  73.1 9.0 %collective-permute-done.6 = bf16[256,1536]{1,0:T(8,128)(2,1)} collective-permute-done((bf16[256,1536]{1,0:T(8,128)(2,1)}, bf16[256,1536]{1,0:T(8,128)(2,1)}, u32[]{:S(2)}, u32[]{:S(2)}) %collective-permute-start.6) | collective-permute-done | bytes 786464 | tf_op jit(solution)/shard_map/ppermute | solution.py:23
  82.1 2.8 %pad_maximum_fusion.1.refs_2_ = bf16[2,256,1536]{2,1,0:T(8,128)(2,1)} fusion(bf16[1,256,1536]{2,1,0:T(8,128)(2,1)} %bitcast.12, bf16[1,256,1536]{2,1,0:T(8,128)(2,1)} %bitcast.11), kind=kLoop, calls=%fused_computation.3 | loop fusion | flops 786432 | bytes 3145728 | tf_op jit(solution)/shard_map/stack | solution.py:328
  85.0 1.8 collective-permute-start.12
  86.8 1.6 collective-permute-start.13
  88.4 12.4 %collective-permute-done.12 = bf16[192,1536]{1,0:T(8,128)(2,1)S(1)} collective-permute-done((bf16[192,1536]{1,0:T(8,128)(2,1)S(1)}, bf16[192,1536]{1,0:T(8,128)(2,1)S(1)}, u32[]{:S(2)}, u32[]{:S(2)}) %collective-permute-start.12) | collective-permute-done | bytes 589856 | tf_op jit(solution)/shard_map/ppermute | solution.py:23
  100.8 1.5 collective-permute-done.13
  102.3 1.2 maximum_bitcast_fusion.refs_4_
  103.5 0.1 pad_add_fusion.at_ref
  103.6 1.4 copy-done.3
  105.0 5.7 %rows.2 = (bf16[2,384,1024]{2,1,0:T(8,128)(2,1)}, bf16[2,384,512]{2,1,0:T(8,128)(2,1)S(1)}) custom-call(s32[4]{0:T(128)S(1)} %pad_add_fusion.at_ref, bf16[4,384,512]{2,1,0:T(8,128)(2,1)S(1)} %copy-done.3, bf16[4,384,512]{2,1,0:T(8,128)(2,1)} %collective-permute-done.5.refs_1_, bf16[2,256,1536]{2,1,0:T(8,128)(2,1)} %pad_maximum_fusion.1.refs_2_, ...), custom_call_target="tpu_custom_call" | custom-call | flops 1024 | bytes 1024 | tf_op jit(solution)/shard_map/rows/pallas_call | solution.py:107
  110.7 0.9 copy-done.7
  111.6 1.5 collective-permute-start.17
  113.1 0.1 stack.70.at_ref
  113.2 6.6 %partial.3 = (bf16[256,768]{1,0:T(8,128)(2,1)}, bf16[256,768]{1,0:T(8,128)(2,1)S(1)}) custom-call(s32[8]{0:T(128)S(1)} %stack.70.at_ref, bf16[128,3072]{1,0:T(8,128)(2,1)} %collective-permute-done.2.refs_2_.own, bf16[128,3072]{1,0:T(8,128)(2,1)} %collective-permute-done.4.refs_3_.far, bf16[1,384,1536]{2,1,0:T(8,128)(2,1)} %bitcast.13.refs_0_, ...), custom_call_target="tpu_custom_call" | custom-call | flops 1024 | bytes 1024 | tf_op jit(solution)/shard_map/partial/pallas_call | solution.py:107
  119.8 0.7 copy-done.8
  120.5 3.4 %collective-permute-start.15 = (bf16[256,768]{1,0:T(8,128)(2,1)}, bf16[256,768]{1,0:T(8,128)(2,1)}, u32[]{:S(2)}, u32[]{:S(2)}) collective-permute-start(bf16[256,768]{1,0:T(8,128)(2,1)} %get-tuple-element.45), channel_id=1, source_target_pairs={{0,16},{16,0},{1,17},{17,1},{2,18},{18,2},{3,19},{19,3},{4,20},{20... | collective-permute-start | bytes 1179656 | tf_op jit(solution)/shard_map/ppermute | solution.py:23
  123.9 0.7 collective-permute-start.18
  124.6 0.1 pad_add_fusion.1.at_ref
  124.7 6.3 %partial.2 = (f32[256,768]{1,0:T(8,128)S(1)}, f32[256,768]{1,0:T(8,128)S(1)}) custom-call(s32[8]{0:T(128)S(1)} %stack.70.at_ref, bf16[128,3072]{1,0:T(8,128)(2,1)} %get-tuple-element.40.refs_0_.own, bf16[128,3072]{1,0:T(8,128)(2,1)} %collective-permute-done.3.refs_1_.far, bf16[1,384,1536]{2,1,0:T(8,128)(2,1)} %bitcast.13.refs_0_, ...), custom_call_target="tpu_custom_call" | custom-call | flops 1024 | bytes 1024 | tf_op jit(solution)/shard_map/partial/pallas_call | solution.py:107
  131.0 5.1 %rows.3 = (f32[2,384,1024]{2,1,0:T(8,128)S(1)}, f32[2,384,512]{2,1,0:T(8,128)S(1)}) custom-call(s32[4]{0:T(128)S(1)} %pad_add_fusion.1.at_ref, bf16[4,384,512]{2,1,0:T(8,128)(2,1)S(1)} %copy-done.4, bf16[4,384,512]{2,1,0:T(8,128)(2,1)} %collective-permute-done.5.refs_1_, bf16[2,256,1536]{2,1,0:T(8,128)(2,1)} %pad_maximum_fusion.1.refs_2_, ...), custom_call_target="tpu_custom_call" | custom-call | flops 1024 | bytes 1024 | tf_op jit(solution)/shard_map/rows/pallas_call | solution.py:107
  136.1 5.9 %collective-permute-done.15.refs_1_ = bf16[256,768]{1,0:T(8,128)(2,1)} collective-permute-done((bf16[256,768]{1,0:T(8,128)(2,1)}, bf16[256,768]{1,0:T(8,128)(2,1)}, u32[]{:S(2)}, u32[]{:S(2)}) %collective-permute-start.15) | collective-permute-done | bytes 393248 | tf_op jit(solution)/shard_map/ppermute | solution.py:23
  142.0 5.5 %backward.2 = (bf16[3,128,768]{2,1,0:T(8,128)(2,1)S(1)}, bf16[3,128,768]{2,1,0:T(8,128)(2,1)S(1)}) custom-call(bf16[3,128,1536]{2,1,0:T(8,128)(2,1)S(1)} %pad_maximum_fusion.2.own, bf16[2,128,1536]{2,1,0:T(8,128)(2,1)S(1)} %copy-done.1, bf16[1,128,1536]{2,1,0:T(8,128)(2,1)S(1)} %copy-done.6, f32[256,768]{1,0:T(8,128)S(1)} %get-tuple-element.44.refs_0_, ...), custom_call_target="tpu_custom_call" | custom-call | flops 1024 | bytes 1024 | tf_op jit(solution)/shard_map/backward/pallas_call | solution.py:107
  147.5 1.1 collective-permute-start.19
  148.6 0.1 broadcast_in_dim.8.clone
  148.7 0.1 broadcast_in_dim.8.clone.1
  148.8 0.1 broadcast_in_dim.8.clone.2
  148.9 7.8 %collective-permute-done.18 = bf16[2,384,512]{2,1,0:T(8,128)(2,1)S(1)} collective-permute-done((bf16[2,384,512]{2,1,0:T(8,128)(2,1)}, bf16[2,384,512]{2,1,0:T(8,128)(2,1)S(1)}, u32[]{:S(2)}, u32[]{:S(2)}) %collective-permute-start.18) | collective-permute-done | bytes 786464 | tf_op jit(solution)/shard_map/ppermute | solution.py:23
  156.7 0.3 convert_add_fusion.1
  157.0 0.1 dynamic-slice_convert_fusion.1
  157.0 0.6 collective-permute-start.22
  157.6 2.4 %convert_add_fusion = f32[2,384,1024]{2,1,0:T(8,128)S(1)} fusion(f32[2,384,1024]{2,1,0:T(8,128)S(1)} %get-tuple-element.49, bf16[2,384,1024]{2,1,0:T(8,128)(2,1)} %collective-permute-done.17), kind=kLoop, calls=%fused_computation | loop fusion | flops 1572864 | bytes 7864320 | tf_op jit(solution)/shard_map/add | solution.py:392
  160.0 0.1 dynamic-slice_convert_fusion
  160.1 0.1 collective-permute-start.21
  160.2 2.3 %collective-permute-done.16.refs_1_ = bf16[256,768]{1,0:T(8,128)(2,1)S(1)} collective-permute-done((bf16[256,768]{1,0:T(8,128)(2,1)S(1)}, bf16[256,768]{1,0:T(8,128)(2,1)S(1)}, u32[]{:S(2)}, u32[]{:S(2)}) %collective-permute-start.16) | collective-permute-done | bytes 393248 | tf_op jit(solution)/shard_map/ppermute | solution.py:23
  162.5 4.5 %backward.3 = (bf16[3,128,768]{2,1,0:T(8,128)(2,1)S(1)}, bf16[3,128,768]{2,1,0:T(8,128)(2,1)S(1)}) custom-call(bf16[3,128,1536]{2,1,0:T(8,128)(2,1)S(1)} %pad_maximum_fusion.2.own, bf16[2,128,1536]{2,1,0:T(8,128)(2,1)S(1)} %copy-done.1, bf16[1,128,1536]{2,1,0:T(8,128)(2,1)S(1)} %copy-done.6, f32[256,768]{1,0:T(8,128)S(1)} %get-tuple-element.46.refs_0_, ...), custom_call_target="tpu_custom_call" | custom-call | flops 1024 | bytes 1024 | tf_op jit(solution)/shard_map/backward/pallas_call | solution.py:107
  167.0 1.1 collective-permute-start.20
  168.1 0.1 slice_dynamic-update-slice_fusion.1
  168.2 0.1 add_bitcast_fusion.1
  168.3 13.0 %collective-permute-done.20 = bf16[3,128,768]{2,1,0:T(8,128)(2,1)S(1)} collective-permute-done((bf16[3,128,768]{2,1,0:T(8,128)(2,1)S(1)}, bf16[3,128,768]{2,1,0:T(8,128)(2,1)S(1)}, u32[]{:S(2)}, u32[]{:S(2)}) %collective-permute-start.20) | collective-permute-done | bytes 589856 | tf_op jit(solution)/shard_map/ppermute | solution.py:23
  181.5 0.3 add_bitcast_fusion
  181.8 0.5 copy-done.17
  182.3 0.3 copy-done.18
  182.6 0.3 copy-done.19
  182.8 1.6 maximum_multiply_fusion
  (63 shorter events, 0.4 us)
Async XLA Ops:
  3.0 3.9 %copy-start.14 = (bf16[1,128,6144]{2,1,0:T(8,128)(2,1)S(1)}, bf16[1,128,6144]{2,1,0:T(8,128)(2,1)}, u32[]{:S(2)}) copy-start(bf16[1,128,6144]{2,1,0:T(8,128)(2,1)} %param.5) | copy-start | bytes 4718596
  3.9 30.9 %collective-permute-start = (bf16[2,128,1536]{2,1,0:T(8,128)(2,1)}, bf16[2,128,1536]{2,1,0:T(8,128)(2,1)S(1)}, u32[]{:S(2)}, u32[]{:S(2)}) collective-permute-start(bf16[2,128,1536]{2,1,0:T(8,128)(2,1)} %pad_maximum_fusion.3), channel_id=1, source_target_pairs={{0,1},{1,0},{2,3},{3,2},{4,5},{5,4},{6,7},{7,6},{8,9},{9,8},{10,11... | collective-permute-start | bytes 2359304 | tf_op jit(solution)/shard_map/ppermute | solution.py:23
  6.9 6.7 %copy-start.20 = (bf16[1,128,3072]{2,1,0:T(8,128)(2,1)S(1)}, bf16[1,128,3072]{2,1,0:T(8,128)(2,1)}, u32[]{:S(2)}) copy-start(bf16[1,128,3072]{2,1,0:T(8,128)(2,1)} %param.8) | copy-start | bytes 2359300
  7.9 6.5 %copy-start.15 = (bf16[1,128,1536]{2,1,0:T(8,128)(2,1)S(1)}, bf16[1,128,1536]{2,1,0:T(8,128)(2,1)}, u32[]{:S(2)}) copy-start(bf16[1,128,1536]{2,1,0:T(8,128)(2,1)} %get-tuple-element.69) | copy-start | bytes 1179652
  7.9 6.5 %copy-start.16 = (bf16[1,128,1536]{2,1,0:T(8,128)(2,1)S(1)}, bf16[1,128,1536]{2,1,0:T(8,128)(2,1)}, u32[]{:S(2)}) copy-start(bf16[1,128,1536]{2,1,0:T(8,128)(2,1)} %get-tuple-element.79) | copy-start | bytes 1179652
  7.9 37.0 %collective-permute-start.2 = (bf16[128,3072]{1,0:T(8,128)(2,1)S(1)}, bf16[128,3072]{1,0:T(8,128)(2,1)}, u32[]{:S(2)}, u32[]{:S(2)}) collective-permute-start(bf16[128,3072]{1,0:T(8,128)(2,1)S(1)} %get-tuple-element.62), channel_id=1, source_target_pairs={{0,16},{16,0},{1,17},{17,1},{2,18},{18,2},{3,19},{19,3},{4,20},{20... | collective-permute-start | bytes 2359304 | tf_op jit(solution)/shard_map/ppermute | solution.py:23
  10.5 49.1 %collective-permute-start.10 = (bf16[384,1536]{1,0:T(8,128)(2,1)}, bf16[384,1536]{1,0:T(8,128)(2,1)S(1)}, u32[]{:S(2)}, u32[]{:S(2)}) collective-permute-start(bf16[384,1536]{1,0:T(8,128)(2,1)} %param.9), channel_id=1, source_target_pairs={{0,8},{8,0},{1,9},{9,1},{2,10},{10,2},{3,11},{11,3},{4,12},{12,4},... | collective-permute-start | bytes 3538952 | tf_op jit(solution)/shard_map/ppermute | solution.py:23
  12.1 47.5 %collective-permute-start.9 = (bf16[384,1536]{1,0:T(8,128)(2,1)}, bf16[384,1536]{1,0:T(8,128)(2,1)S(1)}, u32[]{:S(2)}, u32[]{:S(2)}) collective-permute-start(bf16[384,1536]{1,0:T(8,128)(2,1)} %param.9), channel_id=1, source_target_pairs={{0,4},{4,0},{1,5},{5,1},{2,6},{6,2},{3,7},{7,3},{8,12},{12,8},{9,1... | collective-permute-start | bytes 3538952 | tf_op jit(solution)/shard_map/ppermute | solution.py:23
  13.6 19.5 %collective-permute-start.1 = (bf16[1,128,1536]{2,1,0:T(8,128)(2,1)S(1)}, bf16[1,128,1536]{2,1,0:T(8,128)(2,1)S(1)}, u32[]{:S(2)}, u32[]{:S(2)}) collective-permute-start(bf16[1,128,1536]{2,1,0:T(8,128)(2,1)S(1)} %get-tuple-element.64), channel_id=1, source_target_pairs={{0,1},{1,0},{2,3},{3,2},{4,5},{5,4},{6,7},{7,6},{8,9},{9,8},{10,11... | collective-permute-start | bytes 1179656 | tf_op jit(solution)/shard_map/ppermute | solution.py:23
  33.1 4.7 %copy-start.5 = (bf16[1,128,1536]{2,1,0:T(8,128)(2,1)}, bf16[1,128,1536]{2,1,0:T(8,128)(2,1)S(1)}, u32[]{:S(2)}) copy-start(bf16[1,128,1536]{2,1,0:T(8,128)(2,1)S(1)} %collective-permute-done.1.far_values) | copy-start | bytes 1179652
  33.1 27.9 %collective-permute-start.3 = (bf16[128,3072]{1,0:T(8,128)(2,1)}, bf16[128,3072]{1,0:T(8,128)(2,1)}, u32[]{:S(2)}, u32[]{:S(2)}) collective-permute-start(bf16[128,3072]{1,0:T(8,128)(2,1)} %get-tuple-element.40.refs_0_.own), channel_id=1, source_target_pairs={{0,1},{1,0},{2,3},{3,2},{4,5},{5,4},{6,7},{7,6},{8,9},{9,8},{10,11... | collective-permute-start | bytes 2359304 | tf_op jit(solution)/shard_map/ppermute | solution.py:23
  34.8 24.7 %copy-start = (bf16[2,128,1536]{2,1,0:T(8,128)(2,1)}, bf16[2,128,1536]{2,1,0:T(8,128)(2,1)S(1)}, u32[]{:S(2)}) copy-start(bf16[2,128,1536]{2,1,0:T(8,128)(2,1)S(1)} %collective-permute-done.far_both) | copy-start | bytes 2359300
  44.9 24.2 %collective-permute-start.4 = (bf16[128,3072]{1,0:T(8,128)(2,1)}, bf16[128,3072]{1,0:T(8,128)(2,1)}, u32[]{:S(2)}, u32[]{:S(2)}) collective-permute-start(bf16[128,3072]{1,0:T(8,128)(2,1)} %collective-permute-done.2.refs_2_.own), channel_id=1, source_target_pairs={{0,1},{1,0},{2,3},{3,2},{4,5},{5,4},{6,7},{7,6},{8,9},{9,8},{10,11... | collective-permute-start | bytes 2359304 | tf_op jit(solution)/shard_map/ppermute | solution.py:23
  45.9 36.2 %collective-permute-start.6 = (bf16[256,1536]{1,0:T(8,128)(2,1)}, bf16[256,1536]{1,0:T(8,128)(2,1)}, u32[]{:S(2)}, u32[]{:S(2)}) collective-permute-start(bf16[256,1536]{1,0:T(8,128)(2,1)} %forward.1), channel_id=1, source_target_pairs={{0,16},{16,0},{1,17},{17,1},{2,18},{18,2},{3,19},{19,3},{4,20},{20... | collective-permute-start | bytes 2359304 | tf_op jit(solution)/shard_map/ppermute | solution.py:23
  59.6 1.0 copy-start.10
  59.6 1.4 copy-start.12
  61.0 52.2 %collective-permute-start.11 = (bf16[2,384,1536]{2,1,0:T(8,128)(2,1)S(1)}, bf16[2,384,1536]{2,1,0:T(8,128)(2,1)}, u32[]{:S(2)}, u32[]{:S(2)}) collective-permute-start(bf16[2,384,1536]{2,1,0:T(8,128)(2,1)S(1)} %pad_maximum_fusion.refs_2_), channel_id=1, source_target_pairs={{0,2},{2,0},{1,3},{3,1},{4,6},{6,4},{5,7},{7,5},{8,10},{10,8},{9,1... | collective-permute-start | bytes 7077896 | tf_op jit(solution)/shard_map/ppermute | solution.py:23
  73.1 11.8 %copy-start.2 = (bf16[4,384,512]{2,1,0:T(8,128)(2,1)}, bf16[4,384,512]{2,1,0:T(8,128)(2,1)S(1)}, u32[]{:S(2)}) copy-start(bf16[4,384,512]{2,1,0:T(8,128)(2,1)S(1)} %get-tuple-element.47.refs_0_) | copy-start | bytes 4718596
  73.1 30.4 %collective-permute-start.5 = (bf16[4,384,512]{2,1,0:T(8,128)(2,1)}, bf16[4,384,512]{2,1,0:T(8,128)(2,1)}, u32[]{:S(2)}, u32[]{:S(2)}) collective-permute-start(bf16[4,384,512]{2,1,0:T(8,128)(2,1)} %get-tuple-element.35), channel_id=1, source_target_pairs={{0,2},{2,0},{1,3},{3,1},{4,6},{6,4},{5,7},{7,5},{8,10},{10,8},{9,1... | collective-permute-start | bytes 4718600 | tf_op jit(solution)/shard_map/ppermute | solution.py:23
  82.1 2.8 %copy-start.13 = (bf16[384,1536]{1,0:T(8,128)(2,1)S(1)}, bf16[384,1536]{1,0:T(8,128)(2,1)}, u32[]{:S(2)}) copy-start(bf16[384,1536]{1,0:T(8,128)(2,1)} %copy-done.12) | copy-start | bytes 3538948
  82.1 4.7 %copy-start.11 = (bf16[384,1536]{1,0:T(8,128)(2,1)S(1)}, bf16[384,1536]{1,0:T(8,128)(2,1)}, u32[]{:S(2)}) copy-start(bf16[384,1536]{1,0:T(8,128)(2,1)} %copy-done.10) | copy-start | bytes 3538948
  84.9 18.6 %collective-permute-start.7 = (bf16[2,256,1536]{2,1,0:T(8,128)(2,1)}, bf16[2,256,1536]{2,1,0:T(8,128)(2,1)}, u32[]{:S(2)}, u32[]{:S(2)}) collective-permute-start(bf16[2,256,1536]{2,1,0:T(8,128)(2,1)} %pad_maximum_fusion.1.refs_2_), channel_id=1, source_target_pairs={{0,2},{2,0},{1,3},{3,1},{4,6},{6,4},{5,7},{7,5},{8,10},{10,8},{9,1... | collective-permute-start | bytes 4718600 | tf_op jit(solution)/shard_map/ppermute | solution.py:23
  85.0 15.8 %collective-permute-start.12 = (bf16[192,1536]{1,0:T(8,128)(2,1)S(1)}, bf16[192,1536]{1,0:T(8,128)(2,1)S(1)}, u32[]{:S(2)}, u32[]{:S(2)}) collective-permute-start(bf16[192,1536]{1,0:T(8,128)(2,1)S(1)} %slice.8), channel_id=1, source_target_pairs={{0,8},{8,0},{1,9},{9,1},{2,10},{10,2},{3,11},{11,3},{4,12},{12,4},... | collective-permute-start | bytes 1769480 | tf_op jit(solution)/shard_map/ppermute | solution.py:23
  86.8 15.5 %collective-permute-start.13 = (bf16[192,1536]{1,0:T(8,128)(2,1)S(1)}, bf16[192,1536]{1,0:T(8,128)(2,1)S(1)}, u32[]{:S(2)}, u32[]{:S(2)}) collective-permute-start(bf16[192,1536]{1,0:T(8,128)(2,1)S(1)} %slice.9), channel_id=1, source_target_pairs={{0,4},{4,0},{1,5},{5,1},{2,6},{6,2},{3,7},{7,3},{8,12},{12,8},{9,1... | collective-permute-start | bytes 1769480 | tf_op jit(solution)/shard_map/ppermute | solution.py:23
  100.8 12.4 %collective-permute-start.8 = (bf16[1,384,1536]{2,1,0:T(8,128)(2,1)}, bf16[1,384,1536]{2,1,0:T(8,128)(2,1)}, u32[]{:S(2)}, u32[]{:S(2)}) collective-permute-start(bf16[1,384,1536]{2,1,0:T(8,128)(2,1)} %bitcast.13.refs_0_), channel_id=1, source_target_pairs={{0,2},{2,0},{1,3},{3,1},{4,6},{6,4},{5,7},{7,5},{8,10},{10,8},{9,1... | collective-permute-start | bytes 3538952 | tf_op jit(solution)/shard_map/ppermute | solution.py:23
  103.5 9.7 %collective-permute-start.14 = (bf16[1,384,1536]{2,1,0:T(8,128)(2,1)}, bf16[1,384,1536]{2,1,0:T(8,128)(2,1)}, u32[]{:S(2)}, u32[]{:S(2)}) collective-permute-start(bf16[1,384,1536]{2,1,0:T(8,128)(2,1)} %maximum_bitcast_fusion.refs_4_), channel_id=1, source_target_pairs={{0,2},{2,0},{1,3},{3,1},{4,6},{6,4},{5,7},{7,5},{8,10},{10,8},{9,1... | collective-permute-start | bytes 3538952 | tf_op jit(solution)/shard_map/ppermute | solution.py:23
  103.6 1.4 copy-start.3
  110.7 0.9 copy-start.7
  111.6 45.1 %collective-permute-start.17 = (bf16[2,384,1024]{2,1,0:T(8,128)(2,1)}, bf16[2,384,1024]{2,1,0:T(8,128)(2,1)}, u32[]{:S(2)}, u32[]{:S(2)}) collective-permute-start(bf16[2,384,1024]{2,1,0:T(8,128)(2,1)} %get-tuple-element.38), channel_id=1, source_target_pairs={{0,4},{4,0},{1,5},{5,1},{2,6},{6,2},{3,7},{7,3},{8,12},{12,8},{9,1... | collective-permute-start | bytes 4718600 | tf_op jit(solution)/shard_map/ppermute | solution.py:23
  119.8 0.7 copy-start.8
  120.5 21.5 %collective-permute-start.15 = (bf16[256,768]{1,0:T(8,128)(2,1)}, bf16[256,768]{1,0:T(8,128)(2,1)}, u32[]{:S(2)}, u32[]{:S(2)}) collective-permute-start(bf16[256,768]{1,0:T(8,128)(2,1)} %get-tuple-element.45), channel_id=1, source_target_pairs={{0,16},{16,0},{1,17},{17,1},{2,18},{18,2},{3,19},{19,3},{4,20},{20... | collective-permute-start | bytes 1179656 | tf_op jit(solution)/shard_map/ppermute | solution.py:23
  123.9 32.7 %collective-permute-start.18 = (bf16[2,384,512]{2,1,0:T(8,128)(2,1)}, bf16[2,384,512]{2,1,0:T(8,128)(2,1)S(1)}, u32[]{:S(2)}, u32[]{:S(2)}) collective-permute-start(bf16[2,384,512]{2,1,0:T(8,128)(2,1)} %copy-done.7), channel_id=1, source_target_pairs={{0,8},{8,0},{1,9},{9,1},{2,10},{10,2},{3,11},{11,3},{4,12},{12,4},... | collective-permute-start | bytes 2359304 | tf_op jit(solution)/shard_map/ppermute | solution.py:23
  124.7 6.3 %copy-start.4 = (bf16[4,384,512]{2,1,0:T(8,128)(2,1)S(1)}, bf16[4,384,512]{2,1,0:T(8,128)(2,1)}, u32[]{:S(2)}) copy-start(bf16[4,384,512]{2,1,0:T(8,128)(2,1)} %copy-done.2) | copy-start | bytes 4718596
  131.0 11.0 %copy-start.9 = (bf16[256,768]{1,0:T(8,128)(2,1)S(1)}, bf16[256,768]{1,0:T(8,128)(2,1)}, u32[]{:S(2)}) copy-start(bf16[256,768]{1,0:T(8,128)(2,1)} %copy-done.8) | copy-start | bytes 1179652
  131.0 11.0 %copy-start.1 = (bf16[2,128,1536]{2,1,0:T(8,128)(2,1)S(1)}, bf16[2,128,1536]{2,1,0:T(8,128)(2,1)}, u32[]{:S(2)}) copy-start(bf16[2,128,1536]{2,1,0:T(8,128)(2,1)} %copy-done) | copy-start | bytes 2359300
  131.0 11.0 %copy-start.6 = (bf16[1,128,1536]{2,1,0:T(8,128)(2,1)S(1)}, bf16[1,128,1536]{2,1,0:T(8,128)(2,1)}, u32[]{:S(2)}) copy-start(bf16[1,128,1536]{2,1,0:T(8,128)(2,1)} %copy-done.5) | copy-start | bytes 1179652
  142.0 20.5 %collective-permute-start.16 = (bf16[256,768]{1,0:T(8,128)(2,1)S(1)}, bf16[256,768]{1,0:T(8,128)(2,1)S(1)}, u32[]{:S(2)}, u32[]{:S(2)}) collective-permute-start(bf16[256,768]{1,0:T(8,128)(2,1)S(1)} %copy-done.9), channel_id=1, source_target_pairs={{0,16},{16,0},{1,17},{17,1},{2,18},{18,2},{3,19},{19,3},{4,20},{20... | collective-permute-start | bytes 1179656 | tf_op jit(solution)/shard_map/ppermute | solution.py:23
  147.5 20.6 %collective-permute-start.19 = (bf16[3,128,768]{2,1,0:T(8,128)(2,1)S(1)}, bf16[3,128,768]{2,1,0:T(8,128)(2,1)S(1)}, u32[]{:S(2)}, u32[]{:S(2)}) collective-permute-start(bf16[3,128,768]{2,1,0:T(8,128)(2,1)S(1)} %get-tuple-element.60), channel_id=1, source_target_pairs={{0,1},{1,0},{2,3},{3,2},{4,5},{5,4},{6,7},{7,6},{8,9},{9,8},{10,11... | collective-permute-start | bytes 1769480 | tf_op jit(solution)/shard_map/ppermute | solution.py:23
  157.0 11.2 %collective-permute-start.22 = (bf16[1,384,512]{2,1,0:T(8,128)(2,1)S(1)}, bf16[1,384,512]{2,1,0:T(8,128)(2,1)S(1)}, u32[]{:S(2)}, u32[]{:S(2)}) collective-permute-start(bf16[1,384,512]{2,1,0:T(8,128)(2,1)S(1)} %dynamic-slice_convert_fusion.1), channel_id=1, source_target_pairs={{0,4},{4,0},{1,5},{5,1},{2,6},{6,2},{3,7},{7,3},{8,12},{12,8},{9,1... | collective-permute-start | bytes 1179656 | tf_op jit(solution)/shard_map/ppermute | solution.py:23
  160.1 21.3 %collective-permute-start.21 = (bf16[1,384,1024]{2,1,0:T(8,128)(2,1)S(1)}, bf16[1,384,1024]{2,1,0:T(8,128)(2,1)S(1)}, u32[]{:S(2)}, u32[]{:S(2)}) collective-permute-start(bf16[1,384,1024]{2,1,0:T(8,128)(2,1)S(1)} %dynamic-slice_convert_fusion), channel_id=1, source_target_pairs={{0,8},{8,0},{1,9},{9,1},{2,10},{10,2},{3,11},{11,3},{4,12},{12,4},... | collective-permute-start | bytes 2359304 | tf_op jit(solution)/shard_map/ppermute | solution.py:23
  167.0 14.4 %collective-permute-start.20 = (bf16[3,128,768]{2,1,0:T(8,128)(2,1)S(1)}, bf16[3,128,768]{2,1,0:T(8,128)(2,1)S(1)}, u32[]{:S(2)}, u32[]{:S(2)}) collective-permute-start(bf16[3,128,768]{2,1,0:T(8,128)(2,1)S(1)} %get-tuple-element.61), channel_id=1, source_target_pairs={{0,1},{1,0},{2,3},{3,2},{4,5},{5,4},{6,7},{7,6},{8,9},{9,8},{10,11... | collective-permute-start | bytes 1769480 | tf_op jit(solution)/shard_map/ppermute | solution.py:23
  181.4 0.9 copy-start.17
  181.4 1.1 copy-start.18
  181.4 1.4 copy-start.19

commit v9 on v8

--- a/solution.py
+++ b/solution.py
@@ -325,7 +325,7 @@
         shift(array, "core", by) for by, array in zip(others("core"), by_rows[1:])
     ]
 
-    pair = jnp.stack(after([attended] + attends, by_rows_here))
+    pair = jnp.stack(after([attended] + attends, by_rows_here, first, last))
     attends = [pair] + across(pair)
     first, last = after((first, last), pair)
     diagonal = jnp.stack(

time: 185 us -> 171 us (0.924)
  waiting for transfers between devices: 99.3 us -> 76.9 us
  local copies, waits for them, and re-layouts: 9.42 us -> 16.6 us
  other arithmetic: 10.2 us -> 12.9 us
    ppermute x23, waiting for transfers between devices: 99.3 us -> 76.9 us  [shift(): lax.ppermute(array, axis, [(i, (i + by) % count) for i in range(count)])]
    unnamed x42 -> x46, local copies, waits for them, and re-layouts: 5.27 us -> 9.55 us
    slice x1, local copies, waits for them, and re-layouts: 0.04 us -> 1.93 us  [shards(): block[:upper]]
    slice x1, local copies, waits for them, and re-layouts: 0.04 us -> 1.93 us  [shards(): block[upper:]]
  transfers between devices with their start and end apart: 23 -> 23, of which waited for: 11 -> 9; matrix products, arithmetic and copies ran while one was open for 5% -> 11% of each run, Pallas kernels for 22% -> 23%
where the time goes in v9:
time: 171 us
  waiting for transfers between devices  76.9 us (45%)
  Pallas kernels  39.8 us (23%)
  starting transfers between devices  23.6 us (14%)
  local copies, waits for them, and re-layouts  16.6 us (10%)
  other arithmetic  12.9 us (8%)
    ppermute x23, waiting for transfers between devices, shift(): lax.ppermute(array, axis, [(i, (i + by) % count) for i in range(count)])  76.9 us
    pallas_call x8, Pallas kernels, whole_call(): pl.pallas_call(kernel, in_specs=in_specs, out_specs=jax.tree.map(lambda _...  39.8 us
    ppermute x23, starting transfers between devices, shift(): lax.ppermute(array, axis, [(i, (i + by) % count) for i in range(count)])  23.6 us
    unnamed x46, local copies, waits for them, and re-layouts  9.55 us
  transfers between devices with their start and end apart: 23, of which 9 were waited for; matrix products, arithmetic and copies ran while one was open for 11% of the time, Pallas kernels for 23%

profile of v9, /device:TPU:0, one launch (start us, length us, event | category | flops | bytes accessed | tf_op | source)
XLA Modules:
  0.0 170.7 jit_solution(16241178997778375815)
XLA Ops:
  0.6 3.0 %collective-permute-start.7 = (bf16[384,1536]{1,0:T(8,128)(2,1)}, bf16[384,1536]{1,0:T(8,128)(2,1)}, u32[]{:S(2)}, u32[]{:S(2)}) collective-permute-start(bf16[384,1536]{1,0:T(8,128)(2,1)} %param.9), channel_id=1, source_target_pairs={{0,4},{4,0},{1,5},{5,1},{2,6},{6,2},{3,7},{7,3},{8,12},{12,8},{9,1... | collective-permute-start | bytes 3538952 | tf_op jit(solution)/shard_map/ppermute | solution.py:23
  3.6 1.6 collective-permute-start.9
  5.2 2.3 %constant_dynamic-slice_fusion.1 = (bf16[1,128,1536]{2,1,0:T(8,128)(2,1)S(1)}, bf16[1,128,1536]{2,1,0:T(8,128)(2,1)}, bf16[1,128,1536]{2,1,0:T(8,128)(2,1)}, bf16[1,128,1536]{2,1,0:T(8,128)(2,1)S(1)}) fusion(bf16[1,128,3072]{2,1,0:T(8,128)(2,1)} %param.7, s32[]{:T(128)S(6)} %select_n.162, s32[]{:T(128)S(6)} %select_n.160, bf16[1,128,3072]{2,1,0:T(8,128)(2,1)} %param.6), kind=kLoop, calls=%fused_computation.27 | loop fusion | bytes 3145736 | tf_op jit(solution)/shard_map/dynamic_slice | solution.py:34
  7.5 0.9 pad_maximum_fusion.3
  8.5 1.5 collective-permute-start
  10.0 0.1 dynamic-slice_bitcast_fusion
  10.2 2.7 %collective-permute-start.2 = (bf16[128,3072]{1,0:T(8,128)(2,1)S(1)}, bf16[128,3072]{1,0:T(8,128)(2,1)}, u32[]{:S(2)}, u32[]{:S(2)}) collective-permute-start(bf16[128,3072]{1,0:T(8,128)(2,1)S(1)} %get-tuple-element.62), channel_id=1, source_target_pairs={{0,16},{16,0},{1,17},{17,1},{2,18},{18,2},{3,19},{19,3},{4,20},{20... | collective-permute-start | bytes 2359304 | tf_op jit(solution)/shard_map/ppermute | solution.py:23
  12.9 0.8 collective-permute-start.1
  13.7 22.2 %collective-permute-done.1.far_values = bf16[1,128,1536]{2,1,0:T(8,128)(2,1)S(1)} collective-permute-done((bf16[1,128,1536]{2,1,0:T(8,128)(2,1)S(1)}, bf16[1,128,1536]{2,1,0:T(8,128)(2,1)S(1)}, u32[]{:S(2)}, u32[]{:S(2)}) %collective-permute-start.1) | collective-permute-done | bytes 393248 | tf_op jit(solution)/shard_map/ppermute | solution.py:23
  35.9 1.5 collective-permute-start.3
  37.4 0.1 pad_maximum_fusion.2.own
  37.5 3.0 %forward.1 = bf16[256,1536]{1,0:T(8,128)(2,1)} custom-call(bf16[3,128,1536]{2,1,0:T(8,128)(2,1)S(1)} %pad_maximum_fusion.2.own, bf16[2,128,1536]{2,1,0:T(8,128)(2,1)S(1)} %collective-permute-done.far_both, bf16[1,128,1536]{2,1,0:T(8,128)(2,1)S(1)} %collective-permute-done.1.far_values), custom_call_target="tpu_custom_call" | custom-call | flops 1024 | bytes 1024 | tf_op jit(solution)/shard_map/forward/pallas_call | solution.py:107
  40.6 6.6 %collective-permute-done.2.refs_2_.own = bf16[128,3072]{1,0:T(8,128)(2,1)} collective-permute-done((bf16[128,3072]{1,0:T(8,128)(2,1)S(1)}, bf16[128,3072]{1,0:T(8,128)(2,1)}, u32[]{:S(2)}, u32[]{:S(2)}) %collective-permute-start.2) | collective-permute-done | bytes 786464 | tf_op jit(solution)/shard_map/ppermute | solution.py:23
  47.2 1.5 collective-permute-start.4
  48.7 3.5 %collective-permute-start.6 = (bf16[256,1536]{1,0:T(8,128)(2,1)}, bf16[256,1536]{1,0:T(8,128)(2,1)}, u32[]{:S(2)}, u32[]{:S(2)}) collective-permute-start(bf16[256,1536]{1,0:T(8,128)(2,1)} %forward.1), channel_id=1, source_target_pairs={{0,16},{16,0},{1,17},{17,1},{2,18},{18,2},{3,19},{19,3},{4,20},{20... | collective-permute-start | bytes 2359304 | tf_op jit(solution)/shard_map/ppermute | solution.py:23
  52.2 1.9 %slice.8 = bf16[192,1536]{1,0:T(8,128)(2,1)} slice(bf16[384,1536]{1,0:T(8,128)(2,1)} %collective-permute-done.7), slice={[0:192], [0:1536]} | slice | bytes 1179648 | tf_op jit(solution)/shard_map/slice | solution.py:316
  54.2 0.1 collective-permute-start.8
  54.3 1.9 %slice.9 = bf16[192,1536]{1,0:T(8,128)(2,1)} slice(bf16[384,1536]{1,0:T(8,128)(2,1)} %collective-permute-done.9), slice={[192:384], [0:1536]} | slice | bytes 1179648 | tf_op jit(solution)/shard_map/slice | solution.py:317
  56.2 0.5 collective-permute-start.10
  56.7 1.8 %pad_maximum_fusion.refs_2_ = bf16[2,384,1536]{2,1,0:T(8,128)(2,1)S(1)} fusion(bf16[1,384,1536]{2,1,0:T(8,128)(2,1)} %bitcast.15, bf16[1,384,1536]{2,1,0:T(8,128)(2,1)} %bitcast.14), kind=kLoop, calls=%fused_computation.1 | loop fusion | flops 1179648 | bytes 4718592 | tf_op jit(solution)/shard_map/stack | solution.py:318
  58.6 0.9 copy-done.10
  59.5 11.2 %collective-permute-done.4.refs_3_.far = bf16[128,3072]{1,0:T(8,128)(2,1)} collective-permute-done((bf16[128,3072]{1,0:T(8,128)(2,1)}, bf16[128,3072]{1,0:T(8,128)(2,1)}, u32[]{:S(2)}, u32[]{:S(2)}) %collective-permute-start.4) | collective-permute-done | bytes 786464 | tf_op jit(solution)/shard_map/ppermute | solution.py:23
  70.7 1.1 copy-done.3
  71.8 1.1 copy-done.11
  73.0 3.6 %turn.1 = (bf16[4,384,512]{2,1,0:T(8,128)(2,1)S(1)}, bf16[4,384,512]{2,1,0:T(8,128)(2,1)}) custom-call(s32[1]{0:T(128)} %bitcast.10.core_ref, bf16[128,3072]{1,0:T(8,128)(2,1)S(1)} %copy-done.3, bf16[128,3072]{1,0:T(8,128)(2,1)S(1)} %copy-done.11, bf16[128,3072]{1,0:T(8,128)(2,1)} %collective-permute-done.2.refs_2_.own, ...), custom_call_target="tpu_custom_call" | custom-call | flops 1024 | bytes 1024 | tf_op jit(solution)/shard_map/turn/pallas_call | solution.py:107
  76.5 8.9 %collective-permute-done.6 = bf16[256,1536]{1,0:T(8,128)(2,1)} collective-permute-done((bf16[256,1536]{1,0:T(8,128)(2,1)}, bf16[256,1536]{1,0:T(8,128)(2,1)}, u32[]{:S(2)}, u32[]{:S(2)}) %collective-permute-start.6) | collective-permute-done | bytes 786464 | tf_op jit(solution)/shard_map/ppermute | solution.py:23
  85.5 2.7 %pad_maximum_fusion.1.refs_2_ = bf16[2,256,1536]{2,1,0:T(8,128)(2,1)} fusion(bf16[1,256,1536]{2,1,0:T(8,128)(2,1)} %bitcast.12, bf16[1,256,1536]{2,1,0:T(8,128)(2,1)} %bitcast.11), kind=kLoop, calls=%fused_computation.3 | loop fusion | flops 786432 | bytes 3145728 | tf_op jit(solution)/shard_map/stack | solution.py:328
  88.1 0.5 collective-permute-start.12
  88.7 2.4 %maximum_bitcast_fusion.refs_4_ = bf16[1,384,1536]{2,1,0:T(8,128)(2,1)} fusion(bf16[192,1536]{1,0:T(8,128)(2,1)} %collective-permute-done.10, bf16[192,1536]{1,0:T(8,128)(2,1)} %collective-permute-done.8), kind=kLoop, calls=%fused_computation.8 | loop fusion | flops 2359296 | bytes 2359296 | tf_op jit(solution)/shard_map/stack | solution.py:331
  91.1 0.1 pad_add_fusion.at_ref
  91.2 0.7 collective-permute-done.11.refs_3_
  91.9 1.4 copy-done.6
  93.3 5.7 %rows.2 = (bf16[2,384,1024]{2,1,0:T(8,128)(2,1)}, bf16[2,384,512]{2,1,0:T(8,128)(2,1)S(1)}) custom-call(s32[4]{0:T(128)S(1)} %pad_add_fusion.at_ref, bf16[4,384,512]{2,1,0:T(8,128)(2,1)S(1)} %copy-done.6, bf16[4,384,512]{2,1,0:T(8,128)(2,1)} %collective-permute-done.5.refs_1_, bf16[2,256,1536]{2,1,0:T(8,128)(2,1)} %pad_maximum_fusion.1.refs_2_, ...), custom_call_target="tpu_custom_call" | custom-call | flops 1024 | bytes 1024 | tf_op jit(solution)/shard_map/rows/pallas_call | solution.py:107
  99.0 0.9 copy-done.13
  99.9 0.5 collective-permute-start.17
  100.4 0.1 stack.70.at_ref
  100.6 6.6 %partial.3 = (bf16[256,768]{1,0:T(8,128)(2,1)}, bf16[256,768]{1,0:T(8,128)(2,1)S(1)}) custom-call(s32[8]{0:T(128)S(1)} %stack.70.at_ref, bf16[128,3072]{1,0:T(8,128)(2,1)} %collective-permute-done.2.refs_2_.own, bf16[128,3072]{1,0:T(8,128)(2,1)} %collective-permute-done.4.refs_3_.far, bf16[1,384,1536]{2,1,0:T(8,128)(2,1)} %bitcast.13.refs_0_, ...), custom_call_target="tpu_custom_call" | custom-call | flops 1024 | bytes 1024 | tf_op jit(solution)/shard_map/partial/pallas_call | solution.py:107
  107.2 0.8 copy-done.14
  107.9 3.0 %collective-permute-start.18 = (bf16[2,384,512]{2,1,0:T(8,128)(2,1)}, bf16[2,384,512]{2,1,0:T(8,128)(2,1)S(1)}, u32[]{:S(2)}, u32[]{:S(2)}) collective-permute-start(bf16[2,384,512]{2,1,0:T(8,128)(2,1)} %copy-done.13), channel_id=1, source_target_pairs={{0,8},{8,0},{1,9},{9,1},{2,10},{10,2},{3,11},{11,3},{4,12},{12,4},... | collective-permute-start | bytes 2359304 | tf_op jit(solution)/shard_map/ppermute | solution.py:23
  111.0 0.1 pad_add_fusion.1.at_ref
  111.0 1.1 copy-done.4
  112.2 1.1 copy-done.12
  113.3 5.9 %partial.2 = (f32[256,768]{1,0:T(8,128)S(1)}, f32[256,768]{1,0:T(8,128)S(1)}) custom-call(s32[8]{0:T(128)S(1)} %stack.70.at_ref, bf16[128,3072]{1,0:T(8,128)(2,1)S(1)} %copy-done.4, bf16[128,3072]{1,0:T(8,128)(2,1)S(1)} %copy-done.12, bf16[1,384,1536]{2,1,0:T(8,128)(2,1)} %bitcast.13.refs_0_, bf16[1,384,1536]{2,1,0:T(8,128)(2,1)} %collective-permute-done.12.refs_1_, ...), custom_call_target="tpu_custom_call" | custom-call | flops 1024 | bytes 1024 | tf_op jit(solution)/shard_map/partial/pallas_call | solution.py:107
  119.2 5.1 %rows.3 = (f32[2,384,1024]{2,1,0:T(8,128)S(1)}, f32[2,384,512]{2,1,0:T(8,128)S(1)}) custom-call(s32[4]{0:T(128)S(1)} %pad_add_fusion.1.at_ref, bf16[4,384,512]{2,1,0:T(8,128)(2,1)S(1)} %copy-done.7, bf16[4,384,512]{2,1,0:T(8,128)(2,1)} %collective-permute-done.5.refs_1_, bf16[2,256,1536]{2,1,0:T(8,128)(2,1)} %pad_maximum_fusion.1.refs_2_, ...), custom_call_target="tpu_custom_call" | custom-call | flops 1024 | bytes 1024 | tf_op jit(solution)/shard_map/rows/pallas_call | solution.py:107
  124.3 4.1 %collective-permute-done.15.refs_1_ = bf16[256,768]{1,0:T(8,128)(2,1)} collective-permute-done((bf16[256,768]{1,0:T(8,128)(2,1)}, bf16[256,768]{1,0:T(8,128)(2,1)}, u32[]{:S(2)}, u32[]{:S(2)}) %collective-permute-start.15) | collective-permute-done | bytes 393248 | tf_op jit(solution)/shard_map/ppermute | solution.py:23
  128.4 5.5 %backward.2 = (bf16[3,128,768]{2,1,0:T(8,128)(2,1)S(1)}, bf16[3,128,768]{2,1,0:T(8,128)(2,1)S(1)}) custom-call(bf16[3,128,1536]{2,1,0:T(8,128)(2,1)S(1)} %pad_maximum_fusion.2.own, bf16[2,128,1536]{2,1,0:T(8,128)(2,1)S(1)} %copy-done.1, bf16[1,128,1536]{2,1,0:T(8,128)(2,1)S(1)} %copy-done.9, f32[256,768]{1,0:T(8,128)S(1)} %get-tuple-element.44.refs_0_, ...), custom_call_target="tpu_custom_call" | custom-call | flops 1024 | bytes 1024 | tf_op jit(solution)/shard_map/backward/pallas_call | solution.py:107
  133.9 0.6 collective-permute-start.19
  134.6 0.1 broadcast_in_dim.8.clone.2
  134.8 7.0 %collective-permute-done.18 = bf16[2,384,512]{2,1,0:T(8,128)(2,1)S(1)} collective-permute-done((bf16[2,384,512]{2,1,0:T(8,128)(2,1)}, bf16[2,384,512]{2,1,0:T(8,128)(2,1)S(1)}, u32[]{:S(2)}, u32[]{:S(2)}) %collective-permute-start.18) | collective-permute-done | bytes 786464 | tf_op jit(solution)/shard_map/ppermute | solution.py:23
  141.7 0.3 convert_add_fusion.1
  142.1 1.6 collective-permute-start.22
  143.7 2.4 %convert_add_fusion = f32[2,384,1024]{2,1,0:T(8,128)S(1)} fusion(f32[2,384,1024]{2,1,0:T(8,128)S(1)} %get-tuple-element.49, bf16[2,384,1024]{2,1,0:T(8,128)(2,1)} %collective-permute-done.17), kind=kLoop, calls=%fused_computation | loop fusion | flops 1572864 | bytes 7864320 | tf_op jit(solution)/shard_map/add | solution.py:392
  146.0 0.1 dynamic-slice_convert_fusion
  146.1 0.1 collective-permute-start.21
  146.2 2.6 %collective-permute-done.16.refs_1_ = bf16[256,768]{1,0:T(8,128)(2,1)S(1)} collective-permute-done((bf16[256,768]{1,0:T(8,128)(2,1)S(1)}, bf16[256,768]{1,0:T(8,128)(2,1)S(1)}, u32[]{:S(2)}, u32[]{:S(2)}) %collective-permute-start.16) | collective-permute-done | bytes 393248 | tf_op jit(solution)/shard_map/ppermute | solution.py:23
  148.8 4.5 %backward.3 = (bf16[3,128,768]{2,1,0:T(8,128)(2,1)S(1)}, bf16[3,128,768]{2,1,0:T(8,128)(2,1)S(1)}) custom-call(bf16[3,128,1536]{2,1,0:T(8,128)(2,1)S(1)} %pad_maximum_fusion.2.own, bf16[2,128,1536]{2,1,0:T(8,128)(2,1)S(1)} %copy-done.1, bf16[1,128,1536]{2,1,0:T(8,128)(2,1)S(1)} %copy-done.9, f32[256,768]{1,0:T(8,128)S(1)} %get-tuple-element.46.refs_0_, ...), custom_call_target="tpu_custom_call" | custom-call | flops 1024 | bytes 1024 | tf_op jit(solution)/shard_map/backward/pallas_call | solution.py:107
  153.3 0.6 collective-permute-start.20
  154.0 0.1 add_bitcast_fusion.1
  154.1 13.5 %collective-permute-done.20 = bf16[3,128,768]{2,1,0:T(8,128)(2,1)S(1)} collective-permute-done((bf16[3,128,768]{2,1,0:T(8,128)(2,1)S(1)}, bf16[3,128,768]{2,1,0:T(8,128)(2,1)S(1)}, u32[]{:S(2)}, u32[]{:S(2)}) %collective-permute-start.20) | collective-permute-done | bytes 589856 | tf_op jit(solution)/shard_map/ppermute | solution.py:23
  167.8 0.3 add_bitcast_fusion
  168.1 0.5 copy-done.19
  168.6 0.3 copy-done.20
  168.8 0.3 copy-done.21
  169.1 1.6 maximum_multiply_fusion
  (67 shorter events, 0.6 us)
Async XLA Ops:
  0.6 51.6 %collective-permute-start.7 = (bf16[384,1536]{1,0:T(8,128)(2,1)}, bf16[384,1536]{1,0:T(8,128)(2,1)}, u32[]{:S(2)}, u32[]{:S(2)}) collective-permute-start(bf16[384,1536]{1,0:T(8,128)(2,1)} %param.9), channel_id=1, source_target_pairs={{0,4},{4,0},{1,5},{5,1},{2,6},{6,2},{3,7},{7,3},{8,12},{12,8},{9,1... | collective-permute-start | bytes 3538952 | tf_op jit(solution)/shard_map/ppermute | solution.py:23
  3.6 50.6 %collective-permute-start.9 = (bf16[384,1536]{1,0:T(8,128)(2,1)}, bf16[384,1536]{1,0:T(8,128)(2,1)}, u32[]{:S(2)}, u32[]{:S(2)}) collective-permute-start(bf16[384,1536]{1,0:T(8,128)(2,1)} %param.9), channel_id=1, source_target_pairs={{0,8},{8,0},{1,9},{9,1},{2,10},{10,2},{3,11},{11,3},{4,12},{12,4},... | collective-permute-start | bytes 3538952 | tf_op jit(solution)/shard_map/ppermute | solution.py:23
  7.5 2.5 %copy-start.16 = (bf16[1,128,6144]{2,1,0:T(8,128)(2,1)S(1)}, bf16[1,128,6144]{2,1,0:T(8,128)(2,1)}, u32[]{:S(2)}) copy-start(bf16[1,128,6144]{2,1,0:T(8,128)(2,1)} %param.5) | copy-start | bytes 4718596
  8.5 29.0 %collective-permute-start = (bf16[2,128,1536]{2,1,0:T(8,128)(2,1)}, bf16[2,128,1536]{2,1,0:T(8,128)(2,1)S(1)}, u32[]{:S(2)}, u32[]{:S(2)}) collective-permute-start(bf16[2,128,1536]{2,1,0:T(8,128)(2,1)} %pad_maximum_fusion.3), channel_id=1, source_target_pairs={{0,1},{1,0},{2,3},{3,2},{4,5},{5,4},{6,7},{7,6},{8,9},{9,8},{10,11... | collective-permute-start | bytes 2359304 | tf_op jit(solution)/shard_map/ppermute | solution.py:23
  10.0 2.8 %copy-start.22 = (bf16[1,128,3072]{2,1,0:T(8,128)(2,1)S(1)}, bf16[1,128,3072]{2,1,0:T(8,128)(2,1)}, u32[]{:S(2)}) copy-start(bf16[1,128,3072]{2,1,0:T(8,128)(2,1)} %param.8) | copy-start | bytes 2359300
  10.1 27.4 %copy-start.2 = (bf16[128,3072]{1,0:T(8,128)(2,1)}, bf16[128,3072]{1,0:T(8,128)(2,1)S(1)}, u32[]{:S(2)}) copy-start(bf16[128,3072]{1,0:T(8,128)(2,1)S(1)} %get-tuple-element.40.refs_0_.own) | copy-start | bytes 2359300
  10.1 27.2 %copy-start.17 = (bf16[1,128,1536]{2,1,0:T(8,128)(2,1)S(1)}, bf16[1,128,1536]{2,1,0:T(8,128)(2,1)}, u32[]{:S(2)}) copy-start(bf16[1,128,1536]{2,1,0:T(8,128)(2,1)} %get-tuple-element.69) | copy-start | bytes 1179652
  10.2 27.2 %copy-start.18 = (bf16[1,128,1536]{2,1,0:T(8,128)(2,1)S(1)}, bf16[1,128,1536]{2,1,0:T(8,128)(2,1)}, u32[]{:S(2)}) copy-start(bf16[1,128,1536]{2,1,0:T(8,128)(2,1)} %get-tuple-element.79) | copy-start | bytes 1179652
  10.2 37.1 %collective-permute-start.2 = (bf16[128,3072]{1,0:T(8,128)(2,1)S(1)}, bf16[128,3072]{1,0:T(8,128)(2,1)}, u32[]{:S(2)}, u32[]{:S(2)}) collective-permute-start(bf16[128,3072]{1,0:T(8,128)(2,1)S(1)} %get-tuple-element.62), channel_id=1, source_target_pairs={{0,16},{16,0},{1,17},{17,1},{2,18},{18,2},{3,19},{19,3},{4,20},{20... | collective-permute-start | bytes 2359304 | tf_op jit(solution)/shard_map/ppermute | solution.py:23
  12.9 23.0 %collective-permute-start.1 = (bf16[1,128,1536]{2,1,0:T(8,128)(2,1)S(1)}, bf16[1,128,1536]{2,1,0:T(8,128)(2,1)S(1)}, u32[]{:S(2)}, u32[]{:S(2)}) collective-permute-start(bf16[1,128,1536]{2,1,0:T(8,128)(2,1)S(1)} %get-tuple-element.64), channel_id=1, source_target_pairs={{0,1},{1,0},{2,3},{3,2},{4,5},{5,4},{6,7},{7,6},{8,9},{9,8},{10,11... | collective-permute-start | bytes 1179656 | tf_op jit(solution)/shard_map/ppermute | solution.py:23
  35.8 4.7 %copy-start.8 = (bf16[1,128,1536]{2,1,0:T(8,128)(2,1)}, bf16[1,128,1536]{2,1,0:T(8,128)(2,1)S(1)}, u32[]{:S(2)}) copy-start(bf16[1,128,1536]{2,1,0:T(8,128)(2,1)S(1)} %collective-permute-done.1.far_values) | copy-start | bytes 1179652
  35.9 22.7 %collective-permute-start.3 = (bf16[128,3072]{1,0:T(8,128)(2,1)S(1)}, bf16[128,3072]{1,0:T(8,128)(2,1)S(1)}, u32[]{:S(2)}, u32[]{:S(2)}) collective-permute-start(bf16[128,3072]{1,0:T(8,128)(2,1)S(1)} %get-tuple-element.40.refs_0_.own), channel_id=1, source_target_pairs={{0,1},{1,0},{2,3},{3,2},{4,5},{5,4},{6,7},{7,6},{8,9},{9,8},{10,11... | collective-permute-start | bytes 2359304 | tf_op jit(solution)/shard_map/ppermute | solution.py:23
  37.5 16.6 %copy-start = (bf16[2,128,1536]{2,1,0:T(8,128)(2,1)}, bf16[2,128,1536]{2,1,0:T(8,128)(2,1)S(1)}, u32[]{:S(2)}) copy-start(bf16[2,128,1536]{2,1,0:T(8,128)(2,1)S(1)} %collective-permute-done.far_both) | copy-start | bytes 2359300
  47.2 23.5 %collective-permute-start.4 = (bf16[128,3072]{1,0:T(8,128)(2,1)}, bf16[128,3072]{1,0:T(8,128)(2,1)}, u32[]{:S(2)}, u32[]{:S(2)}) collective-permute-start(bf16[128,3072]{1,0:T(8,128)(2,1)} %collective-permute-done.2.refs_2_.own), channel_id=1, source_target_pairs={{0,1},{1,0},{2,3},{3,2},{4,5},{5,4},{6,7},{7,6},{8,9},{9,8},{10,11... | collective-permute-start | bytes 2359304 | tf_op jit(solution)/shard_map/ppermute | solution.py:23
  48.7 36.7 %collective-permute-start.6 = (bf16[256,1536]{1,0:T(8,128)(2,1)}, bf16[256,1536]{1,0:T(8,128)(2,1)}, u32[]{:S(2)}, u32[]{:S(2)}) collective-permute-start(bf16[256,1536]{1,0:T(8,128)(2,1)} %forward.1), channel_id=1, source_target_pairs={{0,16},{16,0},{1,17},{17,1},{2,18},{18,2},{3,19},{19,3},{4,20},{20... | collective-permute-start | bytes 2359304 | tf_op jit(solution)/shard_map/ppermute | solution.py:23
  54.2 31.3 %collective-permute-start.8 = (bf16[192,1536]{1,0:T(8,128)(2,1)}, bf16[192,1536]{1,0:T(8,128)(2,1)}, u32[]{:S(2)}, u32[]{:S(2)}) collective-permute-start(bf16[192,1536]{1,0:T(8,128)(2,1)} %slice.8), channel_id=1, source_target_pairs={{0,8},{8,0},{1,9},{9,1},{2,10},{10,2},{3,11},{11,3},{4,12},{12,4},... | collective-permute-start | bytes 1769480 | tf_op jit(solution)/shard_map/ppermute | solution.py:23
  56.2 29.3 %collective-permute-start.10 = (bf16[192,1536]{1,0:T(8,128)(2,1)}, bf16[192,1536]{1,0:T(8,128)(2,1)}, u32[]{:S(2)}, u32[]{:S(2)}) collective-permute-start(bf16[192,1536]{1,0:T(8,128)(2,1)} %slice.9), channel_id=1, source_target_pairs={{0,4},{4,0},{1,5},{5,1},{2,6},{6,2},{3,7},{7,3},{8,12},{12,8},{9,1... | collective-permute-start | bytes 1769480 | tf_op jit(solution)/shard_map/ppermute | solution.py:23
  58.6 0.9 copy-start.10
  59.5 41.1 %collective-permute-start.13 = (bf16[2,384,1536]{2,1,0:T(8,128)(2,1)S(1)}, bf16[2,384,1536]{2,1,0:T(8,128)(2,1)}, u32[]{:S(2)}, u32[]{:S(2)}) collective-permute-start(bf16[2,384,1536]{2,1,0:T(8,128)(2,1)S(1)} %pad_maximum_fusion.refs_2_), channel_id=1, source_target_pairs={{0,2},{2,0},{1,3},{3,1},{4,6},{6,4},{5,7},{7,5},{8,10},{10,8},{9,1... | collective-permute-start | bytes 7077896 | tf_op jit(solution)/shard_map/ppermute | solution.py:23
  70.7 1.1 copy-start.3
  71.8 1.1 copy-start.11
  76.5 11.6 %copy-start.5 = (bf16[4,384,512]{2,1,0:T(8,128)(2,1)}, bf16[4,384,512]{2,1,0:T(8,128)(2,1)S(1)}, u32[]{:S(2)}) copy-start(bf16[4,384,512]{2,1,0:T(8,128)(2,1)S(1)} %get-tuple-element.47.refs_0_) | copy-start | bytes 4718596
  76.5 14.6 %collective-permute-start.5 = (bf16[4,384,512]{2,1,0:T(8,128)(2,1)}, bf16[4,384,512]{2,1,0:T(8,128)(2,1)}, u32[]{:S(2)}, u32[]{:S(2)}) collective-permute-start(bf16[4,384,512]{2,1,0:T(8,128)(2,1)} %get-tuple-element.35), channel_id=1, source_target_pairs={{0,2},{2,0},{1,3},{3,1},{4,6},{6,4},{5,7},{7,5},{8,10},{10,8},{9,1... | collective-permute-start | bytes 4718600 | tf_op jit(solution)/shard_map/ppermute | solution.py:23
  88.1 3.8 %collective-permute-start.11 = (bf16[2,256,1536]{2,1,0:T(8,128)(2,1)}, bf16[2,256,1536]{2,1,0:T(8,128)(2,1)}, u32[]{:S(2)}, u32[]{:S(2)}) collective-permute-start(bf16[2,256,1536]{2,1,0:T(8,128)(2,1)} %pad_maximum_fusion.1.refs_2_), channel_id=1, source_target_pairs={{0,2},{2,0},{1,3},{3,1},{4,6},{6,4},{5,7},{7,5},{8,10},{10,8},{9,1... | collective-permute-start | bytes 4718600 | tf_op jit(solution)/shard_map/ppermute | solution.py:23
  88.1 12.4 %collective-permute-start.12 = (bf16[1,384,1536]{2,1,0:T(8,128)(2,1)}, bf16[1,384,1536]{2,1,0:T(8,128)(2,1)}, u32[]{:S(2)}, u32[]{:S(2)}) collective-permute-start(bf16[1,384,1536]{2,1,0:T(8,128)(2,1)} %bitcast.13.refs_0_), channel_id=1, source_target_pairs={{0,2},{2,0},{1,3},{3,1},{4,6},{6,4},{5,7},{7,5},{8,10},{10,8},{9,1... | collective-permute-start | bytes 3538952 | tf_op jit(solution)/shard_map/ppermute | solution.py:23
  91.1 9.5 %collective-permute-start.14 = (bf16[1,384,1536]{2,1,0:T(8,128)(2,1)}, bf16[1,384,1536]{2,1,0:T(8,128)(2,1)}, u32[]{:S(2)}, u32[]{:S(2)}) collective-permute-start(bf16[1,384,1536]{2,1,0:T(8,128)(2,1)} %maximum_bitcast_fusion.refs_4_), channel_id=1, source_target_pairs={{0,2},{2,0},{1,3},{3,1},{4,6},{6,4},{5,7},{7,5},{8,10},{10,8},{9,1... | collective-permute-start | bytes 3538952 | tf_op jit(solution)/shard_map/ppermute | solution.py:23
  91.9 1.4 copy-start.6
  99.0 0.9 copy-start.13
  99.9 41.8 %collective-permute-start.17 = (bf16[2,384,1024]{2,1,0:T(8,128)(2,1)}, bf16[2,384,1024]{2,1,0:T(8,128)(2,1)}, u32[]{:S(2)}, u32[]{:S(2)}) collective-permute-start(bf16[2,384,1024]{2,1,0:T(8,128)(2,1)} %get-tuple-element.38), channel_id=1, source_target_pairs={{0,4},{4,0},{1,5},{5,1},{2,6},{6,2},{3,7},{7,3},{8,12},{12,8},{9,1... | collective-permute-start | bytes 4718600 | tf_op jit(solution)/shard_map/ppermute | solution.py:23
  107.2 0.8 copy-start.14
  107.9 20.5 %collective-permute-start.15 = (bf16[256,768]{1,0:T(8,128)(2,1)}, bf16[256,768]{1,0:T(8,128)(2,1)}, u32[]{:S(2)}, u32[]{:S(2)}) collective-permute-start(bf16[256,768]{1,0:T(8,128)(2,1)} %get-tuple-element.45), channel_id=1, source_target_pairs={{0,16},{16,0},{1,17},{17,1},{2,18},{18,2},{3,19},{19,3},{4,20},{20... | collective-permute-start | bytes 1179656 | tf_op jit(solution)/shard_map/ppermute | solution.py:23
  107.9 33.8 %collective-permute-start.18 = (bf16[2,384,512]{2,1,0:T(8,128)(2,1)}, bf16[2,384,512]{2,1,0:T(8,128)(2,1)S(1)}, u32[]{:S(2)}, u32[]{:S(2)}) collective-permute-start(bf16[2,384,512]{2,1,0:T(8,128)(2,1)} %copy-done.13), channel_id=1, source_target_pairs={{0,8},{8,0},{1,9},{9,1},{2,10},{10,2},{3,11},{11,3},{4,12},{12,4},... | collective-permute-start | bytes 2359304 | tf_op jit(solution)/shard_map/ppermute | solution.py:23
  111.0 1.1 copy-start.4
  112.2 1.1 copy-start.12
  113.3 5.9 %copy-start.7 = (bf16[4,384,512]{2,1,0:T(8,128)(2,1)S(1)}, bf16[4,384,512]{2,1,0:T(8,128)(2,1)}, u32[]{:S(2)}) copy-start(bf16[4,384,512]{2,1,0:T(8,128)(2,1)} %copy-done.5) | copy-start | bytes 4718596
  119.2 9.2 %copy-start.15 = (bf16[256,768]{1,0:T(8,128)(2,1)S(1)}, bf16[256,768]{1,0:T(8,128)(2,1)}, u32[]{:S(2)}) copy-start(bf16[256,768]{1,0:T(8,128)(2,1)} %copy-done.14) | copy-start | bytes 1179652
  119.2 9.2 %copy-start.1 = (bf16[2,128,1536]{2,1,0:T(8,128)(2,1)S(1)}, bf16[2,128,1536]{2,1,0:T(8,128)(2,1)}, u32[]{:S(2)}) copy-start(bf16[2,128,1536]{2,1,0:T(8,128)(2,1)} %copy-done) | copy-start | bytes 2359300
  119.2 9.2 %copy-start.9 = (bf16[1,128,1536]{2,1,0:T(8,128)(2,1)S(1)}, bf16[1,128,1536]{2,1,0:T(8,128)(2,1)}, u32[]{:S(2)}) copy-start(bf16[1,128,1536]{2,1,0:T(8,128)(2,1)} %copy-done.8) | copy-start | bytes 1179652
  128.4 20.5 %collective-permute-start.16 = (bf16[256,768]{1,0:T(8,128)(2,1)S(1)}, bf16[256,768]{1,0:T(8,128)(2,1)S(1)}, u32[]{:S(2)}, u32[]{:S(2)}) collective-permute-start(bf16[256,768]{1,0:T(8,128)(2,1)S(1)} %copy-done.15), channel_id=1, source_target_pairs={{0,16},{16,0},{1,17},{17,1},{2,18},{18,2},{3,19},{19,3},{4,20},{20... | collective-permute-start | bytes 1179656 | tf_op jit(solution)/shard_map/ppermute | solution.py:23
  133.9 20.1 %collective-permute-start.19 = (bf16[3,128,768]{2,1,0:T(8,128)(2,1)S(1)}, bf16[3,128,768]{2,1,0:T(8,128)(2,1)S(1)}, u32[]{:S(2)}, u32[]{:S(2)}) collective-permute-start(bf16[3,128,768]{2,1,0:T(8,128)(2,1)S(1)} %get-tuple-element.60), channel_id=1, source_target_pairs={{0,1},{1,0},{2,3},{3,2},{4,5},{5,4},{6,7},{7,6},{8,9},{9,8},{10,11... | collective-permute-start | bytes 1769480 | tf_op jit(solution)/shard_map/ppermute | solution.py:23
  142.1 11.9 %collective-permute-start.22 = (bf16[1,384,512]{2,1,0:T(8,128)(2,1)S(1)}, bf16[1,384,512]{2,1,0:T(8,128)(2,1)S(1)}, u32[]{:S(2)}, u32[]{:S(2)}) collective-permute-start(bf16[1,384,512]{2,1,0:T(8,128)(2,1)S(1)} %dynamic-slice_convert_fusion.1), channel_id=1, source_target_pairs={{0,4},{4,0},{1,5},{5,1},{2,6},{6,2},{3,7},{7,3},{8,12},{12,8},{9,1... | collective-permute-start | bytes 1179656 | tf_op jit(solution)/shard_map/ppermute | solution.py:23
  146.1 21.6 %collective-permute-start.21 = (bf16[1,384,1024]{2,1,0:T(8,128)(2,1)S(1)}, bf16[1,384,1024]{2,1,0:T(8,128)(2,1)S(1)}, u32[]{:S(2)}, u32[]{:S(2)}) collective-permute-start(bf16[1,384,1024]{2,1,0:T(8,128)(2,1)S(1)} %dynamic-slice_convert_fusion), channel_id=1, source_target_pairs={{0,8},{8,0},{1,9},{9,1},{2,10},{10,2},{3,11},{11,3},{4,12},{12,4},... | collective-permute-start | bytes 2359304 | tf_op jit(solution)/shard_map/ppermute | solution.py:23
  153.3 14.3 %collective-permute-start.20 = (bf16[3,128,768]{2,1,0:T(8,128)(2,1)S(1)}, bf16[3,128,768]{2,1,0:T(8,128)(2,1)S(1)}, u32[]{:S(2)}, u32[]{:S(2)}) collective-permute-start(bf16[3,128,768]{2,1,0:T(8,128)(2,1)S(1)} %get-tuple-element.61), channel_id=1, source_target_pairs={{0,1},{1,0},{2,3},{3,2},{4,5},{5,4},{6,7},{7,6},{8,9},{9,8},{10,11... | collective-permute-start | bytes 1769480 | tf_op jit(solution)/shard_map/ppermute | solution.py:23
  167.7 0.9 copy-start.19
  167.7 1.1 copy-start.20
  167.7 1.4 copy-start.21

commit v10 on v9

--- a/solution.py
+++ b/solution.py
@@ -280,7 +280,7 @@
     def across(array):
         return [shift(array, "core", by) for by in others("core")]
 
-    groups = 2 if heads % 4 == 0 else 1
+    groups = 3 if heads % 3 == 0 else 1
     wide = features // groups
     larger = 2 * heads // 3
     widths = [count * HEAD_DIM for count in (larger, heads - larger) if count]
@@ -386,7 +386,7 @@
             sent = leaving[:, (by - 1) * tokens : by * tokens]
             column = ((mine + by) % seq) * features + start
             arrivals.append((column, shift(sent, "seq", -by)))
-        if group == 0:
+        if group == max(groups - 2, 0):
             for (_, axis), arrived, total in zip(orders, after(arrive, staying), kept):
                 for term in arrived:
                     total = total + term.astype(jnp.float32)
@@ -394,7 +394,7 @@
                 final = part_of(total, axis, 0, 0)
                 second.append((final, passed))
             if groups > 1:
-                terms[1] = after(terms[1], [passed for _, passed in second])
+                terms[-1] = after(terms[-1], [passed for _, passed in second])
 
     columns = []
     for (_, axis), (final, passed) in zip(orders, second):

time: 171 us -> 171 us (level)
  starting transfers between devices: 23.6 us -> 27.7 us
  waiting for transfers between devices: 76.9 us -> 73 us
    ppermute x23 -> x25, starting transfers between devices: 23.6 us -> 27.7 us  [shift(): lax.ppermute(array, axis, [(i, (i + by) % count) for i in range(count)])]
    ppermute x23 -> x25, waiting for transfers between devices: 76.9 us -> 73 us  [shift(): lax.ppermute(array, axis, [(i, (i + by) % count) for i in range(count)])]
    unnamed x46 -> x50, local copies, waits for them, and re-layouts: 9.55 us -> 9.2 us
    pallas_call x8 -> x9, Pallas kernels: 39.8 us -> 40 us  [whole_call(): pl.pallas_call(kernel, in_specs=in_specs, out_specs=jax.tree.map(lambda _...]
  transfers between devices with their start and end apart: 23 -> 25, of which waited for: 9 -> 9; matrix products, arithmetic and copies ran while one was open for 11% -> 10% of each run, Pallas kernels for 23% -> 23%
where the time goes in v10:
time: 171 us
  waiting for transfers between devices  73 us (43%)
  Pallas kernels  40 us (23%)
  starting transfers between devices  27.7 us (16%)
  local copies, waits for them, and re-layouts  16.3 us (10%)
  other arithmetic  12.7 us (7%)
    ppermute x25, waiting for transfers between devices, shift(): lax.ppermute(array, axis, [(i, (i + by) % count) for i in range(count)])  73 us
    pallas_call x9, Pallas kernels, whole_call(): pl.pallas_call(kernel, in_specs=in_specs, out_specs=jax.tree.map(lambda _...  40 us
    ppermute x25, starting transfers between devices, shift(): lax.ppermute(array, axis, [(i, (i + by) % count) for i in range(count)])  27.7 us
    unnamed x50, local copies, waits for them, and re-layouts  9.2 us
  transfers between devices with their start and end apart: 25, of which 9 were waited for; matrix products, arithmetic and copies ran while one was open for 10% of the time, Pallas kernels for 23%

profile of v10, /device:TPU:0, one launch (start us, length us, event | category | flops | bytes accessed | tf_op | source)
XLA Modules:
  0.0 170.7 jit_solution(16565480969344627522)
XLA Ops:
  0.6 3.0 %collective-permute-start.7 = (bf16[384,1536]{1,0:T(8,128)(2,1)}, bf16[384,1536]{1,0:T(8,128)(2,1)}, u32[]{:S(2)}, u32[]{:S(2)}) collective-permute-start(bf16[384,1536]{1,0:T(8,128)(2,1)} %param.9), channel_id=1, source_target_pairs={{0,4},{4,0},{1,5},{5,1},{2,6},{6,2},{3,7},{7,3},{8,12},{12,8},{9,1... | collective-permute-start | bytes 3538952 | tf_op jit(solution)/shard_map/ppermute | solution.py:23
  3.6 1.6 collective-permute-start.9
  5.2 2.3 %constant_dynamic-slice_fusion.1 = (bf16[1,128,1536]{2,1,0:T(8,128)(2,1)S(1)}, bf16[1,128,1536]{2,1,0:T(8,128)(2,1)}, bf16[1,128,1536]{2,1,0:T(8,128)(2,1)}, bf16[1,128,1536]{2,1,0:T(8,128)(2,1)S(1)}) fusion(bf16[1,128,3072]{2,1,0:T(8,128)(2,1)} %param.7, s32[]{:T(128)S(6)} %select_n.174, s32[]{:T(128)S(6)} %select_n.172, bf16[1,128,3072]{2,1,0:T(8,128)(2,1)} %param.6), kind=kLoop, calls=%fused_computation.33 | loop fusion | bytes 3145736 | tf_op jit(solution)/shard_map/dynamic_slice | solution.py:34
  7.5 0.9 pad_maximum_fusion.3
  8.5 1.5 collective-permute-start
  10.0 0.1 dynamic-slice_bitcast_fusion
  10.2 2.7 %collective-permute-start.2 = (bf16[128,3072]{1,0:T(8,128)(2,1)S(1)}, bf16[128,3072]{1,0:T(8,128)(2,1)}, u32[]{:S(2)}, u32[]{:S(2)}) collective-permute-start(bf16[128,3072]{1,0:T(8,128)(2,1)S(1)} %get-tuple-element.74), channel_id=1, source_target_pairs={{0,16},{16,0},{1,17},{17,1},{2,18},{18,2},{3,19},{19,3},{4,20},{20... | collective-permute-start | bytes 2359304 | tf_op jit(solution)/shard_map/ppermute | solution.py:23
  12.9 0.8 collective-permute-start.1
  13.7 22.2 %collective-permute-done.1.far_values = bf16[1,128,1536]{2,1,0:T(8,128)(2,1)S(1)} collective-permute-done((bf16[1,128,1536]{2,1,0:T(8,128)(2,1)S(1)}, bf16[1,128,1536]{2,1,0:T(8,128)(2,1)S(1)}, u32[]{:S(2)}, u32[]{:S(2)}) %collective-permute-start.1) | collective-permute-done | bytes 393248 | tf_op jit(solution)/shard_map/ppermute | solution.py:23
  35.9 1.5 collective-permute-start.3
  37.4 0.1 pad_maximum_fusion.2.own
  37.5 3.0 %forward.1 = bf16[256,1536]{1,0:T(8,128)(2,1)} custom-call(bf16[3,128,1536]{2,1,0:T(8,128)(2,1)S(1)} %pad_maximum_fusion.2.own, bf16[2,128,1536]{2,1,0:T(8,128)(2,1)S(1)} %collective-permute-done.far_both, bf16[1,128,1536]{2,1,0:T(8,128)(2,1)S(1)} %collective-permute-done.1.far_values), custom_call_target="tpu_custom_call" | custom-call | flops 1024 | bytes 1024 | tf_op jit(solution)/shard_map/forward/pallas_call | solution.py:107
  40.5 6.7 %collective-permute-done.2.refs_2_.own = bf16[128,3072]{1,0:T(8,128)(2,1)} collective-permute-done((bf16[128,3072]{1,0:T(8,128)(2,1)S(1)}, bf16[128,3072]{1,0:T(8,128)(2,1)}, u32[]{:S(2)}, u32[]{:S(2)}) %collective-permute-start.2) | collective-permute-done | bytes 786464 | tf_op jit(solution)/shard_map/ppermute | solution.py:23
  47.2 1.5 collective-permute-start.4
  48.7 3.5 %collective-permute-start.6 = (bf16[256,1536]{1,0:T(8,128)(2,1)}, bf16[256,1536]{1,0:T(8,128)(2,1)}, u32[]{:S(2)}, u32[]{:S(2)}) collective-permute-start(bf16[256,1536]{1,0:T(8,128)(2,1)} %forward.1), channel_id=1, source_target_pairs={{0,16},{16,0},{1,17},{17,1},{2,18},{18,2},{3,19},{19,3},{4,20},{20... | collective-permute-start | bytes 2359304 | tf_op jit(solution)/shard_map/ppermute | solution.py:23
  52.2 1.9 %slice.8 = bf16[192,1536]{1,0:T(8,128)(2,1)} slice(bf16[384,1536]{1,0:T(8,128)(2,1)} %collective-permute-done.7), slice={[0:192], [0:1536]} | slice | bytes 1179648 | tf_op jit(solution)/shard_map/slice | solution.py:316
  54.2 0.1 collective-permute-start.8
  54.3 1.9 %slice.9 = bf16[192,1536]{1,0:T(8,128)(2,1)} slice(bf16[384,1536]{1,0:T(8,128)(2,1)} %collective-permute-done.9), slice={[192:384], [0:1536]} | slice | bytes 1179648 | tf_op jit(solution)/shard_map/slice | solution.py:317
  56.2 0.5 collective-permute-start.10
  56.7 1.8 %pad_maximum_fusion.refs_2_ = bf16[2,384,1536]{2,1,0:T(8,128)(2,1)S(1)} fusion(bf16[1,384,1536]{2,1,0:T(8,128)(2,1)} %bitcast.15, bf16[1,384,1536]{2,1,0:T(8,128)(2,1)} %bitcast.14), kind=kLoop, calls=%fused_computation.1 | loop fusion | flops 1179648 | bytes 4718592 | tf_op jit(solution)/shard_map/stack | solution.py:318
  58.6 0.9 copy-done.10
  59.5 11.2 %collective-permute-done.4.refs_3_.far = bf16[128,3072]{1,0:T(8,128)(2,1)} collective-permute-done((bf16[128,3072]{1,0:T(8,128)(2,1)}, bf16[128,3072]{1,0:T(8,128)(2,1)}, u32[]{:S(2)}, u32[]{:S(2)}) %collective-permute-start.4) | collective-permute-done | bytes 786464 | tf_op jit(solution)/shard_map/ppermute | solution.py:23
  70.7 1.1 copy-done.3
  71.8 1.1 copy-done.11
  73.0 3.6 %turn.1 = (bf16[4,384,512]{2,1,0:T(8,128)(2,1)S(1)}, bf16[4,384,512]{2,1,0:T(8,128)(2,1)}) custom-call(s32[1]{0:T(128)} %bitcast.10.core_ref, bf16[128,3072]{1,0:T(8,128)(2,1)S(1)} %copy-done.3, bf16[128,3072]{1,0:T(8,128)(2,1)S(1)} %copy-done.11, bf16[128,3072]{1,0:T(8,128)(2,1)} %collective-permute-done.2.refs_2_.own, ...), custom_call_target="tpu_custom_call" | custom-call | flops 1024 | bytes 1024 | tf_op jit(solution)/shard_map/turn/pallas_call | solution.py:107
  76.5 8.9 %collective-permute-done.6 = bf16[256,1536]{1,0:T(8,128)(2,1)} collective-permute-done((bf16[256,1536]{1,0:T(8,128)(2,1)}, bf16[256,1536]{1,0:T(8,128)(2,1)}, u32[]{:S(2)}, u32[]{:S(2)}) %collective-permute-start.6) | collective-permute-done | bytes 786464 | tf_op jit(solution)/shard_map/ppermute | solution.py:23
  85.5 2.7 %pad_maximum_fusion.1.refs_2_ = bf16[2,256,1536]{2,1,0:T(8,128)(2,1)} fusion(bf16[1,256,1536]{2,1,0:T(8,128)(2,1)} %bitcast.12, bf16[1,256,1536]{2,1,0:T(8,128)(2,1)} %bitcast.11), kind=kLoop, calls=%fused_computation.3 | loop fusion | flops 786432 | bytes 3145728 | tf_op jit(solution)/shard_map/stack | solution.py:328
  88.1 0.5 collective-permute-start.12
  88.7 2.4 %maximum_bitcast_fusion.refs_4_ = bf16[1,384,1536]{2,1,0:T(8,128)(2,1)} fusion(bf16[192,1536]{1,0:T(8,128)(2,1)} %collective-permute-done.10, bf16[192,1536]{1,0:T(8,128)(2,1)} %collective-permute-done.8), kind=kLoop, calls=%fused_computation.8 | loop fusion | flops 2359296 | bytes 2359296 | tf_op jit(solution)/shard_map/stack | solution.py:331
  91.1 0.1 pad_add_fusion.at_ref
  91.2 0.7 collective-permute-done.11.refs_3_
  91.9 1.4 copy-done.8
  93.3 5.7 %rows.2 = (bf16[2,384,1024]{2,1,0:T(8,128)(2,1)}, bf16[2,384,512]{2,1,0:T(8,128)(2,1)S(1)}) custom-call(s32[4]{0:T(128)S(1)} %pad_add_fusion.at_ref, bf16[4,384,512]{2,1,0:T(8,128)(2,1)S(1)} %copy-done.8, bf16[4,384,512]{2,1,0:T(8,128)(2,1)} %collective-permute-done.5.refs_1_, bf16[2,256,1536]{2,1,0:T(8,128)(2,1)} %pad_maximum_fusion.1.refs_2_, ...), custom_call_target="tpu_custom_call" | custom-call | flops 1024 | bytes 1024 | tf_op jit(solution)/shard_map/rows/pallas_call | solution.py:107
  99.0 0.9 copy-done.13
  99.9 0.5 collective-permute-start.18
  100.4 0.1 stack.70.at_ref
  100.6 6.5 %partial.3 = (bf16[256,512]{1,0:T(8,128)(2,1)}, bf16[256,512]{1,0:T(8,128)(2,1)S(1)}, bf16[256,512]{1,0:T(8,128)(2,1)S(1)}) custom-call(s32[8]{0:T(128)S(1)} %stack.70.at_ref, bf16[128,3072]{1,0:T(8,128)(2,1)} %collective-permute-done.2.refs_2_.own, bf16[128,3072]{1,0:T(8,128)(2,1)} %collective-permute-done.4.refs_3_.far, ...), custom_call_target="tpu_custom_call" | custom-call | flops 1024 | bytes 1024 | tf_op jit(solution)/shard_map/partial/pallas_call | solution.py:107
  107.1 0.7 copy-done.14
  107.8 0.7 copy-done.16
  108.5 0.1 pad_add_fusion.1.at_ref
  108.6 3.0 %collective-permute-start.19 = (bf16[2,384,512]{2,1,0:T(8,128)(2,1)}, bf16[2,384,512]{2,1,0:T(8,128)(2,1)S(1)}, u32[]{:S(2)}, u32[]{:S(2)}) collective-permute-start(bf16[2,384,512]{2,1,0:T(8,128)(2,1)} %copy-done.13), channel_id=1, source_target_pairs={{0,8},{8,0},{1,9},{9,1},{2,10},{10,2},{3,11},{11,3},{4,12},{12,4},... | collective-permute-start | bytes 2359304 | tf_op jit(solution)/shard_map/ppermute | solution.py:23
  111.6 1.1 copy-done.4
  112.8 1.1 copy-done.12
  113.9 5.9 %partial.2 = (f32[256,512]{1,0:T(8,128)S(1)}, f32[256,512]{1,0:T(8,128)S(1)}, f32[256,512]{1,0:T(8,128)S(1)}) custom-call(s32[8]{0:T(128)S(1)} %stack.70.at_ref, bf16[128,3072]{1,0:T(8,128)(2,1)S(1)} %copy-done.4, bf16[128,3072]{1,0:T(8,128)(2,1)S(1)} %copy-done.12, bf16[1,384,1536]{2,1,0:T(8,128)(2,1)} %bitcast.13.refs_0_, ...), custom_call_target="tpu_custom_call" | custom-call | flops 1024 | bytes 1024 | tf_op jit(solution)/shard_map/partial/pallas_call | solution.py:107
  119.8 5.1 %rows.3 = (f32[2,384,1024]{2,1,0:T(8,128)S(1)}, f32[2,384,512]{2,1,0:T(8,128)S(1)}) custom-call(s32[4]{0:T(128)S(1)} %pad_add_fusion.1.at_ref, bf16[4,384,512]{2,1,0:T(8,128)(2,1)S(1)} %copy-done.9, bf16[4,384,512]{2,1,0:T(8,128)(2,1)} %collective-permute-done.5.refs_1_, bf16[2,256,1536]{2,1,0:T(8,128)(2,1)} %pad_maximum_fusion.1.refs_2_, ...), custom_call_target="tpu_custom_call" | custom-call | flops 1024 | bytes 1024 | tf_op jit(solution)/shard_map/rows/pallas_call | solution.py:107
  125.0 4.0 %backward.3 = (bf16[3,128,512]{2,1,0:T(8,128)(2,1)S(1)}, bf16[3,128,512]{2,1,0:T(8,128)(2,1)S(1)}) custom-call(bf16[3,128,1536]{2,1,0:T(8,128)(2,1)S(1)} %pad_maximum_fusion.2.own, bf16[2,128,1536]{2,1,0:T(8,128)(2,1)S(1)} %copy-done.1, bf16[1,128,1536]{2,1,0:T(8,128)(2,1)S(1)} %copy-done.6, f32[256,512]{1,0:T(8,128)S(1)} %get-tuple-element.50.refs_0_, ...), custom_call_target="tpu_custom_call" | custom-call | flops 1024 | bytes 1024 | tf_op jit(solution)/shard_map/backward/pallas_call | solution.py:107
  129.2 0.6 collective-permute-start.20
  129.9 7.2 %collective-permute-done.16.refs_1_ = bf16[256,512]{1,0:T(8,128)(2,1)S(1)} collective-permute-done((bf16[256,512]{1,0:T(8,128)(2,1)S(1)}, bf16[256,512]{1,0:T(8,128)(2,1)S(1)}, u32[]{:S(2)}, u32[]{:S(2)}) %collective-permute-start.16) | collective-permute-done | bytes 262176 | tf_op jit(solution)/shard_map/ppermute | solution.py:23
  137.1 3.4 %collective-permute-start.17 = (bf16[256,512]{1,0:T(8,128)(2,1)S(1)}, bf16[256,512]{1,0:T(8,128)(2,1)S(1)}, u32[]{:S(2)}, u32[]{:S(2)}) collective-permute-start(bf16[256,512]{1,0:T(8,128)(2,1)S(1)} %copy-done.15), channel_id=1, source_target_pairs={{0,16},{16,0},{1,17},{17,1},{2,18},{18,2},{3,19},{19,3},{4,20},{20... | collective-permute-start | bytes 786440 | tf_op jit(solution)/shard_map/ppermute | solution.py:23
  140.5 3.2 %backward.4 = (bf16[3,128,512]{2,1,0:T(8,128)(2,1)S(1)}, bf16[3,128,512]{2,1,0:T(8,128)(2,1)S(1)}) custom-call(bf16[3,128,1536]{2,1,0:T(8,128)(2,1)S(1)} %pad_maximum_fusion.2.own, bf16[2,128,1536]{2,1,0:T(8,128)(2,1)S(1)} %copy-done.1, bf16[1,128,1536]{2,1,0:T(8,128)(2,1)S(1)} %copy-done.6, f32[256,512]{1,0:T(8,128)S(1)} %get-tuple-element.52.refs_0_, ...), custom_call_target="tpu_custom_call" | custom-call | flops 1024 | bytes 1024 | tf_op jit(solution)/shard_map/backward/pallas_call | solution.py:107
  143.7 0.6 collective-permute-start.21
  144.4 2.2 %convert_add_fusion = f32[2,384,1024]{2,1,0:T(8,128)S(1)} fusion(f32[2,384,1024]{2,1,0:T(8,128)S(1)} %get-tuple-element.56, bf16[2,384,1024]{2,1,0:T(8,128)(2,1)} %collective-permute-done.18), kind=kLoop, calls=%fused_computation | loop fusion | flops 1572864 | bytes 7864320 | tf_op jit(solution)/shard_map/add | solution.py:392
  146.5 0.3 convert_add_fusion.1
  146.9 1.6 collective-permute-start.24
  148.5 0.1 dynamic-slice_convert_fusion
  148.6 0.2 collective-permute-start.23
  148.8 3.2 %collective-permute-done.17.refs_1_ = bf16[256,512]{1,0:T(8,128)(2,1)S(1)} collective-permute-done((bf16[256,512]{1,0:T(8,128)(2,1)S(1)}, bf16[256,512]{1,0:T(8,128)(2,1)S(1)}, u32[]{:S(2)}, u32[]{:S(2)}) %collective-permute-start.17) | collective-permute-done | bytes 262176 | tf_op jit(solution)/shard_map/ppermute | solution.py:23
  152.0 3.0 %backward.5 = (bf16[3,128,512]{2,1,0:T(8,128)(2,1)S(1)}, bf16[3,128,512]{2,1,0:T(8,128)(2,1)S(1)}) custom-call(bf16[3,128,1536]{2,1,0:T(8,128)(2,1)S(1)} %pad_maximum_fusion.2.own, bf16[2,128,1536]{2,1,0:T(8,128)(2,1)S(1)} %copy-done.1, bf16[1,128,1536]{2,1,0:T(8,128)(2,1)S(1)} %copy-done.6, f32[256,512]{1,0:T(8,128)S(1)} %get-tuple-element.53.refs_0_, ...), custom_call_target="tpu_custom_call" | custom-call | flops 1024 | bytes 1024 | tf_op jit(solution)/shard_map/backward/pallas_call | solution.py:107
  155.0 0.6 collective-permute-start.22
  155.8 8.9 %collective-permute-done.22 = bf16[3,128,512]{2,1,0:T(8,128)(2,1)S(1)} collective-permute-done((bf16[3,128,512]{2,1,0:T(8,128)(2,1)S(1)}, bf16[3,128,512]{2,1,0:T(8,128)(2,1)S(1)}, u32[]{:S(2)}, u32[]{:S(2)}) %collective-permute-start.22) | collective-permute-done | bytes 393248 | tf_op jit(solution)/shard_map/ppermute | solution.py:23
  164.8 0.1 add_bitcast_fusion.1
  164.9 3.8 %collective-permute-done.23 = bf16[1,384,1024]{2,1,0:T(8,128)(2,1)S(1)} collective-permute-done((bf16[1,384,1024]{2,1,0:T(8,128)(2,1)S(1)}, bf16[1,384,1024]{2,1,0:T(8,128)(2,1)S(1)}, u32[]{:S(2)}, u32[]{:S(2)}) %collective-permute-start.23) | collective-permute-done | bytes 786464 | tf_op jit(solution)/shard_map/ppermute | solution.py:23
  168.7 0.3 add_bitcast_fusion
  169.1 1.6 maximum_multiply_fusion
  (78 shorter events, 0.8 us)
Async XLA Ops:
  0.6 51.6 %collective-permute-start.7 = (bf16[384,1536]{1,0:T(8,128)(2,1)}, bf16[384,1536]{1,0:T(8,128)(2,1)}, u32[]{:S(2)}, u32[]{:S(2)}) collective-permute-start(bf16[384,1536]{1,0:T(8,128)(2,1)} %param.9), channel_id=1, source_target_pairs={{0,4},{4,0},{1,5},{5,1},{2,6},{6,2},{3,7},{7,3},{8,12},{12,8},{9,1... | collective-permute-start | bytes 3538952 | tf_op jit(solution)/shard_map/ppermute | solution.py:23
  3.6 50.6 %collective-permute-start.9 = (bf16[384,1536]{1,0:T(8,128)(2,1)}, bf16[384,1536]{1,0:T(8,128)(2,1)}, u32[]{:S(2)}, u32[]{:S(2)}) collective-permute-start(bf16[384,1536]{1,0:T(8,128)(2,1)} %param.9), channel_id=1, source_target_pairs={{0,8},{8,0},{1,9},{9,1},{2,10},{10,2},{3,11},{11,3},{4,12},{12,4},... | collective-permute-start | bytes 3538952 | tf_op jit(solution)/shard_map/ppermute | solution.py:23
  7.5 2.5 %copy-start.18 = (bf16[1,128,6144]{2,1,0:T(8,128)(2,1)S(1)}, bf16[1,128,6144]{2,1,0:T(8,128)(2,1)}, u32[]{:S(2)}) copy-start(bf16[1,128,6144]{2,1,0:T(8,128)(2,1)} %param.5) | copy-start | bytes 4718596
  8.5 29.0 %collective-permute-start = (bf16[2,128,1536]{2,1,0:T(8,128)(2,1)}, bf16[2,128,1536]{2,1,0:T(8,128)(2,1)S(1)}, u32[]{:S(2)}, u32[]{:S(2)}) collective-permute-start(bf16[2,128,1536]{2,1,0:T(8,128)(2,1)} %pad_maximum_fusion.3), channel_id=1, source_target_pairs={{0,1},{1,0},{2,3},{3,2},{4,5},{5,4},{6,7},{7,6},{8,9},{9,8},{10,11... | collective-permute-start | bytes 2359304 | tf_op jit(solution)/shard_map/ppermute | solution.py:23
  10.0 2.8 %copy-start.24 = (bf16[1,128,3072]{2,1,0:T(8,128)(2,1)S(1)}, bf16[1,128,3072]{2,1,0:T(8,128)(2,1)}, u32[]{:S(2)}) copy-start(bf16[1,128,3072]{2,1,0:T(8,128)(2,1)} %param.8) | copy-start | bytes 2359300
  10.1 27.4 %copy-start.2 = (bf16[128,3072]{1,0:T(8,128)(2,1)}, bf16[128,3072]{1,0:T(8,128)(2,1)S(1)}, u32[]{:S(2)}) copy-start(bf16[128,3072]{1,0:T(8,128)(2,1)S(1)} %get-tuple-element.46.refs_0_.own) | copy-start | bytes 2359300
  10.1 27.2 %copy-start.19 = (bf16[1,128,1536]{2,1,0:T(8,128)(2,1)S(1)}, bf16[1,128,1536]{2,1,0:T(8,128)(2,1)}, u32[]{:S(2)}) copy-start(bf16[1,128,1536]{2,1,0:T(8,128)(2,1)} %get-tuple-element.81) | copy-start | bytes 1179652
  10.2 27.2 %copy-start.20 = (bf16[1,128,1536]{2,1,0:T(8,128)(2,1)S(1)}, bf16[1,128,1536]{2,1,0:T(8,128)(2,1)}, u32[]{:S(2)}) copy-start(bf16[1,128,1536]{2,1,0:T(8,128)(2,1)} %get-tuple-element.97) | copy-start | bytes 1179652
  10.2 37.1 %collective-permute-start.2 = (bf16[128,3072]{1,0:T(8,128)(2,1)S(1)}, bf16[128,3072]{1,0:T(8,128)(2,1)}, u32[]{:S(2)}, u32[]{:S(2)}) collective-permute-start(bf16[128,3072]{1,0:T(8,128)(2,1)S(1)} %get-tuple-element.74), channel_id=1, source_target_pairs={{0,16},{16,0},{1,17},{17,1},{2,18},{18,2},{3,19},{19,3},{4,20},{20... | collective-permute-start | bytes 2359304 | tf_op jit(solution)/shard_map/ppermute | solution.py:23
  12.9 23.0 %collective-permute-start.1 = (bf16[1,128,1536]{2,1,0:T(8,128)(2,1)S(1)}, bf16[1,128,1536]{2,1,0:T(8,128)(2,1)S(1)}, u32[]{:S(2)}, u32[]{:S(2)}) collective-permute-start(bf16[1,128,1536]{2,1,0:T(8,128)(2,1)S(1)} %get-tuple-element.76), channel_id=1, source_target_pairs={{0,1},{1,0},{2,3},{3,2},{4,5},{5,4},{6,7},{7,6},{8,9},{9,8},{10,11... | collective-permute-start | bytes 1179656 | tf_op jit(solution)/shard_map/ppermute | solution.py:23
  35.8 4.7 %copy-start.5 = (bf16[1,128,1536]{2,1,0:T(8,128)(2,1)}, bf16[1,128,1536]{2,1,0:T(8,128)(2,1)S(1)}, u32[]{:S(2)}) copy-start(bf16[1,128,1536]{2,1,0:T(8,128)(2,1)S(1)} %collective-permute-done.1.far_values) | copy-start | bytes 1179652
  35.9 22.7 %collective-permute-start.3 = (bf16[128,3072]{1,0:T(8,128)(2,1)S(1)}, bf16[128,3072]{1,0:T(8,128)(2,1)S(1)}, u32[]{:S(2)}, u32[]{:S(2)}) collective-permute-start(bf16[128,3072]{1,0:T(8,128)(2,1)S(1)} %get-tuple-element.46.refs_0_.own), channel_id=1, source_target_pairs={{0,1},{1,0},{2,3},{3,2},{4,5},{5,4},{6,7},{7,6},{8,9},{9,8},{10,11... | collective-permute-start | bytes 2359304 | tf_op jit(solution)/shard_map/ppermute | solution.py:23
  37.5 3.0 %copy-start = (bf16[2,128,1536]{2,1,0:T(8,128)(2,1)}, bf16[2,128,1536]{2,1,0:T(8,128)(2,1)S(1)}, u32[]{:S(2)}) copy-start(bf16[2,128,1536]{2,1,0:T(8,128)(2,1)S(1)} %collective-permute-done.far_both) | copy-start | bytes 2359300
  47.2 23.5 %collective-permute-start.4 = (bf16[128,3072]{1,0:T(8,128)(2,1)}, bf16[128,3072]{1,0:T(8,128)(2,1)}, u32[]{:S(2)}, u32[]{:S(2)}) collective-permute-start(bf16[128,3072]{1,0:T(8,128)(2,1)} %collective-permute-done.2.refs_2_.own), channel_id=1, source_target_pairs={{0,1},{1,0},{2,3},{3,2},{4,5},{5,4},{6,7},{7,6},{8,9},{9,8},{10,11... | collective-permute-start | bytes 2359304 | tf_op jit(solution)/shard_map/ppermute | solution.py:23
  48.7 36.7 %collective-permute-start.6 = (bf16[256,1536]{1,0:T(8,128)(2,1)}, bf16[256,1536]{1,0:T(8,128)(2,1)}, u32[]{:S(2)}, u32[]{:S(2)}) collective-permute-start(bf16[256,1536]{1,0:T(8,128)(2,1)} %forward.1), channel_id=1, source_target_pairs={{0,16},{16,0},{1,17},{17,1},{2,18},{18,2},{3,19},{19,3},{4,20},{20... | collective-permute-start | bytes 2359304 | tf_op jit(solution)/shard_map/ppermute | solution.py:23
  54.2 31.3 %collective-permute-start.8 = (bf16[192,1536]{1,0:T(8,128)(2,1)}, bf16[192,1536]{1,0:T(8,128)(2,1)}, u32[]{:S(2)}, u32[]{:S(2)}) collective-permute-start(bf16[192,1536]{1,0:T(8,128)(2,1)} %slice.8), channel_id=1, source_target_pairs={{0,8},{8,0},{1,9},{9,1},{2,10},{10,2},{3,11},{11,3},{4,12},{12,4},... | collective-permute-start | bytes 1769480 | tf_op jit(solution)/shard_map/ppermute | solution.py:23
  56.2 29.3 %collective-permute-start.10 = (bf16[192,1536]{1,0:T(8,128)(2,1)}, bf16[192,1536]{1,0:T(8,128)(2,1)}, u32[]{:S(2)}, u32[]{:S(2)}) collective-permute-start(bf16[192,1536]{1,0:T(8,128)(2,1)} %slice.9), channel_id=1, source_target_pairs={{0,4},{4,0},{1,5},{5,1},{2,6},{6,2},{3,7},{7,3},{8,12},{12,8},{9,1... | collective-permute-start | bytes 1769480 | tf_op jit(solution)/shard_map/ppermute | solution.py:23
  58.6 0.9 copy-start.10
  59.5 41.1 %collective-permute-start.13 = (bf16[2,384,1536]{2,1,0:T(8,128)(2,1)S(1)}, bf16[2,384,1536]{2,1,0:T(8,128)(2,1)}, u32[]{:S(2)}, u32[]{:S(2)}) collective-permute-start(bf16[2,384,1536]{2,1,0:T(8,128)(2,1)S(1)} %pad_maximum_fusion.refs_2_), channel_id=1, source_target_pairs={{0,2},{2,0},{1,3},{3,1},{4,6},{6,4},{5,7},{7,5},{8,10},{10,8},{9,1... | collective-permute-start | bytes 7077896 | tf_op jit(solution)/shard_map/ppermute | solution.py:23
  70.7 1.1 copy-start.3
  71.8 1.1 copy-start.11
  76.5 11.6 %copy-start.7 = (bf16[4,384,512]{2,1,0:T(8,128)(2,1)}, bf16[4,384,512]{2,1,0:T(8,128)(2,1)S(1)}, u32[]{:S(2)}) copy-start(bf16[4,384,512]{2,1,0:T(8,128)(2,1)S(1)} %get-tuple-element.54.refs_0_) | copy-start | bytes 4718596
  76.5 14.6 %collective-permute-start.5 = (bf16[4,384,512]{2,1,0:T(8,128)(2,1)}, bf16[4,384,512]{2,1,0:T(8,128)(2,1)}, u32[]{:S(2)}, u32[]{:S(2)}) collective-permute-start(bf16[4,384,512]{2,1,0:T(8,128)(2,1)} %get-tuple-element.41), channel_id=1, source_target_pairs={{0,2},{2,0},{1,3},{3,1},{4,6},{6,4},{5,7},{7,5},{8,10},{10,8},{9,1... | collective-permute-start | bytes 4718600 | tf_op jit(solution)/shard_map/ppermute | solution.py:23
  88.1 3.8 %collective-permute-start.11 = (bf16[2,256,1536]{2,1,0:T(8,128)(2,1)}, bf16[2,256,1536]{2,1,0:T(8,128)(2,1)}, u32[]{:S(2)}, u32[]{:S(2)}) collective-permute-start(bf16[2,256,1536]{2,1,0:T(8,128)(2,1)} %pad_maximum_fusion.1.refs_2_), channel_id=1, source_target_pairs={{0,2},{2,0},{1,3},{3,1},{4,6},{6,4},{5,7},{7,5},{8,10},{10,8},{9,1... | collective-permute-start | bytes 4718600 | tf_op jit(solution)/shard_map/ppermute | solution.py:23
  88.1 12.4 %collective-permute-start.12 = (bf16[1,384,1536]{2,1,0:T(8,128)(2,1)}, bf16[1,384,1536]{2,1,0:T(8,128)(2,1)}, u32[]{:S(2)}, u32[]{:S(2)}) collective-permute-start(bf16[1,384,1536]{2,1,0:T(8,128)(2,1)} %bitcast.13.refs_0_), channel_id=1, source_target_pairs={{0,2},{2,0},{1,3},{3,1},{4,6},{6,4},{5,7},{7,5},{8,10},{10,8},{9,1... | collective-permute-start | bytes 3538952 | tf_op jit(solution)/shard_map/ppermute | solution.py:23
  91.1 9.5 %collective-permute-start.14 = (bf16[1,384,1536]{2,1,0:T(8,128)(2,1)}, bf16[1,384,1536]{2,1,0:T(8,128)(2,1)}, u32[]{:S(2)}, u32[]{:S(2)}) collective-permute-start(bf16[1,384,1536]{2,1,0:T(8,128)(2,1)} %maximum_bitcast_fusion.refs_4_), channel_id=1, source_target_pairs={{0,2},{2,0},{1,3},{3,1},{4,6},{6,4},{5,7},{7,5},{8,10},{10,8},{9,1... | collective-permute-start | bytes 3538952 | tf_op jit(solution)/shard_map/ppermute | solution.py:23
  91.9 1.4 copy-start.8
  99.0 0.9 copy-start.13
  99.9 44.5 %collective-permute-start.18 = (bf16[2,384,1024]{2,1,0:T(8,128)(2,1)}, bf16[2,384,1024]{2,1,0:T(8,128)(2,1)}, u32[]{:S(2)}, u32[]{:S(2)}) collective-permute-start(bf16[2,384,1024]{2,1,0:T(8,128)(2,1)} %get-tuple-element.44), channel_id=1, source_target_pairs={{0,4},{4,0},{1,5},{5,1},{2,6},{6,2},{3,7},{7,3},{8,12},{12,8},{9,1... | collective-permute-start | bytes 4718600 | tf_op jit(solution)/shard_map/ppermute | solution.py:23
  107.1 0.7 copy-start.14
  107.8 0.7 copy-start.16
  108.5 16.4 %collective-permute-start.15 = (bf16[256,512]{1,0:T(8,128)(2,1)}, bf16[256,512]{1,0:T(8,128)(2,1)}, u32[]{:S(2)}, u32[]{:S(2)}) collective-permute-start(bf16[256,512]{1,0:T(8,128)(2,1)} %get-tuple-element.51), channel_id=1, source_target_pairs={{0,16},{16,0},{1,17},{17,1},{2,18},{18,2},{3,19},{19,3},{4,20},{20... | collective-permute-start | bytes 786440 | tf_op jit(solution)/shard_map/ppermute | solution.py:23
  108.6 35.8 %collective-permute-start.19 = (bf16[2,384,512]{2,1,0:T(8,128)(2,1)}, bf16[2,384,512]{2,1,0:T(8,128)(2,1)S(1)}, u32[]{:S(2)}, u32[]{:S(2)}) collective-permute-start(bf16[2,384,512]{2,1,0:T(8,128)(2,1)} %copy-done.13), channel_id=1, source_target_pairs={{0,8},{8,0},{1,9},{9,1},{2,10},{10,2},{3,11},{11,3},{4,12},{12,4},... | collective-permute-start | bytes 2359304 | tf_op jit(solution)/shard_map/ppermute | solution.py:23
  111.6 1.1 copy-start.4
  112.8 1.1 copy-start.12
  113.9 5.9 %copy-start.9 = (bf16[4,384,512]{2,1,0:T(8,128)(2,1)S(1)}, bf16[4,384,512]{2,1,0:T(8,128)(2,1)}, u32[]{:S(2)}) copy-start(bf16[4,384,512]{2,1,0:T(8,128)(2,1)} %copy-done.7) | copy-start | bytes 4718596
  119.8 5.1 %copy-start.17 = (bf16[256,512]{1,0:T(8,128)(2,1)S(1)}, bf16[256,512]{1,0:T(8,128)(2,1)}, u32[]{:S(2)}) copy-start(bf16[256,512]{1,0:T(8,128)(2,1)} %copy-done.16) | copy-start | bytes 786436
  119.8 5.2 %copy-start.1 = (bf16[2,128,1536]{2,1,0:T(8,128)(2,1)S(1)}, bf16[2,128,1536]{2,1,0:T(8,128)(2,1)}, u32[]{:S(2)}) copy-start(bf16[2,128,1536]{2,1,0:T(8,128)(2,1)} %copy-done) | copy-start | bytes 2359300
  119.8 5.2 %copy-start.6 = (bf16[1,128,1536]{2,1,0:T(8,128)(2,1)S(1)}, bf16[1,128,1536]{2,1,0:T(8,128)(2,1)}, u32[]{:S(2)}) copy-start(bf16[1,128,1536]{2,1,0:T(8,128)(2,1)} %copy-done.5) | copy-start | bytes 1179652
  124.9 12.2 %collective-permute-start.16 = (bf16[256,512]{1,0:T(8,128)(2,1)S(1)}, bf16[256,512]{1,0:T(8,128)(2,1)S(1)}, u32[]{:S(2)}, u32[]{:S(2)}) collective-permute-start(bf16[256,512]{1,0:T(8,128)(2,1)S(1)} %copy-done.17), channel_id=1, source_target_pairs={{0,16},{16,0},{1,17},{17,1},{2,18},{18,2},{3,19},{19,3},{4,20},{20... | collective-permute-start | bytes 786440 | tf_op jit(solution)/shard_map/ppermute | solution.py:23
  129.0 8.1 %copy-start.15 = (bf16[256,512]{1,0:T(8,128)(2,1)S(1)}, bf16[256,512]{1,0:T(8,128)(2,1)}, u32[]{:S(2)}) copy-start(bf16[256,512]{1,0:T(8,128)(2,1)} %copy-done.14) | copy-start | bytes 786436
  129.2 26.4 %collective-permute-start.20 = (bf16[3,128,512]{2,1,0:T(8,128)(2,1)S(1)}, bf16[3,128,512]{2,1,0:T(8,128)(2,1)S(1)}, u32[]{:S(2)}, u32[]{:S(2)}) collective-permute-start(bf16[3,128,512]{2,1,0:T(8,128)(2,1)S(1)} %get-tuple-element.71), channel_id=1, source_target_pairs={{0,1},{1,0},{2,3},{3,2},{4,5},{5,4},{6,7},{7,6},{8,9},{9,8},{10,11... | collective-permute-start | bytes 1179656 | tf_op jit(solution)/shard_map/ppermute | solution.py:23
  137.1 14.9 %collective-permute-start.17 = (bf16[256,512]{1,0:T(8,128)(2,1)S(1)}, bf16[256,512]{1,0:T(8,128)(2,1)S(1)}, u32[]{:S(2)}, u32[]{:S(2)}) collective-permute-start(bf16[256,512]{1,0:T(8,128)(2,1)S(1)} %copy-done.15), channel_id=1, source_target_pairs={{0,16},{16,0},{1,17},{17,1},{2,18},{18,2},{3,19},{19,3},{4,20},{20... | collective-permute-start | bytes 786440 | tf_op jit(solution)/shard_map/ppermute | solution.py:23
  143.7 12.0 %collective-permute-start.21 = (bf16[3,128,512]{2,1,0:T(8,128)(2,1)S(1)}, bf16[3,128,512]{2,1,0:T(8,128)(2,1)S(1)}, u32[]{:S(2)}, u32[]{:S(2)}) collective-permute-start(bf16[3,128,512]{2,1,0:T(8,128)(2,1)S(1)} %get-tuple-element.72), channel_id=1, source_target_pairs={{0,1},{1,0},{2,3},{3,2},{4,5},{5,4},{6,7},{7,6},{8,9},{9,8},{10,11... | collective-permute-start | bytes 1179656 | tf_op jit(solution)/shard_map/ppermute | solution.py:23
  146.9 17.9 %collective-permute-start.24 = (bf16[1,384,512]{2,1,0:T(8,128)(2,1)S(1)}, bf16[1,384,512]{2,1,0:T(8,128)(2,1)S(1)}, u32[]{:S(2)}, u32[]{:S(2)}) collective-permute-start(bf16[1,384,512]{2,1,0:T(8,128)(2,1)S(1)} %dynamic-slice_convert_fusion.1), channel_id=1, source_target_pairs={{0,4},{4,0},{1,5},{5,1},{2,6},{6,2},{3,7},{7,3},{8,12},{12,8},{9,1... | collective-permute-start | bytes 1179656 | tf_op jit(solution)/shard_map/ppermute | solution.py:23
  148.6 20.2 %collective-permute-start.23 = (bf16[1,384,1024]{2,1,0:T(8,128)(2,1)S(1)}, bf16[1,384,1024]{2,1,0:T(8,128)(2,1)S(1)}, u32[]{:S(2)}, u32[]{:S(2)}) collective-permute-start(bf16[1,384,1024]{2,1,0:T(8,128)(2,1)S(1)} %dynamic-slice_convert_fusion), channel_id=1, source_target_pairs={{0,8},{8,0},{1,9},{9,1},{2,10},{10,2},{3,11},{11,3},{4,12},{12,4},... | collective-permute-start | bytes 2359304 | tf_op jit(solution)/shard_map/ppermute | solution.py:23
  155.0 9.7 %collective-permute-start.22 = (bf16[3,128,512]{2,1,0:T(8,128)(2,1)S(1)}, bf16[3,128,512]{2,1,0:T(8,128)(2,1)S(1)}, u32[]{:S(2)}, u32[]{:S(2)}) collective-permute-start(bf16[3,128,512]{2,1,0:T(8,128)(2,1)S(1)} %get-tuple-element.73), channel_id=1, source_target_pairs={{0,1},{1,0},{2,3},{3,2},{4,5},{5,4},{6,7},{7,6},{8,9},{9,8},{10,11... | collective-permute-start | bytes 1179656 | tf_op jit(solution)/shard_map/ppermute | solution.py:23
  164.8 4.3 %copy-start.21 = (bf16[1,128,3072]{2,1,0:T(8,128)(2,1)}, bf16[1,128,3072]{2,1,0:T(8,128)(2,1)S(1)}, u32[]{:S(2)}) copy-start(bf16[1,128,3072]{2,1,0:T(8,128)(2,1)S(1)} %get-tuple-element.84) | copy-start | bytes 2359300
  164.8 4.3 %copy-start.22 = (bf16[1,128,3072]{2,1,0:T(8,128)(2,1)}, bf16[1,128,3072]{2,1,0:T(8,128)(2,1)S(1)}, u32[]{:S(2)}) copy-start(bf16[1,128,3072]{2,1,0:T(8,128)(2,1)S(1)} %get-tuple-element.82) | copy-start | bytes 2359300
  164.8 4.3 %copy-start.23 = (bf16[1,128,3072]{2,1,0:T(8,128)(2,1)}, bf16[1,128,3072]{2,1,0:T(8,128)(2,1)S(1)}, u32[]{:S(2)}) copy-start(bf16[1,128,3072]{2,1,0:T(8,128)(2,1)S(1)} %get-tuple-element.83) | copy-start | bytes 2359300

commit v11 on v10

--- a/solution.py
+++ b/solution.py
@@ -374,7 +374,7 @@
     ]
     kept = rows_products(jobs, after(by_rows, partial), attends, jnp.float32)
     for group in range(1, groups):
-        terms.append(returned(group, terms[group - 1], kept))
+        terms.append(returned(group, terms[group - 1], partial))
 
     stays, arrivals = [], []
     second = []
@@ -386,15 +386,18 @@
             sent = leaving[:, (by - 1) * tokens : by * tokens]
             column = ((mine + by) % seq) * features + start
             arrivals.append((column, shift(sent, "seq", -by)))
-        if group == max(groups - 2, 0):
-            for (_, axis), arrived, total in zip(orders, after(arrive, staying), kept):
-                for term in arrived:
-                    total = total + term.astype(jnp.float32)
-                passed = [part_of(total, axis, by, 0).astype(jnp.bfloat16) for by in others(axis)]
-                final = part_of(total, axis, 0, 0)
-                second.append((final, passed))
-            if groups > 1:
-                terms[-1] = after(terms[-1], [passed for _, passed in second])
+        last = len(orders) if group == groups - 1 else group + 1
+        for split in range(len(second), min(last, len(orders))):
+            axis = orders[split][1]
+            arrived, total = after(arrive[split], staying), kept[split]
+            for term in arrived:
+                total = total + term.astype(jnp.float32)
+            passed = [part_of(total, axis, by, 0).astype(jnp.bfloat16) for by in others(axis)]
+            second.append((part_of(total, axis, 0, 0), passed))
+            if group + 1 < groups:
+                terms[group + 1] = after(terms[group + 1], passed)
+        if group > 0 and group + 1 < groups:
+            terms[group + 1] = after(terms[group + 1], [array for _, array in arrivals])
 
     columns = []
     for (_, axis), (final, passed) in zip(orders, second):

time: 171 us -> 170 us (level)
  local copies, waits for them, and re-layouts: 16.3 us -> 13.4 us
  waiting for transfers between devices: 73 us -> 74.9 us
    unnamed x50 -> x36, local copies, waits for them, and re-layouts: 9.2 us -> 5.1 us
    dynamic_slice x3, local copies, waits for them, and re-layouts: 2.48 us -> 4.7 us  [part_of(): return lax.dynamic_slice_in_dim(array, at * size, size, dim)]
    ppermute x25, waiting for transfers between devices: 73 us -> 74.9 us  [shift(): lax.ppermute(array, axis, [(i, (i + by) % count) for i in range(count)])]
  transfers between devices with their start and end apart: 25 -> 25, of which waited for: 9 -> 11; matrix products, arithmetic and copies ran while one was open for 10% -> 12% of each run, Pallas kernels for 23% -> 24%
where the time goes in v11:
time: 170 us
  waiting for transfers between devices  74.9 us (44%)
  Pallas kernels  40.8 us (24%)
  starting transfers between devices  27.5 us (16%)
  local copies, waits for them, and re-layouts  13.4 us (8%)
  other arithmetic  12.5 us (7%)
    ppermute x25, waiting for transfers between devices, shift(): lax.ppermute(array, axis, [(i, (i + by) % count) for i in range(count)])  74.9 us
    pallas_call x9, Pallas kernels, whole_call(): pl.pallas_call(kernel, in_specs=in_specs, out_specs=jax.tree.map(lambda _...  40.8 us
    ppermute x25, starting transfers between devices, shift(): lax.ppermute(array, axis, [(i, (i + by) % count) for i in range(count)])  27.5 us
    unnamed x36, local copies, waits for them, and re-layouts  5.1 us
    dynamic_slice x3, local copies, waits for them, and re-layouts, part_of(): return lax.dynamic_slice_in_dim(array, at * size, size, dim)  4.7 us
  transfers between devices with their start and end apart: 25, of which 11 were waited for; matrix products, arithmetic and copies ran while one was open for 12% of the time, Pallas kernels for 24%

profile of v11, /device:TPU:0, one launch (start us, length us, event | category | flops | bytes accessed | tf_op | source)
XLA Modules:
  0.0 170.0 jit_solution(17495255630599991557)
XLA Ops:
  0.6 3.0 %collective-permute-start.7 = (bf16[384,1536]{1,0:T(8,128)(2,1)}, bf16[384,1536]{1,0:T(8,128)(2,1)S(1)}, u32[]{:S(2)}, u32[]{:S(2)}) collective-permute-start(bf16[384,1536]{1,0:T(8,128)(2,1)} %param.9), channel_id=1, source_target_pairs={{0,4},{4,0},{1,5},{5,1},{2,6},{6,2},{3,7},{7,3},{8,12},{12,8},{9,1... | collective-permute-start | bytes 3538952 | tf_op jit(solution)/shard_map/ppermute | solution.py:23
  3.6 1.6 collective-permute-start.9
  5.2 2.2 %constant_dynamic-slice_fusion.1 = (bf16[1,128,1536]{2,1,0:T(8,128)(2,1)S(1)}, bf16[1,128,1536]{2,1,0:T(8,128)(2,1)S(1)}, bf16[1,128,1536]{2,1,0:T(8,128)(2,1)}, bf16[1,128,1536]{2,1,0:T(8,128)(2,1)S(1)}) fusion(bf16[1,128,3072]{2,1,0:T(8,128)(2,1)} %param.7, s32[]{:T(128)S(6)} %select_n.174, s32[]{:T(128)S(6)} %select_n.172, bf16[1,128,3072]{2,1,0:T(8,128)(2,1)} %param.6), kind=kLoop, calls=%fused_computation.33 | loop fusion | bytes 3145736 | tf_op jit(solution)/shard_map/dynamic_slice | solution.py:34
  7.4 0.9 pad_maximum_fusion.3
  8.4 1.5 collective-permute-start
  9.9 2.4 %dynamic-slice_bitcast_fusion = (bf16[128,3072]{1,0:T(8,128)(2,1)S(1)}, bf16[128,3072]{1,0:T(8,128)(2,1)}) fusion(bf16[1,128,6144]{2,1,0:T(8,128)(2,1)} %param.5, s32[]{:T(128)S(6)} %select_n.184, s32[]{:T(128)S(6)} %select_n.182), kind=kLoop, calls=%fused_computation.12 | loop fusion | bytes 3145736 | tf_op jit(solution)/shard_map/dynamic_slice | solution.py:34
  12.3 2.6 %collective-permute-start.2 = (bf16[128,3072]{1,0:T(8,128)(2,1)S(1)}, bf16[128,3072]{1,0:T(8,128)(2,1)}, u32[]{:S(2)}, u32[]{:S(2)}) collective-permute-start(bf16[128,3072]{1,0:T(8,128)(2,1)S(1)} %get-tuple-element.78), channel_id=1, source_target_pairs={{0,16},{16,0},{1,17},{17,1},{2,18},{18,2},{3,19},{19,3},{4,20},{20... | collective-permute-start | bytes 2359304 | tf_op jit(solution)/shard_map/ppermute | solution.py:23
  15.0 0.6 collective-permute-start.1
  15.6 0.1 pad_maximum_fusion.2.own
  15.7 20.1 %collective-permute-done.1.far_values = bf16[1,128,1536]{2,1,0:T(8,128)(2,1)S(1)} collective-permute-done((bf16[1,128,1536]{2,1,0:T(8,128)(2,1)S(1)}, bf16[1,128,1536]{2,1,0:T(8,128)(2,1)S(1)}, u32[]{:S(2)}, u32[]{:S(2)}) %collective-permute-start.1) | collective-permute-done | bytes 393248 | tf_op jit(solution)/shard_map/ppermute | solution.py:23
  35.7 1.5 collective-permute-start.3
  37.3 2.9 %forward.1 = bf16[256,1536]{1,0:T(8,128)(2,1)} custom-call(bf16[3,128,1536]{2,1,0:T(8,128)(2,1)S(1)} %pad_maximum_fusion.2.own, bf16[2,128,1536]{2,1,0:T(8,128)(2,1)S(1)} %collective-permute-done.far_both, bf16[1,128,1536]{2,1,0:T(8,128)(2,1)S(1)} %collective-permute-done.1.far_values), custom_call_target="tpu_custom_call" | custom-call | flops 1024 | bytes 1024 | tf_op jit(solution)/shard_map/forward/pallas_call | solution.py:107
  40.2 7.0 %collective-permute-done.2.refs_2_.own = bf16[128,3072]{1,0:T(8,128)(2,1)} collective-permute-done((bf16[128,3072]{1,0:T(8,128)(2,1)S(1)}, bf16[128,3072]{1,0:T(8,128)(2,1)}, u32[]{:S(2)}, u32[]{:S(2)}) %collective-permute-start.2) | collective-permute-done | bytes 786464 | tf_op jit(solution)/shard_map/ppermute | solution.py:23
  47.2 1.5 collective-permute-start.4
  48.7 3.5 %collective-permute-start.6 = (bf16[256,1536]{1,0:T(8,128)(2,1)}, bf16[256,1536]{1,0:T(8,128)(2,1)}, u32[]{:S(2)}, u32[]{:S(2)}) collective-permute-start(bf16[256,1536]{1,0:T(8,128)(2,1)} %forward.1), channel_id=1, source_target_pairs={{0,16},{16,0},{1,17},{17,1},{2,18},{18,2},{3,19},{19,3},{4,20},{20... | collective-permute-start | bytes 2359304 | tf_op jit(solution)/shard_map/ppermute | solution.py:23
  52.2 0.9 slice.8
  53.2 0.1 collective-permute-start.8
  53.3 1.9 %slice.9 = bf16[192,1536]{1,0:T(8,128)(2,1)} slice(bf16[384,1536]{1,0:T(8,128)(2,1)} %collective-permute-done.9), slice={[192:384], [0:1536]} | slice | bytes 1179648 | tf_op jit(solution)/shard_map/slice | solution.py:317
  55.2 0.5 collective-permute-start.10
  55.8 1.8 %pad_maximum_fusion.refs_2_ = bf16[2,384,1536]{2,1,0:T(8,128)(2,1)S(1)} fusion(bf16[1,384,1536]{2,1,0:T(8,128)(2,1)} %bitcast.15, bf16[1,384,1536]{2,1,0:T(8,128)(2,1)} %bitcast.24), kind=kLoop, calls=%fused_computation.1 | loop fusion | flops 1179648 | bytes 4718592 | tf_op jit(solution)/shard_map/stack | solution.py:318
  57.7 13.1 %collective-permute-done.4.refs_3_.far = bf16[128,3072]{1,0:T(8,128)(2,1)} collective-permute-done((bf16[128,3072]{1,0:T(8,128)(2,1)}, bf16[128,3072]{1,0:T(8,128)(2,1)}, u32[]{:S(2)}, u32[]{:S(2)}) %collective-permute-start.4) | collective-permute-done | bytes 786464 | tf_op jit(solution)/shard_map/ppermute | solution.py:23
  70.8 4.0 %turn.1 = (bf16[4,384,512]{2,1,0:T(8,128)(2,1)S(1)}, bf16[4,384,512]{2,1,0:T(8,128)(2,1)}) custom-call(s32[1]{0:T(128)} %bitcast.10.core_ref, bf16[128,3072]{1,0:T(8,128)(2,1)} %get-tuple-element.48.refs_0_.own, bf16[128,3072]{1,0:T(8,128)(2,1)} %collective-permute-done.3.refs_1_.far, bf16[128,3072]{1,0:T(8,128)(2,1)} %collective-permute-done.2.refs_2_.own, ...), custom_call_target="tpu_custom_call" | custom-call | flops 1024 | bytes 1024 | tf_op jit(solution)/shard_map/turn/pallas_call | solution.py:107
  74.9 10.6 %collective-permute-done.6 = bf16[256,1536]{1,0:T(8,128)(2,1)} collective-permute-done((bf16[256,1536]{1,0:T(8,128)(2,1)}, bf16[256,1536]{1,0:T(8,128)(2,1)}, u32[]{:S(2)}, u32[]{:S(2)}) %collective-permute-start.6) | collective-permute-done | bytes 786464 | tf_op jit(solution)/shard_map/ppermute | solution.py:23
  85.5 2.7 %pad_maximum_fusion.1.refs_2_ = bf16[2,256,1536]{2,1,0:T(8,128)(2,1)} fusion(bf16[1,256,1536]{2,1,0:T(8,128)(2,1)} %bitcast.12, bf16[1,256,1536]{2,1,0:T(8,128)(2,1)} %bitcast.11), kind=kLoop, calls=%fused_computation.3 | loop fusion | flops 786432 | bytes 3145728 | tf_op jit(solution)/shard_map/stack | solution.py:328
  88.1 0.5 collective-permute-start.12
  88.7 2.4 %maximum_bitcast_fusion.refs_4_ = bf16[1,384,1536]{2,1,0:T(8,128)(2,1)} fusion(bf16[192,1536]{1,0:T(8,128)(2,1)} %collective-permute-done.10, bf16[192,1536]{1,0:T(8,128)(2,1)} %collective-permute-done.8), kind=kLoop, calls=%fused_computation.8 | loop fusion | flops 2359296 | bytes 2359296 | tf_op jit(solution)/shard_map/stack | solution.py:331
  91.1 0.1 pad_add_fusion.at_ref
  91.2 0.7 collective-permute-done.11.refs_3_
  91.9 1.4 copy-done.5
  93.3 5.7 %rows.2 = (bf16[2,384,1024]{2,1,0:T(8,128)(2,1)}, bf16[2,384,512]{2,1,0:T(8,128)(2,1)S(1)}) custom-call(s32[4]{0:T(128)S(1)} %pad_add_fusion.at_ref, bf16[4,384,512]{2,1,0:T(8,128)(2,1)S(1)} %copy-done.5, bf16[4,384,512]{2,1,0:T(8,128)(2,1)} %collective-permute-done.5.refs_1_, bf16[2,256,1536]{2,1,0:T(8,128)(2,1)} %pad_maximum_fusion.1.refs_2_, ...), custom_call_target="tpu_custom_call" | custom-call | flops 1024 | bytes 1024 | tf_op jit(solution)/shard_map/rows/pallas_call | solution.py:107
  99.0 0.9 copy-done.7
  99.9 0.5 collective-permute-start.17
  100.4 0.1 stack.70.at_ref
  100.5 6.5 %partial.3 = (bf16[256,512]{1,0:T(8,128)(2,1)}, bf16[256,512]{1,0:T(8,128)(2,1)S(1)}, bf16[256,512]{1,0:T(8,128)(2,1)S(1)}) custom-call(s32[8]{0:T(128)S(1)} %stack.70.at_ref, bf16[128,3072]{1,0:T(8,128)(2,1)} %collective-permute-done.2.refs_2_.own, bf16[128,3072]{1,0:T(8,128)(2,1)} %collective-permute-done.4.refs_3_.far, ...), custom_call_target="tpu_custom_call" | custom-call | flops 1024 | bytes 1024 | tf_op jit(solution)/shard_map/partial/pallas_call | solution.py:107
  107.1 0.7 copy-done.8
  107.8 0.7 copy-done.10
  108.5 0.1 pad_add_fusion.1.at_ref
  108.6 3.0 %collective-permute-start.19 = (bf16[2,384,512]{2,1,0:T(8,128)(2,1)}, bf16[2,384,512]{2,1,0:T(8,128)(2,1)S(1)}, u32[]{:S(2)}, u32[]{:S(2)}) collective-permute-start(bf16[2,384,512]{2,1,0:T(8,128)(2,1)} %copy-done.7), channel_id=1, source_target_pairs={{0,8},{8,0},{1,9},{9,1},{2,10},{10,2},{3,11},{11,3},{4,12},{12,4},... | collective-permute-start | bytes 2359304 | tf_op jit(solution)/shard_map/ppermute | solution.py:23
  111.6 6.2 %partial.2 = (f32[256,512]{1,0:T(8,128)S(1)}, f32[256,512]{1,0:T(8,128)S(1)}, f32[256,512]{1,0:T(8,128)S(1)}) custom-call(s32[8]{0:T(128)S(1)} %stack.70.at_ref, bf16[128,3072]{1,0:T(8,128)(2,1)} %get-tuple-element.48.refs_0_.own, bf16[128,3072]{1,0:T(8,128)(2,1)} %collective-permute-done.3.refs_1_.far, bf16[1,384,1536]{2,1,0:T(8,128)(2,1)} %bitcast.13.refs_0_, ...), custom_call_target="tpu_custom_call" | custom-call | flops 1024 | bytes 1024 | tf_op jit(solution)/shard_map/partial/pallas_call | solution.py:107
  117.9 5.1 %rows.3 = (f32[2,384,1024]{2,1,0:T(8,128)S(1)}, f32[2,384,512]{2,1,0:T(8,128)S(1)}) custom-call(s32[4]{0:T(128)S(1)} %pad_add_fusion.1.at_ref, bf16[4,384,512]{2,1,0:T(8,128)(2,1)S(1)} %copy-done.6, bf16[4,384,512]{2,1,0:T(8,128)(2,1)} %collective-permute-done.5.refs_1_, bf16[2,256,1536]{2,1,0:T(8,128)(2,1)} %pad_maximum_fusion.1.refs_2_, ...), custom_call_target="tpu_custom_call" | custom-call | flops 1024 | bytes 1024 | tf_op jit(solution)/shard_map/rows/pallas_call | solution.py:107
  123.0 0.4 collective-permute-done.15.refs_1_
  123.3 4.0 %backward.3 = (bf16[3,128,512]{2,1,0:T(8,128)(2,1)S(1)}, bf16[3,128,512]{2,1,0:T(8,128)(2,1)S(1)}) custom-call(bf16[3,128,1536]{2,1,0:T(8,128)(2,1)S(1)} %pad_maximum_fusion.2.own, bf16[2,128,1536]{2,1,0:T(8,128)(2,1)S(1)} %copy-done.1, bf16[1,128,1536]{2,1,0:T(8,128)(2,1)S(1)} %copy-done.3, f32[256,512]{1,0:T(8,128)S(1)} %get-tuple-element.52.refs_0_, ...), custom_call_target="tpu_custom_call" | custom-call | flops 1024 | bytes 1024 | tf_op jit(solution)/shard_map/backward/pallas_call | solution.py:107
  127.5 0.6 collective-permute-start.20
  128.2 8.9 %collective-permute-done.16.refs_1_ = bf16[256,512]{1,0:T(8,128)(2,1)S(1)} collective-permute-done((bf16[256,512]{1,0:T(8,128)(2,1)S(1)}, bf16[256,512]{1,0:T(8,128)(2,1)S(1)}, u32[]{:S(2)}, u32[]{:S(2)}) %collective-permute-start.16) | collective-permute-done | bytes 262176 | tf_op jit(solution)/shard_map/ppermute | solution.py:23
  137.1 3.4 %collective-permute-start.18 = (bf16[256,512]{1,0:T(8,128)(2,1)S(1)}, bf16[256,512]{1,0:T(8,128)(2,1)S(1)}, u32[]{:S(2)}, u32[]{:S(2)}) collective-permute-start(bf16[256,512]{1,0:T(8,128)(2,1)S(1)} %copy-done.9), channel_id=1, source_target_pairs={{0,16},{16,0},{1,17},{17,1},{2,18},{18,2},{3,19},{19,3},{4,20},{20... | collective-permute-start | bytes 786440 | tf_op jit(solution)/shard_map/ppermute | solution.py:23
  140.5 2.1 %convert_add_fusion = f32[2,384,1024]{2,1,0:T(8,128)S(1)} fusion(f32[2,384,1024]{2,1,0:T(8,128)S(1)} %get-tuple-element.58, bf16[2,384,1024]{2,1,0:T(8,128)(2,1)} %collective-permute-done.17), kind=kLoop, calls=%fused_computation | loop fusion | flops 1572864 | bytes 7864320 | tf_op jit(solution)/shard_map/add | solution.py:394
  142.6 0.1 dynamic-slice_convert_fusion
  142.7 0.2 collective-permute-start.23
  142.9 3.2 %backward.4 = (bf16[3,128,512]{2,1,0:T(8,128)(2,1)S(1)}, bf16[3,128,512]{2,1,0:T(8,128)(2,1)S(1)}) custom-call(bf16[3,128,1536]{2,1,0:T(8,128)(2,1)S(1)} %pad_maximum_fusion.2.own, bf16[2,128,1536]{2,1,0:T(8,128)(2,1)S(1)} %copy-done.1, bf16[1,128,1536]{2,1,0:T(8,128)(2,1)S(1)} %copy-done.3, f32[256,512]{1,0:T(8,128)S(1)} %get-tuple-element.54.refs_0_, ...), custom_call_target="tpu_custom_call" | custom-call | flops 1024 | bytes 1024 | tf_op jit(solution)/shard_map/backward/pallas_call | solution.py:107
  146.2 0.6 collective-permute-start.21
  146.8 0.3 convert_add_fusion.1
  147.1 1.6 collective-permute-start.24
  148.7 3.3 %collective-permute-done.18.refs_1_ = bf16[256,512]{1,0:T(8,128)(2,1)S(1)} collective-permute-done((bf16[256,512]{1,0:T(8,128)(2,1)S(1)}, bf16[256,512]{1,0:T(8,128)(2,1)S(1)}, u32[]{:S(2)}, u32[]{:S(2)}) %collective-permute-start.18) | collective-permute-done | bytes 262176 | tf_op jit(solution)/shard_map/ppermute | solution.py:23
  152.0 4.3 %collective-permute-done.21 = bf16[3,128,512]{2,1,0:T(8,128)(2,1)S(1)} collective-permute-done((bf16[3,128,512]{2,1,0:T(8,128)(2,1)S(1)}, bf16[3,128,512]{2,1,0:T(8,128)(2,1)S(1)}, u32[]{:S(2)}, u32[]{:S(2)}) %collective-permute-start.21) | collective-permute-done | bytes 393248 | tf_op jit(solution)/shard_map/ppermute | solution.py:23
  156.3 3.0 %backward.5 = (bf16[3,128,512]{2,1,0:T(8,128)(2,1)S(1)}, bf16[3,128,512]{2,1,0:T(8,128)(2,1)S(1)}) custom-call(bf16[3,128,1536]{2,1,0:T(8,128)(2,1)S(1)} %pad_maximum_fusion.2.own, bf16[2,128,1536]{2,1,0:T(8,128)(2,1)S(1)} %copy-done.1, bf16[1,128,1536]{2,1,0:T(8,128)(2,1)S(1)} %copy-done.3, f32[256,512]{1,0:T(8,128)S(1)} %get-tuple-element.55.refs_0_, ...), custom_call_target="tpu_custom_call" | custom-call | flops 1024 | bytes 1024 | tf_op jit(solution)/shard_map/backward/pallas_call | solution.py:107
  159.3 0.6 collective-permute-start.22
  160.1 0.1 add_bitcast_fusion.1
  160.2 4.4 %collective-permute-done.23 = bf16[1,384,1024]{2,1,0:T(8,128)(2,1)S(1)} collective-permute-done((bf16[1,384,1024]{2,1,0:T(8,128)(2,1)S(1)}, bf16[1,384,1024]{2,1,0:T(8,128)(2,1)S(1)}, u32[]{:S(2)}, u32[]{:S(2)}) %collective-permute-start.23) | collective-permute-done | bytes 786464 | tf_op jit(solution)/shard_map/ppermute | solution.py:23
  164.6 0.2 add_bitcast_fusion
  164.8 1.6 maximum_multiply_fusion
  166.4 2.1 %collective-permute-done.22 = bf16[3,128,512]{2,1,0:T(8,128)(2,1)S(1)} collective-permute-done((bf16[3,128,512]{2,1,0:T(8,128)(2,1)S(1)}, bf16[3,128,512]{2,1,0:T(8,128)(2,1)S(1)}, u32[]{:S(2)}, u32[]{:S(2)}) %collective-permute-start.22) | collective-permute-done | bytes 393248 | tf_op jit(solution)/shard_map/ppermute | solution.py:23
  168.6 0.9 copy-done.14
  169.5 0.3 copy-done.15
  169.7 0.3 copy-done.16
  (64 shorter events, 0.8 us)
Async XLA Ops:
  0.6 51.6 %collective-permute-start.7 = (bf16[384,1536]{1,0:T(8,128)(2,1)}, bf16[384,1536]{1,0:T(8,128)(2,1)S(1)}, u32[]{:S(2)}, u32[]{:S(2)}) collective-permute-start(bf16[384,1536]{1,0:T(8,128)(2,1)} %param.9), channel_id=1, source_target_pairs={{0,4},{4,0},{1,5},{5,1},{2,6},{6,2},{3,7},{7,3},{8,12},{12,8},{9,1... | collective-permute-start | bytes 3538952 | tf_op jit(solution)/shard_map/ppermute | solution.py:23
  3.6 49.7 %collective-permute-start.9 = (bf16[384,1536]{1,0:T(8,128)(2,1)}, bf16[384,1536]{1,0:T(8,128)(2,1)}, u32[]{:S(2)}, u32[]{:S(2)}) collective-permute-start(bf16[384,1536]{1,0:T(8,128)(2,1)} %param.9), channel_id=1, source_target_pairs={{0,8},{8,0},{1,9},{9,1},{2,10},{10,2},{3,11},{11,3},{4,12},{12,4},... | collective-permute-start | bytes 3538952 | tf_op jit(solution)/shard_map/ppermute | solution.py:23
  8.4 28.9 %collective-permute-start = (bf16[2,128,1536]{2,1,0:T(8,128)(2,1)}, bf16[2,128,1536]{2,1,0:T(8,128)(2,1)S(1)}, u32[]{:S(2)}, u32[]{:S(2)}) collective-permute-start(bf16[2,128,1536]{2,1,0:T(8,128)(2,1)} %pad_maximum_fusion.3), channel_id=1, source_target_pairs={{0,1},{1,0},{2,3},{3,2},{4,5},{5,4},{6,7},{7,6},{8,9},{9,8},{10,11... | collective-permute-start | bytes 2359304 | tf_op jit(solution)/shard_map/ppermute | solution.py:23
  9.9 5.0 %copy-start.17 = (bf16[1,128,3072]{2,1,0:T(8,128)(2,1)S(1)}, bf16[1,128,3072]{2,1,0:T(8,128)(2,1)}, u32[]{:S(2)}) copy-start(bf16[1,128,3072]{2,1,0:T(8,128)(2,1)} %param.8) | copy-start | bytes 2359300
  12.3 3.2 %copy-start.13 = (bf16[1,128,1536]{2,1,0:T(8,128)(2,1)S(1)}, bf16[1,128,1536]{2,1,0:T(8,128)(2,1)}, u32[]{:S(2)}) copy-start(bf16[1,128,1536]{2,1,0:T(8,128)(2,1)} %get-tuple-element.101) | copy-start | bytes 1179652
  12.3 34.9 %collective-permute-start.2 = (bf16[128,3072]{1,0:T(8,128)(2,1)S(1)}, bf16[128,3072]{1,0:T(8,128)(2,1)}, u32[]{:S(2)}, u32[]{:S(2)}) collective-permute-start(bf16[128,3072]{1,0:T(8,128)(2,1)S(1)} %get-tuple-element.78), channel_id=1, source_target_pairs={{0,16},{16,0},{1,17},{17,1},{2,18},{18,2},{3,19},{19,3},{4,20},{20... | collective-permute-start | bytes 2359304 | tf_op jit(solution)/shard_map/ppermute | solution.py:23
  15.0 20.8 %collective-permute-start.1 = (bf16[1,128,1536]{2,1,0:T(8,128)(2,1)S(1)}, bf16[1,128,1536]{2,1,0:T(8,128)(2,1)S(1)}, u32[]{:S(2)}, u32[]{:S(2)}) collective-permute-start(bf16[1,128,1536]{2,1,0:T(8,128)(2,1)S(1)} %get-tuple-element.80), channel_id=1, source_target_pairs={{0,1},{1,0},{2,3},{3,2},{4,5},{5,4},{6,7},{7,6},{8,9},{9,8},{10,11... | collective-permute-start | bytes 1179656 | tf_op jit(solution)/shard_map/ppermute | solution.py:23
  35.7 4.5 %copy-start.2 = (bf16[1,128,1536]{2,1,0:T(8,128)(2,1)}, bf16[1,128,1536]{2,1,0:T(8,128)(2,1)S(1)}, u32[]{:S(2)}) copy-start(bf16[1,128,1536]{2,1,0:T(8,128)(2,1)S(1)} %collective-permute-done.1.far_values) | copy-start | bytes 1179652
  35.7 21.9 %collective-permute-start.3 = (bf16[128,3072]{1,0:T(8,128)(2,1)}, bf16[128,3072]{1,0:T(8,128)(2,1)}, u32[]{:S(2)}, u32[]{:S(2)}) collective-permute-start(bf16[128,3072]{1,0:T(8,128)(2,1)} %get-tuple-element.48.refs_0_.own), channel_id=1, source_target_pairs={{0,1},{1,0},{2,3},{3,2},{4,5},{5,4},{6,7},{7,6},{8,9},{9,8},{10,11... | collective-permute-start | bytes 2359304 | tf_op jit(solution)/shard_map/ppermute | solution.py:23
  37.3 2.9 %copy-start = (bf16[2,128,1536]{2,1,0:T(8,128)(2,1)}, bf16[2,128,1536]{2,1,0:T(8,128)(2,1)S(1)}, u32[]{:S(2)}) copy-start(bf16[2,128,1536]{2,1,0:T(8,128)(2,1)S(1)} %collective-permute-done.far_both) | copy-start | bytes 2359300
  47.2 23.6 %collective-permute-start.4 = (bf16[128,3072]{1,0:T(8,128)(2,1)}, bf16[128,3072]{1,0:T(8,128)(2,1)}, u32[]{:S(2)}, u32[]{:S(2)}) collective-permute-start(bf16[128,3072]{1,0:T(8,128)(2,1)} %collective-permute-done.2.refs_2_.own), channel_id=1, source_target_pairs={{0,1},{1,0},{2,3},{3,2},{4,5},{5,4},{6,7},{7,6},{8,9},{9,8},{10,11... | collective-permute-start | bytes 2359304 | tf_op jit(solution)/shard_map/ppermute | solution.py:23
  48.7 36.7 %collective-permute-start.6 = (bf16[256,1536]{1,0:T(8,128)(2,1)}, bf16[256,1536]{1,0:T(8,128)(2,1)}, u32[]{:S(2)}, u32[]{:S(2)}) collective-permute-start(bf16[256,1536]{1,0:T(8,128)(2,1)} %forward.1), channel_id=1, source_target_pairs={{0,16},{16,0},{1,17},{17,1},{2,18},{18,2},{3,19},{19,3},{4,20},{20... | collective-permute-start | bytes 2359304 | tf_op jit(solution)/shard_map/ppermute | solution.py:23
  52.2 3.5 %copy-start.12 = (bf16[384,1536]{1,0:T(8,128)(2,1)}, bf16[384,1536]{1,0:T(8,128)(2,1)S(1)}, u32[]{:S(2)}) copy-start(bf16[384,1536]{1,0:T(8,128)(2,1)S(1)} %collective-permute-done.7) | copy-start | bytes 3538948
  53.2 32.3 %collective-permute-start.8 = (bf16[192,1536]{1,0:T(8,128)(2,1)}, bf16[192,1536]{1,0:T(8,128)(2,1)}, u32[]{:S(2)}, u32[]{:S(2)}) collective-permute-start(bf16[192,1536]{1,0:T(8,128)(2,1)} %slice.8), channel_id=1, source_target_pairs={{0,8},{8,0},{1,9},{9,1},{2,10},{10,2},{3,11},{11,3},{4,12},{12,4},... | collective-permute-start | bytes 1769480 | tf_op jit(solution)/shard_map/ppermute | solution.py:23
  55.2 30.2 %collective-permute-start.10 = (bf16[192,1536]{1,0:T(8,128)(2,1)}, bf16[192,1536]{1,0:T(8,128)(2,1)}, u32[]{:S(2)}, u32[]{:S(2)}) collective-permute-start(bf16[192,1536]{1,0:T(8,128)(2,1)} %slice.9), channel_id=1, source_target_pairs={{0,4},{4,0},{1,5},{5,1},{2,6},{6,2},{3,7},{7,3},{8,12},{12,8},{9,1... | collective-permute-start | bytes 1769480 | tf_op jit(solution)/shard_map/ppermute | solution.py:23
  57.6 42.9 %collective-permute-start.13 = (bf16[2,384,1536]{2,1,0:T(8,128)(2,1)S(1)}, bf16[2,384,1536]{2,1,0:T(8,128)(2,1)}, u32[]{:S(2)}, u32[]{:S(2)}) collective-permute-start(bf16[2,384,1536]{2,1,0:T(8,128)(2,1)S(1)} %pad_maximum_fusion.refs_2_), channel_id=1, source_target_pairs={{0,2},{2,0},{1,3},{3,1},{4,6},{6,4},{5,7},{7,5},{8,10},{10,8},{9,1... | collective-permute-start | bytes 7077896 | tf_op jit(solution)/shard_map/ppermute | solution.py:23
  74.8 13.3 %copy-start.4 = (bf16[4,384,512]{2,1,0:T(8,128)(2,1)}, bf16[4,384,512]{2,1,0:T(8,128)(2,1)S(1)}, u32[]{:S(2)}) copy-start(bf16[4,384,512]{2,1,0:T(8,128)(2,1)S(1)} %get-tuple-element.56.refs_0_) | copy-start | bytes 4718596
  74.8 16.3 %collective-permute-start.5 = (bf16[4,384,512]{2,1,0:T(8,128)(2,1)}, bf16[4,384,512]{2,1,0:T(8,128)(2,1)}, u32[]{:S(2)}, u32[]{:S(2)}) collective-permute-start(bf16[4,384,512]{2,1,0:T(8,128)(2,1)} %get-tuple-element.43), channel_id=1, source_target_pairs={{0,2},{2,0},{1,3},{3,1},{4,6},{6,4},{5,7},{7,5},{8,10},{10,8},{9,1... | collective-permute-start | bytes 4718600 | tf_op jit(solution)/shard_map/ppermute | solution.py:23
  88.1 3.8 %collective-permute-start.11 = (bf16[2,256,1536]{2,1,0:T(8,128)(2,1)}, bf16[2,256,1536]{2,1,0:T(8,128)(2,1)}, u32[]{:S(2)}, u32[]{:S(2)}) collective-permute-start(bf16[2,256,1536]{2,1,0:T(8,128)(2,1)} %pad_maximum_fusion.1.refs_2_), channel_id=1, source_target_pairs={{0,2},{2,0},{1,3},{3,1},{4,6},{6,4},{5,7},{7,5},{8,10},{10,8},{9,1... | collective-permute-start | bytes 4718600 | tf_op jit(solution)/shard_map/ppermute | solution.py:23
  88.1 12.4 %collective-permute-start.12 = (bf16[1,384,1536]{2,1,0:T(8,128)(2,1)}, bf16[1,384,1536]{2,1,0:T(8,128)(2,1)}, u32[]{:S(2)}, u32[]{:S(2)}) collective-permute-start(bf16[1,384,1536]{2,1,0:T(8,128)(2,1)} %bitcast.13.refs_0_), channel_id=1, source_target_pairs={{0,2},{2,0},{1,3},{3,1},{4,6},{6,4},{5,7},{7,5},{8,10},{10,8},{9,1... | collective-permute-start | bytes 3538952 | tf_op jit(solution)/shard_map/ppermute | solution.py:23
  91.1 9.5 %collective-permute-start.14 = (bf16[1,384,1536]{2,1,0:T(8,128)(2,1)}, bf16[1,384,1536]{2,1,0:T(8,128)(2,1)}, u32[]{:S(2)}, u32[]{:S(2)}) collective-permute-start(bf16[1,384,1536]{2,1,0:T(8,128)(2,1)} %maximum_bitcast_fusion.refs_4_), channel_id=1, source_target_pairs={{0,2},{2,0},{1,3},{3,1},{4,6},{6,4},{5,7},{7,5},{8,10},{10,8},{9,1... | collective-permute-start | bytes 3538952 | tf_op jit(solution)/shard_map/ppermute | solution.py:23
  91.9 1.4 copy-start.5
  99.0 0.9 copy-start.7
  99.9 40.6 %collective-permute-start.17 = (bf16[2,384,1024]{2,1,0:T(8,128)(2,1)}, bf16[2,384,1024]{2,1,0:T(8,128)(2,1)}, u32[]{:S(2)}, u32[]{:S(2)}) collective-permute-start(bf16[2,384,1024]{2,1,0:T(8,128)(2,1)} %get-tuple-element.46), channel_id=1, source_target_pairs={{0,4},{4,0},{1,5},{5,1},{2,6},{6,2},{3,7},{7,3},{8,12},{12,8},{9,1... | collective-permute-start | bytes 4718600 | tf_op jit(solution)/shard_map/ppermute | solution.py:23
  107.1 0.7 copy-start.8
  107.8 0.7 copy-start.10
  108.5 14.8 %collective-permute-start.15 = (bf16[256,512]{1,0:T(8,128)(2,1)}, bf16[256,512]{1,0:T(8,128)(2,1)}, u32[]{:S(2)}, u32[]{:S(2)}) collective-permute-start(bf16[256,512]{1,0:T(8,128)(2,1)} %get-tuple-element.53), channel_id=1, source_target_pairs={{0,16},{16,0},{1,17},{17,1},{2,18},{18,2},{3,19},{19,3},{4,20},{20... | collective-permute-start | bytes 786440 | tf_op jit(solution)/shard_map/ppermute | solution.py:23
  108.6 9.3 %copy-start.6 = (bf16[4,384,512]{2,1,0:T(8,128)(2,1)S(1)}, bf16[4,384,512]{2,1,0:T(8,128)(2,1)}, u32[]{:S(2)}) copy-start(bf16[4,384,512]{2,1,0:T(8,128)(2,1)} %copy-done.4) | copy-start | bytes 4718596
  108.6 37.6 %collective-permute-start.19 = (bf16[2,384,512]{2,1,0:T(8,128)(2,1)}, bf16[2,384,512]{2,1,0:T(8,128)(2,1)S(1)}, u32[]{:S(2)}, u32[]{:S(2)}) collective-permute-start(bf16[2,384,512]{2,1,0:T(8,128)(2,1)} %copy-done.7), channel_id=1, source_target_pairs={{0,8},{8,0},{1,9},{9,1},{2,10},{10,2},{3,11},{11,3},{4,12},{12,4},... | collective-permute-start | bytes 2359304 | tf_op jit(solution)/shard_map/ppermute | solution.py:23
  117.9 5.5 %copy-start.11 = (bf16[256,512]{1,0:T(8,128)(2,1)S(1)}, bf16[256,512]{1,0:T(8,128)(2,1)}, u32[]{:S(2)}) copy-start(bf16[256,512]{1,0:T(8,128)(2,1)} %copy-done.10) | copy-start | bytes 786436
  117.9 5.5 %copy-start.1 = (bf16[2,128,1536]{2,1,0:T(8,128)(2,1)S(1)}, bf16[2,128,1536]{2,1,0:T(8,128)(2,1)}, u32[]{:S(2)}) copy-start(bf16[2,128,1536]{2,1,0:T(8,128)(2,1)} %copy-done) | copy-start | bytes 2359300
  117.9 5.5 %copy-start.3 = (bf16[1,128,1536]{2,1,0:T(8,128)(2,1)S(1)}, bf16[1,128,1536]{2,1,0:T(8,128)(2,1)}, u32[]{:S(2)}) copy-start(bf16[1,128,1536]{2,1,0:T(8,128)(2,1)} %copy-done.2) | copy-start | bytes 1179652
  123.3 13.7 %collective-permute-start.16 = (bf16[256,512]{1,0:T(8,128)(2,1)S(1)}, bf16[256,512]{1,0:T(8,128)(2,1)S(1)}, u32[]{:S(2)}, u32[]{:S(2)}) collective-permute-start(bf16[256,512]{1,0:T(8,128)(2,1)S(1)} %copy-done.11), channel_id=1, source_target_pairs={{0,16},{16,0},{1,17},{17,1},{2,18},{18,2},{3,19},{19,3},{4,20},{20... | collective-permute-start | bytes 786440 | tf_op jit(solution)/shard_map/ppermute | solution.py:23
  127.3 9.7 %copy-start.9 = (bf16[256,512]{1,0:T(8,128)(2,1)S(1)}, bf16[256,512]{1,0:T(8,128)(2,1)}, u32[]{:S(2)}) copy-start(bf16[256,512]{1,0:T(8,128)(2,1)} %copy-done.8) | copy-start | bytes 786436
  127.5 24.5 %collective-permute-start.20 = (bf16[3,128,512]{2,1,0:T(8,128)(2,1)S(1)}, bf16[3,128,512]{2,1,0:T(8,128)(2,1)S(1)}, u32[]{:S(2)}, u32[]{:S(2)}) collective-permute-start(bf16[3,128,512]{2,1,0:T(8,128)(2,1)S(1)} %get-tuple-element.72), channel_id=1, source_target_pairs={{0,1},{1,0},{2,3},{3,2},{4,5},{5,4},{6,7},{7,6},{8,9},{9,8},{10,11... | collective-permute-start | bytes 1179656 | tf_op jit(solution)/shard_map/ppermute | solution.py:23
  137.1 14.9 %collective-permute-start.18 = (bf16[256,512]{1,0:T(8,128)(2,1)S(1)}, bf16[256,512]{1,0:T(8,128)(2,1)S(1)}, u32[]{:S(2)}, u32[]{:S(2)}) collective-permute-start(bf16[256,512]{1,0:T(8,128)(2,1)S(1)} %copy-done.9), channel_id=1, source_target_pairs={{0,16},{16,0},{1,17},{17,1},{2,18},{18,2},{3,19},{19,3},{4,20},{20... | collective-permute-start | bytes 786440 | tf_op jit(solution)/shard_map/ppermute | solution.py:23
  142.7 21.9 %collective-permute-start.23 = (bf16[1,384,1024]{2,1,0:T(8,128)(2,1)S(1)}, bf16[1,384,1024]{2,1,0:T(8,128)(2,1)S(1)}, u32[]{:S(2)}, u32[]{:S(2)}) collective-permute-start(bf16[1,384,1024]{2,1,0:T(8,128)(2,1)S(1)} %dynamic-slice_convert_fusion), channel_id=1, source_target_pairs={{0,8},{8,0},{1,9},{9,1},{2,10},{10,2},{3,11},{11,3},{4,12},{12,4},... | collective-permute-start | bytes 2359304 | tf_op jit(solution)/shard_map/ppermute | solution.py:23
  146.2 10.1 %collective-permute-start.21 = (bf16[3,128,512]{2,1,0:T(8,128)(2,1)S(1)}, bf16[3,128,512]{2,1,0:T(8,128)(2,1)S(1)}, u32[]{:S(2)}, u32[]{:S(2)}) collective-permute-start(bf16[3,128,512]{2,1,0:T(8,128)(2,1)S(1)} %get-tuple-element.73), channel_id=1, source_target_pairs={{0,1},{1,0},{2,3},{3,2},{4,5},{5,4},{6,7},{7,6},{8,9},{9,8},{10,11... | collective-permute-start | bytes 1179656 | tf_op jit(solution)/shard_map/ppermute | solution.py:23
  147.1 13.0 %collective-permute-start.24 = (bf16[1,384,512]{2,1,0:T(8,128)(2,1)S(1)}, bf16[1,384,512]{2,1,0:T(8,128)(2,1)S(1)}, u32[]{:S(2)}, u32[]{:S(2)}) collective-permute-start(bf16[1,384,512]{2,1,0:T(8,128)(2,1)S(1)} %dynamic-slice_convert_fusion.1), channel_id=1, source_target_pairs={{0,4},{4,0},{1,5},{5,1},{2,6},{6,2},{3,7},{7,3},{8,12},{12,8},{9,1... | collective-permute-start | bytes 1179656 | tf_op jit(solution)/shard_map/ppermute | solution.py:23
  159.3 9.2 %collective-permute-start.22 = (bf16[3,128,512]{2,1,0:T(8,128)(2,1)S(1)}, bf16[3,128,512]{2,1,0:T(8,128)(2,1)S(1)}, u32[]{:S(2)}, u32[]{:S(2)}) collective-permute-start(bf16[3,128,512]{2,1,0:T(8,128)(2,1)S(1)} %get-tuple-element.77), channel_id=1, source_target_pairs={{0,1},{1,0},{2,3},{3,2},{4,5},{5,4},{6,7},{7,6},{8,9},{9,8},{10,11... | collective-permute-start | bytes 1179656 | tf_op jit(solution)/shard_map/ppermute | solution.py:23
  168.6 0.9 copy-start.14
  168.6 1.1 copy-start.15
  168.6 1.4 copy-start.16

commit v12 on v11

--- a/solution.py
+++ b/solution.py
@@ -82,7 +82,7 @@
 
 
 def params(length):
-    mebibytes = 32 if length <= 512 else 48
+    mebibytes = 16 if length <= 512 else 48
     return pltpu.CompilerParams(vmem_limit_bytes=mebibytes * 1024 * 1024)
 
 

time: 170 us -> 170 us (level)
  no operation moved by 1% of the time
where the time goes in v12:
time: 170 us
  waiting for transfers between devices  74.8 us (44%)
  Pallas kernels  40.8 us (24%)
  starting transfers between devices  27.5 us (16%)
  local copies, waits for them, and re-layouts  13.4 us (8%)
  other arithmetic  12.5 us (7%)
    ppermute x25, waiting for transfers between devices, shift(): lax.ppermute(array, axis, [(i, (i + by) % count) for i in range(count)])  74.8 us
    pallas_call x9, Pallas kernels, whole_call(): pl.pallas_call(kernel, in_specs=in_specs, out_specs=jax.tree.map(lambda _...  40.8 us
    ppermute x25, starting transfers between devices, shift(): lax.ppermute(array, axis, [(i, (i + by) % count) for i in range(count)])  27.5 us
    unnamed x36, local copies, waits for them, and re-layouts  5.1 us
    dynamic_slice x3, local copies, waits for them, and re-layouts, part_of(): return lax.dynamic_slice_in_dim(array, at * size, size, dim)  4.7 us
  transfers between devices with their start and end apart: 25, of which 11 were waited for; matrix products, arithmetic and copies ran while one was open for 12% of the time, Pallas kernels for 24%

profile of v12, /device:TPU:0, one launch (start us, length us, event | category | flops | bytes accessed | tf_op | source)
XLA Modules:
  0.0 170.0 jit_solution(3504554121975734709)
XLA Ops:
  0.6 3.0 %collective-permute-start.7 = (bf16[384,1536]{1,0:T(8,128)(2,1)}, bf16[384,1536]{1,0:T(8,128)(2,1)S(1)}, u32[]{:S(2)}, u32[]{:S(2)}) collective-permute-start(bf16[384,1536]{1,0:T(8,128)(2,1)} %param.9), channel_id=1, source_target_pairs={{0,4},{4,0},{1,5},{5,1},{2,6},{6,2},{3,7},{7,3},{8,12},{12,8},{9,1... | collective-permute-start | bytes 3538952 | tf_op jit(solution)/shard_map/ppermute | solution.py:23
  3.6 1.6 collective-permute-start.9
  5.2 2.2 %constant_dynamic-slice_fusion.1 = (bf16[1,128,1536]{2,1,0:T(8,128)(2,1)S(1)}, bf16[1,128,1536]{2,1,0:T(8,128)(2,1)S(1)}, bf16[1,128,1536]{2,1,0:T(8,128)(2,1)}, bf16[1,128,1536]{2,1,0:T(8,128)(2,1)S(1)}) fusion(bf16[1,128,3072]{2,1,0:T(8,128)(2,1)} %param.7, s32[]{:T(128)S(6)} %select_n.174, s32[]{:T(128)S(6)} %select_n.172, bf16[1,128,3072]{2,1,0:T(8,128)(2,1)} %param.6), kind=kLoop, calls=%fused_computation.33 | loop fusion | bytes 3145736 | tf_op jit(solution)/shard_map/dynamic_slice | solution.py:34
  7.4 0.9 pad_maximum_fusion.3
  8.4 1.5 collective-permute-start
  9.9 2.4 %dynamic-slice_bitcast_fusion = (bf16[128,3072]{1,0:T(8,128)(2,1)S(1)}, bf16[128,3072]{1,0:T(8,128)(2,1)}) fusion(bf16[1,128,6144]{2,1,0:T(8,128)(2,1)} %param.5, s32[]{:T(128)S(6)} %select_n.184, s32[]{:T(128)S(6)} %select_n.182), kind=kLoop, calls=%fused_computation.12 | loop fusion | bytes 3145736 | tf_op jit(solution)/shard_map/dynamic_slice | solution.py:34
  12.3 2.6 %collective-permute-start.2 = (bf16[128,3072]{1,0:T(8,128)(2,1)S(1)}, bf16[128,3072]{1,0:T(8,128)(2,1)}, u32[]{:S(2)}, u32[]{:S(2)}) collective-permute-start(bf16[128,3072]{1,0:T(8,128)(2,1)S(1)} %get-tuple-element.78), channel_id=1, source_target_pairs={{0,16},{16,0},{1,17},{17,1},{2,18},{18,2},{3,19},{19,3},{4,20},{20... | collective-permute-start | bytes 2359304 | tf_op jit(solution)/shard_map/ppermute | solution.py:23
  15.0 0.6 collective-permute-start.1
  15.6 0.1 pad_maximum_fusion.2.own
  15.7 20.1 %collective-permute-done.1.far_values = bf16[1,128,1536]{2,1,0:T(8,128)(2,1)S(1)} collective-permute-done((bf16[1,128,1536]{2,1,0:T(8,128)(2,1)S(1)}, bf16[1,128,1536]{2,1,0:T(8,128)(2,1)S(1)}, u32[]{:S(2)}, u32[]{:S(2)}) %collective-permute-start.1) | collective-permute-done | bytes 393248 | tf_op jit(solution)/shard_map/ppermute | solution.py:23
  35.7 1.5 collective-permute-start.3
  37.3 2.9 %forward.1 = bf16[256,1536]{1,0:T(8,128)(2,1)} custom-call(bf16[3,128,1536]{2,1,0:T(8,128)(2,1)S(1)} %pad_maximum_fusion.2.own, bf16[2,128,1536]{2,1,0:T(8,128)(2,1)S(1)} %collective-permute-done.far_both, bf16[1,128,1536]{2,1,0:T(8,128)(2,1)S(1)} %collective-permute-done.1.far_values), custom_call_target="tpu_custom_call" | custom-call | flops 1024 | bytes 1024 | tf_op jit(solution)/shard_map/forward/pallas_call | solution.py:107
  40.2 7.0 %collective-permute-done.2.refs_2_.own = bf16[128,3072]{1,0:T(8,128)(2,1)} collective-permute-done((bf16[128,3072]{1,0:T(8,128)(2,1)S(1)}, bf16[128,3072]{1,0:T(8,128)(2,1)}, u32[]{:S(2)}, u32[]{:S(2)}) %collective-permute-start.2) | collective-permute-done | bytes 786464 | tf_op jit(solution)/shard_map/ppermute | solution.py:23
  47.2 1.5 collective-permute-start.4
  48.7 3.5 %collective-permute-start.6 = (bf16[256,1536]{1,0:T(8,128)(2,1)}, bf16[256,1536]{1,0:T(8,128)(2,1)}, u32[]{:S(2)}, u32[]{:S(2)}) collective-permute-start(bf16[256,1536]{1,0:T(8,128)(2,1)} %forward.1), channel_id=1, source_target_pairs={{0,16},{16,0},{1,17},{17,1},{2,18},{18,2},{3,19},{19,3},{4,20},{20... | collective-permute-start | bytes 2359304 | tf_op jit(solution)/shard_map/ppermute | solution.py:23
  52.2 0.9 slice.8
  53.2 0.1 collective-permute-start.8
  53.3 1.9 %slice.9 = bf16[192,1536]{1,0:T(8,128)(2,1)} slice(bf16[384,1536]{1,0:T(8,128)(2,1)} %collective-permute-done.9), slice={[192:384], [0:1536]} | slice | bytes 1179648 | tf_op jit(solution)/shard_map/slice | solution.py:317
  55.2 0.5 collective-permute-start.10
  55.8 1.8 %pad_maximum_fusion.refs_2_ = bf16[2,384,1536]{2,1,0:T(8,128)(2,1)S(1)} fusion(bf16[1,384,1536]{2,1,0:T(8,128)(2,1)} %bitcast.15, bf16[1,384,1536]{2,1,0:T(8,128)(2,1)} %bitcast.24), kind=kLoop, calls=%fused_computation.1 | loop fusion | flops 1179648 | bytes 4718592 | tf_op jit(solution)/shard_map/stack | solution.py:318
  57.7 13.1 %collective-permute-done.4.refs_3_.far = bf16[128,3072]{1,0:T(8,128)(2,1)} collective-permute-done((bf16[128,3072]{1,0:T(8,128)(2,1)}, bf16[128,3072]{1,0:T(8,128)(2,1)}, u32[]{:S(2)}, u32[]{:S(2)}) %collective-permute-start.4) | collective-permute-done | bytes 786464 | tf_op jit(solution)/shard_map/ppermute | solution.py:23
  70.8 4.0 %turn.1 = (bf16[4,384,512]{2,1,0:T(8,128)(2,1)S(1)}, bf16[4,384,512]{2,1,0:T(8,128)(2,1)}) custom-call(s32[1]{0:T(128)} %bitcast.10.core_ref, bf16[128,3072]{1,0:T(8,128)(2,1)} %get-tuple-element.48.refs_0_.own, bf16[128,3072]{1,0:T(8,128)(2,1)} %collective-permute-done.3.refs_1_.far, bf16[128,3072]{1,0:T(8,128)(2,1)} %collective-permute-done.2.refs_2_.own, ...), custom_call_target="tpu_custom_call" | custom-call | flops 1024 | bytes 1024 | tf_op jit(solution)/shard_map/turn/pallas_call | solution.py:107
  74.9 10.6 %collective-permute-done.6 = bf16[256,1536]{1,0:T(8,128)(2,1)} collective-permute-done((bf16[256,1536]{1,0:T(8,128)(2,1)}, bf16[256,1536]{1,0:T(8,128)(2,1)}, u32[]{:S(2)}, u32[]{:S(2)}) %collective-permute-start.6) | collective-permute-done | bytes 786464 | tf_op jit(solution)/shard_map/ppermute | solution.py:23
  85.5 2.7 %pad_maximum_fusion.1.refs_2_ = bf16[2,256,1536]{2,1,0:T(8,128)(2,1)} fusion(bf16[1,256,1536]{2,1,0:T(8,128)(2,1)} %bitcast.12, bf16[1,256,1536]{2,1,0:T(8,128)(2,1)} %bitcast.11), kind=kLoop, calls=%fused_computation.3 | loop fusion | flops 786432 | bytes 3145728 | tf_op jit(solution)/shard_map/stack | solution.py:328
  88.1 0.5 collective-permute-start.12
  88.7 2.4 %maximum_bitcast_fusion.refs_4_ = bf16[1,384,1536]{2,1,0:T(8,128)(2,1)} fusion(bf16[192,1536]{1,0:T(8,128)(2,1)} %collective-permute-done.10, bf16[192,1536]{1,0:T(8,128)(2,1)} %collective-permute-done.8), kind=kLoop, calls=%fused_computation.8 | loop fusion | flops 2359296 | bytes 2359296 | tf_op jit(solution)/shard_map/stack | solution.py:331
  91.1 0.1 pad_add_fusion.at_ref
  91.2 0.7 collective-permute-done.11.refs_3_
  91.9 1.4 copy-done.5
  93.3 5.7 %rows.2 = (bf16[2,384,1024]{2,1,0:T(8,128)(2,1)}, bf16[2,384,512]{2,1,0:T(8,128)(2,1)S(1)}) custom-call(s32[4]{0:T(128)S(1)} %pad_add_fusion.at_ref, bf16[4,384,512]{2,1,0:T(8,128)(2,1)S(1)} %copy-done.5, bf16[4,384,512]{2,1,0:T(8,128)(2,1)} %collective-permute-done.5.refs_1_, bf16[2,256,1536]{2,1,0:T(8,128)(2,1)} %pad_maximum_fusion.1.refs_2_, ...), custom_call_target="tpu_custom_call" | custom-call | flops 1024 | bytes 1024 | tf_op jit(solution)/shard_map/rows/pallas_call | solution.py:107
  99.0 0.9 copy-done.7
  99.9 0.5 collective-permute-start.17
  100.4 0.1 stack.70.at_ref
  100.5 6.5 %partial.3 = (bf16[256,512]{1,0:T(8,128)(2,1)}, bf16[256,512]{1,0:T(8,128)(2,1)S(1)}, bf16[256,512]{1,0:T(8,128)(2,1)S(1)}) custom-call(s32[8]{0:T(128)S(1)} %stack.70.at_ref, bf16[128,3072]{1,0:T(8,128)(2,1)} %collective-permute-done.2.refs_2_.own, bf16[128,3072]{1,0:T(8,128)(2,1)} %collective-permute-done.4.refs_3_.far, ...), custom_call_target="tpu_custom_call" | custom-call | flops 1024 | bytes 1024 | tf_op jit(solution)/shard_map/partial/pallas_call | solution.py:107
  107.1 0.7 copy-done.8
  107.8 0.7 copy-done.10
  108.5 0.1 pad_add_fusion.1.at_ref
  108.6 3.0 %collective-permute-start.19 = (bf16[2,384,512]{2,1,0:T(8,128)(2,1)}, bf16[2,384,512]{2,1,0:T(8,128)(2,1)S(1)}, u32[]{:S(2)}, u32[]{:S(2)}) collective-permute-start(bf16[2,384,512]{2,1,0:T(8,128)(2,1)} %copy-done.7), channel_id=1, source_target_pairs={{0,8},{8,0},{1,9},{9,1},{2,10},{10,2},{3,11},{11,3},{4,12},{12,4},... | collective-permute-start | bytes 2359304 | tf_op jit(solution)/shard_map/ppermute | solution.py:23
  111.6 6.2 %partial.2 = (f32[256,512]{1,0:T(8,128)S(1)}, f32[256,512]{1,0:T(8,128)S(1)}, f32[256,512]{1,0:T(8,128)S(1)}) custom-call(s32[8]{0:T(128)S(1)} %stack.70.at_ref, bf16[128,3072]{1,0:T(8,128)(2,1)} %get-tuple-element.48.refs_0_.own, bf16[128,3072]{1,0:T(8,128)(2,1)} %collective-permute-done.3.refs_1_.far, bf16[1,384,1536]{2,1,0:T(8,128)(2,1)} %bitcast.13.refs_0_, ...), custom_call_target="tpu_custom_call" | custom-call | flops 1024 | bytes 1024 | tf_op jit(solution)/shard_map/partial/pallas_call | solution.py:107
  117.9 5.1 %rows.3 = (f32[2,384,1024]{2,1,0:T(8,128)S(1)}, f32[2,384,512]{2,1,0:T(8,128)S(1)}) custom-call(s32[4]{0:T(128)S(1)} %pad_add_fusion.1.at_ref, bf16[4,384,512]{2,1,0:T(8,128)(2,1)S(1)} %copy-done.6, bf16[4,384,512]{2,1,0:T(8,128)(2,1)} %collective-permute-done.5.refs_1_, bf16[2,256,1536]{2,1,0:T(8,128)(2,1)} %pad_maximum_fusion.1.refs_2_, ...), custom_call_target="tpu_custom_call" | custom-call | flops 1024 | bytes 1024 | tf_op jit(solution)/shard_map/rows/pallas_call | solution.py:107
  123.0 0.4 collective-permute-done.15.refs_1_
  123.3 4.0 %backward.3 = (bf16[3,128,512]{2,1,0:T(8,128)(2,1)S(1)}, bf16[3,128,512]{2,1,0:T(8,128)(2,1)S(1)}) custom-call(bf16[3,128,1536]{2,1,0:T(8,128)(2,1)S(1)} %pad_maximum_fusion.2.own, bf16[2,128,1536]{2,1,0:T(8,128)(2,1)S(1)} %copy-done.1, bf16[1,128,1536]{2,1,0:T(8,128)(2,1)S(1)} %copy-done.3, f32[256,512]{1,0:T(8,128)S(1)} %get-tuple-element.52.refs_0_, ...), custom_call_target="tpu_custom_call" | custom-call | flops 1024 | bytes 1024 | tf_op jit(solution)/shard_map/backward/pallas_call | solution.py:107
  127.5 0.6 collective-permute-start.20
  128.2 8.9 %collective-permute-done.16.refs_1_ = bf16[256,512]{1,0:T(8,128)(2,1)S(1)} collective-permute-done((bf16[256,512]{1,0:T(8,128)(2,1)S(1)}, bf16[256,512]{1,0:T(8,128)(2,1)S(1)}, u32[]{:S(2)}, u32[]{:S(2)}) %collective-permute-start.16) | collective-permute-done | bytes 262176 | tf_op jit(solution)/shard_map/ppermute | solution.py:23
  137.1 3.4 %collective-permute-start.18 = (bf16[256,512]{1,0:T(8,128)(2,1)S(1)}, bf16[256,512]{1,0:T(8,128)(2,1)S(1)}, u32[]{:S(2)}, u32[]{:S(2)}) collective-permute-start(bf16[256,512]{1,0:T(8,128)(2,1)S(1)} %copy-done.9), channel_id=1, source_target_pairs={{0,16},{16,0},{1,17},{17,1},{2,18},{18,2},{3,19},{19,3},{4,20},{20... | collective-permute-start | bytes 786440 | tf_op jit(solution)/shard_map/ppermute | solution.py:23
  140.5 2.1 %convert_add_fusion = f32[2,384,1024]{2,1,0:T(8,128)S(1)} fusion(f32[2,384,1024]{2,1,0:T(8,128)S(1)} %get-tuple-element.58, bf16[2,384,1024]{2,1,0:T(8,128)(2,1)} %collective-permute-done.17), kind=kLoop, calls=%fused_computation | loop fusion | flops 1572864 | bytes 7864320 | tf_op jit(solution)/shard_map/add | solution.py:394
  142.6 0.1 dynamic-slice_convert_fusion
  142.7 0.2 collective-permute-start.23
  142.9 3.2 %backward.4 = (bf16[3,128,512]{2,1,0:T(8,128)(2,1)S(1)}, bf16[3,128,512]{2,1,0:T(8,128)(2,1)S(1)}) custom-call(bf16[3,128,1536]{2,1,0:T(8,128)(2,1)S(1)} %pad_maximum_fusion.2.own, bf16[2,128,1536]{2,1,0:T(8,128)(2,1)S(1)} %copy-done.1, bf16[1,128,1536]{2,1,0:T(8,128)(2,1)S(1)} %copy-done.3, f32[256,512]{1,0:T(8,128)S(1)} %get-tuple-element.54.refs_0_, ...), custom_call_target="tpu_custom_call" | custom-call | flops 1024 | bytes 1024 | tf_op jit(solution)/shard_map/backward/pallas_call | solution.py:107
  146.2 0.6 collective-permute-start.21
  146.7 0.2 convert_add_fusion.1
  147.1 1.6 collective-permute-start.24
  148.6 3.3 %collective-permute-done.18.refs_1_ = bf16[256,512]{1,0:T(8,128)(2,1)S(1)} collective-permute-done((bf16[256,512]{1,0:T(8,128)(2,1)S(1)}, bf16[256,512]{1,0:T(8,128)(2,1)S(1)}, u32[]{:S(2)}, u32[]{:S(2)}) %collective-permute-start.18) | collective-permute-done | bytes 262176 | tf_op jit(solution)/shard_map/ppermute | solution.py:23
  152.0 4.3 %collective-permute-done.21 = bf16[3,128,512]{2,1,0:T(8,128)(2,1)S(1)} collective-permute-done((bf16[3,128,512]{2,1,0:T(8,128)(2,1)S(1)}, bf16[3,128,512]{2,1,0:T(8,128)(2,1)S(1)}, u32[]{:S(2)}, u32[]{:S(2)}) %collective-permute-start.21) | collective-permute-done | bytes 393248 | tf_op jit(solution)/shard_map/ppermute | solution.py:23
  156.3 3.0 %backward.5 = (bf16[3,128,512]{2,1,0:T(8,128)(2,1)S(1)}, bf16[3,128,512]{2,1,0:T(8,128)(2,1)S(1)}) custom-call(bf16[3,128,1536]{2,1,0:T(8,128)(2,1)S(1)} %pad_maximum_fusion.2.own, bf16[2,128,1536]{2,1,0:T(8,128)(2,1)S(1)} %copy-done.1, bf16[1,128,1536]{2,1,0:T(8,128)(2,1)S(1)} %copy-done.3, f32[256,512]{1,0:T(8,128)S(1)} %get-tuple-element.55.refs_0_, ...), custom_call_target="tpu_custom_call" | custom-call | flops 1024 | bytes 1024 | tf_op jit(solution)/shard_map/backward/pallas_call | solution.py:107
  159.3 0.6 collective-permute-start.22
  160.1 0.1 add_bitcast_fusion.1
  160.2 4.4 %collective-permute-done.23 = bf16[1,384,1024]{2,1,0:T(8,128)(2,1)S(1)} collective-permute-done((bf16[1,384,1024]{2,1,0:T(8,128)(2,1)S(1)}, bf16[1,384,1024]{2,1,0:T(8,128)(2,1)S(1)}, u32[]{:S(2)}, u32[]{:S(2)}) %collective-permute-start.23) | collective-permute-done | bytes 786464 | tf_op jit(solution)/shard_map/ppermute | solution.py:23
  164.6 0.3 add_bitcast_fusion
  164.9 1.6 maximum_multiply_fusion
  166.4 2.1 %collective-permute-done.22 = bf16[3,128,512]{2,1,0:T(8,128)(2,1)S(1)} collective-permute-done((bf16[3,128,512]{2,1,0:T(8,128)(2,1)S(1)}, bf16[3,128,512]{2,1,0:T(8,128)(2,1)S(1)}, u32[]{:S(2)}, u32[]{:S(2)}) %collective-permute-start.22) | collective-permute-done | bytes 393248 | tf_op jit(solution)/shard_map/ppermute | solution.py:23
  168.6 0.8 copy-done.14
  169.4 0.3 copy-done.15
  169.7 0.3 copy-done.16
  (64 shorter events, 0.8 us)
Async XLA Ops:
  0.6 51.6 %collective-permute-start.7 = (bf16[384,1536]{1,0:T(8,128)(2,1)}, bf16[384,1536]{1,0:T(8,128)(2,1)S(1)}, u32[]{:S(2)}, u32[]{:S(2)}) collective-permute-start(bf16[384,1536]{1,0:T(8,128)(2,1)} %param.9), channel_id=1, source_target_pairs={{0,4},{4,0},{1,5},{5,1},{2,6},{6,2},{3,7},{7,3},{8,12},{12,8},{9,1... | collective-permute-start | bytes 3538952 | tf_op jit(solution)/shard_map/ppermute | solution.py:23
  3.6 49.7 %collective-permute-start.9 = (bf16[384,1536]{1,0:T(8,128)(2,1)}, bf16[384,1536]{1,0:T(8,128)(2,1)}, u32[]{:S(2)}, u32[]{:S(2)}) collective-permute-start(bf16[384,1536]{1,0:T(8,128)(2,1)} %param.9), channel_id=1, source_target_pairs={{0,8},{8,0},{1,9},{9,1},{2,10},{10,2},{3,11},{11,3},{4,12},{12,4},... | collective-permute-start | bytes 3538952 | tf_op jit(solution)/shard_map/ppermute | solution.py:23
  8.4 28.9 %collective-permute-start = (bf16[2,128,1536]{2,1,0:T(8,128)(2,1)}, bf16[2,128,1536]{2,1,0:T(8,128)(2,1)S(1)}, u32[]{:S(2)}, u32[]{:S(2)}) collective-permute-start(bf16[2,128,1536]{2,1,0:T(8,128)(2,1)} %pad_maximum_fusion.3), channel_id=1, source_target_pairs={{0,1},{1,0},{2,3},{3,2},{4,5},{5,4},{6,7},{7,6},{8,9},{9,8},{10,11... | collective-permute-start | bytes 2359304 | tf_op jit(solution)/shard_map/ppermute | solution.py:23
  9.9 5.0 %copy-start.17 = (bf16[1,128,3072]{2,1,0:T(8,128)(2,1)S(1)}, bf16[1,128,3072]{2,1,0:T(8,128)(2,1)}, u32[]{:S(2)}) copy-start(bf16[1,128,3072]{2,1,0:T(8,128)(2,1)} %param.8) | copy-start | bytes 2359300
  12.3 3.2 %copy-start.13 = (bf16[1,128,1536]{2,1,0:T(8,128)(2,1)S(1)}, bf16[1,128,1536]{2,1,0:T(8,128)(2,1)}, u32[]{:S(2)}) copy-start(bf16[1,128,1536]{2,1,0:T(8,128)(2,1)} %get-tuple-element.101) | copy-start | bytes 1179652
  12.3 34.9 %collective-permute-start.2 = (bf16[128,3072]{1,0:T(8,128)(2,1)S(1)}, bf16[128,3072]{1,0:T(8,128)(2,1)}, u32[]{:S(2)}, u32[]{:S(2)}) collective-permute-start(bf16[128,3072]{1,0:T(8,128)(2,1)S(1)} %get-tuple-element.78), channel_id=1, source_target_pairs={{0,16},{16,0},{1,17},{17,1},{2,18},{18,2},{3,19},{19,3},{4,20},{20... | collective-permute-start | bytes 2359304 | tf_op jit(solution)/shard_map/ppermute | solution.py:23
  15.0 20.8 %collective-permute-start.1 = (bf16[1,128,1536]{2,1,0:T(8,128)(2,1)S(1)}, bf16[1,128,1536]{2,1,0:T(8,128)(2,1)S(1)}, u32[]{:S(2)}, u32[]{:S(2)}) collective-permute-start(bf16[1,128,1536]{2,1,0:T(8,128)(2,1)S(1)} %get-tuple-element.80), channel_id=1, source_target_pairs={{0,1},{1,0},{2,3},{3,2},{4,5},{5,4},{6,7},{7,6},{8,9},{9,8},{10,11... | collective-permute-start | bytes 1179656 | tf_op jit(solution)/shard_map/ppermute | solution.py:23
  35.7 4.5 %copy-start.2 = (bf16[1,128,1536]{2,1,0:T(8,128)(2,1)}, bf16[1,128,1536]{2,1,0:T(8,128)(2,1)S(1)}, u32[]{:S(2)}) copy-start(bf16[1,128,1536]{2,1,0:T(8,128)(2,1)S(1)} %collective-permute-done.1.far_values) | copy-start | bytes 1179652
  35.7 21.9 %collective-permute-start.3 = (bf16[128,3072]{1,0:T(8,128)(2,1)}, bf16[128,3072]{1,0:T(8,128)(2,1)}, u32[]{:S(2)}, u32[]{:S(2)}) collective-permute-start(bf16[128,3072]{1,0:T(8,128)(2,1)} %get-tuple-element.48.refs_0_.own), channel_id=1, source_target_pairs={{0,1},{1,0},{2,3},{3,2},{4,5},{5,4},{6,7},{7,6},{8,9},{9,8},{10,11... | collective-permute-start | bytes 2359304 | tf_op jit(solution)/shard_map/ppermute | solution.py:23
  37.3 3.0 %copy-start = (bf16[2,128,1536]{2,1,0:T(8,128)(2,1)}, bf16[2,128,1536]{2,1,0:T(8,128)(2,1)S(1)}, u32[]{:S(2)}) copy-start(bf16[2,128,1536]{2,1,0:T(8,128)(2,1)S(1)} %collective-permute-done.far_both) | copy-start | bytes 2359300
  47.2 23.6 %collective-permute-start.4 = (bf16[128,3072]{1,0:T(8,128)(2,1)}, bf16[128,3072]{1,0:T(8,128)(2,1)}, u32[]{:S(2)}, u32[]{:S(2)}) collective-permute-start(bf16[128,3072]{1,0:T(8,128)(2,1)} %collective-permute-done.2.refs_2_.own), channel_id=1, source_target_pairs={{0,1},{1,0},{2,3},{3,2},{4,5},{5,4},{6,7},{7,6},{8,9},{9,8},{10,11... | collective-permute-start | bytes 2359304 | tf_op jit(solution)/shard_map/ppermute | solution.py:23
  48.7 36.7 %collective-permute-start.6 = (bf16[256,1536]{1,0:T(8,128)(2,1)}, bf16[256,1536]{1,0:T(8,128)(2,1)}, u32[]{:S(2)}, u32[]{:S(2)}) collective-permute-start(bf16[256,1536]{1,0:T(8,128)(2,1)} %forward.1), channel_id=1, source_target_pairs={{0,16},{16,0},{1,17},{17,1},{2,18},{18,2},{3,19},{19,3},{4,20},{20... | collective-permute-start | bytes 2359304 | tf_op jit(solution)/shard_map/ppermute | solution.py:23
  52.2 3.5 %copy-start.12 = (bf16[384,1536]{1,0:T(8,128)(2,1)}, bf16[384,1536]{1,0:T(8,128)(2,1)S(1)}, u32[]{:S(2)}) copy-start(bf16[384,1536]{1,0:T(8,128)(2,1)S(1)} %collective-permute-done.7) | copy-start | bytes 3538948
  53.2 32.3 %collective-permute-start.8 = (bf16[192,1536]{1,0:T(8,128)(2,1)}, bf16[192,1536]{1,0:T(8,128)(2,1)}, u32[]{:S(2)}, u32[]{:S(2)}) collective-permute-start(bf16[192,1536]{1,0:T(8,128)(2,1)} %slice.8), channel_id=1, source_target_pairs={{0,8},{8,0},{1,9},{9,1},{2,10},{10,2},{3,11},{11,3},{4,12},{12,4},... | collective-permute-start | bytes 1769480 | tf_op jit(solution)/shard_map/ppermute | solution.py:23
  55.2 30.2 %collective-permute-start.10 = (bf16[192,1536]{1,0:T(8,128)(2,1)}, bf16[192,1536]{1,0:T(8,128)(2,1)}, u32[]{:S(2)}, u32[]{:S(2)}) collective-permute-start(bf16[192,1536]{1,0:T(8,128)(2,1)} %slice.9), channel_id=1, source_target_pairs={{0,4},{4,0},{1,5},{5,1},{2,6},{6,2},{3,7},{7,3},{8,12},{12,8},{9,1... | collective-permute-start | bytes 1769480 | tf_op jit(solution)/shard_map/ppermute | solution.py:23
  57.6 42.9 %collective-permute-start.13 = (bf16[2,384,1536]{2,1,0:T(8,128)(2,1)S(1)}, bf16[2,384,1536]{2,1,0:T(8,128)(2,1)}, u32[]{:S(2)}, u32[]{:S(2)}) collective-permute-start(bf16[2,384,1536]{2,1,0:T(8,128)(2,1)S(1)} %pad_maximum_fusion.refs_2_), channel_id=1, source_target_pairs={{0,2},{2,0},{1,3},{3,1},{4,6},{6,4},{5,7},{7,5},{8,10},{10,8},{9,1... | collective-permute-start | bytes 7077896 | tf_op jit(solution)/shard_map/ppermute | solution.py:23
  74.8 13.3 %copy-start.4 = (bf16[4,384,512]{2,1,0:T(8,128)(2,1)}, bf16[4,384,512]{2,1,0:T(8,128)(2,1)S(1)}, u32[]{:S(2)}) copy-start(bf16[4,384,512]{2,1,0:T(8,128)(2,1)S(1)} %get-tuple-element.56.refs_0_) | copy-start | bytes 4718596
  74.8 16.3 %collective-permute-start.5 = (bf16[4,384,512]{2,1,0:T(8,128)(2,1)}, bf16[4,384,512]{2,1,0:T(8,128)(2,1)}, u32[]{:S(2)}, u32[]{:S(2)}) collective-permute-start(bf16[4,384,512]{2,1,0:T(8,128)(2,1)} %get-tuple-element.43), channel_id=1, source_target_pairs={{0,2},{2,0},{1,3},{3,1},{4,6},{6,4},{5,7},{7,5},{8,10},{10,8},{9,1... | collective-permute-start | bytes 4718600 | tf_op jit(solution)/shard_map/ppermute | solution.py:23
  88.1 3.8 %collective-permute-start.11 = (bf16[2,256,1536]{2,1,0:T(8,128)(2,1)}, bf16[2,256,1536]{2,1,0:T(8,128)(2,1)}, u32[]{:S(2)}, u32[]{:S(2)}) collective-permute-start(bf16[2,256,1536]{2,1,0:T(8,128)(2,1)} %pad_maximum_fusion.1.refs_2_), channel_id=1, source_target_pairs={{0,2},{2,0},{1,3},{3,1},{4,6},{6,4},{5,7},{7,5},{8,10},{10,8},{9,1... | collective-permute-start | bytes 4718600 | tf_op jit(solution)/shard_map/ppermute | solution.py:23
  88.1 12.4 %collective-permute-start.12 = (bf16[1,384,1536]{2,1,0:T(8,128)(2,1)}, bf16[1,384,1536]{2,1,0:T(8,128)(2,1)}, u32[]{:S(2)}, u32[]{:S(2)}) collective-permute-start(bf16[1,384,1536]{2,1,0:T(8,128)(2,1)} %bitcast.13.refs_0_), channel_id=1, source_target_pairs={{0,2},{2,0},{1,3},{3,1},{4,6},{6,4},{5,7},{7,5},{8,10},{10,8},{9,1... | collective-permute-start | bytes 3538952 | tf_op jit(solution)/shard_map/ppermute | solution.py:23
  91.1 9.5 %collective-permute-start.14 = (bf16[1,384,1536]{2,1,0:T(8,128)(2,1)}, bf16[1,384,1536]{2,1,0:T(8,128)(2,1)}, u32[]{:S(2)}, u32[]{:S(2)}) collective-permute-start(bf16[1,384,1536]{2,1,0:T(8,128)(2,1)} %maximum_bitcast_fusion.refs_4_), channel_id=1, source_target_pairs={{0,2},{2,0},{1,3},{3,1},{4,6},{6,4},{5,7},{7,5},{8,10},{10,8},{9,1... | collective-permute-start | bytes 3538952 | tf_op jit(solution)/shard_map/ppermute | solution.py:23
  91.9 1.4 copy-start.5
  99.0 0.9 copy-start.7
  99.9 40.6 %collective-permute-start.17 = (bf16[2,384,1024]{2,1,0:T(8,128)(2,1)}, bf16[2,384,1024]{2,1,0:T(8,128)(2,1)}, u32[]{:S(2)}, u32[]{:S(2)}) collective-permute-start(bf16[2,384,1024]{2,1,0:T(8,128)(2,1)} %get-tuple-element.46), channel_id=1, source_target_pairs={{0,4},{4,0},{1,5},{5,1},{2,6},{6,2},{3,7},{7,3},{8,12},{12,8},{9,1... | collective-permute-start | bytes 4718600 | tf_op jit(solution)/shard_map/ppermute | solution.py:23
  107.1 0.7 copy-start.8
  107.8 0.7 copy-start.10
  108.5 14.8 %collective-permute-start.15 = (bf16[256,512]{1,0:T(8,128)(2,1)}, bf16[256,512]{1,0:T(8,128)(2,1)}, u32[]{:S(2)}, u32[]{:S(2)}) collective-permute-start(bf16[256,512]{1,0:T(8,128)(2,1)} %get-tuple-element.53), channel_id=1, source_target_pairs={{0,16},{16,0},{1,17},{17,1},{2,18},{18,2},{3,19},{19,3},{4,20},{20... | collective-permute-start | bytes 786440 | tf_op jit(solution)/shard_map/ppermute | solution.py:23
  108.6 9.3 %copy-start.6 = (bf16[4,384,512]{2,1,0:T(8,128)(2,1)S(1)}, bf16[4,384,512]{2,1,0:T(8,128)(2,1)}, u32[]{:S(2)}) copy-start(bf16[4,384,512]{2,1,0:T(8,128)(2,1)} %copy-done.4) | copy-start | bytes 4718596
  108.6 37.6 %collective-permute-start.19 = (bf16[2,384,512]{2,1,0:T(8,128)(2,1)}, bf16[2,384,512]{2,1,0:T(8,128)(2,1)S(1)}, u32[]{:S(2)}, u32[]{:S(2)}) collective-permute-start(bf16[2,384,512]{2,1,0:T(8,128)(2,1)} %copy-done.7), channel_id=1, source_target_pairs={{0,8},{8,0},{1,9},{9,1},{2,10},{10,2},{3,11},{11,3},{4,12},{12,4},... | collective-permute-start | bytes 2359304 | tf_op jit(solution)/shard_map/ppermute | solution.py:23
  117.9 5.5 %copy-start.11 = (bf16[256,512]{1,0:T(8,128)(2,1)S(1)}, bf16[256,512]{1,0:T(8,128)(2,1)}, u32[]{:S(2)}) copy-start(bf16[256,512]{1,0:T(8,128)(2,1)} %copy-done.10) | copy-start | bytes 786436
  117.9 5.5 %copy-start.1 = (bf16[2,128,1536]{2,1,0:T(8,128)(2,1)S(1)}, bf16[2,128,1536]{2,1,0:T(8,128)(2,1)}, u32[]{:S(2)}) copy-start(bf16[2,128,1536]{2,1,0:T(8,128)(2,1)} %copy-done) | copy-start | bytes 2359300
  117.9 5.5 %copy-start.3 = (bf16[1,128,1536]{2,1,0:T(8,128)(2,1)S(1)}, bf16[1,128,1536]{2,1,0:T(8,128)(2,1)}, u32[]{:S(2)}) copy-start(bf16[1,128,1536]{2,1,0:T(8,128)(2,1)} %copy-done.2) | copy-start | bytes 1179652
  123.3 13.7 %collective-permute-start.16 = (bf16[256,512]{1,0:T(8,128)(2,1)S(1)}, bf16[256,512]{1,0:T(8,128)(2,1)S(1)}, u32[]{:S(2)}, u32[]{:S(2)}) collective-permute-start(bf16[256,512]{1,0:T(8,128)(2,1)S(1)} %copy-done.11), channel_id=1, source_target_pairs={{0,16},{16,0},{1,17},{17,1},{2,18},{18,2},{3,19},{19,3},{4,20},{20... | collective-permute-start | bytes 786440 | tf_op jit(solution)/shard_map/ppermute | solution.py:23
  127.3 9.7 %copy-start.9 = (bf16[256,512]{1,0:T(8,128)(2,1)S(1)}, bf16[256,512]{1,0:T(8,128)(2,1)}, u32[]{:S(2)}) copy-start(bf16[256,512]{1,0:T(8,128)(2,1)} %copy-done.8) | copy-start | bytes 786436
  127.5 24.5 %collective-permute-start.20 = (bf16[3,128,512]{2,1,0:T(8,128)(2,1)S(1)}, bf16[3,128,512]{2,1,0:T(8,128)(2,1)S(1)}, u32[]{:S(2)}, u32[]{:S(2)}) collective-permute-start(bf16[3,128,512]{2,1,0:T(8,128)(2,1)S(1)} %get-tuple-element.72), channel_id=1, source_target_pairs={{0,1},{1,0},{2,3},{3,2},{4,5},{5,4},{6,7},{7,6},{8,9},{9,8},{10,11... | collective-permute-start | bytes 1179656 | tf_op jit(solution)/shard_map/ppermute | solution.py:23
  137.1 14.9 %collective-permute-start.18 = (bf16[256,512]{1,0:T(8,128)(2,1)S(1)}, bf16[256,512]{1,0:T(8,128)(2,1)S(1)}, u32[]{:S(2)}, u32[]{:S(2)}) collective-permute-start(bf16[256,512]{1,0:T(8,128)(2,1)S(1)} %copy-done.9), channel_id=1, source_target_pairs={{0,16},{16,0},{1,17},{17,1},{2,18},{18,2},{3,19},{19,3},{4,20},{20... | collective-permute-start | bytes 786440 | tf_op jit(solution)/shard_map/ppermute | solution.py:23
  142.7 21.9 %collective-permute-start.23 = (bf16[1,384,1024]{2,1,0:T(8,128)(2,1)S(1)}, bf16[1,384,1024]{2,1,0:T(8,128)(2,1)S(1)}, u32[]{:S(2)}, u32[]{:S(2)}) collective-permute-start(bf16[1,384,1024]{2,1,0:T(8,128)(2,1)S(1)} %dynamic-slice_convert_fusion), channel_id=1, source_target_pairs={{0,8},{8,0},{1,9},{9,1},{2,10},{10,2},{3,11},{11,3},{4,12},{12,4},... | collective-permute-start | bytes 2359304 | tf_op jit(solution)/shard_map/ppermute | solution.py:23
  146.2 10.1 %collective-permute-start.21 = (bf16[3,128,512]{2,1,0:T(8,128)(2,1)S(1)}, bf16[3,128,512]{2,1,0:T(8,128)(2,1)S(1)}, u32[]{:S(2)}, u32[]{:S(2)}) collective-permute-start(bf16[3,128,512]{2,1,0:T(8,128)(2,1)S(1)} %get-tuple-element.73), channel_id=1, source_target_pairs={{0,1},{1,0},{2,3},{3,2},{4,5},{5,4},{6,7},{7,6},{8,9},{9,8},{10,11... | collective-permute-start | bytes 1179656 | tf_op jit(solution)/shard_map/ppermute | solution.py:23
  147.1 13.0 %collective-permute-start.24 = (bf16[1,384,512]{2,1,0:T(8,128)(2,1)S(1)}, bf16[1,384,512]{2,1,0:T(8,128)(2,1)S(1)}, u32[]{:S(2)}, u32[]{:S(2)}) collective-permute-start(bf16[1,384,512]{2,1,0:T(8,128)(2,1)S(1)} %dynamic-slice_convert_fusion.1), channel_id=1, source_target_pairs={{0,4},{4,0},{1,5},{5,1},{2,6},{6,2},{3,7},{7,3},{8,12},{12,8},{9,1... | collective-permute-start | bytes 1179656 | tf_op jit(solution)/shard_map/ppermute | solution.py:23
  159.3 9.2 %collective-permute-start.22 = (bf16[3,128,512]{2,1,0:T(8,128)(2,1)S(1)}, bf16[3,128,512]{2,1,0:T(8,128)(2,1)S(1)}, u32[]{:S(2)}, u32[]{:S(2)}) collective-permute-start(bf16[3,128,512]{2,1,0:T(8,128)(2,1)S(1)} %get-tuple-element.77), channel_id=1, source_target_pairs={{0,1},{1,0},{2,3},{3,2},{4,5},{5,4},{6,7},{7,6},{8,9},{9,8},{10,11... | collective-permute-start | bytes 1179656 | tf_op jit(solution)/shard_map/ppermute | solution.py:23
  168.6 0.9 copy-start.14
  168.6 1.1 copy-start.15
  168.6 1.4 copy-start.16
